TPU v7x, 32 devices: a whole 2x2x4 slice. The times are simulated.
32 devices in a mesh: groups: 2 (over y), wide: 4 (over z), rep: 2 (over x), sub: 2 (over core).
Axes of the slice: x: 2, y: 2, z: 4, core: 2. Of those that a mesh axis runs over, the one named last changes fastest.
Arguments:
- samples: bfloat16 [8, 2, 10, 128, 1024], P(('groups', 'wide'), 'rep', None, None, 'sub'), parts along dimension 0, may hold values from -8 to 8
- centroids: float32 [8192, 1024], P(('groups', 'wide'), 'sub'), parts along dimension 0, may hold values from -6 to 6
- move_target: int32 [8, 2, 10], P(('groups', 'wide'), 'rep'), parts along dimension 0, may hold values from -1 to 31, as said below
- fetch_ids: int32 [8, 2, 24], P(('groups', 'wide'), 'rep'), parts along dimension 0, may hold values from 0 to 31, as said below
- cand: int32 [8, 2, 8, 8], P(('groups', 'wide'), 'rep'), parts along dimension 0, may hold values from 0 to 23
Outputs:
- new_centroids: float32 [8192, 1024], P(('groups', 'wide', 'rep'), 'sub'), parts along dimension 0
- energy: float32 [8, 2, 8, 128], P(('groups', 'wide'), 'rep', None, 'sub'), parts along dimension 0
There are 2 independent parts, one for each index of `groups`. A program takes and returns all parts, laid end to end along the dimension named above; each array names one. Nothing has to cross between parts.
Inputs may be any that keep to these rules, and one draw needn't show every extreme that they name: `move_target`: entry slots below 8 keep their block on its own device or are -1; entry slot 8 + k - 1, for k = 1 to 2, goes to a work slot of the device k indices further along wide (cyclically) or is -1; within each index of rep the targets are distinct, and a device's filled work slots are the lowest ones; some device hands away 2 blocks. `fetch_ids`: at most 9 of one device's fetched blocks belong to one owner (owner of block g: index g // 8 of wide), and some owner has exactly 9 for every device.
All inputs are finite; a program needn't handle non-finite values.
Results may differ from a plain program's by a relative error of at most 0.0033.
Values may be sent and summed in bfloat16 or wider, within the bound.
No kernel may reach another device: no remote copies, remote signals or barrier semaphores. Data moves between devices by JAX's collectives and lax.ppermute only.
A program may use at most 64 MiB of HBM per device.

v0:
```python
import math

import jax
import jax.numpy as jnp
from jax import lax
from jax.sharding import PartitionSpec as P

D = 1024


PRIOR = 1.0


def passed_along(value, axis, steps):
    count = lax.axis_size(axis)
    pairs = [(source, (source + steps) % count) for source in range(count)]
    return lax.ppermute(value, axis, pairs)


def pick_rows(table, index, present):
    picked = jnp.take(table, jnp.maximum(index, 0), axis=0)
    shape = (present.shape[0],) + (1,) * (picked.ndim - 1)
    return jnp.where(present.reshape(shape), picked, jnp.zeros_like(picked))


def soften(scores, tau):
    logits = scores / tau
    top = jnp.max(logits, axis=-1, keepdims=True)
    expo = jnp.exp(logits - top)
    total = jnp.sum(expo, axis=-1, keepdims=True)
    weights = (expo / total).astype(jnp.bfloat16)
    energy = -tau * (top[..., 0] + jnp.log(total[..., 0])) / D
    return (weights, energy)


def body(samples, centroids, move_target, fetch_ids, cand):
    rows = samples.shape[3]
    width = samples.shape[4]
    slots_in = samples.shape[2]
    bal = cand.shape[2]
    lists = cand.shape[3]
    pool = fetch_ids.shape[2]
    owned = centroids.shape[0] // rows
    peers = lax.axis_size("wide")
    myself = lax.axis_index("wide")
    cap = max(1, 3 * pool // (2 * peers))
    tau = 2.0 * math.sqrt(D)
    handed = slots_in - bal
    blocks = samples.reshape(slots_in, rows, width)
    target = move_target.reshape(slots_in)
    dest = jnp.where(target >= 0, target // bal, -1)
    dest_slot = jnp.where(target >= 0, target % bal, -1)
    got_list = []
    slot_list = []
    for step in range(handed):
        entry = bal + step
        present = target[entry] >= 0
        send_block = jnp.where(present, blocks[entry], jnp.zeros_like(blocks[entry]))[None]
        send_slot = jnp.where(present, target[entry] % bal, -1).reshape(1)
        got_block, got_slot = passed_along((send_block, send_slot), "wide", step + 1)
        got_list.append(got_block)
        slot_list.append(got_slot)
    ids = fetch_ids.reshape(pool)
    owner = ids // owned
    local = ids % owned
    before = jnp.arange(pool)[None, :] < jnp.arange(pool)[:, None]
    position = jnp.sum(((owner[None, :] == owner[:, None]) & before).astype(jnp.int32), axis=1)
    slot_of = owner * cap + position
    slot_match = slot_of[None, :] == jnp.arange(peers * cap, dtype=jnp.int32)[:, None]
    slot_used = jnp.any(slot_match, axis=1)
    slot_item = jnp.sum(
        jnp.where(slot_match, jnp.arange(pool, dtype=jnp.int32)[None, :], 0), axis=1
    )
    asks = jnp.where(slot_used, jnp.take(local, slot_item), -1).reshape(peers, cap)
    wanted = lax.all_to_all(asks, "wide", split_axis=0, concat_axis=0, tiled=True)
    table = centroids.reshape(owned, rows, width)
    table_half = table.astype(jnp.bfloat16)
    wanted_flat = wanted.reshape(peers * cap)
    reply = pick_rows(table_half, wanted_flat, wanted_flat >= 0).reshape(peers, cap, rows, width)
    answered = lax.all_to_all(reply, "wide", split_axis=0, concat_axis=0, tiled=True)
    fetched = jnp.take(answered.reshape(peers * cap, rows, width), slot_of, axis=0)
    keep_here = dest == myself
    source_blocks = jnp.concatenate([blocks] + got_list, axis=0)
    source_slots = jnp.concatenate([jnp.where(keep_here, dest_slot, -1)] + slot_list, axis=0)
    fill_match = source_slots[None, :] == jnp.arange(bal, dtype=jnp.int32)[:, None]
    live = jnp.any(fill_match, axis=1)
    anchor = jnp.sum(
        jnp.where(fill_match, jnp.arange(slots_in + handed, dtype=jnp.int32)[None, :], 0), axis=1
    )
    work = pick_rows(source_blocks, anchor, live)
    flat_lists = cand.reshape(bal * lists)
    fetched_sq = jnp.sum(jnp.square(fetched.astype(jnp.float32)), axis=-1)

    def slot_scores(carry, items):
        work_one, lists_one = items
        chosen = jnp.take(fetched, lists_one, axis=0).reshape(lists * rows, width)
        dots = jnp.dot(work_one, chosen.T, preferred_element_type=jnp.float32)
        cent_sq = jnp.take(fetched_sq, lists_one, axis=0).reshape(lists * rows)
        work_sq = jnp.sum(jnp.square(work_one.astype(jnp.float32)), axis=-1)
        return (carry, 2.0 * dots - cent_sq[None, :] - work_sq[:, None])

    unused, partial_scores = lax.scan(slot_scores, 0, (work, cand.reshape(bal, lists)))
    half = rows // lax.axis_size("sub")
    lowest = lax.axis_index("sub") * half
    scores = lax.psum(partial_scores, "sub")
    weights, energy = soften(scores, tau)
    energy = lax.dynamic_slice_in_dim(energy, lowest, half, 1)
    weights = jnp.where(live[:, None, None], weights, jnp.zeros_like(weights))
    energy = jnp.where(live[:, None], energy, jnp.zeros_like(energy))
    pool_range = jnp.arange(pool, dtype=jnp.int32)

    def slot_sums(total, items):
        weights_one, work_one, lists_one = items
        term = jnp.dot(weights_one.T, work_one, preferred_element_type=jnp.float32).reshape(
            lists, rows * width
        )
        hot = (lists_one[None, :] == pool_range[:, None]).astype(jnp.float32)
        return (total + jnp.dot(hot, term, precision=lax.Precision.HIGHEST), 0)

    start_sums = jnp.zeros((pool, rows * width), jnp.float32)
    pooled, unused_two = lax.scan(slot_sums, start_sums, (weights, work, cand.reshape(bal, lists)))
    pool_sums = pooled.astype(jnp.bfloat16)
    mass = jnp.sum(weights.astype(jnp.float32), axis=1).reshape(bal * lists, rows)
    onehot = (flat_lists[None, :] == pool_range[:, None]).astype(jnp.float32)
    pool_mass = jnp.dot(onehot, mass, precision=lax.Precision.HIGHEST).astype(jnp.bfloat16)
    back_sums = pick_rows(pool_sums, slot_item, slot_used).reshape(peers, cap, rows, width)
    back_mass = pick_rows(pool_mass, slot_item, slot_used).reshape(peers, cap, rows)
    came_sums, came_mass = (
        lax.all_to_all(back_sums, "wide", split_axis=0, concat_axis=0, tiled=True),
        lax.all_to_all(back_mass, "wide", split_axis=0, concat_axis=0, tiled=True),
    )
    owner_hot = (wanted_flat[None, :] == jnp.arange(owned, dtype=jnp.int32)[:, None]).astype(
        jnp.bfloat16
    )
    owner_sums = jnp.dot(
        owner_hot, came_sums.reshape(peers * cap, rows * width), preferred_element_type=jnp.float32
    )
    owner_mass = jnp.dot(
        owner_hot, came_mass.reshape(peers * cap, rows), preferred_element_type=jnp.float32
    )
    share_sums, share_mass = (
        lax.psum_scatter(
            owner_sums.reshape(owned, rows, width).astype(jnp.bfloat16),
            "rep",
            scatter_dimension=0,
            tiled=True,
        ).astype(jnp.float32),
        lax.psum_scatter(
            owner_mass.astype(jnp.bfloat16), "rep", scatter_dimension=0, tiled=True
        ).astype(jnp.float32),
    )
    share = share_sums.shape[0]
    first_block = lax.axis_index("rep") * share
    previous = lax.dynamic_slice_in_dim(table, first_block, share, 0)
    fresh = (share_sums + PRIOR * previous) / (share_mass[:, :, None] + PRIOR)
    return (fresh.reshape(share * rows, width), energy.reshape(1, 1, bal, half))


def solution(mesh):
    return jax.shard_map(
        body,
        mesh=mesh,
        in_specs=(
            P(("groups", "wide"), "rep", None, None, "sub"),
            P(("groups", "wide"), "sub"),
            P(("groups", "wide"), "rep", None),
            P(("groups", "wide"), "rep", None),
            P(("groups", "wide"), "rep", None, None),
        ),
        out_specs=(P(("groups", "wide", "rep"), "sub"), P(("groups", "wide"), "rep", None, "sub")),
        check_vma=False,
    )
```

profile of v0, /device:TPU:0, one launch (start us, length us, event | category | flops | bytes accessed | tf_op | source)
XLA Modules:
  0.0 502.1 jit_solution(3141592760214678823)
XLA Ops:
  9.8 6.3 %all-to-all-start = ((s32[4,1,9]{2,1,0:T(1,128)}), s32[4,1,9]{2,1,0:T(1,128)S(1)}, u32[]{:S(2)}, u32[]{:S(2)}) async-start(s32[4,1,9]{2,1,0:T(1,128)} %bitcast.10), calls=%async_computation | async-start | bytes 4096 | tf_op jit(solution)/shard_map/all_to_all | solution.py:75
  16.2 1.7 convert_element_type.40
  17.9 3.7 all-to-all-done
  21.7 4.5 gather_fusion.4
  26.3 5.1 %select_select_fusion.1 = bf16[4,9,128,512]{3,2,1,0:T(8,128)(2,1)} fusion(bf16[4,9,128,512]{3,2,1,0:T(8,128)(2,1)} %bitcast.154, pred[4,9]{1,0:T(4,128)(4,1)S(1)} %get-tuple-element.119, pred[4,9]{1,0:T(4,128)(4,1)S(1)} %get-tuple-element.118), kind=kLoop, calls=%fused_computation.42 | loop fusion | flops 4718592 | bytes 9437256 | tf_op jit(solution)/shard_map/jit(_where)/select_n | solution.py:23
  31.4 5.1 %all-to-all-start.1 = ((bf16[4,9,128,512]{3,2,1,0:T(8,128)(2,1)}), bf16[4,9,128,512]{3,2,1,0:T(8,128)(2,1)}, u32[]{:S(2)}, u32[]{:S(2)}) async-start(bf16[4,9,128,512]{3,2,1,0:T(8,128)(2,1)} %select_select_fusion.1), calls=%async_computation.1 | async-start | bytes 9437184 | tf_op jit(solution)/shard_map/all_to_all | solution.py:80
  39.7 71.7 %collective-permute-start = (s32[1]{0:T(128)}, s32[1]{0:T(128)}, u32[]{:S(2)}, u32[]{:S(2)}) collective-permute-start(s32[1]{0:T(128)} %bitcast.15), channel_id=1, source_target_pairs={{0,4},{4,8},{8,12},{12,0},{1,5},{5,9},{9,13},{13,1},{2,6},{6,10},{... | collective-permute-start | bytes 20 | tf_op jit(solution)/shard_map/ppermute | solution.py:17
  115.5 27.0 %collective-permute-start.2 = (bf16[1,128,512]{2,1,0:T(8,128)(2,1)S(1)}, bf16[1,128,512]{2,1,0:T(8,128)(2,1)S(1)}, u32[]{:S(2)}, u32[]{:S(2)}) collective-permute-start(bf16[1,128,512]{2,1,0:T(8,128)(2,1)S(1)} %get-tuple-element.116), channel_id=1, source_target_pairs={{0,4},{4,8},{8,12},{12,0},{1,5},{5,9},{9,13},{13,1},{2,6},{6,10},{... | collective-permute-start | bytes 393224 | tf_op jit(solution)/shard_map/ppermute | solution.py:17
  142.5 2.9 collective-permute-start.3
  147.9 2.9 collective-permute-done.3
  152.7 3.1 gather_fusion.5
  155.8 2.7 multiply_reduce_fusion.1
  158.5 52.5 %while.21 = (s32[]{:T(128)}, f32[8,128,1024]{2,1,0:T(8,128)}, bf16[8,128,512]{2,1,0:T(8,128)(2,1)}, s32[8,8]{1,0:T(8,128)S(1)}, bf16[24,128,512]{2,1,0:T(8,128)(2,1)}, /*index=5*/f32[24,128]{1,0:T(8,128)S(1)}, s32[]{:T(128)}) while((s32[]{:T(128)}, f32[8,128,1024]{2,1,0:T(8,128)}, bf16[8,128,512]{2,1,0:T(8,128)(2,1)}, s32[8,8]{1,0:T(8,128)S(1)}, ...), condition=%wide.region_8.9_spmd, body=%wide.region_6.8_spmd.sunk | while | flops 135333840 | bytes 6056249 | solution.py:102
  160.2 2.5 gather_fusion
  162.9 2.2 fusion.54
  166.8 2.5 gather_fusion
  169.4 2.2 fusion.54
  173.3 2.5 gather_fusion
  176.0 2.2 fusion.54
  179.9 2.5 gather_fusion
  182.6 2.2 fusion.54
  186.5 2.5 gather_fusion
  189.2 2.2 fusion.54
  193.1 2.5 gather_fusion
  195.7 2.2 fusion.54
  199.6 2.5 gather_fusion
  202.3 2.2 fusion.54
  206.2 2.5 gather_fusion
  208.9 2.2 fusion.54
  211.3 26.6 %all-reduce.3.cloned.1.call-done = f32[8,128,1024]{2,1,0:T(8,128)} async-done(((f32[8,128,1024]{2,1,0:T(8,128)}), f32[8,128,1024]{2,1,0:T(8,128)}) %all-reduce.3.cloned.1.call-update) | async-done | bytes 4194320 | tf_op jit(solution)/shard_map/psum | solution.py:105
  237.9 2.7 multiply_reduce_fusion.2
  242.2 2.4 convert_reduce_fusion
  244.6 94.3 %while.22 = (s32[]{:T(128)}, f32[24,65536]{1,0:T(8,128)}, s32[8,8]{1,0:T(8,128)S(1)}, bf16[8,128,1024]{2,1,0:T(8,128)(2,1)}, bf16[8,128,512]{2,1,0:T(8,128)(2,1)}, /*index=5*/s32[]{:T(128)}, s32[]{:T(128)}) while((s32[]{:T(128)}, f32[24,65536]{1,0:T(8,128)}, s32[8,8]{1,0:T(8,128)S(1)}, bf16[8,128,1024]{2,1,0:T(8,128)(2,1)}, ...), condition=%wide.region_13.14_spmd.clone, body=%wide.region_12.13_spmd.clone.sunk | while | flops 288358592 | bytes 21365956 | solution.py:121
  244.6 1.4 fusion.58
  246.1 1.7 reshape.602
  247.7 7.1 %convolution_add_fusion.2 = f32[24,65536]{1,0:T(8,128)} fusion(f32[8,65536]{1,0:T(8,128)} %reshape.602, f32[24,65536]{1,0:T(8,128)} %get-tuple-element.225, pred[]{:T(512)S(6)} %compare.36, s32[8]{0:T(128)S(1)} %fusion.59), kind=kOutput, calls=%fused_computation.26.clone.1 | convolution fusion | flops 154140864 | bytes 14680097 | tf_op jit(solution)/shard_map/while/body/eval_jaxpr/dot_general | solution.py:118
  256.2 1.7 reshape.602
  257.9 8.9 %convolution_add_fusion.2 = f32[24,65536]{1,0:T(8,128)} fusion(f32[8,65536]{1,0:T(8,128)} %reshape.602, f32[24,65536]{1,0:T(8,128)} %get-tuple-element.225, pred[]{:T(512)S(6)} %compare.36, s32[8]{0:T(128)S(1)} %fusion.59), kind=kOutput, calls=%fused_computation.26.clone.1 | convolution fusion | flops 154140864 | bytes 14680097 | tf_op jit(solution)/shard_map/while/body/eval_jaxpr/dot_general | solution.py:118
  266.8 1.4 fusion.58
  268.3 1.7 reshape.602
  269.9 8.9 %convolution_add_fusion.2 = f32[24,65536]{1,0:T(8,128)} fusion(f32[8,65536]{1,0:T(8,128)} %reshape.602, f32[24,65536]{1,0:T(8,128)} %get-tuple-element.225, pred[]{:T(512)S(6)} %compare.36, s32[8]{0:T(128)S(1)} %fusion.59), kind=kOutput, calls=%fused_computation.26.clone.1 | convolution fusion | flops 154140864 | bytes 14680097 | tf_op jit(solution)/shard_map/while/body/eval_jaxpr/dot_general | solution.py:118
  280.3 1.7 reshape.602
  281.9 8.9 %convolution_add_fusion.2 = f32[24,65536]{1,0:T(8,128)} fusion(f32[8,65536]{1,0:T(8,128)} %reshape.602, f32[24,65536]{1,0:T(8,128)} %get-tuple-element.225, pred[]{:T(512)S(6)} %compare.36, s32[8]{0:T(128)S(1)} %fusion.59), kind=kOutput, calls=%fused_computation.26.clone.1 | convolution fusion | flops 154140864 | bytes 14680097 | tf_op jit(solution)/shard_map/while/body/eval_jaxpr/dot_general | solution.py:118
  292.3 1.7 reshape.602
  294.0 8.9 %convolution_add_fusion.2 = f32[24,65536]{1,0:T(8,128)} fusion(f32[8,65536]{1,0:T(8,128)} %reshape.602, f32[24,65536]{1,0:T(8,128)} %get-tuple-element.225, pred[]{:T(512)S(6)} %compare.36, s32[8]{0:T(128)S(1)} %fusion.59), kind=kOutput, calls=%fused_computation.26.clone.1 | convolution fusion | flops 154140864 | bytes 14680097 | tf_op jit(solution)/shard_map/while/body/eval_jaxpr/dot_general | solution.py:118
  304.3 1.7 reshape.602
  306.0 8.9 %convolution_add_fusion.2 = f32[24,65536]{1,0:T(8,128)} fusion(f32[8,65536]{1,0:T(8,128)} %reshape.602, f32[24,65536]{1,0:T(8,128)} %get-tuple-element.225, pred[]{:T(512)S(6)} %compare.36, s32[8]{0:T(128)S(1)} %fusion.59), kind=kOutput, calls=%fused_computation.26.clone.1 | convolution fusion | flops 154140864 | bytes 14680097 | tf_op jit(solution)/shard_map/while/body/eval_jaxpr/dot_general | solution.py:118
  316.3 1.7 reshape.602
  318.0 8.9 %convolution_add_fusion.2 = f32[24,65536]{1,0:T(8,128)} fusion(f32[8,65536]{1,0:T(8,128)} %reshape.602, f32[24,65536]{1,0:T(8,128)} %get-tuple-element.225, pred[]{:T(512)S(6)} %compare.36, s32[8]{0:T(128)S(1)} %fusion.59), kind=kOutput, calls=%fused_computation.26.clone.1 | convolution fusion | flops 154140864 | bytes 14680097 | tf_op jit(solution)/shard_map/while/body/eval_jaxpr/dot_general | solution.py:118
  328.3 1.7 reshape.602
  330.0 8.9 %convolution_add_fusion.2 = f32[24,65536]{1,0:T(8,128)} fusion(f32[8,65536]{1,0:T(8,128)} %reshape.602, f32[24,65536]{1,0:T(8,128)} %get-tuple-element.225, pred[]{:T(512)S(6)} %compare.36, s32[8]{0:T(128)S(1)} %fusion.59), kind=kOutput, calls=%fused_computation.26.clone.1 | convolution fusion | flops 154140864 | bytes 14680097 | tf_op jit(solution)/shard_map/while/body/eval_jaxpr/dot_general | solution.py:118
  338.9 3.1 convert_element_type.43
  342.0 6.0 %gather_fusion.6 = bf16[36,65536]{1,0:T(8,128)(2,1)} fusion(bf16[24,65536]{1,0:T(8,128)(2,1)S(1)} %convert_element_type.43, s32[1024]{0:T(1024)S(1)} %get-tuple-element.126), kind=kCustom, calls=%fused_computation.6 | custom fusion | bytes 9437328 | tf_op jit(solution)/shard_map/jit(_take)/gather | solution.py:21
  348.1 4.5 copy.23
  353.0 2.8 select_select_fusion
  355.8 5.2 %all-to-all-start.2 = ((bf16[4,9,128,512]{3,2,1,0:T(8,128)(2,1)}), bf16[4,9,128,512]{3,2,1,0:T(8,128)(2,1)}, u32[]{:S(2)}, u32[]{:S(2)}) async-start(bf16[4,9,128,512]{3,2,1,0:T(8,128)(2,1)} %select_select_fusion), calls=%async_computation.2 | async-start | bytes 9437184 | tf_op jit(solution)/shard_map/all_to_all | solution.py:129
  362.3 103.9 %all-to-all-done.2 = bf16[4,9,128,512]{3,2,1,0:T(8,128)(2,1)} async-done(((bf16[4,9,128,512]{3,2,1,0:T(8,128)(2,1)}), bf16[4,9,128,512]{3,2,1,0:T(8,128)(2,1)}, u32[]{:S(2)}, u32[]{:S(2)}) %all-to-all-start.2) | async-done | bytes 4718624 | tf_op jit(solution)/shard_map/all_to_all | solution.py:129
  466.2 2.6 slice_bitcast_fusion
  468.8 3.1 fusion.22
  476.1 3.3 all-to-all-start.3
  480.0 4.9 all-to-all-done.3
  485.0 5.0 all-reduce
  490.0 3.1 reduce-scatter.2.cloned.1.call-done
  493.1 2.2 add_divide_fusion
  (146 shorter events, 40.5 us)
Async XLA Ops:
  9.8 11.8 %all-to-all-start = ((s32[4,1,9]{2,1,0:T(1,128)}), s32[4,1,9]{2,1,0:T(1,128)S(1)}, u32[]{:S(2)}, u32[]{:S(2)}) async-start(s32[4,1,9]{2,1,0:T(1,128)} %bitcast.10), calls=%async_computation | async-start | bytes 4096 | tf_op jit(solution)/shard_map/all_to_all | solution.py:75
  31.4 5.2 %copy-start.4 = (s32[1,1,10]{2,1,0:T(1,128)S(1)}, s32[1,1,10]{2,1,0:T(1,128)}, u32[]{:S(2)}) copy-start(s32[1,1,10]{2,1,0:T(1,128)} %param.11) | copy-start | bytes 124
  31.4 84.1 %copy-start.2 = (bf16[1,1,10,128,512]{4,3,2,1,0:T(8,128)(2,1)S(1)}, bf16[1,1,10,128,512]{4,3,2,1,0:T(8,128)(2,1)}, u32[]{:S(2)}) copy-start(bf16[1,1,10,128,512]{4,3,2,1,0:T(8,128)(2,1)} %param.9) | copy-start | bytes 3932164
  31.4 114.0 %copy-start.5 = (s32[1,1,24]{2,1,0:T(1,128)S(1)}, s32[1,1,24]{2,1,0:T(1,128)}, u32[]{:S(2)}) copy-start(s32[1,1,24]{2,1,0:T(1,128)} %param.12) | copy-start | bytes 292
  31.4 121.4 %all-to-all-start.1 = ((bf16[4,9,128,512]{3,2,1,0:T(8,128)(2,1)}), bf16[4,9,128,512]{3,2,1,0:T(8,128)(2,1)}, u32[]{:S(2)}, u32[]{:S(2)}) async-start(bf16[4,9,128,512]{3,2,1,0:T(8,128)(2,1)} %select_select_fusion.1), calls=%async_computation.1 | async-start | bytes 9437184 | tf_op jit(solution)/shard_map/all_to_all | solution.py:80
  36.5 201.4 %all-reduce.3.cloned.1.call-start = ((), (), s32[]{:S(2)}) async-start(), calls=%async_computation.5 | async-start | bytes 8388608 | tf_op jit(solution)/shard_map/psum | solution.py:105
  39.7 105.7 %collective-permute-start = (s32[1]{0:T(128)}, s32[1]{0:T(128)}, u32[]{:S(2)}, u32[]{:S(2)}) collective-permute-start(s32[1]{0:T(128)} %bitcast.15), channel_id=1, source_target_pairs={{0,4},{4,8},{8,12},{12,0},{1,5},{5,9},{9,13},{13,1},{2,6},{6,10},{... | collective-permute-start | bytes 20 | tf_op jit(solution)/shard_map/ppermute | solution.py:17
  114.1 31.4 %collective-permute-start.1 = (s32[1]{0:T(128)}, s32[1]{0:T(128)}, u32[]{:S(2)}, u32[]{:S(2)}) collective-permute-start(s32[1]{0:T(128)} %bitcast.17), channel_id=1, source_target_pairs={{0,8},{4,12},{8,0},{12,4},{1,9},{5,13},{9,1},{13,5},{2,10},{6,14},... | collective-permute-start | bytes 20 | tf_op jit(solution)/shard_map/ppermute | solution.py:17
  115.5 32.4 %collective-permute-start.2 = (bf16[1,128,512]{2,1,0:T(8,128)(2,1)S(1)}, bf16[1,128,512]{2,1,0:T(8,128)(2,1)S(1)}, u32[]{:S(2)}, u32[]{:S(2)}) collective-permute-start(bf16[1,128,512]{2,1,0:T(8,128)(2,1)S(1)} %get-tuple-element.116), channel_id=1, source_target_pairs={{0,4},{4,8},{8,12},{12,0},{1,5},{5,9},{9,13},{13,1},{2,6},{6,10},{... | collective-permute-start | bytes 393224 | tf_op jit(solution)/shard_map/ppermute | solution.py:17
  142.5 8.3 %collective-permute-start.3 = (bf16[1,128,512]{2,1,0:T(8,128)(2,1)S(1)}, bf16[1,128,512]{2,1,0:T(8,128)(2,1)S(1)}, u32[]{:S(2)}, u32[]{:S(2)}) collective-permute-start(bf16[1,128,512]{2,1,0:T(8,128)(2,1)S(1)} %get-tuple-element.117), channel_id=1, source_target_pairs={{0,8},{4,12},{8,0},{12,4},{1,9},{5,13},{9,1},{13,5},{2,10},{6,14},... | collective-permute-start | bytes 393224 | tf_op jit(solution)/shard_map/ppermute | solution.py:17
  155.8 2.7 copy-start.3
  237.9 3.4 copy-start
  355.8 110.4 %all-to-all-start.2 = ((bf16[4,9,128,512]{3,2,1,0:T(8,128)(2,1)}), bf16[4,9,128,512]{3,2,1,0:T(8,128)(2,1)}, u32[]{:S(2)}, u32[]{:S(2)}) async-start(bf16[4,9,128,512]{3,2,1,0:T(8,128)(2,1)} %select_select_fusion), calls=%async_computation.2 | async-start | bytes 9437184 | tf_op jit(solution)/shard_map/all_to_all | solution.py:129
  361.0 132.1 %reduce-scatter.2.cloned.1.call-start = ((), (), s32[]{:S(2)}) async-start(), calls=%async_computation.6 | async-start | bytes 1572864 | tf_op jit(solution)/shard_map/reduce_scatter | solution.py:142
  468.8 4.5 copy-start.6
  468.8 24.2 %copy-start.1 = (f32[1024,512]{1,0:T(8,128)S(1)}, f32[1024,512]{1,0:T(8,128)}, u32[]{:S(2)}) copy-start(f32[1024,512]{1,0:T(8,128)} %param.10) | copy-start | bytes 6291460
  476.1 8.8 %all-to-all-start.3 = ((bf16[4,9,128]{2,1,0:T(8,128)(2,1)}), bf16[4,9,128]{2,1,0:T(8,128)(2,1)S(1)}, u32[]{:S(2)}, u32[]{:S(2)}) async-start(bf16[4,9,128]{2,1,0:T(8,128)(2,1)} %select_select_fusion.3), calls=%async_computation.4 | async-start | bytes 32768 | tf_op jit(solution)/shard_map/all_to_all | solution.py:130
Sparse Core Ops, SparseCore 0:
  211.2 26.6 all-reduce.2
  473.4 19.6 reduce-scatter.1
where the time goes:
time: 504 us; the launch traced here: 502 us
  waiting for transfers between devices  146 us (29%)
  starting transfers between devices  123 us (24%)
  matrix products  102 us (20%)
  local copies, waits for them, and re-layouts  65.6 us (13%)
  other arithmetic  40.3 us (8%)
  between operations  20.1 us (4%)
    all_to_all x1, waiting for transfers between devices, body(): lax.all_to_all(back_sums, 'wide', split_axis=0, concat_axis=0, tiled=True)  104 us
    ppermute x4, starting transfers between devices, passed_along(): return lax.ppermute(value, axis, pairs)  103 us
    dot_general x8, matrix products, slot_sums(): return (total + jnp.dot(hot, term, precision=lax.Precision.HIGHEST), 0)  69.4 us
    psum x1, waiting for transfers between devices, body(): scores = lax.psum(partial_scores, 'sub')  26.6 us
    gather x8, local copies, waits for them, and re-layouts, slot_scores(): chosen = jnp.take(fetched, lists_one, axis=0).reshape(lists * rows, width)  20 us
    dot_general x8, matrix products, slot_scores(): dots = jnp.dot(work_one, chosen.T, preferred_element_type=jnp.float32)  17.6 us
    reshape x8, local copies, waits for them, and re-layouts, slot_sums(): jnp.dot(weights_one.T, work_one, preferred_element_type=jnp.float32)  13.4 us
    gather x5, local copies, waits for them, and re-layouts, pick_rows(): picked = jnp.take(table, jnp.maximum(index, 0), axis=0)  11.8 us
  transfers between devices with their start and end apart: 10, of which 7 were waited for; matrix products, arithmetic and copies ran while one was open for 2% of the time, Pallas kernels for 0%

commit v1 on v0

--- a/solution.py
+++ b/solution.py
@@ -3,6 +3,8 @@
 import jax
 import jax.numpy as jnp
 from jax import lax
+from jax.experimental import pallas as pl
+from jax.experimental.pallas import tpu as pltpu
 from jax.sharding import PartitionSpec as P
 
 D = 1024
@@ -33,7 +35,7 @@
     return (weights, energy)
 
 
-def body(samples, centroids, move_target, fetch_ids, cand):
+def exchange_plan(samples, centroids, move_target, fetch_ids, cand):
     rows = samples.shape[3]
     width = samples.shape[4]
     slots_in = samples.shape[2]
@@ -156,6 +158,269 @@
     return (fresh.reshape(share * rows, width), energy.reshape(1, 1, bal, half))
 
 
+LOW = -1e30
+MEGA = 2**20
+
+
+def swapped(value, axis):
+    return lax.ppermute(value, axis, [(0, 1), (1, 0)])
+
+
+def score_kernel(mult_ref, x_ref, c_ref, csq_ref, em_ref, stats_ref, *, span, tau):
+    tile = x_ref.shape[0]
+    count = mult_ref.shape[0]
+    rows = c_ref.shape[0] // count
+    places = tile // span
+    first = pl.program_id(0) * places
+    em_ref[...] = lax.dot_general(
+        c_ref[...], x_ref[...], (((1,), (1,)), ((), ())), preferred_element_type=jnp.float32
+    )
+    place = lax.broadcasted_iota(jnp.int32, (1, tile), 1) // span
+    top = jnp.full((1, tile), LOW, jnp.float32)
+    weight = []
+    for g in range(count):
+        m = jnp.zeros((1, tile), jnp.float32)
+        for p in range(places):
+            m = jnp.where(place == p, mult_ref[g, first + p].astype(jnp.float32), m)
+        weight.append(m)
+        part = pl.ds(g * rows, rows)
+        logits = (2.0 * em_ref[part, :] - csq_ref[part, 0:1]) / tau
+        em_ref[part, :] = logits
+        best = jnp.max(logits, axis=0, keepdims=True)
+        top = jnp.maximum(top, jnp.where(m > 0, best, LOW))
+    total = jnp.zeros((1, tile), jnp.float32)
+    for g in range(count):
+        part = pl.ds(g * rows, rows)
+        listed = weight[g] > 0
+        expo = jnp.where(listed, jnp.exp(jnp.where(listed, em_ref[part, :] - top, 0.0)), 0.0)
+        expo = expo * weight[g]
+        em_ref[part, :] = expo
+        total = total + jnp.sum(expo, axis=0, keepdims=True)
+    stats_ref[...] = jnp.concatenate([top, total], axis=0)
+
+
+def score_chunk(mult, x, cent, cent_sq, span, tau):
+    lanes, depth = x.shape
+    owned_rows = cent.shape[0]
+    tile = 256
+    return pl.pallas_call(
+        lambda *refs: score_kernel(*refs, span=span, tau=tau),
+        grid=(lanes // tile,),
+        in_specs=[
+            pl.BlockSpec(memory_space=pltpu.SMEM),
+            pl.BlockSpec((tile, depth), lambda i: (i, 0)),
+            pl.BlockSpec((owned_rows, depth), lambda i: (0, 0)),
+            pl.BlockSpec((owned_rows, 128), lambda i: (0, 0)),
+        ],
+        out_specs=[
+            pl.BlockSpec((owned_rows, tile), lambda i: (0, i)),
+            pl.BlockSpec((2, tile), lambda i: (0, i)),
+        ],
+        out_shape=[
+            jax.ShapeDtypeStruct((owned_rows, lanes), jnp.float32),
+            jax.ShapeDtypeStruct((2, lanes), jnp.float32),
+        ],
+        compiler_params=pltpu.CompilerParams(vmem_limit_bytes=40 * MEGA),
+        cost_estimate=pl.CostEstimate(
+            flops=2 * lanes * owned_rows * depth,
+            bytes_accessed=4 * lanes * owned_rows,
+            transcendentals=lanes * owned_rows,
+        ),
+        name="chunk_scores",
+    )(mult, x, cent, cent_sq)
+
+
+def aligned(stats, chunk, chunks):
+    return [stats[k][(chunk - k) % chunks] for k in range(chunks)]
+
+
+def combine(parts):
+    top = parts[0][0:1]
+    for part in parts[1:]:
+        top = jnp.maximum(top, part[0:1])
+    total = jnp.zeros_like(top)
+    for part in parts:
+        total = total + part[1:2] * jnp.exp(part[0:1] - top)
+    return top, total
+
+
+def sums_kernel(half_ref, *refs, chunks):
+    em = refs[:chunks]
+    xs = refs[chunks : 2 * chunks]
+    stats = refs[2 * chunks : 3 * chunks]
+    own_ref, other_ref = refs[3 * chunks : 3 * chunks + 2]
+    em_v, x_v, sems = refs[3 * chunks + 2 :]
+    count, lanes = em_v.shape[1:]
+    width = own_ref.shape[1]
+    start = pl.multiple_of(half_ref[0] * count, count)
+    copies = []
+    for s in range(chunks):
+        pair = (
+            pltpu.make_async_copy(em[s].at[pl.ds(start, count), :], em_v.at[s], sems.at[2 * s]),
+            pltpu.make_async_copy(xs[s], x_v.at[s], sems.at[2 * s + 1]),
+        )
+        for copy in pair:
+            copy.start()
+        copies.append(pair)
+    sums = jnp.zeros((count, 2 * width), jnp.float32)
+    mass = jnp.zeros((count, 128), jnp.float32)
+    for s in range(chunks):
+        parts = []
+        for k in range(chunks):
+            c = (s - k) % chunks
+            parts.append(stats[k][:, c * lanes : (c + 1) * lanes])
+        top, total = combine(parts)
+        scale = jnp.exp(parts[0][0:1] - top) * jnp.where(total > 0, 1.0 / total, 0.0)
+        for copy in copies[s]:
+            copy.wait()
+        weights = (em_v[s] * scale).astype(jnp.bfloat16)
+        sums = sums + jnp.dot(weights, x_v[s], preferred_element_type=jnp.float32)
+        wide = weights.astype(jnp.float32)
+        for lane in range(0, lanes, 128):
+            mass = mass + wide[:, lane : lane + 128]
+    mass = jnp.sum(mass, axis=1, keepdims=True)
+    mass = jnp.broadcast_to(mass, (count, 128)).T[0:16]
+    own_ref[0:count, :] = sums[:, :width]
+    own_ref[count : count + 16, :] = mass
+    other_ref[0:count, :] = sums[:, width:].astype(jnp.bfloat16)
+    other_ref[count : count + 16, :] = mass.astype(jnp.bfloat16)
+
+
+def half_sums(half, em, xs, stats):
+    chunks = len(em)
+    lanes, depth = xs[0].shape
+    count = em[0].shape[0] // 2
+    width = depth // 2
+    return pl.pallas_call(
+        lambda *refs: sums_kernel(*refs, chunks=chunks),
+        in_specs=[pl.BlockSpec(memory_space=pltpu.SMEM)]
+        + [pl.BlockSpec(memory_space=pl.ANY)] * (2 * chunks)
+        + [pl.BlockSpec(memory_space=pltpu.VMEM)] * chunks,
+        out_specs=[pl.BlockSpec(memory_space=pltpu.VMEM)] * 2,
+        out_shape=[
+            jax.ShapeDtypeStruct((count + 16, width), jnp.float32),
+            jax.ShapeDtypeStruct((count + 16, width), jnp.bfloat16),
+        ],
+        scratch_shapes=[
+            pltpu.VMEM((chunks, count, lanes), jnp.float32),
+            pltpu.VMEM((chunks, lanes, depth), jnp.bfloat16),
+            pltpu.SemaphoreType.DMA((2 * chunks,)),
+        ],
+        compiler_params=pltpu.CompilerParams(vmem_limit_bytes=40 * MEGA),
+        cost_estimate=pl.CostEstimate(
+            flops=2 * chunks * lanes * count * depth,
+            bytes_accessed=4 * chunks * lanes * (count + depth),
+            transcendentals=0,
+        ),
+        name="half_sums",
+    )(half.reshape(1), *em, *xs, *stats)
+
+
+def gather_plan(samples, centroids, move_target, fetch_ids, cand):
+    rows = samples.shape[3]
+    width = samples.shape[4]
+    slots_in = samples.shape[2]
+    bal = cand.shape[2]
+    lists = cand.shape[3]
+    owned = centroids.shape[0] // rows
+    peers = lax.axis_size("wide")
+    myself = lax.axis_index("wide")
+    rep = lax.axis_index("rep")
+    sub = lax.axis_index("sub")
+    tau = 2.0 * math.sqrt(D)
+    handed = slots_in - bal
+    base = bal - handed
+    span = rows // 2
+    lanes = bal * span
+
+    blocks = samples.reshape(slots_in, rows, width)
+    mine = lax.dynamic_slice_in_dim(blocks, sub * span, span, 1)
+    theirs = lax.dynamic_slice_in_dim(blocks, (1 - sub) * span, span, 1)
+    full = jnp.concatenate([mine, swapped(theirs, "sub")], axis=2)
+    cent_own = centroids.astype(jnp.bfloat16)
+    cent = jnp.concatenate([cent_own, swapped(cent_own, "sub")], axis=1)
+    cent_sq = jnp.sum(jnp.square(cent.astype(jnp.float32)), axis=1, keepdims=True)
+    cent_sq = jnp.broadcast_to(cent_sq, (owned * rows, 128))
+
+    target = move_target.reshape(slots_in)
+    ids = fetch_ids.reshape(-1)
+    listed = cand.reshape(bal * lists)
+    pool_range = jnp.arange(ids.shape[0], dtype=jnp.int32)
+    global_ids = jnp.sum(jnp.where(listed[:, None] == pool_range[None, :], ids[None, :], 0), axis=1)
+    facts_own = jnp.concatenate([target, global_ids])
+    facts = jnp.stack([facts_own] + [passed_along(facts_own, "wide", k) for k in range(1, peers)])
+    targets = facts[:, :slots_in]
+    ids_all = facts[:, slots_in:].reshape(peers, bal, lists)
+    came = jnp.stack(
+        [jnp.roll(targets[:, bal + h], -(h + 1), axis=0) for h in range(handed)], axis=1
+    )
+    got = came >= 0
+    kept = targets[:, :bal]
+    live = kept >= 0
+    before = jnp.arange(bal)[None, :] < jnp.arange(bal)[:, None]
+    rank = jnp.sum((live[:, None, :] & before[None]).astype(jnp.int32), axis=2)
+    before_h = jnp.arange(handed)[None, :] < jnp.arange(handed)[:, None]
+    free_rank = jnp.sum(((~got)[:, None, :] & before_h[None]).astype(jnp.int32), axis=2)
+    want = jnp.concatenate(
+        [jnp.broadcast_to(jnp.arange(base, dtype=jnp.int32), (peers, base)), base + free_rank],
+        axis=1,
+    )
+    match = live[:, None, :] & (rank[:, None, :] == want[:, :, None])
+    kept_slot = jnp.sum(jnp.where(match, kept[:, None, :] % bal + 1, 0), axis=2) - 1
+    last_slot = jnp.where(got, came % bal, kept_slot[:, base:])
+    slot_at = jnp.concatenate([kept_slot[:, :base], last_slot], axis=1)
+    source = jnp.sum(jnp.where(match[0], jnp.arange(bal, dtype=jnp.int32)[None, :], 0), axis=1)
+    my_blocks = myself * owned + jnp.arange(owned, dtype=jnp.int32)
+    times = jnp.sum((ids_all[:, :, :, None] == my_blocks).astype(jnp.int32), axis=2)
+    at_slot = slot_at[:, :, None] == jnp.arange(bal, dtype=jnp.int32)
+    mult = jnp.sum(jnp.where(at_slot[..., None], times[:, None, :, :], 0), axis=2)
+    mult = jnp.swapaxes(mult, 1, 2)
+
+    came_blocks = jnp.stack([passed_along(full[bal + h], "wide", h + 1) for h in range(handed)])
+    packed = jnp.take(full[:bal], source, axis=0)
+    packed = jnp.concatenate(
+        [packed[:base], jnp.where(got[0][:, None, None], came_blocks, packed[base:])], axis=0
+    )
+    work = packed.reshape(lanes, 2 * width)
+    xs = [work] + [passed_along(work, "wide", k) for k in range(1, peers)]
+
+    em = []
+    stats = []
+    for k in range(peers):
+        em_k, stats_k = score_chunk(mult[k], xs[k], cent, cent_sq, span, tau)
+        em.append(em_k)
+        stats.append(stats_k)
+    local = jnp.concatenate(stats, axis=1)
+    all_stats = [local] + [passed_along(local, "wide", k) for k in range(1, peers)]
+
+    own_far, other_far = half_sums(1 - rep, em, xs, all_stats)
+    far = (own_far + swapped(other_far, "sub").astype(jnp.float32)).astype(jnp.bfloat16)
+    came_far = swapped(far, "rep")
+    own_near, other_near = half_sums(rep, em, xs, all_stats)
+    near = own_near + swapped(other_near, "sub").astype(jnp.float32)
+    total = near + came_far.astype(jnp.float32)
+    share = owned * rows // 2
+    previous = lax.dynamic_slice_in_dim(centroids, rep * share, share, 0)
+    fresh = (total[:share] + PRIOR * previous) / (total[share][:, None] + PRIOR)
+
+    parts = [all_stats[k][:, (-k) % peers * lanes :][:, :lanes] for k in range(peers)]
+    top, denom = combine(parts)
+    work_sq = jnp.sum(jnp.square(work.astype(jnp.float32)), axis=1)
+    energy = -tau * (top[0] - work_sq / tau + jnp.log(denom[0])) / D
+    energy = energy.reshape(bal, span)
+    place = slot_at[0][None, :] == jnp.arange(bal, dtype=jnp.int32)[:, None]
+    energy = jnp.sum(jnp.where(place[:, :, None], energy[None], 0.0), axis=1)
+    return (fresh, energy.reshape(1, 1, bal, span))
+
+
+def body(samples, centroids, move_target, fetch_ids, cand):
+    peers = lax.axis_size("wide")
+    pairs = lax.axis_size("rep") == 2 and lax.axis_size("sub") == 2
+    if pairs and peers * cand.shape[2] <= 2 * fetch_ids.shape[2]:
+        return gather_plan(samples, centroids, move_target, fetch_ids, cand)
+    return exchange_plan(samples, centroids, move_target, fetch_ids, cand)
+
+
 def solution(mesh):
     return jax.shard_map(
         body,

time: 504 us -> 179 us (0.36)
  matrix products: 102 us -> 0 us
  starting transfers between devices: 123 us -> 37 us
  waiting for transfers between devices: 146 us -> 80 us
  local copies, waits for them, and re-layouts: 65.6 us -> 20.8 us
  other arithmetic: 40.3 us -> 17.3 us
  Pallas kernels: 0 us -> 22.6 us
  between operations: 20.1 us -> 1.02 us
    all_to_all x4 -> x0, waiting for transfers between devices: 113 us -> none  [the longest x1 104 us: body(): lax.all_to_all(back_sums, 'wide', split_axis=0, concat_axis=0, tiled=True)]
    dot_general x27 -> x0, matrix products: 102 us -> none  [the longest x8 69.4 us: slot_sums(): return (total + jnp.dot(hot, term, precision=lax.Precision.HIGHEST), 0)]
    ppermute x4 -> x11, starting transfers between devices: 103 us -> 34.4 us  [passed_along(): return lax.ppermute(value, axis, pairs)]
    ppermute x4 -> x11, waiting for transfers between devices: 3.81 us -> 69.4 us  [passed_along(): return lax.ppermute(value, axis, pairs)]
    gather x24 -> x1, local copies, waits for them, and re-layouts: 40.2 us -> 0.62 us  [gather_plan(): packed = jnp.take(full[:bal], source, axis=0)]
    psum x1 -> x0, waiting for transfers between devices: 26.6 us -> none  [body(): scores = lax.psum(partial_scores, 'sub')]
    pallas_call x0 -> x6, Pallas kernels: none -> 22.6 us  [the longest x4 13 us: score_chunk(): pl.pallas_call(lambda *refs: score_kernel(*refs, span=span, tau=tau), gri...]
    all_to_all x4 -> x0, starting transfers between devices: 19.8 us -> none  [the longest x1 6.32 us: body(): lax.all_to_all(asks, 'wide', split_axis=0, concat_axis=0, tiled=True)]
  transfers between devices with their start and end apart: 10 -> 16, of which waited for: 7 -> 9; matrix products, arithmetic and copies ran while one was open for 2% -> 10% of each run, Pallas kernels for 0% -> 8%
where the time goes in v1:
time: 179 us
  waiting for transfers between devices  80 us (45%)
  starting transfers between devices  37 us (21%)
  Pallas kernels  22.6 us (13%)
  local copies, waits for them, and re-layouts  20.8 us (12%)
  other arithmetic  17.3 us (10%)
    ppermute x11, waiting for transfers between devices, passed_along(): return lax.ppermute(value, axis, pairs)  69.4 us
    ppermute x11, starting transfers between devices, passed_along(): return lax.ppermute(value, axis, pairs)  34.4 us
    unnamed x37, local copies, waits for them, and re-layouts  15.5 us
    pallas_call x4, Pallas kernels, score_chunk(): pl.pallas_call(lambda *refs: score_kernel(*refs, span=span, tau=tau), gri...  13 us
    ppermute x5, waiting for transfers between devices, swapped(): return lax.ppermute(value, axis, [(0, 1), (1, 0)])  10.7 us
    pallas_call x2, Pallas kernels, half_sums(): pl.pallas_call(lambda *refs: sums_kernel(*refs, chunks=chunks), in_specs=...  9.65 us
  transfers between devices with their start and end apart: 16, of which 9 were waited for; matrix products, arithmetic and copies ran while one was open for 10% of the time, Pallas kernels for 8%

profile of v1, /device:TPU:0, one launch (start us, length us, event | category | flops | bytes accessed | tf_op | source)
XLA Modules:
  0.0 178.7 jit_solution(3327436668192818328)
XLA Ops:
  0.6 0.9 eq.81
  1.5 0.7 select_reduce_fusion.3
  2.3 0.7 pad_add_fusion.7
  3.0 5.0 %collective-permute-start.2 = (s32[74]{0:T(128)S(1)}, s32[74]{0:T(128)S(1)}, u32[]{:S(2)}, u32[]{:S(2)}) collective-permute-start(s32[74]{0:T(128)S(1)} %pad_add_fusion.7), channel_id=1, source_target_pairs={{0,12},{4,0},{8,4},{12,8},{1,13},{5,1},{9,5},{13,9},{2,14},{6,2},{... | collective-permute-start | bytes 896 | tf_op jit(solution)/shard_map/ppermute | solution.py:19
  8.0 1.0 collective-permute-start
  9.0 1.7 convert_element_type.34
  10.9 1.0 dynamic-slice_bitcast_fusion
  11.8 0.5 collective-permute-start.3
  12.3 0.6 slice.140
  12.9 0.5 collective-permute-done
  13.5 0.2 slice_reduce_fusion.2
  13.7 0.2 slice_reduce_fusion.1
  13.8 0.2 slice_reduce_fusion
  14.0 0.7 add_bitcast_fusion
  15.3 0.1 convert_reduce_fusion.1
  15.6 0.2 select_reduce_fusion.2
  16.1 2.1 %collective-permute-start.4 = (bf16[64,1024]{1,0:T(8,128)(2,1)S(1)}, bf16[64,1024]{1,0:T(8,128)(2,1)}, u32[]{:S(2)}, u32[]{:S(2)}) collective-permute-start(bf16[64,1024]{1,0:T(8,128)(2,1)S(1)} %get-tuple-element.32), channel_id=1, source_target_pairs={{0,4},{4,8},{8,12},{12,0},{1,5},{5,9},{9,13},{13,1},{2,6},{6,10},{... | collective-permute-start | bytes 393224 | tf_op jit(solution)/shard_map/ppermute | solution.py:19
  18.2 0.9 collective-permute-start.5
  19.1 1.2 fusion
  20.3 0.6 gather_fusion
  20.9 0.2 broadcast_select_fusion
  21.2 3.2 %collective-permute-done.4 = bf16[64,1024]{1,0:T(8,128)(2,1)} collective-permute-done((bf16[64,1024]{1,0:T(8,128)(2,1)S(1)}, bf16[64,1024]{1,0:T(8,128)(2,1)}, u32[]{:S(2)}, u32[]{:S(2)}) %collective-permute-start.4) | collective-permute-done | bytes 131104 | tf_op jit(solution)/shard_map/ppermute | solution.py:19
  24.3 4.4 %collective-permute-done.5 = bf16[64,1024]{1,0:T(8,128)(2,1)} collective-permute-done((bf16[64,1024]{1,0:T(8,128)(2,1)S(1)}, bf16[64,1024]{1,0:T(8,128)(2,1)}, u32[]{:S(2)}, u32[]{:S(2)}) %collective-permute-start.5) | collective-permute-done | bytes 131104 | tf_op jit(solution)/shard_map/ppermute | solution.py:19
  28.7 1.1 slice_select_fusion
  30.2 1.9 %collective-permute-start.8 = (bf16[512,1024]{1,0:T(8,128)(2,1)S(1)}, bf16[512,1024]{1,0:T(8,128)(2,1)}, u32[]{:S(2)}, u32[]{:S(2)}) collective-permute-start(bf16[512,1024]{1,0:T(8,128)(2,1)S(1)} %bitcast.47), channel_id=1, source_target_pairs={{0,8},{4,12},{8,0},{12,4},{1,9},{5,13},{9,1},{13,5},{2,10},{6,14},... | collective-permute-start | bytes 3145736 | tf_op jit(solution)/shard_map/ppermute | solution.py:19
  32.2 0.1 select_reduce_fusion
  32.3 2.0 %collective-permute-start.9 = (bf16[512,1024]{1,0:T(8,128)(2,1)S(1)}, bf16[512,1024]{1,0:T(8,128)(2,1)}, u32[]{:S(2)}, u32[]{:S(2)}) collective-permute-start(bf16[512,1024]{1,0:T(8,128)(2,1)S(1)} %bitcast.48), channel_id=1, source_target_pairs={{0,12},{4,0},{8,4},{12,8},{1,13},{5,1},{9,5},{13,9},{2,14},{6,2},{... | collective-permute-start | bytes 3145736 | tf_op jit(solution)/shard_map/ppermute | solution.py:19
  34.6 1.7 multiply_reduce_fusion
  36.3 1.5 pad_maximum_fusion.refs_2_
  37.8 0.2 broadcast_in_dim.140.refs_3_
  38.0 2.9 %chunk_scores.4 = (f32[1024,512]{1,0:T(8,128)S(1)}, f32[2,512]{1,0:T(2,128)S(1)}) custom-call(s32[8,8]{1,0:T(8,128)S(1)} %bitcast.55, bf16[512,1024]{1,0:T(8,128)(2,1)S(1)} %bitcast.49, bf16[1024,1024]{1,0:T(8,128)(2,1)S(1)} %pad_maximum_fusion.refs_2_, f32[1024,128]{1,0:T(8,128)S(1)} %broadcast_in_dim.140.refs_3_), custom_call_target="tpu_custom_call" | custom-call | flops 1073741824 | bytes 2097152 | tf_op jit(solution)/shard_map/chunk_scores/pallas_call | solution.py:206
  40.9 17.1 %collective-permute-done.7.refs_1_.refs_6_ = bf16[512,1024]{1,0:T(8,128)(2,1)} collective-permute-done((bf16[512,1024]{1,0:T(8,128)(2,1)S(1)}, bf16[512,1024]{1,0:T(8,128)(2,1)}, u32[]{:S(2)}, u32[]{:S(2)}) %collective-permute-start.7) | collective-permute-done | bytes 1048608 | tf_op jit(solution)/shard_map/ppermute | solution.py:19
  58.0 3.3 %chunk_scores.5 = (f32[1024,512]{1,0:T(8,128)S(1)}, f32[2,512]{1,0:T(2,128)S(1)}) custom-call(s32[8,8]{1,0:T(8,128)S(1)} %bitcast.54, bf16[512,1024]{1,0:T(8,128)(2,1)} %collective-permute-done.7.refs_1_.refs_6_, bf16[1024,1024]{1,0:T(8,128)(2,1)S(1)} %pad_maximum_fusion.refs_2_, f32[1024,128]{1,0:T(8,128)S(1)} %broadcast_in_dim.140.refs_3_), custom_call_target="tpu_custom_call" | custom-call | flops 1073741824 | bytes 2097152 | tf_op jit(solution)/shard_map/chunk_scores/pallas_call | solution.py:206
  61.4 1.3 copy-done
  62.7 39.3 %collective-permute-done.8.refs_1_.refs_7_ = bf16[512,1024]{1,0:T(8,128)(2,1)} collective-permute-done((bf16[512,1024]{1,0:T(8,128)(2,1)S(1)}, bf16[512,1024]{1,0:T(8,128)(2,1)}, u32[]{:S(2)}, u32[]{:S(2)}) %collective-permute-start.8) | collective-permute-done | bytes 1048608 | tf_op jit(solution)/shard_map/ppermute | solution.py:19
  102.0 3.4 %chunk_scores.6 = (f32[1024,512]{1,0:T(8,128)S(1)}, f32[2,512]{1,0:T(2,128)S(1)}) custom-call(s32[8,8]{1,0:T(8,128)S(1)} %bitcast.53, bf16[512,1024]{1,0:T(8,128)(2,1)} %collective-permute-done.8.refs_1_.refs_7_, bf16[1024,1024]{1,0:T(8,128)(2,1)S(1)} %pad_maximum_fusion.refs_2_, f32[1024,128]{1,0:T(8,128)S(1)} %broadcast_in_dim.140.refs_3_), custom_call_target="tpu_custom_call" | custom-call | flops 1073741824 | bytes 2097152 | tf_op jit(solution)/shard_map/chunk_scores/pallas_call | solution.py:206
  105.4 1.3 copy-done.3
  106.7 3.3 %chunk_scores.7 = (f32[1024,512]{1,0:T(8,128)S(1)}, f32[2,512]{1,0:T(2,128)S(1)}) custom-call(s32[8,8]{1,0:T(8,128)S(1)} %bitcast.52, bf16[512,1024]{1,0:T(8,128)(2,1)} %collective-permute-done.9.refs_1_.refs_8_, bf16[1024,1024]{1,0:T(8,128)(2,1)S(1)} %pad_maximum_fusion.refs_2_, f32[1024,128]{1,0:T(8,128)S(1)} %broadcast_in_dim.140.refs_3_), custom_call_target="tpu_custom_call" | custom-call | flops 1073741824 | bytes 2097152 | tf_op jit(solution)/shard_map/chunk_scores/pallas_call | solution.py:206
  110.0 1.3 copy-done.6
  111.4 20.9 %collective-permute-start.12 = (f32[2,2048]{1,0:T(2,128)S(1)}, f32[2,2048]{1,0:T(2,128)S(1)}, u32[]{:S(2)}, u32[]{:S(2)}) collective-permute-start(f32[2,2048]{1,0:T(2,128)S(1)} %constant_dynamic-update-slice_fusion.refs_9_), channel_id=1, source_target_pairs={{0,12},{4,0},{8,4},{12,8},{1,13},{5,1},{9,5},{13,9},{2,14},{6,2},{... | collective-permute-start | bytes 49160 | tf_op jit(solution)/shard_map/ppermute | solution.py:19
  132.2 0.6 collective-permute-start.10
  132.8 0.9 collective-permute-done.12.refs_12_
  133.7 3.2 %collective-permute-done.11.refs_11_ = f32[2,2048]{1,0:T(2,128)S(1)} collective-permute-done((f32[2,2048]{1,0:T(2,128)S(1)}, f32[2,2048]{1,0:T(2,128)S(1)}, u32[]{:S(2)}, u32[]{:S(2)}) %collective-permute-start.11) | collective-permute-done | bytes 16416 | tf_op jit(solution)/shard_map/ppermute | solution.py:19
  136.9 0.9 collective-permute-done.10.refs_10_
  137.8 1.6 copy-done.1
  139.4 1.6 copy-done.4
  141.0 1.6 copy-done.7
  142.6 4.8 %half_sums.3 = (f32[528,512]{1,0:T(8,128)S(1)}, bf16[528,512]{1,0:T(8,128)(2,1)}) custom-call(s32[1]{0:T(128)} %bitcast.26.refs_0_, f32[1024,512]{1,0:T(8,128)S(1)} %get-tuple-element.14.refs_1_, f32[1024,512]{1,0:T(8,128)S(1)} %copy-done.1, f32[1024,512]{1,0:T(8,128)S(1)} %copy-done.4, f32[1024,512]{1,0:T(8,128)S(1)} %copy-done.7, ...), custom_call_target="tpu_custom_call" | custom-call | flops 2147483648 | bytes 12582912 | tf_op jit(solution)/shard_map/half_sums/pallas_call | solution.py:294
  147.3 1.0 copy-done.11
  148.3 1.6 copy-done.2
  149.9 1.6 copy-done.5
  151.5 1.6 copy-done.8
  153.1 4.9 %half_sums.2 = (f32[528,512]{1,0:T(8,128)S(1)}, bf16[528,512]{1,0:T(8,128)(2,1)}) custom-call(s32[1]{0:T(128)} %bitcast.refs_0_, f32[1024,512]{1,0:T(8,128)S(1)} %get-tuple-element.14.refs_1_, f32[1024,512]{1,0:T(8,128)S(1)} %copy-done.2, f32[1024,512]{1,0:T(8,128)S(1)} %copy-done.5, f32[1024,512]{1,0:T(8,128)S(1)} %copy-done.8, ...), custom_call_target="tpu_custom_call" | custom-call | flops 2147483648 | bytes 12582912 | tf_op jit(solution)/shard_map/half_sums/pallas_call | solution.py:294
  158.0 1.0 copy-done.9
  159.0 0.5 collective-permute-start.13
  159.5 2.0 %add_convert_fusion = bf16[528,512]{1,0:T(8,128)(2,1)} fusion(f32[528,512]{1,0:T(8,128)S(1)} %copy-done.12, bf16[528,512]{1,0:T(8,128)(2,1)} %collective-permute-done.14), kind=kLoop, calls=%fused_computation.9 | loop fusion | flops 811008 | bytes 2162688 | tf_op jit(solution)/shard_map/convert_element_type | solution.py:397
  161.6 1.5 collective-permute-start.15
  163.1 0.3 multiply_reduce_fusion.1
  163.3 0.5 broadcast.132
  163.9 0.7 fusion.14
  164.7 0.7 select_reduce_fusion.1
  165.4 10.7 %collective-permute-done.15 = bf16[528,512]{1,0:T(8,128)(2,1)S(1)} collective-permute-done((bf16[528,512]{1,0:T(8,128)(2,1)}, bf16[528,512]{1,0:T(8,128)(2,1)S(1)}, u32[]{:S(2)}, u32[]{:S(2)}) %collective-permute-start.15) | collective-permute-done | bytes 540704 | tf_op jit(solution)/shard_map/ppermute | solution.py:166
  176.1 0.2 convert_add_fusion
  176.3 2.4 %fusion.1 = f32[512,512]{1,0:T(8,128)} fusion(f32[528,512]{1,0:T(8,128)S(1)} %convert_add_fusion, f32[1024,512]{1,0:T(8,128)} %param.6, s32[]{:T(128)S(6)} %select_n.84, f32[512]{0:T(512)S(1)} %bitcast.58), kind=kLoop, calls=%fused_computation.12 | loop fusion | flops 524288 | bytes 3147780 | tf_op jit(solution)/shard_map/div | solution.py:404
  (83 shorter events, 2.2 us)
Async XLA Ops:
  0.6 10.2 %copy-start.16 = (bf16[1,1,10,128,512]{4,3,2,1,0:T(8,128)(2,1)S(1)}, bf16[1,1,10,128,512]{4,3,2,1,0:T(8,128)(2,1)}, u32[]{:S(2)}) copy-start(bf16[1,1,10,128,512]{4,3,2,1,0:T(8,128)(2,1)} %param.5) | copy-start | bytes 3932164
  3.0 10.4 %collective-permute-start.2 = (s32[74]{0:T(128)S(1)}, s32[74]{0:T(128)S(1)}, u32[]{:S(2)}, u32[]{:S(2)}) collective-permute-start(s32[74]{0:T(128)S(1)} %pad_add_fusion.7), channel_id=1, source_target_pairs={{0,12},{4,0},{8,4},{12,8},{1,13},{5,1},{9,5},{13,9},{2,14},{6,2},{... | collective-permute-start | bytes 896 | tf_op jit(solution)/shard_map/ppermute | solution.py:19
  8.0 5.4 %collective-permute-start.1 = (s32[74]{0:T(128)S(1)}, s32[74]{0:T(128)S(1)}, u32[]{:S(2)}, u32[]{:S(2)}) collective-permute-start(s32[74]{0:T(128)S(1)} %pad_add_fusion.7), channel_id=1, source_target_pairs={{0,8},{4,12},{8,0},{12,4},{1,9},{5,13},{9,1},{13,5},{2,10},{6,14},... | collective-permute-start | bytes 896 | tf_op jit(solution)/shard_map/ppermute | solution.py:19
  8.0 5.3 %collective-permute-start = (s32[74]{0:T(128)S(1)}, s32[74]{0:T(128)S(1)}, u32[]{:S(2)}, u32[]{:S(2)}) collective-permute-start(s32[74]{0:T(128)S(1)} %pad_add_fusion.7), channel_id=1, source_target_pairs={{0,4},{4,8},{8,12},{12,0},{1,5},{5,9},{9,13},{13,1},{2,6},{6,10},{... | collective-permute-start | bytes 896 | tf_op jit(solution)/shard_map/ppermute | solution.py:19
  10.8 23.8 %collective-permute-start.6 = (bf16[1024,512]{1,0:T(8,128)(2,1)S(1)}, bf16[1024,512]{1,0:T(8,128)(2,1)}, u32[]{:S(2)}, u32[]{:S(2)}) collective-permute-start(bf16[1024,512]{1,0:T(8,128)(2,1)S(1)} %convert_element_type.34), channel_id=1, source_target_pairs={{0,1},{1,0},{2,3},{3,2},{4,5},{5,4},{6,7},{7,6},{8,9},{9,8},{10,11... | collective-permute-start | bytes 3145736 | tf_op jit(solution)/shard_map/ppermute | solution.py:166
  11.8 4.3 %collective-permute-start.3 = (bf16[10,64,512]{2,1,0:T(8,128)(2,1)}, bf16[10,64,512]{2,1,0:T(8,128)(2,1)S(1)}, u32[]{:S(2)}, u32[]{:S(2)}) collective-permute-start(bf16[10,64,512]{2,1,0:T(8,128)(2,1)} %get-tuple-element.34), channel_id=1, source_target_pairs={{0,1},{1,0},{2,3},{3,2},{4,5},{5,4},{6,7},{7,6},{8,9},{9,8},{10,11... | collective-permute-start | bytes 1966088 | tf_op jit(solution)/shard_map/ppermute | solution.py:166
  16.1 2.1 %copy-start.15 = (bf16[10,64,512]{2,1,0:T(8,128)(2,1)}, bf16[10,64,512]{2,1,0:T(8,128)(2,1)S(1)}, u32[]{:S(2)}) copy-start(bf16[10,64,512]{2,1,0:T(8,128)(2,1)S(1)} %collective-permute-done.3) | copy-start | bytes 1966084
  16.1 8.2 %collective-permute-start.4 = (bf16[64,1024]{1,0:T(8,128)(2,1)S(1)}, bf16[64,1024]{1,0:T(8,128)(2,1)}, u32[]{:S(2)}, u32[]{:S(2)}) collective-permute-start(bf16[64,1024]{1,0:T(8,128)(2,1)S(1)} %get-tuple-element.32), channel_id=1, source_target_pairs={{0,4},{4,8},{8,12},{12,0},{1,5},{5,9},{9,13},{13,1},{2,6},{6,10},{... | collective-permute-start | bytes 393224 | tf_op jit(solution)/shard_map/ppermute | solution.py:19
  18.2 10.5 %collective-permute-start.5 = (bf16[64,1024]{1,0:T(8,128)(2,1)S(1)}, bf16[64,1024]{1,0:T(8,128)(2,1)}, u32[]{:S(2)}, u32[]{:S(2)}) collective-permute-start(bf16[64,1024]{1,0:T(8,128)(2,1)S(1)} %get-tuple-element.33), channel_id=1, source_target_pairs={{0,8},{4,12},{8,0},{12,4},{1,9},{5,13},{9,1},{13,5},{2,10},{6,14},... | collective-permute-start | bytes 393224 | tf_op jit(solution)/shard_map/ppermute | solution.py:19
  21.2 8.7 %copy-start.13 = (bf16[6,64,1024]{2,1,0:T(8,128)(2,1)}, bf16[6,64,1024]{2,1,0:T(8,128)(2,1)S(1)}, u32[]{:S(2)}) copy-start(bf16[6,64,1024]{2,1,0:T(8,128)(2,1)S(1)} %slice.177) | copy-start | bytes 2359300
  29.9 28.1 %collective-permute-start.7 = (bf16[512,1024]{1,0:T(8,128)(2,1)S(1)}, bf16[512,1024]{1,0:T(8,128)(2,1)}, u32[]{:S(2)}, u32[]{:S(2)}) collective-permute-start(bf16[512,1024]{1,0:T(8,128)(2,1)S(1)} %bitcast.46), channel_id=1, source_target_pairs={{0,4},{4,8},{8,12},{12,0},{1,5},{5,9},{9,13},{13,1},{2,6},{6,10},{... | collective-permute-start | bytes 3145736 | tf_op jit(solution)/shard_map/ppermute | solution.py:19
  30.2 71.8 %collective-permute-start.8 = (bf16[512,1024]{1,0:T(8,128)(2,1)S(1)}, bf16[512,1024]{1,0:T(8,128)(2,1)}, u32[]{:S(2)}, u32[]{:S(2)}) collective-permute-start(bf16[512,1024]{1,0:T(8,128)(2,1)S(1)} %bitcast.47), channel_id=1, source_target_pairs={{0,8},{4,12},{8,0},{12,4},{1,9},{5,13},{9,1},{13,5},{2,10},{6,14},... | collective-permute-start | bytes 3145736 | tf_op jit(solution)/shard_map/ppermute | solution.py:19
  32.3 74.4 %collective-permute-start.9 = (bf16[512,1024]{1,0:T(8,128)(2,1)S(1)}, bf16[512,1024]{1,0:T(8,128)(2,1)}, u32[]{:S(2)}, u32[]{:S(2)}) collective-permute-start(bf16[512,1024]{1,0:T(8,128)(2,1)S(1)} %bitcast.48), channel_id=1, source_target_pairs={{0,12},{4,0},{8,4},{12,8},{1,13},{5,1},{9,5},{13,9},{2,14},{6,2},{... | collective-permute-start | bytes 3145736 | tf_op jit(solution)/shard_map/ppermute | solution.py:19
  61.4 1.3 copy-start
  105.4 1.3 copy-start.3
  110.0 1.3 copy-start.6
  111.4 22.3 %collective-permute-start.12 = (f32[2,2048]{1,0:T(2,128)S(1)}, f32[2,2048]{1,0:T(2,128)S(1)}, u32[]{:S(2)}, u32[]{:S(2)}) collective-permute-start(f32[2,2048]{1,0:T(2,128)S(1)} %constant_dynamic-update-slice_fusion.refs_9_), channel_id=1, source_target_pairs={{0,12},{4,0},{8,4},{12,8},{1,13},{5,1},{9,5},{13,9},{2,14},{6,2},{... | collective-permute-start | bytes 49160 | tf_op jit(solution)/shard_map/ppermute | solution.py:19
  132.2 4.6 %collective-permute-start.11 = (f32[2,2048]{1,0:T(2,128)S(1)}, f32[2,2048]{1,0:T(2,128)S(1)}, u32[]{:S(2)}, u32[]{:S(2)}) collective-permute-start(f32[2,2048]{1,0:T(2,128)S(1)} %constant_dynamic-update-slice_fusion.refs_9_), channel_id=1, source_target_pairs={{0,8},{4,12},{8,0},{12,4},{1,9},{5,13},{9,1},{13,5},{2,10},{6,14},... | collective-permute-start | bytes 49160 | tf_op jit(solution)/shard_map/ppermute | solution.py:19
  132.2 5.5 %collective-permute-start.10 = (f32[2,2048]{1,0:T(2,128)S(1)}, f32[2,2048]{1,0:T(2,128)S(1)}, u32[]{:S(2)}, u32[]{:S(2)}) collective-permute-start(f32[2,2048]{1,0:T(2,128)S(1)} %constant_dynamic-update-slice_fusion.refs_9_), channel_id=1, source_target_pairs={{0,4},{4,8},{8,12},{12,0},{1,5},{5,9},{9,13},{13,1},{2,6},{6,10},{... | collective-permute-start | bytes 49160 | tf_op jit(solution)/shard_map/ppermute | solution.py:19
  137.8 1.6 copy-start.1
  139.4 1.6 copy-start.4
  141.0 1.6 copy-start.7
  147.3 1.0 copy-start.11
  148.3 11.2 %collective-permute-start.14 = (bf16[528,512]{1,0:T(8,128)(2,1)}, bf16[528,512]{1,0:T(8,128)(2,1)}, u32[]{:S(2)}, u32[]{:S(2)}) collective-permute-start(bf16[528,512]{1,0:T(8,128)(2,1)} %get-tuple-element.25), channel_id=1, source_target_pairs={{0,1},{1,0},{2,3},{3,2},{4,5},{5,4},{6,7},{7,6},{8,9},{9,8},{10,11... | collective-permute-start | bytes 1622024 | tf_op jit(solution)/shard_map/ppermute | solution.py:166
  148.3 1.6 copy-start.2
  149.9 1.6 copy-start.5
  151.5 1.6 copy-start.8
  153.1 6.4 %copy-start.12 = (f32[528,512]{1,0:T(8,128)S(1)}, f32[528,512]{1,0:T(8,128)}, u32[]{:S(2)}) copy-start(f32[528,512]{1,0:T(8,128)} %copy-done.11) | copy-start | bytes 3244036
  158.0 1.0 copy-start.9
  159.0 4.1 %copy-start.14 = (bf16[6,64,1024]{2,1,0:T(8,128)(2,1)S(1)}, bf16[6,64,1024]{2,1,0:T(8,128)(2,1)}, u32[]{:S(2)}) copy-start(bf16[6,64,1024]{2,1,0:T(8,128)(2,1)} %copy-done.13) | copy-start | bytes 2359300
  159.0 17.1 %copy-start.10 = (f32[528,512]{1,0:T(8,128)S(1)}, f32[528,512]{1,0:T(8,128)}, u32[]{:S(2)}) copy-start(f32[528,512]{1,0:T(8,128)} %copy-done.9) | copy-start | bytes 3244036
  159.0 6.4 %collective-permute-start.13 = (bf16[528,512]{1,0:T(8,128)(2,1)}, bf16[528,512]{1,0:T(8,128)(2,1)S(1)}, u32[]{:S(2)}, u32[]{:S(2)}) collective-permute-start(bf16[528,512]{1,0:T(8,128)(2,1)} %get-tuple-element.23), channel_id=1, source_target_pairs={{0,1},{1,0},{2,3},{3,2},{4,5},{5,4},{6,7},{7,6},{8,9},{9,8},{10,11... | collective-permute-start | bytes 1622024 | tf_op jit(solution)/shard_map/ppermute | solution.py:166
  161.6 14.5 %collective-permute-start.15 = (bf16[528,512]{1,0:T(8,128)(2,1)}, bf16[528,512]{1,0:T(8,128)(2,1)S(1)}, u32[]{:S(2)}, u32[]{:S(2)}) collective-permute-start(bf16[528,512]{1,0:T(8,128)(2,1)} %add_convert_fusion), channel_id=1, source_target_pairs={{0,2},{2,0},{1,3},{3,1},{4,6},{6,4},{5,7},{7,5},{8,10},{10,8},{9,1... | collective-permute-start | bytes 1622024 | tf_op jit(solution)/shard_map/ppermute | solution.py:166

commit v2 on v0

--- a/solution.py
+++ b/solution.py
@@ -3,6 +3,8 @@
 import jax
 import jax.numpy as jnp
 from jax import lax
+from jax.experimental import pallas as pl
+from jax.experimental.pallas import tpu as pltpu
 from jax.sharding import PartitionSpec as P
 
 D = 1024
@@ -33,7 +35,7 @@
     return (weights, energy)
 
 
-def body(samples, centroids, move_target, fetch_ids, cand):
+def exchange_plan(samples, centroids, move_target, fetch_ids, cand):
     rows = samples.shape[3]
     width = samples.shape[4]
     slots_in = samples.shape[2]
@@ -156,6 +158,413 @@
     return (fresh.reshape(share * rows, width), energy.reshape(1, 1, bal, half))
 
 
+LOW = -1e30
+MEGA = 2**20
+PAD = 16
+HBM = pl.BlockSpec(memory_space=pl.ANY)
+VMEM = pl.BlockSpec(memory_space=pltpu.VMEM)
+SMEM = pl.BlockSpec(memory_space=pltpu.SMEM)
+
+
+def swapped(value, axis):
+    return lax.ppermute(value, axis, [(0, 1), (1, 0)])
+
+
+def paired(value, flip):
+    count = lax.axis_size("wide")
+    return lax.ppermute(value, "wide", [(w, w ^ flip) for w in range(count)])
+
+
+def after(value, *others):
+    return lax.optimization_barrier((value, *others))[0]
+
+
+def shape(dims, dtype=jnp.float32):
+    return jax.ShapeDtypeStruct(dims, dtype)
+
+
+def call(kernel, name, in_specs, args, outs, scratch=(), out_specs=None):
+    return pl.pallas_call(
+        kernel,
+        in_specs=in_specs,
+        out_specs=out_specs or [VMEM] * len(outs),
+        out_shape=outs,
+        scratch_shapes=scratch,
+        compiler_params=pltpu.CompilerParams(vmem_limit_bytes=16 * MEGA),
+        cost_estimate=pl.CostEstimate(flops=1, bytes_accessed=1, transcendentals=0),
+        name=name,
+    )(*args)
+
+
+def bias_kernel(facts_ref, bias_ref, logs_ref, *, slots_in, pool, bal, lists, owned, flips):
+    pair_x, pair_c = flips
+    peers = facts_ref.shape[0]
+    me = lax.axis_index("wide")
+    logs_ref[0] = jnp.float32(LOW)
+    for m in range(1, lists + 1):
+        logs_ref[m] = jnp.float32(math.log(m))
+
+    def entry(at, unused):
+        k, e = at // slots_in, at % slots_in
+        source = jnp.where(k == 0, me, me ^ pair_x)
+        target = facts_ref[(me - source) % peers, e]
+        live = target >= 0
+        target = jnp.maximum(target, 0)
+        row = (me - target // bal) % peers
+        first = slots_in + pool + (target % bal) * lists
+        listed = [facts_ref[row, slots_in + facts_ref[row, first + j]] for j in range(lists)]
+        for s in range(2):
+            owner = me if s == 0 else me ^ pair_c
+            for g in range(owned):
+                times = jnp.int32(0)
+                for block in listed:
+                    times = times + jnp.where(block == owner * owned + g, 1, 0)
+                bias_ref[k, (s * owned + g) * slots_in + e] = logs_ref[jnp.where(live, times, 0)]
+        return unused
+
+    lax.fori_loop(0, 2 * slots_in, entry, 0)
+
+
+def tiles(lanes):
+    return [(lo, min(256, lanes - lo)) for lo in range(0, lanes, 256)]
+
+
+def score_kernel(bias_ref, *refs, pieces, first, span, chunk, entries):
+    x_refs = refs[:pieces]
+    c_refs = refs[pieces : pieces + 6]
+    em_refs = refs[pieces + 6 : pieces + 8]
+    stats_ref, logits_ref = refs[pieces + 8 :]
+    count = bias_ref.shape[1] // (2 * entries)
+    rows = logits_ref.shape[1] // count
+    width = c_refs[0].shape[1]
+    dims = (((1,), (1,)), ((), ()))
+    turn = 0
+    base = 0
+    for x_ref in x_refs:
+        for lo, size in tiles(x_ref.shape[0]):
+            out = base + lo
+            place = lax.broadcasted_iota(jnp.int32, (1, size), 1) // span
+            for s in range(2):
+                c_own_ref, c_oth_ref, csq_ref = c_refs[3 * s : 3 * s + 3]
+                em_ref = em_refs[s]
+                buf = logits_ref.at[turn % 2]
+                turn += 1
+                buf[:, 0:size] = lax.dot_general(
+                    c_own_ref[...], x_ref[lo : lo + size, 0:width], dims,
+                    preferred_element_type=jnp.float32,
+                ) + lax.dot_general(
+                    c_oth_ref[...], x_ref[lo : lo + size, width:], dims,
+                    preferred_element_type=jnp.float32,
+                )
+                best = jnp.full((8, size), 2 * LOW, jnp.float32)
+                for g in range(count):
+                    bias = jnp.zeros((1, size), jnp.float32)
+                    for p in range(size // span):
+                        at = (s * count + g) * entries + first + out // span + p
+                        bias = jnp.where(place == p, bias_ref[chunk, at], bias)
+                    block = pl.ds(g * rows, rows)
+                    less = jnp.concatenate([csq_ref[block, :]] * (size // 128), axis=1)
+                    logits = (buf[block, 0:size] - less) + bias
+                    buf[block, 0:size] = logits
+                    best = jnp.maximum(best, jnp.max(logits.reshape(rows // 8, 8, size), axis=0))
+                top = jnp.max(best, axis=0, keepdims=True)
+                total = jnp.zeros((8, size), jnp.float32)
+                for g in range(count):
+                    block = pl.ds(g * rows, rows)
+                    expo = jnp.exp(buf[block, 0:size] - top)
+                    em_ref[block, out : out + size] = expo.astype(jnp.bfloat16)
+                    total = total + jnp.sum(expo.reshape(rows // 8, 8, size), axis=0)
+                stats_ref[2 * s : 2 * s + 1, out : out + size] = top
+                stats_ref[2 * s + 1 : 2 * s + 2, out : out + size] = jnp.sum(
+                    total, axis=0, keepdims=True
+                )
+        base += x_ref.shape[0]
+
+
+def score(bias, chunk, xs, sets, first, span, entries):
+    lanes = sum(x.shape[0] for x in xs)
+    cols = sets[0][0].shape[0]
+    return call(
+        lambda *refs: score_kernel(
+            *refs, pieces=len(xs), first=first, span=span, chunk=chunk, entries=entries
+        ),
+        "scores",
+        [SMEM] + [VMEM] * (len(xs) + 6),
+        [bias, *xs, *sets[0], *sets[1]],
+        [shape((cols, lanes), jnp.bfloat16)] * 2 + [shape((4, lanes))],
+        [pltpu.VMEM((2, cols, 256), jnp.float32)],
+    )
+
+
+def combine(parts):
+    top = parts[0][0:1]
+    for part in parts[1:]:
+        top = jnp.maximum(top, part[0:1])
+    total = jnp.zeros_like(top)
+    for part in parts:
+        total = total + part[1:2] * jnp.exp(part[0:1] - top)
+    return top, total
+
+
+def chunk_parts(mine, peer, chunk):
+    other = 1 - chunk
+    return [
+        mine[4 * chunk : 4 * chunk + 2],
+        mine[4 * chunk + 2 : 4 * chunk + 4],
+        peer[4 * other : 4 * other + 2],
+        peer[4 * other + 2 : 4 * other + 4],
+    ]
+
+
+def half_rows(mine, count):
+    rep = lax.axis_index("rep")
+    return pl.ds(pl.multiple_of((rep if mine else 1 - rep) * count, count), count)
+
+
+def weighted(mine_ref, peer_ref, em_refs, x_refs, rows, cols, which, mass):
+    stats, peer = mine_ref[...], peer_ref[...]
+    count = rows.size
+    total = jnp.zeros((count, cols.stop - cols.start), jnp.float32)
+    masses = jnp.zeros((count, 128), jnp.float32)
+    pieces = [(0, em_refs[0], x_refs[0:2]), (1, em_refs[1], x_refs[2:3]), (1, em_refs[2], x_refs[3:4])]
+    lo = 0
+    for at, (chunk, em_ref, xs) in enumerate(pieces):
+        parts = chunk_parts(stats, peer, chunk)
+        top, denom = combine(parts)
+        factor = jnp.where(top > 0.5 * LOW, jnp.exp(parts[which][0:1] - top) / denom, 0.0)
+        lo = lo if at == 2 else 0
+        size = em_ref.shape[1]
+        scaled = em_ref[rows, :].astype(jnp.float32) * factor[:, lo : lo + size]
+        weights = scaled.astype(jnp.bfloat16)
+        if mass:
+            wide = weights.astype(jnp.float32)
+            for lane in range(0, size, 128):
+                masses = masses + wide[:, lane : lane + 128]
+        lo += size
+        begin = 0
+        for x_ref in xs:
+            end = begin + x_ref.shape[0]
+            total = total + jnp.dot(
+                weights[:, begin:end], x_ref[:, cols], preferred_element_type=jnp.float32
+            )
+            begin = end
+    return total, masses
+
+
+def far_kernel(*refs, which, mine):
+    stats_ref, peer_ref = refs[0:2]
+    em_refs, x_refs, (far_ref, mass_ref) = refs[2:5], refs[5:9], refs[9:]
+    count, width = far_ref.shape[0] - PAD, far_ref.shape[1]
+    total, masses = weighted(
+        stats_ref, peer_ref, em_refs, x_refs, half_rows(mine, count), slice(width, 2 * width), which, True
+    )
+    masses = jnp.broadcast_to(jnp.sum(masses, axis=1, keepdims=True), (count, 128)).T[0:PAD]
+    far_ref[0:count, :] = total.astype(jnp.bfloat16)
+    far_ref[count:, :] = masses.astype(jnp.bfloat16)
+    mass_ref[...] = masses
+
+
+def near_kernel(*refs, which, mine, final):
+    stats_ref, peer_ref = refs[0:2]
+    em_refs, x_refs, (mass_ref, came_ref) = refs[2:5], refs[5:9], refs[9:11]
+    out_ref = refs[12] if final else refs[11]
+    count, width = out_ref.shape[0] - PAD, out_ref.shape[1]
+    if final:
+        previous_ref, sem = refs[13:]
+        copy = pltpu.make_async_copy(refs[11].at[half_rows(mine, count), :], previous_ref, sem)
+        copy.start()
+    total, unused = weighted(
+        stats_ref, peer_ref, em_refs, x_refs, half_rows(mine, count), slice(0, width), which, False
+    )
+    came = came_ref[...].astype(jnp.float32)
+    total = total + came[0:count]
+    masses = mass_ref[...] + came[count:]
+    if final:
+        copy.wait()
+        total = total + PRIOR * previous_ref[...]
+        masses = masses + PRIOR
+    out_ref[0:count, :] = total.astype(out_ref.dtype)
+    out_ref[count:, :] = masses.astype(out_ref.dtype)
+
+
+def far_sums(stats, peer, em, xs, which, mine):
+    count, width = em[0].shape[0] // 2, xs[0].shape[1] // 2
+    return call(
+        lambda *refs: far_kernel(*refs, which=which, mine=mine),
+        "far",
+        [VMEM] * 9,
+        [stats, peer, *em, *xs],
+        [shape((count + PAD, width), jnp.bfloat16), shape((PAD, width))],
+    )
+
+
+def near_sums(stats, peer, em, xs, which, mine, mass, came, dtype, previous=None):
+    count, width = em[0].shape[0] // 2, xs[0].shape[1] // 2
+    final = previous is not None
+    return call(
+        lambda *refs: near_kernel(*refs, which=which, mine=mine, final=final),
+        "near",
+        [VMEM] * 11 + [HBM] * final,
+        [stats, peer, *em, *xs, mass, came] + [previous] * final,
+        [shape((count + PAD, width), dtype)],
+        [pltpu.VMEM((count, width), jnp.float32), pltpu.SemaphoreType.DMA] * final,
+    )[0]
+
+
+def add_kernel(a_ref, b_ref, out_ref):
+    out_ref[...] = (a_ref[...] + b_ref[...].astype(jnp.float32)).astype(out_ref.dtype)
+
+
+def final_kernel(sums_ref, rep_ref, back_ref, out_ref):
+    count = out_ref.shape[0]
+    sums = sums_ref[...] + rep_ref[...].astype(jnp.float32) + back_ref[...].astype(jnp.float32)
+    mass = jnp.broadcast_to(sums[count : count + 1], (128, count)).T
+    mass = jnp.concatenate([mass] * (out_ref.shape[1] // 128), axis=1)
+    out_ref[...] = sums[0:count] / mass
+
+
+def energy_kernel(stats_ref, peer_ref, square_ref, out_ref, *last_refs, tau, span):
+    top, denom = combine(chunk_parts(stats_ref[...], peer_ref[...], 0))
+    energy = -tau * (top - square_ref[...] / tau + jnp.log(denom)) / D
+    entries = energy.shape[1] // span
+    out_ref[...] = jnp.zeros_like(out_ref)
+    for e in range(entries):
+        part = energy[:, e * span : (e + 1) * span]
+        out_ref[e : e + 1, :] = part
+        back = e - (entries - len(last_refs))
+        if back >= 0:
+            last_refs[back][...] = jnp.broadcast_to(part, last_refs[back].shape)
+
+
+def place_kernel(facts_ref, energy_ref, *refs, bal):
+    came_refs, out_ref = refs[:-1], refs[-1]
+    me = lax.axis_index("wide")
+    out_ref[...] = jnp.zeros_like(out_ref)
+
+    def put(target, row):
+        @pl.when((target >= 0) & (target // bal == me))
+        def _():
+            out_ref[pl.ds(target % bal, 1), :] = row
+
+    for e in range(bal):
+        put(facts_ref[0, e], energy_ref[e : e + 1, :])
+    for h, came_ref in enumerate(came_refs):
+        put(facts_ref[h + 1, bal + h], came_ref[0:1, :])
+
+
+def grid_plan(samples, centroids, move_target, fetch_ids, cand):
+    rows = samples.shape[3]
+    width = samples.shape[4]
+    slots_in = samples.shape[2]
+    bal = cand.shape[2]
+    lists = cand.shape[3]
+    pool = fetch_ids.shape[2]
+    owned = centroids.shape[0] // rows
+    peers = lax.axis_size("wide")
+    sub = lax.axis_index("sub")
+    tau = 2.0 * math.sqrt(D)
+    handed = slots_in - bal
+    span = rows // 2
+    lanes = slots_in * span
+    cut = bal * span
+    pair_x, pair_c = 2, 1
+
+    c0_own = (centroids * (2.0 / tau)).astype(jnp.bfloat16)
+    c0_oth = swapped(c0_own, "sub")
+    c1_own = paired(c0_own, pair_c)
+
+    facts_own = jnp.concatenate(
+        [move_target.reshape(slots_in), fetch_ids.reshape(pool), cand.reshape(bal * lists)]
+    )
+    facts = jnp.stack([facts_own] + [passed_along(facts_own, "wide", k) for k in range(1, peers)])
+    bias = call(
+        lambda *refs: bias_kernel(
+            *refs, slots_in=slots_in, pool=pool, bal=bal, lists=lists, owned=owned, flips=(pair_x, pair_c)
+        ),
+        "bias",
+        [SMEM],
+        [facts],
+        [shape((2, 2 * owned * slots_in))],
+        [pltpu.SMEM((lists + 1,), jnp.float32)],
+        [SMEM],
+    )[0]
+
+    blocks = samples.reshape(slots_in, rows, width)
+    give = lax.dynamic_slice_in_dim(blocks, (1 - sub) * span, span, 1).reshape(lanes, width)
+    took = swapped(give, "sub")
+    own = lax.dynamic_slice_in_dim(blocks, sub * span, span, 1).reshape(lanes, width)
+    full = jnp.concatenate([own, took], axis=1)
+    x0 = (full[:cut], full[cut:])
+    x1a = paired(x0[0], pair_x)
+    c1_own, x1a, bias = lax.optimization_barrier((c1_own, x1a, bias))
+    x1b = paired(after(x0[1], c1_own), pair_x)
+    c1_oth = swapped(c1_own, "sub")
+
+    def squares(*parts):
+        total = sum(jnp.sum(jnp.square(part.astype(jnp.float32)), axis=1, keepdims=True) for part in parts)
+        return jnp.broadcast_to(total * (tau / 4.0), (owned * rows, 128))
+
+    work_sq = jnp.sum(jnp.square(full.astype(jnp.float32)), axis=1).reshape(1, lanes)
+    sets = ((c0_own, c0_oth, squares(c0_own, c0_oth)), (c1_own, c1_oth, squares(c1_own, c1_oth)))
+
+    *em0, stats0 = score(bias, 0, x0, sets, 0, span, slots_in)
+    *em1a, stats1a = score(bias, 1, [x1a], sets, 0, span, slots_in)
+    *em1b, stats1b = score(bias, 1, [x1b], sets, bal, span, slots_in)
+    em = list(zip(em0, em1a, em1b))
+    stats = jnp.concatenate([stats0, jnp.concatenate([stats1a, stats1b], axis=1)], axis=0)
+    peer = paired(stats, pair_x)
+
+    xs = (*x0, x1a, x1b)
+    half = jnp.bfloat16
+    far_a, mass_a = far_sums(stats, peer, em[1], xs, 1, False)
+    far_b, mass_b = far_sums(after(stats, far_a), peer, em[1], xs, 1, True)
+    came = swapped(far_a, "sub")
+    sent_a = near_sums(after(stats, far_b), peer, em[1], xs, 1, False, mass_a, came, half)
+    came_a = swapped(sent_a, "rep")
+    came = swapped(far_b, "sub")
+    part_b = near_sums(after(stats, sent_a), peer, em[1], xs, 1, True, mass_b, came, jnp.float32)
+
+    far_c, mass_c = far_sums(after(stats, part_b), peer, em[0], xs, 0, False)
+    far_d, mass_d = far_sums(after(stats, far_c), peer, em[0], xs, 0, True)
+    came = swapped(far_c, "sub")
+    sent_c = near_sums(after(stats, far_d), peer, em[0], xs, 0, False, mass_c, came, half)
+    came_c = swapped(sent_c, "rep")
+    came = swapped(far_d, "sub")
+    part_d = near_sums(
+        after(stats, sent_c), peer, em[0], xs, 0, True, mass_d, came, jnp.float32, centroids
+    )
+
+    back = call(add_kernel, "add", [VMEM] * 2, [part_b, came_a], [shape(part_b.shape, half)])[0]
+    came_back = paired(back, pair_c)
+    fresh = call(
+        final_kernel, "final", [VMEM] * 3, [part_d, came_c, came_back], [shape((owned * rows // 2, width))]
+    )[0]
+
+    energy, *last = call(
+        lambda *refs: energy_kernel(*refs, tau=tau, span=span),
+        "energy",
+        [VMEM] * 3,
+        [after(stats, part_d), peer, work_sq],
+        [shape((slots_in, span))] + [shape((8, span))] * handed,
+    )
+    came = [passed_along(last[h], "wide", h + 1) for h in range(handed)]
+    energy = call(
+        lambda *refs: place_kernel(*refs, bal=bal),
+        "place",
+        [SMEM] + [VMEM] * (1 + handed),
+        [facts, energy, *came],
+        [shape((bal, span))],
+    )[0]
+    return (fresh, energy.reshape(1, 1, bal, span))
+
+
+def body(samples, centroids, move_target, fetch_ids, cand):
+    sizes = [lax.axis_size(axis) for axis in ("wide", "rep", "sub")]
+    if sizes == [4, 2, 2]:
+        return grid_plan(samples, centroids, move_target, fetch_ids, cand)
+    return exchange_plan(samples, centroids, move_target, fetch_ids, cand)
+
+
 def solution(mesh):
     return jax.shard_map(
         body,

time: 504 us -> 129 us (0.26)
  starting transfers between devices: 123 us -> 20.9 us
  matrix products: 102 us -> 0 us
  waiting for transfers between devices: 146 us -> 68.7 us
  local copies, waits for them, and re-layouts: 65.6 us -> 2.05 us
  other arithmetic: 40.3 us -> 5.14 us
  Pallas kernels: 0 us -> 30.8 us
  between operations: 20.1 us -> 0.97 us
    all_to_all x4 -> x0, waiting for transfers between devices: 113 us -> none  [the longest x1 104 us: body(): lax.all_to_all(back_sums, 'wide', split_axis=0, concat_axis=0, tiled=True)]
    dot_general x27 -> x0, matrix products: 102 us -> none  [the longest x8 69.4 us: slot_sums(): return (total + jnp.dot(hot, term, precision=lax.Precision.HIGHEST), 0)]
    ppermute x4 -> x5, starting transfers between devices: 103 us -> 8.84 us  [passed_along(): return lax.ppermute(value, axis, pairs)]
    ppermute x4 -> x5, waiting for transfers between devices: 3.81 us -> 48.9 us  [passed_along(): return lax.ppermute(value, axis, pairs)]
    gather x24 -> x0, local copies, waits for them, and re-layouts: 40.2 us -> none  [the longest x8 20 us: slot_scores(): chosen = jnp.take(fetched, lists_one, axis=0).reshape(lists * rows, width)]
    pallas_call x0 -> x16, Pallas kernels: none -> 30.8 us  [call(): pl.pallas_call(kernel, in_specs=in_specs, out_specs=out_specs or [VMEM] *...]
    psum x1 -> x0, waiting for transfers between devices: 26.6 us -> none  [body(): scores = lax.psum(partial_scores, 'sub')]
    all_to_all x4 -> x0, starting transfers between devices: 19.8 us -> none  [the longest x1 6.32 us: body(): lax.all_to_all(asks, 'wide', split_axis=0, concat_axis=0, tiled=True)]
  transfers between devices with their start and end apart: 10 -> 19, of which waited for: 7 -> 7; matrix products, arithmetic and copies ran while one was open for 2% -> 4% of each run, Pallas kernels for 0% -> 16%
where the time goes in v2:
time: 129 us
  waiting for transfers between devices  68.7 us (53%)
  Pallas kernels  30.8 us (24%)
  starting transfers between devices  20.9 us (16%)
  other arithmetic  5.14 us (4%)
  local copies, waits for them, and re-layouts  2.05 us (2%)
    ppermute x5, waiting for transfers between devices, passed_along(): return lax.ppermute(value, axis, pairs)  48.9 us
    pallas_call x16, Pallas kernels, call(): pl.pallas_call(kernel, in_specs=in_specs, out_specs=out_specs or [VMEM] *...  30.8 us
    ppermute x5, waiting for transfers between devices, paired(): return lax.ppermute(value, 'wide', [(w, w ^ flip) for w in range(count)])  10.6 us
    ppermute x9, waiting for transfers between devices, swapped(): return lax.ppermute(value, axis, [(0, 1), (1, 0)])  9.22 us
    ppermute x5, starting transfers between devices, passed_along(): return lax.ppermute(value, axis, pairs)  8.84 us
    ppermute x5, starting transfers between devices, paired(): return lax.ppermute(value, 'wide', [(w, w ^ flip) for w in range(count)])  7 us
    ppermute x9, starting transfers between devices, swapped(): return lax.ppermute(value, axis, [(0, 1), (1, 0)])  5.09 us
    reduce_sum x4, other arithmetic, squares(): jnp.sum(jnp.square(part.astype(jnp.float32)), axis=1, keepdims=True)  3.57 us
  transfers between devices with their start and end apart: 19, of which 7 were waited for; matrix products, arithmetic and copies ran while one was open for 4% of the time, Pallas kernels for 16%

profile of v2, /device:TPU:0, one launch (start us, length us, event | category | flops | bytes accessed | tf_op | source)
XLA Modules:
  0.0 128.5 jit_solution(15478156564632542493)
XLA Ops:
  0.6 0.0 copy-start
  0.6 1.5 %constant_dynamic-slice_fusion = (bf16[1,1,10,64,512]{4,3,2,1,0:T(8,128)(2,1)S(1)}, bf16[1,1,10,64,512]{4,3,2,1,0:T(8,128)(2,1)S(1)}) fusion(bf16[1,1,10,128,512]{4,3,2,1,0:T(8,128)(2,1)} %param.5, s32[]{:T(128)S(6)} %select_n.7, s32[]{:T(128)S(6)} %select_n.6), kind=kLoop, calls=%fused_computation.18 | loop fusion | bytes 2621448 | tf_op jit(solution)/shard_map/dynamic_slice | solution.py:493
  2.2 0.0 copy-start.2
  2.2 0.0 copy-start.6
  2.2 0.0 copy-start.7
  2.2 0.0 copy-start.8
  2.2 0.5 collective-permute-start.1
  2.7 0.3 multiply_reduce_fusion.4
  3.1 3.0 %collective-permute-start = (bf16[1024,512]{1,0:T(8,128)(2,1)S(1)}, bf16[1024,512]{1,0:T(8,128)(2,1)}, u32[]{:S(2)}, u32[]{:S(2)}) collective-permute-start(bf16[1024,512]{1,0:T(8,128)(2,1)S(1)} %get-tuple-element.67.refs_3_.refs_2_), channel_id=1, source_target_pairs={{0,4},{4,0},{8,12},{12,8},{1,5},{5,1},{9,13},{13,9},{2,6},{6,2},{1... | collective-permute-start | bytes 3145736 | tf_op jit(solution)/shard_map/ppermute | solution.py:175
  6.0 0.0 collective-permute-done.1
  6.0 0.1 fusion.refs_1_.refs_5_
  6.2 2.7 %collective-permute-start.2 = (bf16[512,1024]{1,0:T(8,128)(2,1)S(1)}, bf16[512,1024]{1,0:T(8,128)(2,1)S(1)}, u32[]{:S(2)}, u32[]{:S(2)}) collective-permute-start(bf16[512,1024]{1,0:T(8,128)(2,1)S(1)} %fusion.refs_1_.refs_5_), channel_id=1, source_target_pairs={{0,8},{4,12},{8,0},{12,4},{1,9},{5,13},{9,1},{13,5},{2,10},{6,14},... | collective-permute-start | bytes 3145736 | tf_op jit(solution)/shard_map/ppermute | solution.py:175
  8.8 0.0 collective-permute-start.6
  8.8 0.1 reshape.50
  8.9 0.1 pad_add_fusion.1
  9.0 1.6 %collective-permute-start.5 = (s32[98]{0:T(128)S(1)}, s32[98]{0:T(128)S(1)}, u32[]{:S(2)}, u32[]{:S(2)}) collective-permute-start(s32[98]{0:T(128)S(1)} %pad_add_fusion.1), channel_id=1, source_target_pairs={{0,12},{4,0},{8,4},{12,8},{1,13},{5,1},{9,5},{13,9},{2,14},{6,2},{... | collective-permute-start | bytes 1184 | tf_op jit(solution)/shard_map/ppermute | solution.py:19
  10.6 1.2 collective-permute-start.4
  11.9 39.9 %collective-permute-done.5 = s32[98]{0:T(128)S(1)} collective-permute-done((s32[98]{0:T(128)S(1)}, s32[98]{0:T(128)S(1)}, u32[]{:S(2)}, u32[]{:S(2)}) %collective-permute-start.5) | collective-permute-done | bytes 424 | tf_op jit(solution)/shard_map/ppermute | solution.py:19
  51.8 3.4 %collective-permute-start.3 = (s32[98]{0:T(128)S(1)}, s32[98]{0:T(128)S(1)}, u32[]{:S(2)}, u32[]{:S(2)}) collective-permute-start(s32[98]{0:T(128)S(1)} %pad_add_fusion.1), channel_id=1, source_target_pairs={{0,4},{4,8},{8,12},{12,0},{1,5},{5,9},{9,13},{13,1},{2,6},{6,10},{... | collective-permute-start | bytes 1184 | tf_op jit(solution)/shard_map/ppermute | solution.py:19
  55.2 1.9 %collective-permute-done.3 = s32[98]{0:T(128)S(1)} collective-permute-done((s32[98]{0:T(128)S(1)}, s32[98]{0:T(128)S(1)}, u32[]{:S(2)}, u32[]{:S(2)}) %collective-permute-start.3) | collective-permute-done | bytes 424 | tf_op jit(solution)/shard_map/ppermute | solution.py:19
  57.1 6.1 %bias.1.refs_0_ = f32[2,160]{1,0:T(2,128)S(1)} custom-call(s32[4,98]{1,0:T(4,128)S(1)} %pad_add_fusion.refs_0_), custom_call_target="tpu_custom_call" | custom-call | flops 1 | bytes 1 | tf_op jit(solution)/shard_map/bias/pallas_call | solution.py:187
  63.3 0.1 collective-permute-start.7
  63.3 1.0 fusion.1.refs_2_.refs_6_
  64.3 0.0 collective-permute-done.6.refs_4_.refs_3_
  64.3 1.5 %multiply_reduce_fusion.3 = f32[1024]{0:T(1024)S(1)} fusion(bf16[1024,512]{1,0:T(8,128)(2,1)} %collective-permute-done.6.refs_4_.refs_3_), kind=kLoop, calls=%fused_computation.3 | loop fusion | flops 1571840 | bytes 1052672 | tf_op jit(solution)/shard_map/reduce_sum | solution.py:504
  65.9 1.2 collective-permute-start.8
  67.1 1.5 %multiply_reduce_fusion.2 = f32[1024]{0:T(1024)S(1)} fusion(bf16[1024,512]{1,0:T(8,128)(2,1)} %collective-permute-done.refs_6_.refs_5_), kind=kLoop, calls=%fused_computation.2 | loop fusion | flops 1571840 | bytes 1052672 | tf_op jit(solution)/shard_map/reduce_sum | solution.py:504
  68.6 0.3 multiply_reduce_fusion.1
  68.9 0.2 broadcast_in_dim.4.refs_5_.refs_4_
  69.1 0.2 broadcast_in_dim.5.refs_8_.refs_7_
  69.3 5.9 %scores.3 = (bf16[1024,640]{1,0:T(8,128)(2,1)S(1)}, bf16[1024,640]{1,0:T(8,128)(2,1)S(1)}, f32[4,640]{1,0:T(4,128)S(1)}) custom-call(f32[2,160]{1,0:T(2,128)S(1)} %bias.1.refs_0_, bf16[512,1024]{1,0:T(8,128)(2,1)S(1)} %fusion.refs_1_.refs_5_, bf16[128,1024]{1,0:T(8,128)(2,1)S(1)} %fusion.1.refs_2_.refs_6_, ...), custom_call_target="tpu_custom_call" | custom-call | flops 1 | bytes 1 | tf_op jit(solution)/shard_map/scores/pallas_call | solution.py:187
  75.2 5.9 %collective-permute-done.8.refs_1_.refs_8_ = bf16[128,1024]{1,0:T(8,128)(2,1)S(1)} collective-permute-done((bf16[128,1024]{1,0:T(8,128)(2,1)S(1)}, bf16[128,1024]{1,0:T(8,128)(2,1)S(1)}, u32[]{:S(2)}, u32[]{:S(2)}) %collective-permute-start.8) | collective-permute-done | bytes 262176 | tf_op jit(solution)/shard_map/ppermute | solution.py:175
  81.1 3.0 %scores.5 = (bf16[1024,128]{1,0:T(8,128)(2,1)S(1)}, bf16[1024,128]{1,0:T(8,128)(2,1)S(1)}, f32[4,128]{1,0:T(4,128)S(1)}) custom-call(f32[2,160]{1,0:T(2,128)S(1)} %bias.1.refs_0_, bf16[128,1024]{1,0:T(8,128)(2,1)S(1)} %collective-permute-done.8.refs_1_.refs_8_, bf16[1024,512]{1,0:T(8,128)(2,1)S(1)} %get-tuple-element.67.refs_3_.refs_2_, ...), custom_call_target="tpu_custom_call" | custom-call | flops 1 | bytes 1 | tf_op jit(solution)/shard_map/scores/pallas_call | solution.py:187
  84.1 4.7 %scores.4 = (bf16[1024,512]{1,0:T(8,128)(2,1)S(1)}, bf16[1024,512]{1,0:T(8,128)(2,1)S(1)}, f32[4,512]{1,0:T(4,128)S(1)}) custom-call(f32[2,160]{1,0:T(2,128)S(1)} %bias.1.refs_0_, bf16[512,1024]{1,0:T(8,128)(2,1)S(1)} %collective-permute-done.2.refs_1_.refs_7_, bf16[1024,512]{1,0:T(8,128)(2,1)S(1)} %get-tuple-element.67.refs_3_.refs_2_, ...), custom_call_target="tpu_custom_call" | custom-call | flops 1 | bytes 1 | tf_op jit(solution)/shard_map/scores/pallas_call | solution.py:187
  88.8 0.1 collective-permute-start.9
  88.9 4.7 %collective-permute-done.9.refs_1_ = f32[8,640]{1,0:T(8,128)S(1)} collective-permute-done((f32[8,640]{1,0:T(8,128)S(1)}, f32[8,640]{1,0:T(8,128)S(1)}, u32[]{:S(2)}, u32[]{:S(2)}) %collective-permute-start.9) | collective-permute-done | bytes 20512 | tf_op jit(solution)/shard_map/ppermute | solution.py:175
  93.6 1.0 far.4
  94.6 0.1 collective-permute-start.10
  94.7 1.0 far.5
  95.7 0.6 collective-permute-start.11
  96.3 0.3 collective-permute-done.10.refs_10_
  96.6 1.0 near.4
  97.6 1.6 %collective-permute-start.15 = (bf16[528,512]{1,0:T(8,128)(2,1)S(1)}, bf16[528,512]{1,0:T(8,128)(2,1)S(1)}, u32[]{:S(2)}, u32[]{:S(2)}) collective-permute-start(bf16[528,512]{1,0:T(8,128)(2,1)S(1)} %near.4), channel_id=1, source_target_pairs={{0,2},{2,0},{1,3},{3,1},{4,6},{6,4},{5,7},{7,5},{8,10},{10,8},{9,1... | collective-permute-start | bytes 1622024 | tf_op jit(solution)/shard_map/ppermute | solution.py:170
  99.2 0.0 collective-permute-done.11.refs_10_
  99.2 1.0 near.5.a_ref
  100.2 1.0 far.6
  101.3 0.1 collective-permute-start.12
  101.3 1.2 far.7
  102.6 0.6 collective-permute-start.13
  103.1 8.9 %collective-permute-done.15.b_ref = bf16[528,512]{1,0:T(8,128)(2,1)S(1)} collective-permute-done((bf16[528,512]{1,0:T(8,128)(2,1)S(1)}, bf16[528,512]{1,0:T(8,128)(2,1)S(1)}, u32[]{:S(2)}, u32[]{:S(2)}) %collective-permute-start.15) | collective-permute-done | bytes 540704 | tf_op jit(solution)/shard_map/ppermute | solution.py:170
  112.0 0.1 add.39
  112.1 0.1 collective-permute-start.16
  112.2 0.0 copy-start.3
  112.2 0.0 copy-start.1
  112.2 1.0 near.6
  113.2 1.6 %collective-permute-start.14 = (bf16[528,512]{1,0:T(8,128)(2,1)S(1)}, bf16[528,512]{1,0:T(8,128)(2,1)S(1)}, u32[]{:S(2)}, u32[]{:S(2)}) collective-permute-start(bf16[528,512]{1,0:T(8,128)(2,1)S(1)} %near.6), channel_id=1, source_target_pairs={{0,2},{2,0},{1,3},{3,1},{4,6},{6,4},{5,7},{7,5},{8,10},{10,8},{9,1... | collective-permute-start | bytes 1622024 | tf_op jit(solution)/shard_map/ppermute | solution.py:170
  114.8 0.3 multiply_reduce_fusion
  115.2 1.2 near.7.sums_ref
  116.4 0.1 energy.1
  116.5 2.0 %collective-permute-start.17 = (f32[8,64]{1,0:T(8,128)S(1)}, f32[8,64]{1,0:T(8,128)S(1)}, u32[]{:S(2)}, u32[]{:S(2)}) collective-permute-start(f32[8,64]{1,0:T(8,128)S(1)} %get-tuple-element.64), channel_id=1, source_target_pairs={{0,4},{4,8},{8,12},{12,0},{1,5},{5,9},{9,13},{13,1},{2,6},{6,10},{... | collective-permute-start | bytes 6152 | tf_op jit(solution)/shard_map/ppermute | solution.py:19
  118.5 0.6 collective-permute-start.18
  119.0 7.0 %collective-permute-done.17.refs_2_ = f32[8,64]{1,0:T(8,128)S(1)} collective-permute-done((f32[8,64]{1,0:T(8,128)S(1)}, f32[8,64]{1,0:T(8,128)S(1)}, u32[]{:S(2)}, u32[]{:S(2)}) %collective-permute-start.17) | collective-permute-done | bytes 2080 | tf_op jit(solution)/shard_map/ppermute | solution.py:19
  126.1 1.3 %place.1 = f32[8,64]{1,0:T(8,128)} custom-call(s32[4,98]{1,0:T(4,128)S(1)} %pad_add_fusion.refs_0_, f32[10,64]{1,0:T(8,128)S(1)} %get-tuple-element.63.refs_1_, f32[8,64]{1,0:T(8,128)S(1)} %collective-permute-done.17.refs_2_, f32[8,64]{1,0:T(8,128)S(1)} %collective-permute-done.18.refs_3_), custom_call_target="tpu_custom_call" | custom-call | flops 1 | bytes 1 | tf_op jit(solution)/shard_map/place/pallas_call | solution.py:187
  127.4 1.2 final.1
  (25 shorter events, 0.1 us)
Async XLA Ops:
  0.6 2.1 %copy-start = (f32[1024,512]{1,0:T(8,128)S(1)}, f32[1024,512]{1,0:T(8,128)}, u32[]{:S(2)}) copy-start(f32[1024,512]{1,0:T(8,128)} %refs_11_.1) | copy-start | bytes 6291460
  2.2 4.0 %copy-start.2 = (bf16[1,1,10,64,512]{4,3,2,1,0:T(8,128)(2,1)}, bf16[1,1,10,64,512]{4,3,2,1,0:T(8,128)(2,1)S(1)}, u32[]{:S(2)}) copy-start(bf16[1,1,10,64,512]{4,3,2,1,0:T(8,128)(2,1)S(1)} %get-tuple-element.69) | copy-start | bytes 1966084
  2.2 6.6 %copy-start.6 = (s32[1,1,8,8]{3,2,1,0:T(8,128)S(1)}, s32[1,1,8,8]{3,2,1,0:T(8,128)}, u32[]{:S(2)}) copy-start(s32[1,1,8,8]{3,2,1,0:T(8,128)} %param.9) | copy-start | bytes 772
  2.2 6.7 %copy-start.7 = (s32[1,1,24]{2,1,0:T(1,128)S(1)}, s32[1,1,24]{2,1,0:T(1,128)}, u32[]{:S(2)}) copy-start(s32[1,1,24]{2,1,0:T(1,128)} %param.8) | copy-start | bytes 292
  2.2 6.7 %copy-start.8 = (s32[1,1,10]{2,1,0:T(1,128)S(1)}, s32[1,1,10]{2,1,0:T(1,128)}, u32[]{:S(2)}) copy-start(s32[1,1,10]{2,1,0:T(1,128)} %param.7) | copy-start | bytes 124
  2.2 3.8 %collective-permute-start.1 = (bf16[640,512]{1,0:T(8,128)(2,1)S(1)}, bf16[640,512]{1,0:T(8,128)(2,1)S(1)}, u32[]{:S(2)}, u32[]{:S(2)}) collective-permute-start(bf16[640,512]{1,0:T(8,128)(2,1)S(1)} %bitcast.14), channel_id=1, source_target_pairs={{0,1},{1,0},{2,3},{3,2},{4,5},{5,4},{6,7},{7,6},{8,9},{9,8},{10,11... | collective-permute-start | bytes 1966088 | tf_op jit(solution)/shard_map/ppermute | solution.py:170
  3.1 60.2 %collective-permute-start = (bf16[1024,512]{1,0:T(8,128)(2,1)S(1)}, bf16[1024,512]{1,0:T(8,128)(2,1)}, u32[]{:S(2)}, u32[]{:S(2)}) collective-permute-start(bf16[1024,512]{1,0:T(8,128)(2,1)S(1)} %get-tuple-element.67.refs_3_.refs_2_), channel_id=1, source_target_pairs={{0,4},{4,0},{8,12},{12,8},{1,5},{5,1},{9,13},{13,9},{2,6},{6,2},{1... | collective-permute-start | bytes 3145736 | tf_op jit(solution)/shard_map/ppermute | solution.py:175
  6.0 2.8 %copy-start.4 = (bf16[640,512]{1,0:T(8,128)(2,1)}, bf16[640,512]{1,0:T(8,128)(2,1)S(1)}, u32[]{:S(2)}) copy-start(bf16[640,512]{1,0:T(8,128)(2,1)S(1)} %collective-permute-done.1) | copy-start | bytes 1966084
  6.2 57.1 %collective-permute-start.2 = (bf16[512,1024]{1,0:T(8,128)(2,1)S(1)}, bf16[512,1024]{1,0:T(8,128)(2,1)S(1)}, u32[]{:S(2)}, u32[]{:S(2)}) collective-permute-start(bf16[512,1024]{1,0:T(8,128)(2,1)S(1)} %fusion.refs_1_.refs_5_), channel_id=1, source_target_pairs={{0,8},{4,12},{8,0},{12,4},{1,9},{5,13},{9,1},{13,5},{2,10},{6,14},... | collective-permute-start | bytes 3145736 | tf_op jit(solution)/shard_map/ppermute | solution.py:175
  8.8 55.5 %collective-permute-start.6 = (bf16[1024,512]{1,0:T(8,128)(2,1)S(1)}, bf16[1024,512]{1,0:T(8,128)(2,1)}, u32[]{:S(2)}, u32[]{:S(2)}) collective-permute-start(bf16[1024,512]{1,0:T(8,128)(2,1)S(1)} %get-tuple-element.67.refs_3_.refs_2_), channel_id=1, source_target_pairs={{0,1},{1,0},{2,3},{3,2},{4,5},{5,4},{6,7},{7,6},{8,9},{9,8},{10,11... | collective-permute-start | bytes 3145736 | tf_op jit(solution)/shard_map/ppermute | solution.py:170
  9.0 42.8 %collective-permute-start.5 = (s32[98]{0:T(128)S(1)}, s32[98]{0:T(128)S(1)}, u32[]{:S(2)}, u32[]{:S(2)}) collective-permute-start(s32[98]{0:T(128)S(1)} %pad_add_fusion.1), channel_id=1, source_target_pairs={{0,12},{4,0},{8,4},{12,8},{1,13},{5,1},{9,5},{13,9},{2,14},{6,2},{... | collective-permute-start | bytes 1184 | tf_op jit(solution)/shard_map/ppermute | solution.py:19
  10.6 44.6 %collective-permute-start.4 = (s32[98]{0:T(128)S(1)}, s32[98]{0:T(128)S(1)}, u32[]{:S(2)}, u32[]{:S(2)}) collective-permute-start(s32[98]{0:T(128)S(1)} %pad_add_fusion.1), channel_id=1, source_target_pairs={{0,8},{4,12},{8,0},{12,4},{1,9},{5,13},{9,1},{13,5},{2,10},{6,14},... | collective-permute-start | bytes 1184 | tf_op jit(solution)/shard_map/ppermute | solution.py:19
  51.8 5.4 %collective-permute-start.3 = (s32[98]{0:T(128)S(1)}, s32[98]{0:T(128)S(1)}, u32[]{:S(2)}, u32[]{:S(2)}) collective-permute-start(s32[98]{0:T(128)S(1)} %pad_add_fusion.1), channel_id=1, source_target_pairs={{0,4},{4,8},{8,12},{12,0},{1,5},{5,9},{9,13},{13,1},{2,6},{6,10},{... | collective-permute-start | bytes 1184 | tf_op jit(solution)/shard_map/ppermute | solution.py:19
  63.3 5.4 %collective-permute-start.7 = (bf16[1024,512]{1,0:T(8,128)(2,1)}, bf16[1024,512]{1,0:T(8,128)(2,1)S(1)}, u32[]{:S(2)}, u32[]{:S(2)}) collective-permute-start(bf16[1024,512]{1,0:T(8,128)(2,1)} %collective-permute-done.refs_6_.refs_5_), channel_id=1, source_target_pairs={{0,1},{1,0},{2,3},{3,2},{4,5},{5,4},{6,7},{7,6},{8,9},{9,8},{10,11... | collective-permute-start | bytes 3145736 | tf_op jit(solution)/shard_map/ppermute | solution.py:170
  65.9 15.3 %collective-permute-start.8 = (bf16[128,1024]{1,0:T(8,128)(2,1)S(1)}, bf16[128,1024]{1,0:T(8,128)(2,1)S(1)}, u32[]{:S(2)}, u32[]{:S(2)}) collective-permute-start(bf16[128,1024]{1,0:T(8,128)(2,1)S(1)} %fusion.1.refs_2_.refs_6_), channel_id=1, source_target_pairs={{0,8},{4,12},{8,0},{12,4},{1,9},{5,13},{9,1},{13,5},{2,10},{6,14},... | collective-permute-start | bytes 786440 | tf_op jit(solution)/shard_map/ppermute | solution.py:175
  88.8 4.7 %collective-permute-start.9 = (f32[8,640]{1,0:T(8,128)S(1)}, f32[8,640]{1,0:T(8,128)S(1)}, u32[]{:S(2)}, u32[]{:S(2)}) collective-permute-start(f32[8,640]{1,0:T(8,128)S(1)} %maximum_maximum_fusion.refs_0_), channel_id=1, source_target_pairs={{0,8},{4,12},{8,0},{12,4},{1,9},{5,13},{9,1},{13,5},{2,10},{6,14},... | collective-permute-start | bytes 61448 | tf_op jit(solution)/shard_map/ppermute | solution.py:175
  94.6 2.0 %collective-permute-start.10 = (bf16[528,512]{1,0:T(8,128)(2,1)S(1)}, bf16[528,512]{1,0:T(8,128)(2,1)S(1)}, u32[]{:S(2)}, u32[]{:S(2)}) collective-permute-start(bf16[528,512]{1,0:T(8,128)(2,1)S(1)} %get-tuple-element.44), channel_id=1, source_target_pairs={{0,1},{1,0},{2,3},{3,2},{4,5},{5,4},{6,7},{7,6},{8,9},{9,8},{10,11... | collective-permute-start | bytes 1622024 | tf_op jit(solution)/shard_map/ppermute | solution.py:170
  95.7 3.5 %collective-permute-start.11 = (bf16[528,512]{1,0:T(8,128)(2,1)S(1)}, bf16[528,512]{1,0:T(8,128)(2,1)S(1)}, u32[]{:S(2)}, u32[]{:S(2)}) collective-permute-start(bf16[528,512]{1,0:T(8,128)(2,1)S(1)} %get-tuple-element.46), channel_id=1, source_target_pairs={{0,1},{1,0},{2,3},{3,2},{4,5},{5,4},{6,7},{7,6},{8,9},{9,8},{10,11... | collective-permute-start | bytes 1622024 | tf_op jit(solution)/shard_map/ppermute | solution.py:170
  97.6 14.4 %collective-permute-start.15 = (bf16[528,512]{1,0:T(8,128)(2,1)S(1)}, bf16[528,512]{1,0:T(8,128)(2,1)S(1)}, u32[]{:S(2)}, u32[]{:S(2)}) collective-permute-start(bf16[528,512]{1,0:T(8,128)(2,1)S(1)} %near.4), channel_id=1, source_target_pairs={{0,2},{2,0},{1,3},{3,1},{4,6},{6,4},{5,7},{7,5},{8,10},{10,8},{9,1... | collective-permute-start | bytes 1622024 | tf_op jit(solution)/shard_map/ppermute | solution.py:170
  101.3 10.9 %collective-permute-start.12 = (bf16[528,512]{1,0:T(8,128)(2,1)S(1)}, bf16[528,512]{1,0:T(8,128)(2,1)S(1)}, u32[]{:S(2)}, u32[]{:S(2)}) collective-permute-start(bf16[528,512]{1,0:T(8,128)(2,1)S(1)} %get-tuple-element.55), channel_id=1, source_target_pairs={{0,1},{1,0},{2,3},{3,2},{4,5},{5,4},{6,7},{7,6},{8,9},{9,8},{10,11... | collective-permute-start | bytes 1622024 | tf_op jit(solution)/shard_map/ppermute | solution.py:170
  102.6 12.6 %collective-permute-start.13 = (bf16[528,512]{1,0:T(8,128)(2,1)S(1)}, bf16[528,512]{1,0:T(8,128)(2,1)S(1)}, u32[]{:S(2)}, u32[]{:S(2)}) collective-permute-start(bf16[528,512]{1,0:T(8,128)(2,1)S(1)} %get-tuple-element.57), channel_id=1, source_target_pairs={{0,1},{1,0},{2,3},{3,2},{4,5},{5,4},{6,7},{7,6},{8,9},{9,8},{10,11... | collective-permute-start | bytes 1622024 | tf_op jit(solution)/shard_map/ppermute | solution.py:170
  112.1 15.3 %collective-permute-start.16 = (bf16[528,512]{1,0:T(8,128)(2,1)S(1)}, bf16[528,512]{1,0:T(8,128)(2,1)S(1)}, u32[]{:S(2)}, u32[]{:S(2)}) collective-permute-start(bf16[528,512]{1,0:T(8,128)(2,1)S(1)} %add.39), channel_id=1, source_target_pairs={{0,4},{4,0},{8,12},{12,8},{1,5},{5,1},{9,13},{13,9},{2,6},{6,2},{1... | collective-permute-start | bytes 1622024 | tf_op jit(solution)/shard_map/ppermute | solution.py:175
  112.2 2.6 %copy-start.3 = (bf16[1,1,10,64,512]{4,3,2,1,0:T(8,128)(2,1)S(1)}, bf16[1,1,10,64,512]{4,3,2,1,0:T(8,128)(2,1)}, u32[]{:S(2)}) copy-start(bf16[1,1,10,64,512]{4,3,2,1,0:T(8,128)(2,1)} %copy-done.2) | copy-start | bytes 1966084
  112.2 2.6 %copy-start.5 = (bf16[640,512]{1,0:T(8,128)(2,1)S(1)}, bf16[640,512]{1,0:T(8,128)(2,1)}, u32[]{:S(2)}) copy-start(bf16[640,512]{1,0:T(8,128)(2,1)} %copy-done.4) | copy-start | bytes 1966084
  112.2 3.0 %copy-start.1 = (f32[1024,512]{1,0:T(8,128)S(1)}, f32[1024,512]{1,0:T(8,128)}, u32[]{:S(2)}) copy-start(f32[1024,512]{1,0:T(8,128)} %refs_11_.1) | copy-start | bytes 6291460
  113.2 14.2 %collective-permute-start.14 = (bf16[528,512]{1,0:T(8,128)(2,1)S(1)}, bf16[528,512]{1,0:T(8,128)(2,1)S(1)}, u32[]{:S(2)}, u32[]{:S(2)}) collective-permute-start(bf16[528,512]{1,0:T(8,128)(2,1)S(1)} %near.6), channel_id=1, source_target_pairs={{0,2},{2,0},{1,3},{3,1},{4,6},{6,4},{5,7},{7,5},{8,10},{10,8},{9,1... | collective-permute-start | bytes 1622024 | tf_op jit(solution)/shard_map/ppermute | solution.py:170
  116.5 9.6 %collective-permute-start.17 = (f32[8,64]{1,0:T(8,128)S(1)}, f32[8,64]{1,0:T(8,128)S(1)}, u32[]{:S(2)}, u32[]{:S(2)}) collective-permute-start(f32[8,64]{1,0:T(8,128)S(1)} %get-tuple-element.64), channel_id=1, source_target_pairs={{0,4},{4,8},{8,12},{12,0},{1,5},{5,9},{9,13},{13,1},{2,6},{6,10},{... | collective-permute-start | bytes 6152 | tf_op jit(solution)/shard_map/ppermute | solution.py:19
  118.5 7.6 %collective-permute-start.18 = (f32[8,64]{1,0:T(8,128)S(1)}, f32[8,64]{1,0:T(8,128)S(1)}, u32[]{:S(2)}, u32[]{:S(2)}) collective-permute-start(f32[8,64]{1,0:T(8,128)S(1)} %get-tuple-element.65), channel_id=1, source_target_pairs={{0,8},{4,12},{8,0},{12,4},{1,9},{5,13},{9,1},{13,5},{2,10},{6,14},... | collective-permute-start | bytes 6152 | tf_op jit(solution)/shard_map/ppermute | solution.py:19

commit v3 on v2

--- a/solution.py
+++ b/solution.py
@@ -159,8 +159,10 @@
 
 
 LOW = -1e30
+FLOOR = -1e29
 MEGA = 2**20
 PAD = 16
+SWAPS = 2
 HBM = pl.BlockSpec(memory_space=pl.ANY)
 VMEM = pl.BlockSpec(memory_space=pltpu.VMEM)
 SMEM = pl.BlockSpec(memory_space=pltpu.SMEM)
@@ -183,115 +185,128 @@
     return jax.ShapeDtypeStruct(dims, dtype)
 
 
-def call(kernel, name, in_specs, args, outs, scratch=(), out_specs=None):
+def call(kernel, name, in_specs, args, outs, scratch=(), needs=()):
+    count = len(args)
+
+    def run(*refs):
+        kernel(*refs[:count], *refs[count + len(needs) :])
+
     return pl.pallas_call(
-        kernel,
-        in_specs=in_specs,
-        out_specs=out_specs or [VMEM] * len(outs),
+        run,
+        in_specs=in_specs + [HBM] * len(needs),
+        out_specs=[VMEM] * len(outs),
         out_shape=outs,
         scratch_shapes=scratch,
         compiler_params=pltpu.CompilerParams(vmem_limit_bytes=16 * MEGA),
         cost_estimate=pl.CostEstimate(flops=1, bytes_accessed=1, transcendentals=0),
         name=name,
-    )(*args)
-
-
-def bias_kernel(facts_ref, bias_ref, logs_ref, *, slots_in, pool, bal, lists, owned, flips):
-    pair_x, pair_c = flips
-    peers = facts_ref.shape[0]
+    )(*args, *needs)
+
+
+def bias_kernel(facts_ref, bias_ref, *, slots_in, pool, bal, lists, owned, flips, span):
     me = lax.axis_index("wide")
-    logs_ref[0] = jnp.float32(LOW)
-    for m in range(1, lists + 1):
-        logs_ref[m] = jnp.float32(math.log(m))
-
-    def entry(at, unused):
-        k, e = at // slots_in, at % slots_in
-        source = jnp.where(k == 0, me, me ^ pair_x)
-        target = facts_ref[(me - source) % peers, e]
-        live = target >= 0
-        target = jnp.maximum(target, 0)
-        row = (me - target // bal) % peers
-        first = slots_in + pool + (target % bal) * lists
-        listed = [facts_ref[row, slots_in + facts_ref[row, first + j]] for j in range(lists)]
-        for s in range(2):
-            owner = me if s == 0 else me ^ pair_c
-            for g in range(owned):
-                times = jnp.int32(0)
-                for block in listed:
-                    times = times + jnp.where(block == owner * owned + g, 1, 0)
-                bias_ref[k, (s * owned + g) * slots_in + e] = logs_ref[jnp.where(live, times, 0)]
-        return unused
-
-    lax.fori_loop(0, 2 * slots_in, entry, 0)
+    lanes = slots_in * span
+    row = lax.broadcasted_iota(jnp.int32, (2 * owned, 128), 0)
+    block_id = jnp.where(row < owned, me * owned + row, (me ^ flips[1]) * owned + row - owned)
+    place = lax.broadcasted_iota(jnp.int32, (1, 128), 1) // span
+    for k in range(2):
+        for lo in range(0, lanes, 128):
+            listed = [jnp.full((1, 128), -1, jnp.int32) for j in range(lists)]
+            for p in range(128 // span):
+                target = facts_ref[flips[0] if k else 0, lo // span + p]
+                live = target >= 0
+                target = jnp.maximum(target, 0)
+                source = me ^ (target // bal)
+                first = slots_in + pool + (target % bal) * lists
+                for j in range(lists):
+                    block = facts_ref[source, slots_in + facts_ref[source, first + j]]
+                    listed[j] = jnp.where(place == p, jnp.where(live, block, -1), listed[j])
+            times = jnp.zeros((2 * owned, 128), jnp.float32)
+            for j in range(lists):
+                times = times + jnp.where(block_id == listed[j], 1.0, 0.0)
+            logs = jnp.log(jnp.maximum(times, 1.0))
+            bias_ref[k, :, lo : lo + 128] = jnp.where(times > 0, logs, LOW)
+
+
+def join_kernel(own_ref, *refs):
+    oth_refs, (c_ref, square_ref) = refs[:-2], refs[-2:]
+    width = own_ref.shape[1]
+    lo = 0
+    for oth_ref in oth_refs:
+        part = pl.ds(lo, oth_ref.shape[0])
+        own, oth = own_ref[part, :], oth_ref[...]
+        c_ref[part, 0:width] = own
+        c_ref[part, width:] = oth
+        total = jnp.zeros((part.size, 128), jnp.float32)
+        for half in (own, oth):
+            for lane in range(0, width, 128):
+                piece = half[:, lane : lane + 128].astype(jnp.float32)
+                total = total + piece * piece
+        total = jnp.sum(total, axis=1, keepdims=True) * (math.sqrt(D) / 2.0)
+        square_ref[part, :] = jnp.broadcast_to(total, (part.size, 128))
+        lo += part.size
+
+
+def joined(own, oths):
+    count, width = own.shape
+    outs = [shape((count, 2 * width), own.dtype), shape((count, 128))]
+    return call(join_kernel, "join", [VMEM] * (1 + len(oths)), [own, *oths], outs)
 
 
 def tiles(lanes):
     return [(lo, min(256, lanes - lo)) for lo in range(0, lanes, 256)]
 
 
-def score_kernel(bias_ref, *refs, pieces, first, span, chunk, entries):
-    x_refs = refs[:pieces]
-    c_refs = refs[pieces : pieces + 6]
-    em_refs = refs[pieces + 6 : pieces + 8]
-    stats_ref, logits_ref = refs[pieces + 8 :]
-    count = bias_ref.shape[1] // (2 * entries)
-    rows = logits_ref.shape[1] // count
-    width = c_refs[0].shape[1]
-    dims = (((1,), (1,)), ((), ()))
+def score_kernel(bias_ref, x_ref, c0_ref, csq0_ref, c1_ref, csq1_ref, *refs, chunk, first):
+    before_refs, em_refs, (stats_ref, dots_ref) = refs[:-4], refs[-4:-2], refs[-2:]
+    lead = 0
+    for ref in before_refs:
+        row, lane = 4 * (lead // stats_ref.shape[1]), lead % stats_ref.shape[1]
+        stats_ref[row : row + 4, lane : lane + ref.shape[1]] = ref[...]
+        lead += ref.shape[1]
+    row, lane = 4 * (lead // stats_ref.shape[1]), lead % stats_ref.shape[1]
+    count = bias_ref.shape[1] // 2
+    rows = dots_ref.shape[1] // count
     turn = 0
-    base = 0
-    for x_ref in x_refs:
-        for lo, size in tiles(x_ref.shape[0]):
-            out = base + lo
-            place = lax.broadcasted_iota(jnp.int32, (1, size), 1) // span
-            for s in range(2):
-                c_own_ref, c_oth_ref, csq_ref = c_refs[3 * s : 3 * s + 3]
-                em_ref = em_refs[s]
-                buf = logits_ref.at[turn % 2]
-                turn += 1
-                buf[:, 0:size] = lax.dot_general(
-                    c_own_ref[...], x_ref[lo : lo + size, 0:width], dims,
-                    preferred_element_type=jnp.float32,
-                ) + lax.dot_general(
-                    c_oth_ref[...], x_ref[lo : lo + size, width:], dims,
-                    preferred_element_type=jnp.float32,
-                )
-                best = jnp.full((8, size), 2 * LOW, jnp.float32)
-                for g in range(count):
-                    bias = jnp.zeros((1, size), jnp.float32)
-                    for p in range(size // span):
-                        at = (s * count + g) * entries + first + out // span + p
-                        bias = jnp.where(place == p, bias_ref[chunk, at], bias)
-                    block = pl.ds(g * rows, rows)
-                    less = jnp.concatenate([csq_ref[block, :]] * (size // 128), axis=1)
-                    logits = (buf[block, 0:size] - less) + bias
-                    buf[block, 0:size] = logits
-                    best = jnp.maximum(best, jnp.max(logits.reshape(rows // 8, 8, size), axis=0))
-                top = jnp.max(best, axis=0, keepdims=True)
-                total = jnp.zeros((8, size), jnp.float32)
-                for g in range(count):
-                    block = pl.ds(g * rows, rows)
-                    expo = jnp.exp(buf[block, 0:size] - top)
-                    em_ref[block, out : out + size] = expo.astype(jnp.bfloat16)
-                    total = total + jnp.sum(expo.reshape(rows // 8, 8, size), axis=0)
-                stats_ref[2 * s : 2 * s + 1, out : out + size] = top
-                stats_ref[2 * s + 1 : 2 * s + 2, out : out + size] = jnp.sum(
-                    total, axis=0, keepdims=True
-                )
-        base += x_ref.shape[0]
-
-
-def score(bias, chunk, xs, sets, first, span, entries):
-    lanes = sum(x.shape[0] for x in xs)
+    for lo, size in tiles(x_ref.shape[0]):
+        for s, (c_ref, csq_ref) in enumerate(((c0_ref, csq0_ref), (c1_ref, csq1_ref))):
+            part = slice(lo, lo + size)
+            buf = dots_ref.at[turn % 2]
+            turn += 1
+            buf[:, 0:size] = lax.dot_general(
+                c_ref[...], x_ref[part, :], (((1,), (1,)), ((), ())), preferred_element_type=jnp.float32
+            )
+
+            def logits(g):
+                block = pl.ds(g * rows, rows)
+                less = jnp.concatenate([csq_ref[block, :]] * (size // 128), axis=1)
+                return (buf[block, 0:size] - less).reshape(rows // 8, 8, size)
+
+            of_chunk = slice(first + lo, first + lo + size)
+            bias = [bias_ref[chunk, s * count + g : s * count + g + 1, of_chunk] for g in range(count)]
+            best = jnp.full((8, size), FLOOR, jnp.float32)
+            for g in range(count):
+                best = jnp.maximum(best, jnp.max(logits(g), axis=0) + bias[g])
+            top = jnp.max(best, axis=0, keepdims=True)
+            total = jnp.zeros((8, size), jnp.float32)
+            for g in range(count):
+                expo = jnp.exp(logits(g) + (bias[g] - top)[None])
+                em_refs[s][pl.ds(g * rows, rows), part] = expo.reshape(rows, size).astype(jnp.bfloat16)
+                total = total + jnp.sum(expo, axis=0)
+            out = slice(lane + lo, lane + lo + size)
+            stats_ref[row + 2 * s : row + 2 * s + 1, out] = top
+            stats_ref[row + 2 * s + 1 : row + 2 * s + 2, out] = jnp.sum(total, axis=0, keepdims=True)
+
+
+def score(bias, chunk, first, x, sets, before=()):
     cols = sets[0][0].shape[0]
+    stats = shape((8, bias.shape[2]) if before else (4, x.shape[0]))
     return call(
-        lambda *refs: score_kernel(
-            *refs, pieces=len(xs), first=first, span=span, chunk=chunk, entries=entries
-        ),
+        lambda *refs: score_kernel(*refs, chunk=chunk, first=first),
         "scores",
-        [SMEM] + [VMEM] * (len(xs) + 6),
-        [bias, *xs, *sets[0], *sets[1]],
-        [shape((cols, lanes), jnp.bfloat16)] * 2 + [shape((4, lanes))],
+        [VMEM] * (6 + len(before)),
+        [bias, x, *sets[0], *sets[1], *before],
+        [shape((cols, x.shape[0]), jnp.bfloat16)] * 2 + [stats],
         [pltpu.VMEM((2, cols, 256), jnp.float32)],
     )
 
@@ -326,34 +341,26 @@
     count = rows.size
     total = jnp.zeros((count, cols.stop - cols.start), jnp.float32)
     masses = jnp.zeros((count, 128), jnp.float32)
-    pieces = [(0, em_refs[0], x_refs[0:2]), (1, em_refs[1], x_refs[2:3]), (1, em_refs[2], x_refs[3:4])]
     lo = 0
-    for at, (chunk, em_ref, xs) in enumerate(pieces):
+    for em_ref, x_ref in zip(em_refs, x_refs):
+        chunk, first = lo // stats.shape[1], lo % stats.shape[1]
+        size = em_ref.shape[1]
         parts = chunk_parts(stats, peer, chunk)
         top, denom = combine(parts)
-        factor = jnp.where(top > 0.5 * LOW, jnp.exp(parts[which][0:1] - top) / denom, 0.0)
-        lo = lo if at == 2 else 0
-        size = em_ref.shape[1]
-        scaled = em_ref[rows, :].astype(jnp.float32) * factor[:, lo : lo + size]
-        weights = scaled.astype(jnp.bfloat16)
+        factor = jnp.where(denom > 0, jnp.exp(parts[which][0:1] - top) / denom, 0.0)
+        weights = (em_ref[rows, :].astype(jnp.float32) * factor[:, first : first + size]).astype(jnp.bfloat16)
         if mass:
             wide = weights.astype(jnp.float32)
             for lane in range(0, size, 128):
                 masses = masses + wide[:, lane : lane + 128]
+        total = total + jnp.dot(weights, x_ref[:, cols], preferred_element_type=jnp.float32)
         lo += size
-        begin = 0
-        for x_ref in xs:
-            end = begin + x_ref.shape[0]
-            total = total + jnp.dot(
-                weights[:, begin:end], x_ref[:, cols], preferred_element_type=jnp.float32
-            )
-            begin = end
     return total, masses
 
 
 def far_kernel(*refs, which, mine):
     stats_ref, peer_ref = refs[0:2]
-    em_refs, x_refs, (far_ref, mass_ref) = refs[2:5], refs[5:9], refs[9:]
+    em_refs, x_refs, (far_ref, mass_ref) = refs[2:5], refs[5:8], refs[8:]
     count, width = far_ref.shape[0] - PAD, far_ref.shape[1]
     total, masses = weighted(
         stats_ref, peer_ref, em_refs, x_refs, half_rows(mine, count), slice(width, 2 * width), which, True
@@ -364,63 +371,73 @@
     mass_ref[...] = masses
 
 
-def near_kernel(*refs, which, mine, final):
+def near_kernel(*refs, which, mine, final, outs):
     stats_ref, peer_ref = refs[0:2]
-    em_refs, x_refs, (mass_ref, came_ref) = refs[2:5], refs[5:9], refs[9:11]
-    out_ref = refs[12] if final else refs[11]
-    count, width = out_ref.shape[0] - PAD, out_ref.shape[1]
+    em_refs, x_refs, (mass_ref, *came_refs) = refs[2:5], refs[5:8], refs[8 : 9 + SWAPS]
+    refs = refs[9 + SWAPS :]
+    out_refs = refs[final : final + outs]
+    count, width = sum(ref.shape[0] for ref in came_refs) - PAD, came_refs[0].shape[1]
     if final:
-        previous_ref, sem = refs[13:]
-        copy = pltpu.make_async_copy(refs[11].at[half_rows(mine, count), :], previous_ref, sem)
+        previous_ref, sem = refs[1 + outs :]
+        copy = pltpu.make_async_copy(refs[0].at[half_rows(mine, count), :], previous_ref, sem)
         copy.start()
     total, unused = weighted(
         stats_ref, peer_ref, em_refs, x_refs, half_rows(mine, count), slice(0, width), which, False
     )
-    came = came_ref[...].astype(jnp.float32)
+    came = jnp.concatenate([ref[...] for ref in came_refs]).astype(jnp.float32)
     total = total + came[0:count]
     masses = mass_ref[...] + came[count:]
     if final:
         copy.wait()
         total = total + PRIOR * previous_ref[...]
         masses = masses + PRIOR
-    out_ref[0:count, :] = total.astype(out_ref.dtype)
-    out_ref[count:, :] = masses.astype(out_ref.dtype)
-
-
-def far_sums(stats, peer, em, xs, which, mine):
+    lo = 0
+    for out_ref in out_refs:
+        size = min(out_ref.shape[0], count - lo)
+        out_ref[0:size, :] = total[lo : lo + size].astype(out_ref.dtype)
+        lo += size
+    out_refs[-1][size:, :] = masses.astype(out_refs[-1].dtype)
+
+
+def far_sums(stats, peer, em, xs, which, mine, needs=()):
     count, width = em[0].shape[0] // 2, xs[0].shape[1] // 2
     return call(
         lambda *refs: far_kernel(*refs, which=which, mine=mine),
         "far",
-        [VMEM] * 9,
+        [VMEM] * 8,
         [stats, peer, *em, *xs],
         [shape((count + PAD, width), jnp.bfloat16), shape((PAD, width))],
-    )
-
-
-def near_sums(stats, peer, em, xs, which, mine, mass, came, dtype, previous=None):
+        needs=needs,
+    )
+
+
+def near_sums(stats, peer, em, xs, which, mine, mass, came, dtype, parts=(), previous=None, needs=()):
     count, width = em[0].shape[0] // 2, xs[0].shape[1] // 2
     final = previous is not None
+    sizes = list(parts) + [count + PAD - sum(parts)]
     return call(
-        lambda *refs: near_kernel(*refs, which=which, mine=mine, final=final),
+        lambda *refs: near_kernel(*refs, which=which, mine=mine, final=final, outs=len(sizes)),
         "near",
-        [VMEM] * 11 + [HBM] * final,
-        [stats, peer, *em, *xs, mass, came] + [previous] * final,
-        [shape((count + PAD, width), dtype)],
+        [VMEM] * (9 + SWAPS) + [HBM] * final,
+        [stats, peer, *em, *xs, mass, *came] + [previous] * final,
+        [shape((size, width), dtype) for size in sizes],
         [pltpu.VMEM((count, width), jnp.float32), pltpu.SemaphoreType.DMA] * final,
-    )[0]
+        needs,
+    )
 
 
 def add_kernel(a_ref, b_ref, out_ref):
     out_ref[...] = (a_ref[...] + b_ref[...].astype(jnp.float32)).astype(out_ref.dtype)
 
 
-def final_kernel(sums_ref, rep_ref, back_ref, out_ref):
-    count = out_ref.shape[0]
-    sums = sums_ref[...] + rep_ref[...].astype(jnp.float32) + back_ref[...].astype(jnp.float32)
-    mass = jnp.broadcast_to(sums[count : count + 1], (128, count)).T
-    mass = jnp.concatenate([mass] * (out_ref.shape[1] // 128), axis=1)
-    out_ref[...] = sums[0:count] / mass
+def final_kernel(sums_ref, *refs):
+    rep_refs, back_refs, out_ref = refs[0:2], refs[2:4], refs[4]
+    count, width = out_ref.shape
+    rep = jnp.concatenate([ref[...] for ref in rep_refs]).astype(jnp.float32)
+    back = jnp.concatenate([ref[...] for ref in back_refs]).astype(jnp.float32)
+    total = sums_ref[...] + rep + back
+    mass = jnp.broadcast_to(total[count : count + 1], (128, count)).T
+    out_ref[...] = total[:count] / jnp.concatenate([mass] * (width // 128), axis=1)
 
 
 def energy_kernel(stats_ref, peer_ref, square_ref, out_ref, *last_refs, tau, span):
@@ -449,7 +466,8 @@
     for e in range(bal):
         put(facts_ref[0, e], energy_ref[e : e + 1, :])
     for h, came_ref in enumerate(came_refs):
-        put(facts_ref[h + 1, bal + h], came_ref[0:1, :])
+        source = (me - h - 1) % facts_ref.shape[0]
+        put(facts_ref[me ^ source, bal + h], came_ref[0:1, :])
 
 
 def grid_plan(samples, centroids, move_target, fetch_ids, cand):
@@ -469,25 +487,24 @@
     cut = bal * span
     pair_x, pair_c = 2, 1
 
-    c0_own = (centroids * (2.0 / tau)).astype(jnp.bfloat16)
-    c0_oth = swapped(c0_own, "sub")
-    c1_own = paired(c0_own, pair_c)
-
-    facts_own = jnp.concatenate(
+    facts = jnp.concatenate(
         [move_target.reshape(slots_in), fetch_ids.reshape(pool), cand.reshape(bal * lists)]
     )
-    facts = jnp.stack([facts_own] + [passed_along(facts_own, "wide", k) for k in range(1, peers)])
+    facts = jnp.stack([facts] + [paired(facts, flip) for flip in range(1, peers)])
     bias = call(
         lambda *refs: bias_kernel(
-            *refs, slots_in=slots_in, pool=pool, bal=bal, lists=lists, owned=owned, flips=(pair_x, pair_c)
+            *refs, slots_in=slots_in, pool=pool, bal=bal, lists=lists, owned=owned,
+            flips=(pair_x, pair_c), span=span,
         ),
         "bias",
         [SMEM],
         [facts],
-        [shape((2, 2 * owned * slots_in))],
-        [pltpu.SMEM((lists + 1,), jnp.float32)],
-        [SMEM],
+        [shape((2, 2 * owned, lanes))],
     )[0]
+
+    c0_own = (centroids * (2.0 / tau)).astype(jnp.bfloat16)
+    c0_oth = swapped(c0_own, "sub")
+    c1_own = paired(after(c0_own, facts), pair_c)
 
     blocks = samples.reshape(slots_in, rows, width)
     give = lax.dynamic_slice_in_dim(blocks, (1 - sub) * span, span, 1).reshape(lanes, width)
@@ -495,65 +512,88 @@
     own = lax.dynamic_slice_in_dim(blocks, sub * span, span, 1).reshape(lanes, width)
     full = jnp.concatenate([own, took], axis=1)
     x0 = (full[:cut], full[cut:])
-    x1a = paired(x0[0], pair_x)
-    c1_own, x1a, bias = lax.optimization_barrier((c1_own, x1a, bias))
-    x1b = paired(after(x0[1], c1_own), pair_x)
-    c1_oth = swapped(c1_own, "sub")
-
-    def squares(*parts):
-        total = sum(jnp.sum(jnp.square(part.astype(jnp.float32)), axis=1, keepdims=True) for part in parts)
-        return jnp.broadcast_to(total * (tau / 4.0), (owned * rows, 128))
-
+    x1 = [paired(after(part, facts), pair_x) for part in x0]
+    quarter = owned * rows // 4
+    c1_oth = [swapped(c1_own[lo : lo + quarter], "sub") for lo in range(0, owned * rows, quarter)]
+    sets = (joined(c0_own, [c0_oth]), joined(c1_own, c1_oth))
     work_sq = jnp.sum(jnp.square(full.astype(jnp.float32)), axis=1).reshape(1, lanes)
-    sets = ((c0_own, c0_oth, squares(c0_own, c0_oth)), (c1_own, c1_oth, squares(c1_own, c1_oth)))
-
-    *em0, stats0 = score(bias, 0, x0, sets, 0, span, slots_in)
-    *em1a, stats1a = score(bias, 1, [x1a], sets, 0, span, slots_in)
-    *em1b, stats1b = score(bias, 1, [x1b], sets, bal, span, slots_in)
+
+    *em0, stats0 = score(bias, 0, 0, full, sets)
+    *em1a, stats1 = score(bias, 1, 0, x1[0], sets)
+    *em1b, stats = score(bias, 1, cut, x1[1], sets, (stats0, stats1))
     em = list(zip(em0, em1a, em1b))
-    stats = jnp.concatenate([stats0, jnp.concatenate([stats1a, stats1b], axis=1)], axis=0)
     peer = paired(stats, pair_x)
 
-    xs = (*x0, x1a, x1b)
+    xs = (full, *x1)
     half = jnp.bfloat16
-    far_a, mass_a = far_sums(stats, peer, em[1], xs, 1, False)
-    far_b, mass_b = far_sums(after(stats, far_a), peer, em[1], xs, 1, True)
-    came = swapped(far_a, "sub")
-    sent_a = near_sums(after(stats, far_b), peer, em[1], xs, 1, False, mass_a, came, half)
-    came_a = swapped(sent_a, "rep")
-    came = swapped(far_b, "sub")
-    part_b = near_sums(after(stats, sent_a), peer, em[1], xs, 1, True, mass_b, came, jnp.float32)
-
-    far_c, mass_c = far_sums(after(stats, part_b), peer, em[0], xs, 0, False)
-    far_d, mass_d = far_sums(after(stats, far_c), peer, em[0], xs, 0, True)
-    came = swapped(far_c, "sub")
-    sent_c = near_sums(after(stats, far_d), peer, em[0], xs, 0, False, mass_c, came, half)
-    came_c = swapped(sent_c, "rep")
-    came = swapped(far_d, "sub")
-    part_d = near_sums(
-        after(stats, sent_c), peer, em[0], xs, 0, True, mass_d, came, jnp.float32, centroids
-    )
-
-    back = call(add_kernel, "add", [VMEM] * 2, [part_b, came_a], [shape(part_b.shape, half)])[0]
-    came_back = paired(back, pair_c)
-    fresh = call(
-        final_kernel, "final", [VMEM] * 3, [part_d, came_c, came_back], [shape((owned * rows // 2, width))]
-    )[0]
-
     energy, *last = call(
         lambda *refs: energy_kernel(*refs, tau=tau, span=span),
         "energy",
         [VMEM] * 3,
-        [after(stats, part_d), peer, work_sq],
+        [stats, peer, work_sq],
         [shape((slots_in, span))] + [shape((8, span))] * handed,
     )
-    came = [passed_along(last[h], "wide", h + 1) for h in range(handed)]
+
+    first = (288,)
+    equal = (264,)
+    far_a, mass_a = far_sums(stats, peer, em[1], xs, 1, False)
+    far_b, mass_b = far_sums(stats, peer, em[1], xs, 1, True, [far_a])
+
+    def split_swap(far):
+        return [swapped(part, "sub") for part in jnp.split(far, SWAPS)]
+
+    near_a, near_b = split_swap(far_a), split_swap(far_b)
+    sent_a = near_sums(
+        stats, peer, em[1], xs, 1, False, mass_a, near_a, half, first, needs=[far_b]
+    )
+    came_a = [swapped(part, "rep") for part in sent_a]
+    far_c, mass_c = far_sums(stats, peer, em[0], xs, 0, False, sent_a[:1])
+    far_d, mass_d = far_sums(stats, peer, em[0], xs, 0, True, [far_c])
+    near_c, near_d = split_swap(far_c), split_swap(far_d)
+    part_b = near_sums(
+        stats, peer, em[1], xs, 1, True, mass_b, near_b, jnp.float32, first, needs=[far_d]
+    )
+    (part_d,) = near_sums(
+        stats, peer, em[0], xs, 0, True, mass_d, near_d, jnp.float32, (), centroids, part_b[:1]
+    )
+
+    energy, *last = call(
+        lambda *refs: energy_kernel(*refs, tau=tau, span=span),
+        "energy",
+        [VMEM] * 3,
+        [stats, peer, work_sq],
+        [shape((slots_in, span))] + [shape((8, span))] * handed,
+        needs=sent_a[:1],
+    )
+    came_last = [passed_along(last[h], "wide", h + 1) for h in range(handed)]
+
+    came_back = []
+    needs = [part_d, *came_last]
+    for part, came in zip(part_b, came_a):
+        back = call(
+            add_kernel, "add", [VMEM] * 2, [part, came], [shape(part.shape, half)], needs=needs
+        )[0]
+        needs = [back]
+        if not came_back:
+            sent_c = near_sums(
+                stats, peer, em[0], xs, 0, False, mass_c, near_c, half, equal, needs=needs
+            )
+            came_c = [swapped(part, "rep") for part in sent_c]
+        came_back.append(paired(back, pair_c))
     energy = call(
         lambda *refs: place_kernel(*refs, bal=bal),
         "place",
         [SMEM] + [VMEM] * (1 + handed),
-        [facts, energy, *came],
+        [facts, energy, *came_last],
         [shape((bal, span))],
+        needs=[back],
+    )[0]
+    fresh = call(
+        final_kernel,
+        "final",
+        [VMEM] * 5,
+        [part_d, *came_c, *came_back],
+        [shape((owned * rows // 2, width))],
     )[0]
     return (fresh, energy.reshape(1, 1, bal, span))
 

time: 129 us -> 112 us (0.87)
  Pallas kernels: 30.8 us -> 22.7 us
  waiting for transfers between devices: 68.7 us -> 63.1 us
  other arithmetic: 5.14 us -> 1.69 us
    ppermute x5 -> x9, waiting for transfers between devices: 10.6 us -> 59.8 us  [paired(): return lax.ppermute(value, 'wide', [(w, w ^ flip) for w in range(count)])]
    ppermute x5 -> x2, waiting for transfers between devices: 48.9 us -> 1.57 us  [passed_along(): return lax.ppermute(value, axis, pairs)]
    pallas_call x16 -> x19, Pallas kernels: 30.8 us -> 22.7 us  [call(): pl.pallas_call(run, in_specs=in_specs + [HBM] * len(needs), out_specs=[VM...]
    ppermute x9 -> x18, waiting for transfers between devices: 9.22 us -> 1.77 us  [swapped(): return lax.ppermute(value, axis, [(0, 1), (1, 0)])]
    ppermute x5 -> x2, starting transfers between devices: 8.84 us -> 3.3 us  [passed_along(): return lax.ppermute(value, axis, pairs)]
    reduce_sum x4 -> x0, other arithmetic: 3.57 us -> none  [squares(): jnp.sum(jnp.square(part.astype(jnp.float32)), axis=1, keepdims=True)]
    ppermute x5 -> x9, starting transfers between devices: 7 us -> 10.5 us  [paired(): return lax.ppermute(value, 'wide', [(w, w ^ flip) for w in range(count)])]
    ppermute x9 -> x18, starting transfers between devices: 5.09 us -> 7.33 us  [swapped(): return lax.ppermute(value, axis, [(0, 1), (1, 0)])]
  transfers between devices with their start and end apart: 19 -> 29, of which waited for: 7 -> 10; matrix products, arithmetic and copies ran while one was open for 4% -> 2% of each run, Pallas kernels for 16% -> 17%
where the time goes in v3:
time: 112 us
  waiting for transfers between devices  63.1 us (56%)
  Pallas kernels  22.7 us (20%)
  starting transfers between devices  21.1 us (19%)
  local copies, waits for them, and re-layouts  2.53 us (2%)
  other arithmetic  1.69 us (2%)
    ppermute x9, waiting for transfers between devices, paired(): return lax.ppermute(value, 'wide', [(w, w ^ flip) for w in range(count)])  59.8 us
    pallas_call x19, Pallas kernels, call(): pl.pallas_call(run, in_specs=in_specs + [HBM] * len(needs), out_specs=[VM...  22.7 us
    ppermute x9, starting transfers between devices, paired(): return lax.ppermute(value, 'wide', [(w, w ^ flip) for w in range(count)])  10.5 us
    ppermute x18, starting transfers between devices, swapped(): return lax.ppermute(value, axis, [(0, 1), (1, 0)])  7.33 us
    ppermute x2, starting transfers between devices, passed_along(): return lax.ppermute(value, axis, pairs)  3.3 us
  transfers between devices with their start and end apart: 29, of which 10 were waited for; matrix products, arithmetic and copies ran while one was open for 2% of the time, Pallas kernels for 17%

profile of v3, /device:TPU:0, one launch (start us, length us, event | category | flops | bytes accessed | tf_op | source)
XLA Modules:
  0.0 112.0 jit_solution(2265866977858106914)
XLA Ops:
  0.6 0.9 reshape.32
  1.6 0.7 pad_add_fusion.1
  2.3 5.1 %collective-permute-start.2 = (s32[98]{0:T(128)S(1)}, s32[98]{0:T(128)S(1)}, u32[]{:S(2)}, u32[]{:S(2)}) collective-permute-start(s32[98]{0:T(128)S(1)} %pad_add_fusion.1), channel_id=1, source_target_pairs={{0,12},{4,8},{8,4},{12,0},{1,13},{5,9},{9,5},{13,1},{2,14},{6,10},... | collective-permute-start | bytes 1184 | tf_op jit(solution)/shard_map/ppermute | solution.py:177
  7.4 0.6 collective-permute-start
  8.0 1.4 %constant_dynamic-slice_fusion = (bf16[1,1,10,64,512]{4,3,2,1,0:T(8,128)(2,1)S(1)}, bf16[1,1,10,64,512]{4,3,2,1,0:T(8,128)(2,1)S(1)}) fusion(bf16[1,1,10,128,512]{4,3,2,1,0:T(8,128)(2,1)} %param.5, s32[]{:T(128)S(6)} %select_n.7, s32[]{:T(128)S(6)} %select_n.6), kind=kLoop, calls=%fused_computation.11 | loop fusion | bytes 2621448 | tf_op jit(solution)/shard_map/dynamic_slice | solution.py:510
  9.4 0.1 collective-permute-start.3
  9.5 0.3 multiply_convert_fusion.refs_0_
  9.8 0.0 collective-permute-done.2
  9.8 2.0 %collective-permute-done.1 = s32[98]{0:T(128)S(1)} collective-permute-done((s32[98]{0:T(128)S(1)}, s32[98]{0:T(128)S(1)}, u32[]{:S(2)}, u32[]{:S(2)}) %collective-permute-start.1) | collective-permute-done | bytes 424 | tf_op jit(solution)/shard_map/ppermute | solution.py:177
  11.8 0.1 collective-permute-start.6
  11.9 0.1 collective-permute-start.5
  12.0 0.0 collective-permute-done.3
  12.0 0.1 fusion
  12.1 2.5 %collective-permute-start.11 = (bf16[512,1024]{1,0:T(8,128)(2,1)S(1)}, bf16[512,1024]{1,0:T(8,128)(2,1)S(1)}, u32[]{:S(2)}, u32[]{:S(2)}) collective-permute-start(bf16[512,1024]{1,0:T(8,128)(2,1)S(1)} %fusion), channel_id=1, source_target_pairs={{0,8},{4,12},{8,0},{12,4},{1,9},{5,13},{9,1},{13,5},{2,10},{6,14},... | collective-permute-start | bytes 3145736 | tf_op jit(solution)/shard_map/ppermute | solution.py:177
  14.6 42.1 %collective-permute-done.6.refs_0_ = bf16[1024,512]{1,0:T(8,128)(2,1)S(1)} collective-permute-done((bf16[1024,512]{1,0:T(8,128)(2,1)S(1)}, bf16[1024,512]{1,0:T(8,128)(2,1)S(1)}, u32[]{:S(2)}, u32[]{:S(2)}) %collective-permute-start.6) | collective-permute-done | bytes 1048608 | tf_op jit(solution)/shard_map/ppermute | solution.py:177
  56.7 0.1 fusion.2
  56.8 0.1 collective-permute-start.10
  56.9 0.5 collective-permute-start.9
  57.4 0.1 collective-permute-start.8
  57.5 0.4 collective-permute-start.7
  57.9 0.5 collective-permute-done.10.refs_4_
  58.4 1.3 %bias.1.refs_0_ = f32[2,16,640]{2,1,0:T(8,128)S(1)} custom-call(s32[4,98]{1,0:T(4,128)S(1)} %pad_add_fusion.refs_0_), custom_call_target="tpu_custom_call" | custom-call | flops 1 | bytes 1 | tf_op jit(solution)/shard_map/bias/pallas_call | solution.py:194
  59.8 0.2 pad_maximum_fusion.refs_1_.refs_5_
  59.9 0.5 join.2
  60.5 0.5 join.3
  61.0 4.5 %scores.3 = (bf16[1024,640]{1,0:T(8,128)(2,1)S(1)}, bf16[1024,640]{1,0:T(8,128)(2,1)S(1)}, f32[4,640]{1,0:T(4,128)S(1)}) custom-call(f32[2,16,640]{2,1,0:T(8,128)S(1)} %bias.1.refs_0_, bf16[640,1024]{1,0:T(8,128)(2,1)S(1)} %pad_maximum_fusion.refs_1_.refs_5_, bf16[1024,1024]{1,0:T(8,128)(2,1)S(1)} %get-tuple-element.36.refs_2_, ...), custom_call_target="tpu_custom_call" | custom-call | flops 1 | bytes 1 | tf_op jit(solution)/shard_map/scores/pallas_call | solution.py:194
  65.5 1.3 %collective-permute-done.11.refs_1_.refs_6_ = bf16[512,1024]{1,0:T(8,128)(2,1)S(1)} collective-permute-done((bf16[512,1024]{1,0:T(8,128)(2,1)S(1)}, bf16[512,1024]{1,0:T(8,128)(2,1)S(1)}, u32[]{:S(2)}, u32[]{:S(2)}) %collective-permute-start.11) | collective-permute-done | bytes 1048608 | tf_op jit(solution)/shard_map/ppermute | solution.py:177
  66.8 3.2 %scores.4 = (bf16[1024,512]{1,0:T(8,128)(2,1)S(1)}, bf16[1024,512]{1,0:T(8,128)(2,1)S(1)}, f32[4,512]{1,0:T(4,128)S(1)}) custom-call(f32[2,16,640]{2,1,0:T(8,128)S(1)} %bias.1.refs_0_, bf16[512,1024]{1,0:T(8,128)(2,1)S(1)} %collective-permute-done.11.refs_1_.refs_6_, bf16[1024,1024]{1,0:T(8,128)(2,1)S(1)} %get-tuple-element.36.refs_2_, ...), custom_call_target="tpu_custom_call" | custom-call | flops 1 | bytes 1 | tf_op jit(solution)/shard_map/scores/pallas_call | solution.py:194
  70.0 2.4 %collective-permute-done.4.refs_1_.refs_7_ = bf16[128,1024]{1,0:T(8,128)(2,1)S(1)} collective-permute-done((bf16[128,1024]{1,0:T(8,128)(2,1)S(1)}, bf16[128,1024]{1,0:T(8,128)(2,1)S(1)}, u32[]{:S(2)}, u32[]{:S(2)}) %collective-permute-start.4) | collective-permute-done | bytes 262176 | tf_op jit(solution)/shard_map/ppermute | solution.py:177
  72.4 1.4 %scores.5 = (bf16[1024,128]{1,0:T(8,128)(2,1)S(1)}, bf16[1024,128]{1,0:T(8,128)(2,1)S(1)}, f32[8,640]{1,0:T(8,128)S(1)}) custom-call(f32[2,16,640]{2,1,0:T(8,128)S(1)} %bias.1.refs_0_, bf16[128,1024]{1,0:T(8,128)(2,1)S(1)} %collective-permute-done.4.refs_1_.refs_7_, bf16[1024,1024]{1,0:T(8,128)(2,1)S(1)} %get-tuple-element.36.refs_2_, ...), custom_call_target="tpu_custom_call" | custom-call | flops 1 | bytes 1 | tf_op jit(solution)/shard_map/scores/pallas_call | solution.py:194
  73.8 0.1 collective-permute-start.12
  73.9 4.7 %collective-permute-done.12.refs_1_ = f32[8,640]{1,0:T(8,128)S(1)} collective-permute-done((f32[8,640]{1,0:T(8,128)S(1)}, f32[8,640]{1,0:T(8,128)S(1)}, u32[]{:S(2)}, u32[]{:S(2)}) %collective-permute-start.12) | collective-permute-done | bytes 20512 | tf_op jit(solution)/shard_map/ppermute | solution.py:177
  78.6 1.0 far.4
  79.6 0.1 collective-permute-start.14
  79.7 0.5 collective-permute-start.13
  80.2 1.2 %far.5 = (bf16[528,512]{1,0:T(8,128)(2,1)S(1)}, f32[16,512]{1,0:T(8,128)S(1)}) custom-call(f32[8,640]{1,0:T(8,128)S(1)} %get-tuple-element.44.refs_0_, f32[8,640]{1,0:T(8,128)S(1)} %collective-permute-done.12.refs_1_, bf16[1024,640]{1,0:T(8,128)(2,1)S(1)} %get-tuple-element.48.refs_2_, bf16[1024,512]{1,0:T(8,128)(2,1)S(1)} %get-tuple-element.49.refs_3_, ...), custom_call_target="tpu_custom_call" | custom-call | flops 1 | bytes 1 | tf_op jit(solution)/shard_map/far/pallas_call | solution.py:194
  81.4 0.1 collective-permute-start.18
  81.6 0.3 multiply_reduce_fusion
  81.9 0.5 collective-permute-start.17
  82.4 1.0 near.4
  83.4 1.6 %collective-permute-start.21 = (bf16[288,512]{1,0:T(8,128)(2,1)S(1)}, bf16[288,512]{1,0:T(8,128)(2,1)S(1)}, u32[]{:S(2)}, u32[]{:S(2)}) collective-permute-start(bf16[288,512]{1,0:T(8,128)(2,1)S(1)} %get-tuple-element.54.refs_8_.refs_3_), channel_id=1, source_target_pairs={{0,2},{2,0},{1,3},{3,1},{4,6},{6,4},{5,7},{7,5},{8,10},{10,8},{9,1... | collective-permute-start | bytes 884744 | tf_op jit(solution)/shard_map/ppermute | solution.py:172
  85.0 0.1 energy.1
  85.1 1.0 collective-permute-start.22
  86.2 1.0 far.6
  87.2 1.0 far.7
  88.3 0.1 collective-permute-start.16
  88.3 0.5 collective-permute-start.15
  88.9 0.2 collective-permute-start.20
  89.0 1.5 %collective-permute-done.22.refs_3_.refs_2_ = f32[8,64]{1,0:T(8,128)S(1)} collective-permute-done((f32[8,64]{1,0:T(8,128)S(1)}, f32[8,64]{1,0:T(8,128)S(1)}, u32[]{:S(2)}, u32[]{:S(2)}) %collective-permute-start.22) | collective-permute-done | bytes 2080 | tf_op jit(solution)/shard_map/ppermute | solution.py:19
  90.6 0.5 collective-permute-start.27
  91.1 2.3 %collective-permute-start.23 = (f32[8,64]{1,0:T(8,128)S(1)}, f32[8,64]{1,0:T(8,128)S(1)}, u32[]{:S(2)}, u32[]{:S(2)}) collective-permute-start(f32[8,64]{1,0:T(8,128)S(1)} %get-tuple-element.62), channel_id=1, source_target_pairs={{0,8},{4,12},{8,0},{12,4},{1,9},{5,13},{9,1},{13,5},{2,10},{6,14},... | collective-permute-start | bytes 6152 | tf_op jit(solution)/shard_map/ppermute | solution.py:19
  93.3 1.0 near.5
  94.3 1.2 %near.6.refs_2_.refs_0_ = f32[528,512]{1,0:T(8,128)S(1)} custom-call(f32[8,640]{1,0:T(8,128)S(1)} %get-tuple-element.44.refs_0_, f32[8,640]{1,0:T(8,128)S(1)} %collective-permute-done.12.refs_1_, bf16[1024,640]{1,0:T(8,128)(2,1)S(1)} %get-tuple-element.45.refs_2_, bf16[1024,512]{1,0:T(8,128)(2,1)S(1)} %get-tuple-element.46.refs_3_, ...), custom_call_target="tpu_custom_call" | custom-call | flops 1 | bytes 1 | tf_op jit(solution)/shard_map/near/pallas_call | solution.py:194
  95.5 0.1 collective-permute-done.23.refs_4_.refs_3_
  95.6 0.1 add.20.refs_11_.refs_2_
  95.7 0.4 collective-permute-start.26
  96.1 1.0 near.7
  97.1 1.6 %collective-permute-start.24 = (bf16[264,512]{1,0:T(8,128)(2,1)S(1)}, bf16[264,512]{1,0:T(8,128)(2,1)S(1)}, u32[]{:S(2)}, u32[]{:S(2)}) collective-permute-start(bf16[264,512]{1,0:T(8,128)(2,1)S(1)} %get-tuple-element.63), channel_id=1, source_target_pairs={{0,2},{2,0},{1,3},{3,1},{4,6},{6,4},{5,7},{7,5},{8,10},{10,8},{9,1... | collective-permute-start | bytes 811016 | tf_op jit(solution)/shard_map/ppermute | solution.py:172
  98.7 0.5 collective-permute-start.25
  99.2 1.7 %collective-permute-start.28 = (bf16[240,512]{1,0:T(8,128)(2,1)S(1)}, bf16[240,512]{1,0:T(8,128)(2,1)S(1)}, u32[]{:S(2)}, u32[]{:S(2)}) collective-permute-start(bf16[240,512]{1,0:T(8,128)(2,1)S(1)} %add.21.refs_4_), channel_id=1, source_target_pairs={{0,4},{4,0},{8,12},{12,8},{1,5},{5,1},{9,13},{13,9},{2,6},{6,2},{1... | collective-permute-start | bytes 737288 | tf_op jit(solution)/shard_map/ppermute | solution.py:177
  101.0 1.3 %place.1 = f32[8,64]{1,0:T(8,128)} custom-call(s32[4,98]{1,0:T(4,128)S(1)} %pad_add_fusion.refs_0_, f32[10,64]{1,0:T(8,128)S(1)} %get-tuple-element.67.refs_1_, f32[8,64]{1,0:T(8,128)S(1)} %collective-permute-done.22.refs_3_.refs_2_, f32[8,64]{1,0:T(8,128)S(1)} %collective-permute-done.23.refs_4_.refs_3_, bf16[240,512]{1,0:T(8,128)(2,1)S(1)} %add.21.refs_4_), custom_call_target="tpu_custom_call" | custom-call | flops 1 | bytes 1 | tf_op jit(solution)/shard_map/place/pallas_call | solution.py:194
  102.3 7.3 %collective-permute-done.28.refs_4_ = bf16[240,512]{1,0:T(8,128)(2,1)S(1)} collective-permute-done((bf16[240,512]{1,0:T(8,128)(2,1)S(1)}, bf16[240,512]{1,0:T(8,128)(2,1)S(1)}, u32[]{:S(2)}, u32[]{:S(2)}) %collective-permute-start.28) | collective-permute-done | bytes 245792 | tf_op jit(solution)/shard_map/ppermute | solution.py:177
  109.6 1.2 %collective-permute-done.25.refs_2_ = bf16[264,512]{1,0:T(8,128)(2,1)S(1)} collective-permute-done((bf16[264,512]{1,0:T(8,128)(2,1)S(1)}, bf16[264,512]{1,0:T(8,128)(2,1)S(1)}, u32[]{:S(2)}, u32[]{:S(2)}) %collective-permute-start.25) | collective-permute-done | bytes 270368 | tf_op jit(solution)/shard_map/ppermute | solution.py:172
  110.8 1.2 %final.1 = f32[512,512]{1,0:T(8,128)} custom-call(f32[528,512]{1,0:T(8,128)S(1)} %near.6.refs_2_.refs_0_, bf16[264,512]{1,0:T(8,128)(2,1)S(1)} %collective-permute-done.24.refs_1_, bf16[264,512]{1,0:T(8,128)(2,1)S(1)} %collective-permute-done.25.refs_2_, bf16[288,512]{1,0:T(8,128)(2,1)S(1)} %collective-permute-done.26.refs_3_, ...), custom_call_target="tpu_custom_call" | custom-call | flops 1 | bytes 1 | tf_op jit(solution)/shard_map/final/pallas_call | solution.py:194
  (30 shorter events, 0.3 us)
Async XLA Ops:
  0.6 8.8 %copy-start = (f32[1024,512]{1,0:T(8,128)S(1)}, f32[1024,512]{1,0:T(8,128)}, u32[]{:S(2)}) copy-start(f32[1024,512]{1,0:T(8,128)} %refs_11_.1) | copy-start | bytes 6291460
  2.3 7.5 %collective-permute-start.2 = (s32[98]{0:T(128)S(1)}, s32[98]{0:T(128)S(1)}, u32[]{:S(2)}, u32[]{:S(2)}) collective-permute-start(s32[98]{0:T(128)S(1)} %pad_add_fusion.1), channel_id=1, source_target_pairs={{0,12},{4,8},{8,4},{12,0},{1,13},{5,9},{9,5},{13,1},{2,14},{6,10},... | collective-permute-start | bytes 1184 | tf_op jit(solution)/shard_map/ppermute | solution.py:177
  7.4 4.4 %collective-permute-start.1 = (s32[98]{0:T(128)S(1)}, s32[98]{0:T(128)S(1)}, u32[]{:S(2)}, u32[]{:S(2)}) collective-permute-start(s32[98]{0:T(128)S(1)} %pad_add_fusion.1), channel_id=1, source_target_pairs={{0,8},{4,12},{8,0},{12,4},{1,9},{5,13},{9,1},{13,5},{2,10},{6,14},... | collective-permute-start | bytes 1184 | tf_op jit(solution)/shard_map/ppermute | solution.py:177
  7.4 4.4 %collective-permute-start = (s32[98]{0:T(128)S(1)}, s32[98]{0:T(128)S(1)}, u32[]{:S(2)}, u32[]{:S(2)}) collective-permute-start(s32[98]{0:T(128)S(1)} %pad_add_fusion.1), channel_id=1, source_target_pairs={{0,4},{4,0},{8,12},{12,8},{1,5},{5,1},{9,13},{13,9},{2,6},{6,2},{1... | collective-permute-start | bytes 1184 | tf_op jit(solution)/shard_map/ppermute | solution.py:177
  9.4 2.6 %collective-permute-start.3 = (bf16[640,512]{1,0:T(8,128)(2,1)S(1)}, bf16[640,512]{1,0:T(8,128)(2,1)S(1)}, u32[]{:S(2)}, u32[]{:S(2)}) collective-permute-start(bf16[640,512]{1,0:T(8,128)(2,1)S(1)} %bitcast.15), channel_id=1, source_target_pairs={{0,1},{1,0},{2,3},{3,2},{4,5},{5,4},{6,7},{7,6},{8,9},{9,8},{10,11... | collective-permute-start | bytes 1966088 | tf_op jit(solution)/shard_map/ppermute | solution.py:172
  11.8 44.9 %collective-permute-start.6 = (bf16[1024,512]{1,0:T(8,128)(2,1)S(1)}, bf16[1024,512]{1,0:T(8,128)(2,1)S(1)}, u32[]{:S(2)}, u32[]{:S(2)}) collective-permute-start(bf16[1024,512]{1,0:T(8,128)(2,1)S(1)} %multiply_convert_fusion.refs_0_), channel_id=1, source_target_pairs={{0,4},{4,0},{8,12},{12,8},{1,5},{5,1},{9,13},{13,9},{2,6},{6,2},{1... | collective-permute-start | bytes 3145736 | tf_op jit(solution)/shard_map/ppermute | solution.py:177
  11.9 45.6 %collective-permute-start.5 = (bf16[1024,512]{1,0:T(8,128)(2,1)S(1)}, bf16[1024,512]{1,0:T(8,128)(2,1)S(1)}, u32[]{:S(2)}, u32[]{:S(2)}) collective-permute-start(bf16[1024,512]{1,0:T(8,128)(2,1)S(1)} %multiply_convert_fusion.refs_0_), channel_id=1, source_target_pairs={{0,1},{1,0},{2,3},{3,2},{4,5},{5,4},{6,7},{7,6},{8,9},{9,8},{10,11... | collective-permute-start | bytes 3145736 | tf_op jit(solution)/shard_map/ppermute | solution.py:172
  12.1 54.7 %collective-permute-start.11 = (bf16[512,1024]{1,0:T(8,128)(2,1)S(1)}, bf16[512,1024]{1,0:T(8,128)(2,1)S(1)}, u32[]{:S(2)}, u32[]{:S(2)}) collective-permute-start(bf16[512,1024]{1,0:T(8,128)(2,1)S(1)} %fusion), channel_id=1, source_target_pairs={{0,8},{4,12},{8,0},{12,4},{1,9},{5,13},{9,1},{13,5},{2,10},{6,14},... | collective-permute-start | bytes 3145736 | tf_op jit(solution)/shard_map/ppermute | solution.py:177
  56.8 1.6 %collective-permute-start.10 = (bf16[256,512]{1,0:T(8,128)(2,1)S(1)}, bf16[256,512]{1,0:T(8,128)(2,1)S(1)}, u32[]{:S(2)}, u32[]{:S(2)}) collective-permute-start(bf16[256,512]{1,0:T(8,128)(2,1)S(1)} %get-tuple-element.70), channel_id=1, source_target_pairs={{0,1},{1,0},{2,3},{3,2},{4,5},{5,4},{6,7},{7,6},{8,9},{9,8},{10,11... | collective-permute-start | bytes 786440 | tf_op jit(solution)/shard_map/ppermute | solution.py:172
  56.9 3.6 %collective-permute-start.9 = (bf16[256,512]{1,0:T(8,128)(2,1)S(1)}, bf16[256,512]{1,0:T(8,128)(2,1)S(1)}, u32[]{:S(2)}, u32[]{:S(2)}) collective-permute-start(bf16[256,512]{1,0:T(8,128)(2,1)S(1)} %get-tuple-element.71), channel_id=1, source_target_pairs={{0,1},{1,0},{2,3},{3,2},{4,5},{5,4},{6,7},{7,6},{8,9},{9,8},{10,11... | collective-permute-start | bytes 786440 | tf_op jit(solution)/shard_map/ppermute | solution.py:172
  57.4 3.1 %collective-permute-start.8 = (bf16[256,512]{1,0:T(8,128)(2,1)S(1)}, bf16[256,512]{1,0:T(8,128)(2,1)S(1)}, u32[]{:S(2)}, u32[]{:S(2)}) collective-permute-start(bf16[256,512]{1,0:T(8,128)(2,1)S(1)} %get-tuple-element.72), channel_id=1, source_target_pairs={{0,1},{1,0},{2,3},{3,2},{4,5},{5,4},{6,7},{7,6},{8,9},{9,8},{10,11... | collective-permute-start | bytes 786440 | tf_op jit(solution)/shard_map/ppermute | solution.py:172
  57.5 3.0 %collective-permute-start.7 = (bf16[256,512]{1,0:T(8,128)(2,1)S(1)}, bf16[256,512]{1,0:T(8,128)(2,1)S(1)}, u32[]{:S(2)}, u32[]{:S(2)}) collective-permute-start(bf16[256,512]{1,0:T(8,128)(2,1)S(1)} %get-tuple-element.73), channel_id=1, source_target_pairs={{0,1},{1,0},{2,3},{3,2},{4,5},{5,4},{6,7},{7,6},{8,9},{9,8},{10,11... | collective-permute-start | bytes 786440 | tf_op jit(solution)/shard_map/ppermute | solution.py:172
  58.4 13.9 %collective-permute-start.4 = (bf16[128,1024]{1,0:T(8,128)(2,1)S(1)}, bf16[128,1024]{1,0:T(8,128)(2,1)S(1)}, u32[]{:S(2)}, u32[]{:S(2)}) collective-permute-start(bf16[128,1024]{1,0:T(8,128)(2,1)S(1)} %fusion.1), channel_id=1, source_target_pairs={{0,8},{4,12},{8,0},{12,4},{1,9},{5,13},{9,1},{13,5},{2,10},{6,14},... | collective-permute-start | bytes 786440 | tf_op jit(solution)/shard_map/ppermute | solution.py:177
  73.8 4.7 %collective-permute-start.12 = (f32[8,640]{1,0:T(8,128)S(1)}, f32[8,640]{1,0:T(8,128)S(1)}, u32[]{:S(2)}, u32[]{:S(2)}) collective-permute-start(f32[8,640]{1,0:T(8,128)S(1)} %get-tuple-element.44.refs_0_), channel_id=1, source_target_pairs={{0,8},{4,12},{8,0},{12,4},{1,9},{5,13},{9,1},{13,5},{2,10},{6,14},... | collective-permute-start | bytes 61448 | tf_op jit(solution)/shard_map/ppermute | solution.py:177
  79.6 2.8 %collective-permute-start.14 = (bf16[264,512]{1,0:T(8,128)(2,1)S(1)}, bf16[264,512]{1,0:T(8,128)(2,1)S(1)}, u32[]{:S(2)}, u32[]{:S(2)}) collective-permute-start(bf16[264,512]{1,0:T(8,128)(2,1)S(1)} %get-tuple-element.80), channel_id=1, source_target_pairs={{0,1},{1,0},{2,3},{3,2},{4,5},{5,4},{6,7},{7,6},{8,9},{9,8},{10,11... | collective-permute-start | bytes 811016 | tf_op jit(solution)/shard_map/ppermute | solution.py:172
  79.7 2.7 %collective-permute-start.13 = (bf16[264,512]{1,0:T(8,128)(2,1)S(1)}, bf16[264,512]{1,0:T(8,128)(2,1)S(1)}, u32[]{:S(2)}, u32[]{:S(2)}) collective-permute-start(bf16[264,512]{1,0:T(8,128)(2,1)S(1)} %get-tuple-element.81), channel_id=1, source_target_pairs={{0,1},{1,0},{2,3},{3,2},{4,5},{5,4},{6,7},{7,6},{8,9},{9,8},{10,11... | collective-permute-start | bytes 811016 | tf_op jit(solution)/shard_map/ppermute | solution.py:172
  81.4 6.9 %collective-permute-start.18 = (bf16[264,512]{1,0:T(8,128)(2,1)S(1)}, bf16[264,512]{1,0:T(8,128)(2,1)S(1)}, u32[]{:S(2)}, u32[]{:S(2)}) collective-permute-start(bf16[264,512]{1,0:T(8,128)(2,1)S(1)} %get-tuple-element.76), channel_id=1, source_target_pairs={{0,1},{1,0},{2,3},{3,2},{4,5},{5,4},{6,7},{7,6},{8,9},{9,8},{10,11... | collective-permute-start | bytes 811016 | tf_op jit(solution)/shard_map/ppermute | solution.py:172
  81.9 7.0 %collective-permute-start.17 = (bf16[264,512]{1,0:T(8,128)(2,1)S(1)}, bf16[264,512]{1,0:T(8,128)(2,1)S(1)}, u32[]{:S(2)}, u32[]{:S(2)}) collective-permute-start(bf16[264,512]{1,0:T(8,128)(2,1)S(1)} %get-tuple-element.77), channel_id=1, source_target_pairs={{0,1},{1,0},{2,3},{3,2},{4,5},{5,4},{6,7},{7,6},{8,9},{9,8},{10,11... | collective-permute-start | bytes 811016 | tf_op jit(solution)/shard_map/ppermute | solution.py:172
  83.4 12.1 %collective-permute-start.21 = (bf16[288,512]{1,0:T(8,128)(2,1)S(1)}, bf16[288,512]{1,0:T(8,128)(2,1)S(1)}, u32[]{:S(2)}, u32[]{:S(2)}) collective-permute-start(bf16[288,512]{1,0:T(8,128)(2,1)S(1)} %get-tuple-element.54.refs_8_.refs_3_), channel_id=1, source_target_pairs={{0,2},{2,0},{1,3},{3,1},{4,6},{6,4},{5,7},{7,5},{8,10},{10,8},{9,1... | collective-permute-start | bytes 884744 | tf_op jit(solution)/shard_map/ppermute | solution.py:172
  85.1 5.4 %collective-permute-start.22 = (f32[8,64]{1,0:T(8,128)S(1)}, f32[8,64]{1,0:T(8,128)S(1)}, u32[]{:S(2)}, u32[]{:S(2)}) collective-permute-start(f32[8,64]{1,0:T(8,128)S(1)} %get-tuple-element.61), channel_id=1, source_target_pairs={{0,4},{4,8},{8,12},{12,0},{1,5},{5,9},{9,13},{13,1},{2,6},{6,10},{... | collective-permute-start | bytes 6152 | tf_op jit(solution)/shard_map/ppermute | solution.py:19
  88.3 2.3 %collective-permute-start.16 = (bf16[264,512]{1,0:T(8,128)(2,1)S(1)}, bf16[264,512]{1,0:T(8,128)(2,1)S(1)}, u32[]{:S(2)}, u32[]{:S(2)}) collective-permute-start(bf16[264,512]{1,0:T(8,128)(2,1)S(1)} %get-tuple-element.78), channel_id=1, source_target_pairs={{0,1},{1,0},{2,3},{3,2},{4,5},{5,4},{6,7},{7,6},{8,9},{9,8},{10,11... | collective-permute-start | bytes 811016 | tf_op jit(solution)/shard_map/ppermute | solution.py:172
  88.3 2.7 %collective-permute-start.15 = (bf16[264,512]{1,0:T(8,128)(2,1)S(1)}, bf16[264,512]{1,0:T(8,128)(2,1)S(1)}, u32[]{:S(2)}, u32[]{:S(2)}) collective-permute-start(bf16[264,512]{1,0:T(8,128)(2,1)S(1)} %get-tuple-element.79), channel_id=1, source_target_pairs={{0,1},{1,0},{2,3},{3,2},{4,5},{5,4},{6,7},{7,6},{8,9},{9,8},{10,11... | collective-permute-start | bytes 811016 | tf_op jit(solution)/shard_map/ppermute | solution.py:172
  88.9 7.2 %collective-permute-start.20 = (bf16[264,512]{1,0:T(8,128)(2,1)S(1)}, bf16[264,512]{1,0:T(8,128)(2,1)S(1)}, u32[]{:S(2)}, u32[]{:S(2)}) collective-permute-start(bf16[264,512]{1,0:T(8,128)(2,1)S(1)} %get-tuple-element.74), channel_id=1, source_target_pairs={{0,1},{1,0},{2,3},{3,2},{4,5},{5,4},{6,7},{7,6},{8,9},{9,8},{10,11... | collective-permute-start | bytes 811016 | tf_op jit(solution)/shard_map/ppermute | solution.py:172
  90.6 5.5 %collective-permute-start.19 = (bf16[264,512]{1,0:T(8,128)(2,1)S(1)}, bf16[264,512]{1,0:T(8,128)(2,1)S(1)}, u32[]{:S(2)}, u32[]{:S(2)}) collective-permute-start(bf16[264,512]{1,0:T(8,128)(2,1)S(1)} %get-tuple-element.75), channel_id=1, source_target_pairs={{0,1},{1,0},{2,3},{3,2},{4,5},{5,4},{6,7},{7,6},{8,9},{9,8},{10,11... | collective-permute-start | bytes 811016 | tf_op jit(solution)/shard_map/ppermute | solution.py:172
  90.6 8.6 %collective-permute-start.27 = (bf16[240,512]{1,0:T(8,128)(2,1)S(1)}, bf16[240,512]{1,0:T(8,128)(2,1)S(1)}, u32[]{:S(2)}, u32[]{:S(2)}) collective-permute-start(bf16[240,512]{1,0:T(8,128)(2,1)S(1)} %get-tuple-element.66), channel_id=1, source_target_pairs={{0,2},{2,0},{1,3},{3,1},{4,6},{6,4},{5,7},{7,5},{8,10},{10,8},{9,1... | collective-permute-start | bytes 737288 | tf_op jit(solution)/shard_map/ppermute | solution.py:172
  91.1 4.5 %collective-permute-start.23 = (f32[8,64]{1,0:T(8,128)S(1)}, f32[8,64]{1,0:T(8,128)S(1)}, u32[]{:S(2)}, u32[]{:S(2)}) collective-permute-start(f32[8,64]{1,0:T(8,128)S(1)} %get-tuple-element.62), channel_id=1, source_target_pairs={{0,8},{4,12},{8,0},{12,4},{1,9},{5,13},{9,1},{13,5},{2,10},{6,14},... | collective-permute-start | bytes 6152 | tf_op jit(solution)/shard_map/ppermute | solution.py:19
  95.7 15.2 %collective-permute-start.26 = (bf16[288,512]{1,0:T(8,128)(2,1)S(1)}, bf16[288,512]{1,0:T(8,128)(2,1)S(1)}, u32[]{:S(2)}, u32[]{:S(2)}) collective-permute-start(bf16[288,512]{1,0:T(8,128)(2,1)S(1)} %add.20.refs_11_.refs_2_), channel_id=1, source_target_pairs={{0,4},{4,0},{8,12},{12,8},{1,5},{5,1},{9,13},{13,9},{2,6},{6,2},{1... | collective-permute-start | bytes 884744 | tf_op jit(solution)/shard_map/ppermute | solution.py:177
  97.1 12.5 %collective-permute-start.24 = (bf16[264,512]{1,0:T(8,128)(2,1)S(1)}, bf16[264,512]{1,0:T(8,128)(2,1)S(1)}, u32[]{:S(2)}, u32[]{:S(2)}) collective-permute-start(bf16[264,512]{1,0:T(8,128)(2,1)S(1)} %get-tuple-element.63), channel_id=1, source_target_pairs={{0,2},{2,0},{1,3},{3,1},{4,6},{6,4},{5,7},{7,5},{8,10},{10,8},{9,1... | collective-permute-start | bytes 811016 | tf_op jit(solution)/shard_map/ppermute | solution.py:172
  98.7 12.1 %collective-permute-start.25 = (bf16[264,512]{1,0:T(8,128)(2,1)S(1)}, bf16[264,512]{1,0:T(8,128)(2,1)S(1)}, u32[]{:S(2)}, u32[]{:S(2)}) collective-permute-start(bf16[264,512]{1,0:T(8,128)(2,1)S(1)} %get-tuple-element.64), channel_id=1, source_target_pairs={{0,2},{2,0},{1,3},{3,1},{4,6},{6,4},{5,7},{7,5},{8,10},{10,8},{9,1... | collective-permute-start | bytes 811016 | tf_op jit(solution)/shard_map/ppermute | solution.py:172
  99.2 10.3 %collective-permute-start.28 = (bf16[240,512]{1,0:T(8,128)(2,1)S(1)}, bf16[240,512]{1,0:T(8,128)(2,1)S(1)}, u32[]{:S(2)}, u32[]{:S(2)}) collective-permute-start(bf16[240,512]{1,0:T(8,128)(2,1)S(1)} %add.21.refs_4_), channel_id=1, source_target_pairs={{0,4},{4,0},{8,12},{12,8},{1,5},{5,1},{9,13},{13,9},{2,6},{6,2},{1... | collective-permute-start | bytes 737288 | tf_op jit(solution)/shard_map/ppermute | solution.py:177

commit v4 on v3

--- a/solution.py
+++ b/solution.py
@@ -162,7 +162,6 @@
 FLOOR = -1e29
 MEGA = 2**20
 PAD = 16
-SWAPS = 2
 HBM = pl.BlockSpec(memory_space=pl.ANY)
 VMEM = pl.BlockSpec(memory_space=pltpu.VMEM)
 SMEM = pl.BlockSpec(memory_space=pltpu.SMEM)
@@ -185,7 +184,7 @@
     return jax.ShapeDtypeStruct(dims, dtype)
 
 
-def call(kernel, name, in_specs, args, outs, scratch=(), needs=()):
+def call(kernel, name, in_specs, args, outs, scratch=(), needs=(), flops=1):
     count = len(args)
 
     def run(*refs):
@@ -198,28 +197,28 @@
         out_shape=outs,
         scratch_shapes=scratch,
         compiler_params=pltpu.CompilerParams(vmem_limit_bytes=16 * MEGA),
-        cost_estimate=pl.CostEstimate(flops=1, bytes_accessed=1, transcendentals=0),
+        cost_estimate=pl.CostEstimate(flops=flops, bytes_accessed=1, transcendentals=0),
         name=name,
     )(*args, *needs)
 
 
-def bias_kernel(facts_ref, bias_ref, *, slots_in, pool, bal, lists, owned, flips, span):
+def bias_kernel(facts_ref, bias_ref, *, slots_in, bal, lists, owned, flips, span):
     me = lax.axis_index("wide")
     lanes = slots_in * span
     row = lax.broadcasted_iota(jnp.int32, (2 * owned, 128), 0)
-    block_id = jnp.where(row < owned, me * owned + row, (me ^ flips[1]) * owned + row - owned)
+    swung = (row + lax.axis_index("rep") * (owned // 2)) % owned
+    block_id = jnp.where(row < owned, me * owned + row, (me ^ flips[1]) * owned + swung)
     place = lax.broadcasted_iota(jnp.int32, (1, 128), 1) // span
     for k in range(2):
         for lo in range(0, lanes, 128):
             listed = [jnp.full((1, 128), -1, jnp.int32) for j in range(lists)]
             for p in range(128 // span):
-                target = facts_ref[flips[0] if k else 0, lo // span + p]
+                target = facts_ref[flips[0] if k else 0, 0, lo // span + p]
                 live = target >= 0
                 target = jnp.maximum(target, 0)
                 source = me ^ (target // bal)
-                first = slots_in + pool + (target % bal) * lists
                 for j in range(lists):
-                    block = facts_ref[source, slots_in + facts_ref[source, first + j]]
+                    block = facts_ref[source, 1, facts_ref[source, 2 + target % bal, j]]
                     listed[j] = jnp.where(place == p, jnp.where(live, block, -1), listed[j])
             times = jnp.zeros((2 * owned, 128), jnp.float32)
             for j in range(lists):
@@ -228,13 +227,13 @@
             bias_ref[k, :, lo : lo + 128] = jnp.where(times > 0, logs, LOW)
 
 
-def join_kernel(own_ref, *refs):
-    oth_refs, (c_ref, square_ref) = refs[:-2], refs[-2:]
-    width = own_ref.shape[1]
+def join_kernel(*refs):
+    half_refs, (c_ref, square_ref) = refs[:-2], refs[-2:]
+    width = half_refs[0].shape[1]
     lo = 0
-    for oth_ref in oth_refs:
+    for own_ref, oth_ref in zip(half_refs[0::2], half_refs[1::2]):
         part = pl.ds(lo, oth_ref.shape[0])
-        own, oth = own_ref[part, :], oth_ref[...]
+        own, oth = own_ref[...], oth_ref[...]
         c_ref[part, 0:width] = own
         c_ref[part, width:] = oth
         total = jnp.zeros((part.size, 128), jnp.float32)
@@ -247,29 +246,29 @@
         lo += part.size
 
 
-def joined(own, oths):
-    count, width = own.shape
-    outs = [shape((count, 2 * width), own.dtype), shape((count, 128))]
-    return call(join_kernel, "join", [VMEM] * (1 + len(oths)), [own, *oths], outs)
+def joined(pairs, needs=()):
+    count, width = sum(own.shape[0] for own, oth in pairs), pairs[0][0].shape[1]
+    outs = [shape((count, 2 * width), jnp.bfloat16), shape((count, 128))]
+    flat = [part for pair in pairs for part in pair]
+    return call(join_kernel, "join", [VMEM] * len(flat), flat, outs, needs=needs)
 
 
 def tiles(lanes):
     return [(lo, min(256, lanes - lo)) for lo in range(0, lanes, 256)]
 
 
-def score_kernel(bias_ref, x_ref, c0_ref, csq0_ref, c1_ref, csq1_ref, *refs, chunk, first):
-    before_refs, em_refs, (stats_ref, dots_ref) = refs[:-4], refs[-4:-2], refs[-2:]
-    lead = 0
-    for ref in before_refs:
-        row, lane = 4 * (lead // stats_ref.shape[1]), lead % stats_ref.shape[1]
-        stats_ref[row : row + 4, lane : lane + ref.shape[1]] = ref[...]
-        lead += ref.shape[1]
-    row, lane = 4 * (lead // stats_ref.shape[1]), lead % stats_ref.shape[1]
+def score_kernel(bias_ref, x_ref, *refs, chunk, sets, at):
+    c_refs, refs = refs[: 2 * len(sets)], refs[2 * len(sets) :]
+    before_refs, refs = refs[: len(at) - 1], refs[len(at) - 1 :]
+    em_refs, (stats_ref, dots_ref) = refs[: len(sets)], refs[len(sets) :]
+    for ref, (row, lane) in zip(before_refs, at[1:]):
+        stats_ref[row : row + ref.shape[0], lane : lane + ref.shape[1]] = ref[...]
     count = bias_ref.shape[1] // 2
     rows = dots_ref.shape[1] // count
     turn = 0
     for lo, size in tiles(x_ref.shape[0]):
-        for s, (c_ref, csq_ref) in enumerate(((c0_ref, csq0_ref), (c1_ref, csq1_ref))):
+        for i, s in enumerate(sets):
+            c_ref, csq_ref = c_refs[2 * i : 2 * i + 2]
             part = slice(lo, lo + size)
             buf = dots_ref.at[turn % 2]
             turn += 1
@@ -282,8 +281,7 @@
                 less = jnp.concatenate([csq_ref[block, :]] * (size // 128), axis=1)
                 return (buf[block, 0:size] - less).reshape(rows // 8, 8, size)
 
-            of_chunk = slice(first + lo, first + lo + size)
-            bias = [bias_ref[chunk, s * count + g : s * count + g + 1, of_chunk] for g in range(count)]
+            bias = [bias_ref[chunk, s * count + g : s * count + g + 1, part] for g in range(count)]
             best = jnp.full((8, size), FLOOR, jnp.float32)
             for g in range(count):
                 best = jnp.maximum(best, jnp.max(logits(g), axis=0) + bias[g])
@@ -291,22 +289,24 @@
             total = jnp.zeros((8, size), jnp.float32)
             for g in range(count):
                 expo = jnp.exp(logits(g) + (bias[g] - top)[None])
-                em_refs[s][pl.ds(g * rows, rows), part] = expo.reshape(rows, size).astype(jnp.bfloat16)
+                em_refs[i][pl.ds(g * rows, rows), part] = expo.reshape(rows, size).astype(jnp.bfloat16)
                 total = total + jnp.sum(expo, axis=0)
-            out = slice(lane + lo, lane + lo + size)
-            stats_ref[row + 2 * s : row + 2 * s + 1, out] = top
-            stats_ref[row + 2 * s + 1 : row + 2 * s + 2, out] = jnp.sum(total, axis=0, keepdims=True)
-
-
-def score(bias, chunk, first, x, sets, before=()):
-    cols = sets[0][0].shape[0]
-    stats = shape((8, bias.shape[2]) if before else (4, x.shape[0]))
+            row, lane = at[0][0] + 2 * i, at[0][1] + lo
+            stats_ref[row : row + 1, lane : lane + size] = top
+            stats_ref[row + 1 : row + 2, lane : lane + size] = jnp.sum(total, axis=0, keepdims=True)
+
+
+def score(bias, chunk, x, sets, before=()):
+    cols = next(iter(sets.values()))[0].shape[0]
+    count = len(sets)
+    at = [(4 * chunk, 0) if before else (0, 0)] + [(row, lane) for part, row, lane in before]
+    stats = shape((8, bias.shape[2]) if before else (2 * count, x.shape[0]))
     return call(
-        lambda *refs: score_kernel(*refs, chunk=chunk, first=first),
+        lambda *refs: score_kernel(*refs, chunk=chunk, sets=list(sets), at=at),
         "scores",
-        [VMEM] * (6 + len(before)),
-        [bias, x, *sets[0], *sets[1], *before],
-        [shape((cols, x.shape[0]), jnp.bfloat16)] * 2 + [stats],
+        [VMEM] * (2 + 2 * count + len(before)),
+        [bias, x, *[part for c in sets.values() for part in c], *[part[0] for part in before]],
+        [shape((cols, x.shape[0]), jnp.bfloat16)] * count + [stats],
         [pltpu.VMEM((2, cols, 256), jnp.float32)],
     )
 
@@ -331,7 +331,9 @@
     ]
 
 
-def half_rows(mine, count):
+def half_rows(mine, count, which=0):
+    if which:
+        return pl.ds(0 if mine else count, count)
     rep = lax.axis_index("rep")
     return pl.ds(pl.multiple_of((rep if mine else 1 - rep) * count, count), count)
 
@@ -360,10 +362,10 @@
 
 def far_kernel(*refs, which, mine):
     stats_ref, peer_ref = refs[0:2]
-    em_refs, x_refs, (far_ref, mass_ref) = refs[2:5], refs[5:8], refs[8:]
+    em_refs, x_refs, (far_ref, mass_ref) = refs[2:4], refs[4:6], refs[6:]
     count, width = far_ref.shape[0] - PAD, far_ref.shape[1]
     total, masses = weighted(
-        stats_ref, peer_ref, em_refs, x_refs, half_rows(mine, count), slice(width, 2 * width), which, True
+        stats_ref, peer_ref, em_refs, x_refs, half_rows(mine, count, which), slice(width, 2 * width), which, True
     )
     masses = jnp.broadcast_to(jnp.sum(masses, axis=1, keepdims=True), (count, 128)).T[0:PAD]
     far_ref[0:count, :] = total.astype(jnp.bfloat16)
@@ -371,10 +373,10 @@
     mass_ref[...] = masses
 
 
-def near_kernel(*refs, which, mine, final, outs):
+def near_kernel(*refs, which, mine, final, outs, swaps):
     stats_ref, peer_ref = refs[0:2]
-    em_refs, x_refs, (mass_ref, *came_refs) = refs[2:5], refs[5:8], refs[8 : 9 + SWAPS]
-    refs = refs[9 + SWAPS :]
+    em_refs, x_refs, (mass_ref, *came_refs) = refs[2:4], refs[4:6], refs[6 : 7 + swaps]
+    refs = refs[7 + swaps :]
     out_refs = refs[final : final + outs]
     count, width = sum(ref.shape[0] for ref in came_refs) - PAD, came_refs[0].shape[1]
     if final:
@@ -382,7 +384,7 @@
         copy = pltpu.make_async_copy(refs[0].at[half_rows(mine, count), :], previous_ref, sem)
         copy.start()
     total, unused = weighted(
-        stats_ref, peer_ref, em_refs, x_refs, half_rows(mine, count), slice(0, width), which, False
+        stats_ref, peer_ref, em_refs, x_refs, half_rows(mine, count, which), slice(0, width), which, False
     )
     came = jnp.concatenate([ref[...] for ref in came_refs]).astype(jnp.float32)
     total = total + came[0:count]
@@ -404,7 +406,7 @@
     return call(
         lambda *refs: far_kernel(*refs, which=which, mine=mine),
         "far",
-        [VMEM] * 8,
+        [VMEM] * 6,
         [stats, peer, *em, *xs],
         [shape((count + PAD, width), jnp.bfloat16), shape((PAD, width))],
         needs=needs,
@@ -416,9 +418,9 @@
     final = previous is not None
     sizes = list(parts) + [count + PAD - sum(parts)]
     return call(
-        lambda *refs: near_kernel(*refs, which=which, mine=mine, final=final, outs=len(sizes)),
+        lambda *refs: near_kernel(*refs, which=which, mine=mine, final=final, outs=len(sizes), swaps=len(came)),
         "near",
-        [VMEM] * (9 + SWAPS) + [HBM] * final,
+        [VMEM] * (7 + len(came)) + [HBM] * final,
         [stats, peer, *em, *xs, mass, *came] + [previous] * final,
         [shape((size, width), dtype) for size in sizes],
         [pltpu.VMEM((count, width), jnp.float32), pltpu.SemaphoreType.DMA] * final,
@@ -430,31 +432,45 @@
     out_ref[...] = (a_ref[...] + b_ref[...].astype(jnp.float32)).astype(out_ref.dtype)
 
 
-def final_kernel(sums_ref, *refs):
-    rep_refs, back_refs, out_ref = refs[0:2], refs[2:4], refs[4]
+def early_kernel(came_ref, out_ref):
+    out_ref[...] = came_ref[...].astype(out_ref.dtype)
+
+
+def final_kernel(early_ref, sums_ref, *refs, parts):
+    rep_refs, back_refs, out_ref = refs[:parts], refs[parts:-1], refs[-1]
     count, width = out_ref.shape
+    first = early_ref.shape[0]
     rep = jnp.concatenate([ref[...] for ref in rep_refs]).astype(jnp.float32)
     back = jnp.concatenate([ref[...] for ref in back_refs]).astype(jnp.float32)
-    total = sums_ref[...] + rep + back
-    mass = jnp.broadcast_to(total[count : count + 1], (128, count)).T
-    out_ref[...] = total[:count] / jnp.concatenate([mass] * (width // 128), axis=1)
-
-
-def energy_kernel(stats_ref, peer_ref, square_ref, out_ref, *last_refs, tau, span):
-    top, denom = combine(chunk_parts(stats_ref[...], peer_ref[...], 0))
-    energy = -tau * (top - square_ref[...] / tau + jnp.log(denom)) / D
-    entries = energy.shape[1] // span
-    out_ref[...] = jnp.zeros_like(out_ref)
-    for e in range(entries):
-        part = energy[:, e * span : (e + 1) * span]
-        out_ref[e : e + 1, :] = part
-        back = e - (entries - len(last_refs))
-        if back >= 0:
-            last_refs[back][...] = jnp.broadcast_to(part, last_refs[back].shape)
-
-
-def place_kernel(facts_ref, energy_ref, *refs, bal):
-    came_refs, out_ref = refs[:-1], refs[-1]
+    later = sums_ref[first:, :] + rep[first:] + back
+    mass = jnp.broadcast_to(later[count - first : count - first + 1], (128, count)).T
+    mass = jnp.concatenate([mass] * (width // 128), axis=1)
+    out_ref[0:first, :] = (sums_ref[0:first, :] + early_ref[...] + rep[0:first]) / mass[0:first]
+    out_ref[first:, :] = later[: count - first] / mass[first:]
+
+
+def energy_kernel(stats_ref, peer_ref, x0_ref, x1_ref, out_ref, last_ref, *, tau, span, handed):
+    last_ref[...] = jnp.zeros_like(last_ref)
+    for chunk, x_ref in enumerate((x0_ref, x1_ref)):
+        lanes, depth = x_ref.shape
+        square = jnp.zeros((lanes, 128), jnp.float32)
+        for lane in range(0, depth, 128):
+            part = x_ref[:, lane : lane + 128].astype(jnp.float32)
+            square = square + part * part
+        square = jnp.sum(jnp.broadcast_to(jnp.sum(square, axis=1, keepdims=True), (lanes, 128)).T[0:1], axis=0, keepdims=True)
+        top, denom = combine(chunk_parts(stats_ref[...], peer_ref[...], chunk))
+        energy = -tau * (top - square / tau + jnp.log(denom)) / D
+        entries = lanes // span
+        for e in range(entries):
+            part = energy[:, e * span : (e + 1) * span]
+            if chunk == 0:
+                out_ref[e : e + 1, :] = part
+            if e >= entries - handed:
+                row = handed * chunk + e - (entries - handed)
+                last_ref[row : row + 1, :] = part
+
+
+def place_kernel(facts_ref, energy_ref, last_ref, came_ref, out_ref, *, bal):
     me = lax.axis_index("wide")
     out_ref[...] = jnp.zeros_like(out_ref)
 
@@ -464,10 +480,11 @@
             out_ref[pl.ds(target % bal, 1), :] = row
 
     for e in range(bal):
-        put(facts_ref[0, e], energy_ref[e : e + 1, :])
-    for h, came_ref in enumerate(came_refs):
-        source = (me - h - 1) % facts_ref.shape[0]
-        put(facts_ref[me ^ source, bal + h], came_ref[0:1, :])
+        put(facts_ref[0, 0, e], energy_ref[e : e + 1, :])
+    odd = me % 2 == 1
+    one = jnp.where(odd, last_ref[2:3, :], came_ref[2:3, :])
+    put(facts_ref[jnp.where(odd, 1, 3), 0, bal], one)
+    put(facts_ref[2, 0, bal + 1], came_ref[1:2, :])
 
 
 def grid_plan(samples, centroids, move_target, fetch_ids, cand):
@@ -484,17 +501,14 @@
     handed = slots_in - bal
     span = rows // 2
     lanes = slots_in * span
-    cut = bal * span
-    pair_x, pair_c = 2, 1
-
-    facts = jnp.concatenate(
-        [move_target.reshape(slots_in), fetch_ids.reshape(pool), cand.reshape(bal * lists)]
-    )
+    pair_x, pair_c = 1, 2
+
+    table = [move_target.reshape(1, slots_in), fetch_ids.reshape(1, pool), cand.reshape(bal, lists)]
+    facts = jnp.concatenate([jnp.pad(part, ((0, 0), (0, pool - part.shape[1]))) for part in table])
     facts = jnp.stack([facts] + [paired(facts, flip) for flip in range(1, peers)])
     bias = call(
         lambda *refs: bias_kernel(
-            *refs, slots_in=slots_in, pool=pool, bal=bal, lists=lists, owned=owned,
-            flips=(pair_x, pair_c), span=span,
+            *refs, slots_in=slots_in, bal=bal, lists=lists, owned=owned, flips=(pair_x, pair_c), span=span
         ),
         "bias",
         [SMEM],
@@ -502,105 +516,104 @@
         [shape((2, 2 * owned, lanes))],
     )[0]
 
+    share = owned * rows // 2
+    c_half = lax.dynamic_slice_in_dim(centroids, lax.axis_index("rep") * share, share, 0)
+    c_half = (c_half * (2.0 / tau)).astype(jnp.bfloat16)
     c0_own = (centroids * (2.0 / tau)).astype(jnp.bfloat16)
+    c1_own = [paired(after(c_half, facts), pair_c)]
+    c1_own.append(swapped(c1_own[0], "rep"))
     c0_oth = swapped(c0_own, "sub")
-    c1_own = paired(after(c0_own, facts), pair_c)
 
     blocks = samples.reshape(slots_in, rows, width)
     give = lax.dynamic_slice_in_dim(blocks, (1 - sub) * span, span, 1).reshape(lanes, width)
     took = swapped(give, "sub")
     own = lax.dynamic_slice_in_dim(blocks, sub * span, span, 1).reshape(lanes, width)
     full = jnp.concatenate([own, took], axis=1)
-    x0 = (full[:cut], full[cut:])
-    x1 = [paired(after(part, facts), pair_x) for part in x0]
-    quarter = owned * rows // 4
-    c1_oth = [swapped(c1_own[lo : lo + quarter], "sub") for lo in range(0, owned * rows, quarter)]
-    sets = (joined(c0_own, [c0_oth]), joined(c1_own, c1_oth))
-    work_sq = jnp.sum(jnp.square(full.astype(jnp.float32)), axis=1).reshape(1, lanes)
-
-    *em0, stats0 = score(bias, 0, 0, full, sets)
-    *em1a, stats1 = score(bias, 1, 0, x1[0], sets)
-    *em1b, stats = score(bias, 1, cut, x1[1], sets, (stats0, stats1))
-    em = list(zip(em0, em1a, em1b))
+    x1 = paired(after(full, facts), pair_x)
+
+    set_a = joined([(c0_own, c0_oth)])
+    em_a0, stats_a0 = score(bias, 0, full, {0: set_a})
+    c1_oth = [swapped(part, "sub") for part in (c1_own[0], after(c1_own[1], stats_a0))]
+    set_b = joined(list(zip(c1_own, c1_oth)), [stats_a0])
+    em_b0, stats_b0 = score(bias, 0, full, {1: set_b})
+    before = [(stats_a0, 0, 0), (stats_b0, 2, 0)]
+    em_a1, em_b1, stats = score(bias, 1, x1, {0: set_a, 1: set_b}, before)
+    em = ((em_a0, em_a1), (em_b0, em_b1))
     peer = paired(stats, pair_x)
 
-    xs = (full, *x1)
+    xs = (full, x1)
     half = jnp.bfloat16
-    energy, *last = call(
-        lambda *refs: energy_kernel(*refs, tau=tau, span=span),
-        "energy",
-        [VMEM] * 3,
-        [stats, peer, work_sq],
-        [shape((slots_in, span))] + [shape((8, span))] * handed,
-    )
-
-    first = (288,)
-    equal = (264,)
+    first, equal = (272,), (264,)
+
     far_a, mass_a = far_sums(stats, peer, em[1], xs, 1, False)
     far_b, mass_b = far_sums(stats, peer, em[1], xs, 1, True, [far_a])
-
-    def split_swap(far):
-        return [swapped(part, "sub") for part in jnp.split(far, SWAPS)]
-
-    near_a, near_b = split_swap(far_a), split_swap(far_b)
+    far_c, mass_c = far_sums(stats, peer, em[0], xs, 0, False, [far_b])
+    near_a = [swapped(part, "sub") for part in jnp.split(far_a, 2)]
+    near_b, near_c = [[swapped(far, "sub")] for far in (far_b, far_c)]
     sent_a = near_sums(
-        stats, peer, em[1], xs, 1, False, mass_a, near_a, half, first, needs=[far_b]
-    )
-    came_a = [swapped(part, "rep") for part in sent_a]
-    far_c, mass_c = far_sums(stats, peer, em[0], xs, 0, False, sent_a[:1])
-    far_d, mass_d = far_sums(stats, peer, em[0], xs, 0, True, [far_c])
-    near_c, near_d = split_swap(far_c), split_swap(far_d)
+        stats, peer, em[1], xs, 1, False, mass_a, near_a, half, first, needs=[far_c]
+    )
     part_b = near_sums(
-        stats, peer, em[1], xs, 1, True, mass_b, near_b, jnp.float32, first, needs=[far_d]
-    )
-    (part_d,) = near_sums(
-        stats, peer, em[0], xs, 0, True, mass_d, near_d, jnp.float32, (), centroids, part_b[:1]
-    )
-
-    energy, *last = call(
-        lambda *refs: energy_kernel(*refs, tau=tau, span=span),
+        stats, peer, em[1], xs, 1, True, mass_b, near_b, jnp.float32, first, needs=sent_a[:1]
+    )
+    energy, last = call(
+        lambda *refs: energy_kernel(*refs, tau=tau, span=span, handed=handed),
         "energy",
-        [VMEM] * 3,
-        [stats, peer, work_sq],
-        [shape((slots_in, span))] + [shape((8, span))] * handed,
-        needs=sent_a[:1],
-    )
-    came_last = [passed_along(last[h], "wide", h + 1) for h in range(handed)]
-
-    came_back = []
-    needs = [part_d, *came_last]
-    for part, came in zip(part_b, came_a):
+        [VMEM] * 4,
+        [stats, peer, *xs],
+        [shape((slots_in, span)), shape((8, span))],
+        needs=part_b[:1],
+    )
+    came_last = paired(last, 2)
+
+    def returned(part, came, needs):
         back = call(
             add_kernel, "add", [VMEM] * 2, [part, came], [shape(part.shape, half)], needs=needs
         )[0]
-        needs = [back]
-        if not came_back:
-            sent_c = near_sums(
-                stats, peer, em[0], xs, 0, False, mass_c, near_c, half, equal, needs=needs
-            )
-            came_c = [swapped(part, "rep") for part in sent_c]
-        came_back.append(paired(back, pair_c))
+        return back, paired(back, pair_c)
+
+    back, came_back_0 = returned(part_b[0], swapped(sent_a[0], "rep"), [came_last])
+    came = swapped(after(sent_a[1], back), "rep")
+    sent_c = near_sums(
+        stats, peer, em[0], xs, 0, False, mass_c, near_c, half, equal, needs=[back]
+    )
+    came_c = [swapped(part, "rep") for part in sent_c]
+    back, came_back_1 = returned(part_b[1], came, [])
+    came_back = [came_back_0, came_back_1]
+    far_d, mass_d = far_sums(stats, peer, em[0], xs, 0, True, [back])
+    near_d = [swapped(far_d, "sub")]
+    (part_d,) = near_sums(
+        stats, peer, em[0], xs, 0, True, mass_d, near_d, jnp.float32, (), centroids, sent_c[:1]
+    )
+    early = call(
+        early_kernel,
+        "early",
+        [VMEM],
+        [came_back[0]],
+        [shape((first[0], width))],
+        flops=2 * 10**10,
+    )[0]
     energy = call(
         lambda *refs: place_kernel(*refs, bal=bal),
         "place",
-        [SMEM] + [VMEM] * (1 + handed),
-        [facts, energy, *came_last],
+        [SMEM] + [VMEM] * 3,
+        [facts, energy, last, came_last],
         [shape((bal, span))],
         needs=[back],
     )[0]
     fresh = call(
-        final_kernel,
+        lambda *refs: final_kernel(*refs, parts=len(came_c)),
         "final",
-        [VMEM] * 5,
-        [part_d, *came_c, *came_back],
-        [shape((owned * rows // 2, width))],
+        [VMEM] * (2 + len(came_c) + len(came_back[1:])),
+        [early, part_d, *came_c, *came_back[1:]],
+        [shape((share, width))],
     )[0]
     return (fresh, energy.reshape(1, 1, bal, span))
 
 
 def body(samples, centroids, move_target, fetch_ids, cand):
     sizes = [lax.axis_size(axis) for axis in ("wide", "rep", "sub")]
-    if sizes == [4, 2, 2]:
+    if sizes == [4, 2, 2] and samples.shape[2] - cand.shape[2] == 2:
         return grid_plan(samples, centroids, move_target, fetch_ids, cand)
     return exchange_plan(samples, centroids, move_target, fetch_ids, cand)
 

time: 112 us -> 105 us (0.938)
  waiting for transfers between devices: 63.1 us -> 51.1 us
  Pallas kernels: 22.7 us -> 25.1 us
  starting transfers between devices: 21.1 us -> 22.8 us
    ppermute x9, waiting for transfers between devices: 59.8 us -> 38.2 us  [paired(): return lax.ppermute(value, 'wide', [(w, w ^ flip) for w in range(count)])]
    ppermute x18 -> x14, waiting for transfers between devices: 1.77 us -> 12.9 us  [swapped(): return lax.ppermute(value, axis, [(0, 1), (1, 0)])]
    ppermute x9, starting transfers between devices: 10.5 us -> 14.3 us  [paired(): return lax.ppermute(value, 'wide', [(w, w ^ flip) for w in range(count)])]
    ppermute x2 -> x0, starting transfers between devices: 3.3 us -> none  [passed_along(): return lax.ppermute(value, axis, pairs)]
    pallas_call x19 -> x20, Pallas kernels: 22.7 us -> 25.1 us  [call(): pl.pallas_call(run, in_specs=in_specs + [HBM] * len(needs), out_specs=[VM...]
    ppermute x2 -> x0, waiting for transfers between devices: 1.57 us -> none  [passed_along(): return lax.ppermute(value, axis, pairs)]
    dynamic_slice x1, local copies, waits for them, and re-layouts: 1.39 us -> 2.63 us  [grid_plan(): lax.dynamic_slice_in_dim(blocks, sub * span, span, 1).reshape(lanes, width)]
    ppermute x18 -> x14, starting transfers between devices: 7.33 us -> 8.55 us  [swapped(): return lax.ppermute(value, axis, [(0, 1), (1, 0)])]
  transfers between devices with their start and end apart: 29 -> 23, of which waited for: 10 -> 11; matrix products, arithmetic and copies ran while one was open for 2% -> 4% of each run, Pallas kernels for 17% -> 17%
where the time goes in v4:
time: 105 us
  waiting for transfers between devices  51.1 us (49%)
  Pallas kernels  25.1 us (24%)
  starting transfers between devices  22.8 us (22%)
  local copies, waits for them, and re-layouts  2.68 us (3%)
  other arithmetic  2.34 us (2%)
    ppermute x9, waiting for transfers between devices, paired(): return lax.ppermute(value, 'wide', [(w, w ^ flip) for w in range(count)])  38.2 us
    pallas_call x20, Pallas kernels, call(): pl.pallas_call(run, in_specs=in_specs + [HBM] * len(needs), out_specs=[VM...  25.1 us
    ppermute x9, starting transfers between devices, paired(): return lax.ppermute(value, 'wide', [(w, w ^ flip) for w in range(count)])  14.3 us
    ppermute x14, waiting for transfers between devices, swapped(): return lax.ppermute(value, axis, [(0, 1), (1, 0)])  12.9 us
    ppermute x14, starting transfers between devices, swapped(): return lax.ppermute(value, axis, [(0, 1), (1, 0)])  8.55 us
    dynamic_slice x1, local copies, waits for them, and re-layouts, grid_plan(): lax.dynamic_slice_in_dim(blocks, sub * span, span, 1).reshape(lanes, width)  2.63 us
  transfers between devices with their start and end apart: 23, of which 11 were waited for; matrix products, arithmetic and copies ran while one was open for 4% of the time, Pallas kernels for 17%

profile of v4, /device:TPU:0, one launch (start us, length us, event | category | flops | bytes accessed | tf_op | source)
XLA Modules:
  0.0 104.9 jit_solution(13792582960228701427)
XLA Ops:
  0.6 0.7 fusion
  1.3 4.1 %collective-permute-start.1 = (s32[10,24]{1,0:T(8,128)S(1)}, s32[10,24]{1,0:T(8,128)S(1)}, u32[]{:S(2)}, u32[]{:S(2)}) collective-permute-start(s32[10,24]{1,0:T(8,128)S(1)} %get-tuple-element.69), channel_id=1, source_target_pairs={{0,8},{4,12},{8,0},{12,4},{1,9},{5,13},{9,1},{13,5},{2,10},{6,14},... | collective-permute-start | bytes 2888 | tf_op jit(solution)/shard_map/ppermute | solution.py:176
  5.4 1.6 %collective-permute-start = (s32[10,24]{1,0:T(8,128)S(1)}, s32[10,24]{1,0:T(8,128)S(1)}, u32[]{:S(2)}, u32[]{:S(2)}) collective-permute-start(s32[10,24]{1,0:T(8,128)S(1)} %get-tuple-element.69), channel_id=1, source_target_pairs={{0,4},{4,0},{8,12},{12,8},{1,5},{5,1},{9,13},{13,9},{2,6},{6,2},{1... | collective-permute-start | bytes 2888 | tf_op jit(solution)/shard_map/ppermute | solution.py:176
  7.0 0.0 collective-permute-start.2
  7.0 2.6 %constant_dynamic-slice_fusion.1 = (bf16[1,1,10,64,512]{4,3,2,1,0:T(8,128)(2,1)}, bf16[1,1,10,64,512]{4,3,2,1,0:T(8,128)(2,1)}) fusion(bf16[1,1,10,128,512]{4,3,2,1,0:T(8,128)(2,1)} %param.5, s32[]{:T(128)S(6)} %select_n.9, s32[]{:T(128)S(6)} %select_n.10), kind=kLoop, calls=%fused_computation.7 | loop fusion | bytes 2621448 | tf_op jit(solution)/shard_map/dynamic_slice | solution.py:530
  9.7 0.0 collective-permute-start.3
  9.7 0.3 multiply_convert_fusion.refs_0_
  9.9 0.6 collective-permute-start.5
  10.5 0.1 multiply_convert_fusion.1
  10.6 0.0 collective-permute-done.1
  10.7 1.8 %collective-permute-done.2 = s32[10,24]{1,0:T(8,128)S(1)} collective-permute-done((s32[10,24]{1,0:T(8,128)S(1)}, s32[10,24]{1,0:T(8,128)S(1)}, u32[]{:S(2)}, u32[]{:S(2)}) %collective-permute-start.2) | collective-permute-done | bytes 992 | tf_op jit(solution)/shard_map/ppermute | solution.py:176
  12.5 0.2 collective-permute-start.6
  12.7 0.0 collective-permute-done.3
  12.7 1.2 %pad_maximum_fusion.refs_1_.refs_4_.refs_2_ = bf16[640,1024]{1,0:T(8,128)(2,1)S(1)} fusion(bf16[640,512]{1,0:T(8,128)(2,1)} %collective-permute-done.3, bf16[640,512]{1,0:T(8,128)(2,1)S(1)} %bitcast.11), kind=kLoop, calls=%fused_computation.1 | loop fusion | flops 2621440 | bytes 2621440 | tf_op jit(solution)/shard_map/concatenate | solution.py:531
  13.9 2.5 %collective-permute-start.4 = (bf16[640,1024]{1,0:T(8,128)(2,1)S(1)}, bf16[640,1024]{1,0:T(8,128)(2,1)S(1)}, u32[]{:S(2)}, u32[]{:S(2)}) collective-permute-start(bf16[640,1024]{1,0:T(8,128)(2,1)S(1)} %pad_maximum_fusion.refs_1_.refs_4_.refs_2_), channel_id=1, source_target_pairs={{0,4},{4,0},{8,12},{12,8},{1,5},{5,1},{9,13},{13,9},{2,6},{6,2},{1... | collective-permute-start | bytes 3932168 | tf_op jit(solution)/shard_map/ppermute | solution.py:176
  16.4 20.4 %collective-permute-done.6.refs_0_ = bf16[512,512]{1,0:T(8,128)(2,1)S(1)} collective-permute-done((bf16[512,512]{1,0:T(8,128)(2,1)S(1)}, bf16[512,512]{1,0:T(8,128)(2,1)S(1)}, u32[]{:S(2)}, u32[]{:S(2)}) %collective-permute-start.6) | collective-permute-done | bytes 524320 | tf_op jit(solution)/shard_map/ppermute | solution.py:176
  36.9 1.7 %collective-permute-start.8 = (bf16[512,512]{1,0:T(8,128)(2,1)S(1)}, bf16[512,512]{1,0:T(8,128)(2,1)S(1)}, u32[]{:S(2)}, u32[]{:S(2)}) collective-permute-start(bf16[512,512]{1,0:T(8,128)(2,1)S(1)} %collective-permute-done.6.refs_0_), channel_id=1, source_target_pairs={{0,2},{2,0},{1,3},{3,1},{4,6},{6,4},{5,7},{7,5},{8,10},{10,8},{9,1... | collective-permute-start | bytes 1572872 | tf_op jit(solution)/shard_map/ppermute | solution.py:171
  38.6 1.6 %bias.1.refs_0_ = f32[2,16,640]{2,1,0:T(8,128)S(1)} custom-call(s32[4,10,24]{2,1,0:T(8,128)S(1)} %pad_add_fusion.refs_0_), custom_call_target="tpu_custom_call" | custom-call | flops 1 | bytes 1 | tf_op jit(solution)/shard_map/bias/pallas_call | solution.py:193
  40.2 0.1 collective-permute-start.7
  40.3 1.7 %join.2 = (bf16[1024,1024]{1,0:T(8,128)(2,1)S(1)}, f32[1024,128]{1,0:T(8,128)S(1)}) custom-call(bf16[1024,512]{1,0:T(8,128)(2,1)S(1)} %multiply_convert_fusion.refs_0_, bf16[1024,512]{1,0:T(8,128)(2,1)} %collective-permute-done.5.refs_1_), custom_call_target="tpu_custom_call" | custom-call | flops 1 | bytes 1 | tf_op jit(solution)/shard_map/join/pallas_call | solution.py:193
  42.0 2.4 %scores.3 = (bf16[1024,640]{1,0:T(8,128)(2,1)S(1)}, f32[2,640]{1,0:T(2,128)S(1)}) custom-call(f32[2,16,640]{2,1,0:T(8,128)S(1)} %bias.1.refs_0_, bf16[640,1024]{1,0:T(8,128)(2,1)S(1)} %pad_maximum_fusion.refs_1_.refs_4_.refs_2_, bf16[1024,1024]{1,0:T(8,128)(2,1)S(1)} %get-tuple-element.34.refs_2_, f32[1024,128]{1,0:T(8,128)S(1)} %get-tuple-element.35.refs_3_), custom_call_target="tpu_custom_call" | custom-call | flops 1 | bytes 1 | tf_op jit(solution)/shard_map/scores/pallas_call | solution.py:193
  44.4 5.2 %collective-permute-done.8.refs_2_ = bf16[512,512]{1,0:T(8,128)(2,1)S(1)} collective-permute-done((bf16[512,512]{1,0:T(8,128)(2,1)S(1)}, bf16[512,512]{1,0:T(8,128)(2,1)S(1)}, u32[]{:S(2)}, u32[]{:S(2)}) %collective-permute-start.8) | collective-permute-done | bytes 524320 | tf_op jit(solution)/shard_map/ppermute | solution.py:171
  49.6 0.0 collective-permute-start.9
  49.6 0.0 collective-permute-done.7.refs_1_
  49.6 1.9 %collective-permute-done.9.refs_3_ = bf16[512,512]{1,0:T(8,128)(2,1)S(1)} collective-permute-done((bf16[512,512]{1,0:T(8,128)(2,1)S(1)}, bf16[512,512]{1,0:T(8,128)(2,1)S(1)}, u32[]{:S(2)}, u32[]{:S(2)}) %collective-permute-start.9) | collective-permute-done | bytes 524320 | tf_op jit(solution)/shard_map/ppermute | solution.py:171
  51.5 0.5 join.3
  52.0 2.4 %scores.4 = (bf16[1024,640]{1,0:T(8,128)(2,1)S(1)}, f32[2,640]{1,0:T(2,128)S(1)}) custom-call(f32[2,16,640]{2,1,0:T(8,128)S(1)} %bias.1.refs_0_, bf16[640,1024]{1,0:T(8,128)(2,1)S(1)} %pad_maximum_fusion.refs_1_.refs_4_.refs_2_, bf16[1024,1024]{1,0:T(8,128)(2,1)S(1)} %get-tuple-element.39.refs_2_.refs_4_, f32[1024,128]{1,0:T(8,128)S(1)} %get-tuple-element.40.refs_3_.refs_5_), custom_call_target="tpu_custom_call" | custom-call | flops 1 | bytes 1 | tf_op jit(solution)/shard_map/scores/pallas_call | solution.py:193
  54.4 0.7 collective-permute-done.4.refs_1_.refs_5_.refs_3_
  55.1 4.6 %scores.5 = (bf16[1024,640]{1,0:T(8,128)(2,1)S(1)}, bf16[1024,640]{1,0:T(8,128)(2,1)S(1)}, f32[8,640]{1,0:T(8,128)S(1)}) custom-call(f32[2,16,640]{2,1,0:T(8,128)S(1)} %bias.1.refs_0_, bf16[640,1024]{1,0:T(8,128)(2,1)S(1)} %collective-permute-done.4.refs_1_.refs_5_.refs_3_, bf16[1024,1024]{1,0:T(8,128)(2,1)S(1)} %get-tuple-element.34.refs_2_, ...), custom_call_target="tpu_custom_call" | custom-call | flops 1 | bytes 1 | tf_op jit(solution)/shard_map/scores/pallas_call | solution.py:193
  59.7 0.4 collective-permute-start.10
  60.1 3.4 %collective-permute-done.10.refs_1_ = f32[8,640]{1,0:T(8,128)S(1)} collective-permute-done((f32[8,640]{1,0:T(8,128)S(1)}, f32[8,640]{1,0:T(8,128)S(1)}, u32[]{:S(2)}, u32[]{:S(2)}) %collective-permute-start.10) | collective-permute-done | bytes 20512 | tf_op jit(solution)/shard_map/ppermute | solution.py:176
  63.5 1.0 far.4
  64.6 0.1 collective-permute-start.13
  64.6 0.5 collective-permute-start.12
  65.1 1.0 far.5
  66.2 0.1 collective-permute-start.11
  66.3 1.1 %far.6 = (bf16[528,512]{1,0:T(8,128)(2,1)S(1)}, f32[16,512]{1,0:T(8,128)S(1)}) custom-call(f32[8,640]{1,0:T(8,128)S(1)} %get-tuple-element.42.refs_0_, f32[8,640]{1,0:T(8,128)S(1)} %collective-permute-done.10.refs_1_, bf16[1024,640]{1,0:T(8,128)(2,1)S(1)} %get-tuple-element.49.refs_2_, bf16[1024,640]{1,0:T(8,128)(2,1)S(1)} %get-tuple-element.50.refs_3_, ...), custom_call_target="tpu_custom_call" | custom-call | flops 1 | bytes 1 | tf_op jit(solution)/shard_map/far/pallas_call | solution.py:193
  67.4 0.0 collective-permute-done.13.refs_8_
  67.4 0.0 collective-permute-done.12.refs_7_
  67.5 1.0 near.4
  68.5 1.8 %collective-permute-start.14 = (bf16[272,512]{1,0:T(8,128)(2,1)S(1)}, bf16[272,512]{1,0:T(8,128)(2,1)S(1)}, u32[]{:S(2)}, u32[]{:S(2)}) collective-permute-start(bf16[272,512]{1,0:T(8,128)(2,1)S(1)} %get-tuple-element.52.refs_8_), channel_id=1, source_target_pairs={{0,2},{2,0},{1,3},{3,1},{4,6},{6,4},{5,7},{7,5},{8,10},{10,8},{9,1... | collective-permute-start | bytes 835592 | tf_op jit(solution)/shard_map/ppermute | solution.py:171
  70.2 0.0 collective-permute-start.19
  70.3 0.0 collective-permute-done.11.refs_7_
  70.3 1.0 near.5
  71.3 0.5 energy.1
  71.8 2.4 %collective-permute-start.15 = (f32[8,64]{1,0:T(8,128)S(1)}, f32[8,64]{1,0:T(8,128)S(1)}, u32[]{:S(2)}, u32[]{:S(2)}) collective-permute-start(f32[8,64]{1,0:T(8,128)S(1)} %get-tuple-element.54.refs_2_), channel_id=1, source_target_pairs={{0,8},{4,12},{8,0},{12,4},{1,9},{5,13},{9,1},{13,5},{2,10},{6,14},... | collective-permute-start | bytes 6152 | tf_op jit(solution)/shard_map/ppermute | solution.py:176
  74.2 2.1 %collective-permute-done.15.refs_2_.refs_3_ = f32[8,64]{1,0:T(8,128)S(1)} collective-permute-done((f32[8,64]{1,0:T(8,128)S(1)}, f32[8,64]{1,0:T(8,128)S(1)}, u32[]{:S(2)}, u32[]{:S(2)}) %collective-permute-start.15) | collective-permute-done | bytes 2080 | tf_op jit(solution)/shard_map/ppermute | solution.py:176
  76.3 1.1 %collective-permute-done.14.refs_1_ = bf16[272,512]{1,0:T(8,128)(2,1)S(1)} collective-permute-done((bf16[272,512]{1,0:T(8,128)(2,1)S(1)}, bf16[272,512]{1,0:T(8,128)(2,1)S(1)}, u32[]{:S(2)}, u32[]{:S(2)}) %collective-permute-start.14) | collective-permute-done | bytes 278560 | tf_op jit(solution)/shard_map/ppermute | solution.py:171
  77.4 2.7 %collective-permute-start.16 = (bf16[272,512]{1,0:T(8,128)(2,1)S(1)}, bf16[272,512]{1,0:T(8,128)(2,1)S(1)}, u32[]{:S(2)}, u32[]{:S(2)}) collective-permute-start(bf16[272,512]{1,0:T(8,128)(2,1)S(1)} %add.34.refs_8_), channel_id=1, source_target_pairs={{0,8},{4,12},{8,0},{12,4},{1,9},{5,13},{9,1},{13,5},{2,10},{6,14},... | collective-permute-start | bytes 835592 | tf_op jit(solution)/shard_map/ppermute | solution.py:176
  80.1 1.5 %collective-permute-start.17 = (bf16[256,512]{1,0:T(8,128)(2,1)S(1)}, bf16[256,512]{1,0:T(8,128)(2,1)S(1)}, u32[]{:S(2)}, u32[]{:S(2)}) collective-permute-start(bf16[256,512]{1,0:T(8,128)(2,1)S(1)} %get-tuple-element.57), channel_id=1, source_target_pairs={{0,2},{2,0},{1,3},{3,1},{4,6},{6,4},{5,7},{7,5},{8,10},{10,8},{9,1... | collective-permute-start | bytes 786440 | tf_op jit(solution)/shard_map/ppermute | solution.py:171
  81.6 0.0 collective-permute-done.19.refs_7_
  81.6 1.0 near.6
  82.6 0.6 collective-permute-start.21
  83.2 1.5 %collective-permute-start.20 = (bf16[264,512]{1,0:T(8,128)(2,1)S(1)}, bf16[264,512]{1,0:T(8,128)(2,1)S(1)}, u32[]{:S(2)}, u32[]{:S(2)}) collective-permute-start(bf16[264,512]{1,0:T(8,128)(2,1)S(1)} %get-tuple-element.61.refs_9_), channel_id=1, source_target_pairs={{0,2},{2,0},{1,3},{3,1},{4,6},{6,4},{5,7},{7,5},{8,10},{10,8},{9,1... | collective-permute-start | bytes 811016 | tf_op jit(solution)/shard_map/ppermute | solution.py:171
  84.7 4.7 %collective-permute-done.17.refs_1_ = bf16[256,512]{1,0:T(8,128)(2,1)S(1)} collective-permute-done((bf16[256,512]{1,0:T(8,128)(2,1)S(1)}, bf16[256,512]{1,0:T(8,128)(2,1)S(1)}, u32[]{:S(2)}, u32[]{:S(2)}) %collective-permute-start.17) | collective-permute-done | bytes 262176 | tf_op jit(solution)/shard_map/ppermute | solution.py:171
  89.4 0.4 collective-permute-start.22
  89.8 1.0 far.7
  90.8 0.1 collective-permute-start.18
  90.9 1.8 %place.1 = f32[8,64]{1,0:T(8,128)} custom-call(s32[4,10,24]{2,1,0:T(8,128)S(1)} %pad_add_fusion.refs_0_, f32[10,64]{1,0:T(8,128)S(1)} %get-tuple-element.63.refs_1_, f32[8,64]{1,0:T(8,128)S(1)} %get-tuple-element.54.refs_2_, f32[8,64]{1,0:T(8,128)S(1)} %collective-permute-done.15.refs_2_.refs_3_, bf16[256,512]{1,0:T(8,128)(2,1)S(1)} %add.35.refs_6_.refs_4_), custom_call_target="tpu_custom_call" | custom-call | flops 1 | bytes 1 | tf_op jit(solution)/shard_map/place/pallas_call | solution.py:193
  92.7 6.9 %collective-permute-done.16.refs_0_ = bf16[272,512]{1,0:T(8,128)(2,1)S(1)} collective-permute-done((bf16[272,512]{1,0:T(8,128)(2,1)S(1)}, bf16[272,512]{1,0:T(8,128)(2,1)S(1)}, u32[]{:S(2)}, u32[]{:S(2)}) %collective-permute-start.16) | collective-permute-done | bytes 278560 | tf_op jit(solution)/shard_map/ppermute | solution.py:176
  99.6 0.0 collective-permute-done.18.refs_7_
  99.6 1.2 %near.7.refs_1_ = f32[528,512]{1,0:T(8,128)S(1)} custom-call(f32[8,640]{1,0:T(8,128)S(1)} %get-tuple-element.42.refs_0_, f32[8,640]{1,0:T(8,128)S(1)} %collective-permute-done.10.refs_1_, bf16[1024,640]{1,0:T(8,128)(2,1)S(1)} %get-tuple-element.49.refs_2_, bf16[1024,640]{1,0:T(8,128)(2,1)S(1)} %get-tuple-element.50.refs_3_, ...), custom_call_target="tpu_custom_call" | custom-call | flops 1 | bytes 1 | tf_op jit(solution)/shard_map/near/pallas_call | solution.py:193
  100.8 2.8 %collective-permute-done.22.refs_4_ = bf16[256,512]{1,0:T(8,128)(2,1)S(1)} collective-permute-done((bf16[256,512]{1,0:T(8,128)(2,1)S(1)}, bf16[256,512]{1,0:T(8,128)(2,1)S(1)}, u32[]{:S(2)}, u32[]{:S(2)}) %collective-permute-start.22) | collective-permute-done | bytes 262176 | tf_op jit(solution)/shard_map/ppermute | solution.py:176
  103.7 1.2 %final.1 = f32[512,512]{1,0:T(8,128)} custom-call(f32[272,512]{1,0:T(8,128)S(1)} %early.1.refs_0_, f32[528,512]{1,0:T(8,128)S(1)} %near.7.refs_1_, bf16[264,512]{1,0:T(8,128)(2,1)S(1)} %collective-permute-done.20.refs_2_, bf16[264,512]{1,0:T(8,128)(2,1)S(1)} %collective-permute-done.21.refs_3_, bf16[256,512]{1,0:T(8,128)(2,1)S(1)} %collective-permute-done.22.refs_4_), custom_call_target="tpu_custom_call" | custom-call | flops 1 | bytes 1 | tf_op jit(solution)/shard_map/final/pallas_call | solution.py:193
  (13 shorter events, 0.2 us)
Async XLA Ops:
  1.3 9.3 %collective-permute-start.1 = (s32[10,24]{1,0:T(8,128)S(1)}, s32[10,24]{1,0:T(8,128)S(1)}, u32[]{:S(2)}, u32[]{:S(2)}) collective-permute-start(s32[10,24]{1,0:T(8,128)S(1)} %get-tuple-element.69), channel_id=1, source_target_pairs={{0,8},{4,12},{8,0},{12,4},{1,9},{5,13},{9,1},{13,5},{2,10},{6,14},... | collective-permute-start | bytes 2888 | tf_op jit(solution)/shard_map/ppermute | solution.py:176
  5.4 5.2 %collective-permute-start = (s32[10,24]{1,0:T(8,128)S(1)}, s32[10,24]{1,0:T(8,128)S(1)}, u32[]{:S(2)}, u32[]{:S(2)}) collective-permute-start(s32[10,24]{1,0:T(8,128)S(1)} %get-tuple-element.69), channel_id=1, source_target_pairs={{0,4},{4,0},{8,12},{12,8},{1,5},{5,1},{9,13},{13,9},{2,6},{6,2},{1... | collective-permute-start | bytes 2888 | tf_op jit(solution)/shard_map/ppermute | solution.py:176
  7.0 5.4 %collective-permute-start.2 = (s32[10,24]{1,0:T(8,128)S(1)}, s32[10,24]{1,0:T(8,128)S(1)}, u32[]{:S(2)}, u32[]{:S(2)}) collective-permute-start(s32[10,24]{1,0:T(8,128)S(1)} %get-tuple-element.69), channel_id=1, source_target_pairs={{0,12},{4,8},{8,4},{12,0},{1,13},{5,9},{9,5},{13,1},{2,14},{6,10},... | collective-permute-start | bytes 2888 | tf_op jit(solution)/shard_map/ppermute | solution.py:176
  7.0 2.6 %copy-start = (f32[1024,512]{1,0:T(8,128)S(1)}, f32[1024,512]{1,0:T(8,128)}, u32[]{:S(2)}) copy-start(f32[1024,512]{1,0:T(8,128)} %refs_8_.1) | copy-start | bytes 6291460
  9.7 3.0 %collective-permute-start.3 = (bf16[640,512]{1,0:T(8,128)(2,1)}, bf16[640,512]{1,0:T(8,128)(2,1)}, u32[]{:S(2)}, u32[]{:S(2)}) collective-permute-start(bf16[640,512]{1,0:T(8,128)(2,1)} %bitcast.8), channel_id=1, source_target_pairs={{0,1},{1,0},{2,3},{3,2},{4,5},{5,4},{6,7},{7,6},{8,9},{9,8},{10,11... | collective-permute-start | bytes 1966088 | tf_op jit(solution)/shard_map/ppermute | solution.py:171
  9.9 30.4 %collective-permute-start.5 = (bf16[1024,512]{1,0:T(8,128)(2,1)S(1)}, bf16[1024,512]{1,0:T(8,128)(2,1)}, u32[]{:S(2)}, u32[]{:S(2)}) collective-permute-start(bf16[1024,512]{1,0:T(8,128)(2,1)S(1)} %multiply_convert_fusion.refs_0_), channel_id=1, source_target_pairs={{0,1},{1,0},{2,3},{3,2},{4,5},{5,4},{6,7},{7,6},{8,9},{9,8},{10,11... | collective-permute-start | bytes 3145736 | tf_op jit(solution)/shard_map/ppermute | solution.py:171
  10.5 2.2 %copy-start.1 = (bf16[1,1,10,64,512]{4,3,2,1,0:T(8,128)(2,1)S(1)}, bf16[1,1,10,64,512]{4,3,2,1,0:T(8,128)(2,1)}, u32[]{:S(2)}) copy-start(bf16[1,1,10,64,512]{4,3,2,1,0:T(8,128)(2,1)} %get-tuple-element.64) | copy-start | bytes 1966084
  12.5 24.4 %collective-permute-start.6 = (bf16[512,512]{1,0:T(8,128)(2,1)S(1)}, bf16[512,512]{1,0:T(8,128)(2,1)S(1)}, u32[]{:S(2)}, u32[]{:S(2)}) collective-permute-start(bf16[512,512]{1,0:T(8,128)(2,1)S(1)} %multiply_convert_fusion.1), channel_id=1, source_target_pairs={{0,8},{4,12},{8,0},{12,4},{1,9},{5,13},{9,1},{13,5},{2,10},{6,14},... | collective-permute-start | bytes 1572872 | tf_op jit(solution)/shard_map/ppermute | solution.py:176
  13.9 41.2 %collective-permute-start.4 = (bf16[640,1024]{1,0:T(8,128)(2,1)S(1)}, bf16[640,1024]{1,0:T(8,128)(2,1)S(1)}, u32[]{:S(2)}, u32[]{:S(2)}) collective-permute-start(bf16[640,1024]{1,0:T(8,128)(2,1)S(1)} %pad_maximum_fusion.refs_1_.refs_4_.refs_2_), channel_id=1, source_target_pairs={{0,4},{4,0},{8,12},{12,8},{1,5},{5,1},{9,13},{13,9},{2,6},{6,2},{1... | collective-permute-start | bytes 3932168 | tf_op jit(solution)/shard_map/ppermute | solution.py:176
  36.9 12.7 %collective-permute-start.8 = (bf16[512,512]{1,0:T(8,128)(2,1)S(1)}, bf16[512,512]{1,0:T(8,128)(2,1)S(1)}, u32[]{:S(2)}, u32[]{:S(2)}) collective-permute-start(bf16[512,512]{1,0:T(8,128)(2,1)S(1)} %collective-permute-done.6.refs_0_), channel_id=1, source_target_pairs={{0,2},{2,0},{1,3},{3,1},{4,6},{6,4},{5,7},{7,5},{8,10},{10,8},{9,1... | collective-permute-start | bytes 1572872 | tf_op jit(solution)/shard_map/ppermute | solution.py:171
  40.2 9.4 %collective-permute-start.7 = (bf16[512,512]{1,0:T(8,128)(2,1)S(1)}, bf16[512,512]{1,0:T(8,128)(2,1)S(1)}, u32[]{:S(2)}, u32[]{:S(2)}) collective-permute-start(bf16[512,512]{1,0:T(8,128)(2,1)S(1)} %collective-permute-done.6.refs_0_), channel_id=1, source_target_pairs={{0,1},{1,0},{2,3},{3,2},{4,5},{5,4},{6,7},{7,6},{8,9},{9,8},{10,11... | collective-permute-start | bytes 1572872 | tf_op jit(solution)/shard_map/ppermute | solution.py:171
  49.6 1.9 %collective-permute-start.9 = (bf16[512,512]{1,0:T(8,128)(2,1)S(1)}, bf16[512,512]{1,0:T(8,128)(2,1)S(1)}, u32[]{:S(2)}, u32[]{:S(2)}) collective-permute-start(bf16[512,512]{1,0:T(8,128)(2,1)S(1)} %collective-permute-done.8.refs_2_), channel_id=1, source_target_pairs={{0,1},{1,0},{2,3},{3,2},{4,5},{5,4},{6,7},{7,6},{8,9},{9,8},{10,11... | collective-permute-start | bytes 1572872 | tf_op jit(solution)/shard_map/ppermute | solution.py:171
  59.7 3.8 %collective-permute-start.10 = (f32[8,640]{1,0:T(8,128)S(1)}, f32[8,640]{1,0:T(8,128)S(1)}, u32[]{:S(2)}, u32[]{:S(2)}) collective-permute-start(f32[8,640]{1,0:T(8,128)S(1)} %get-tuple-element.42.refs_0_), channel_id=1, source_target_pairs={{0,4},{4,0},{8,12},{12,8},{1,5},{5,1},{9,13},{13,9},{2,6},{6,2},{1... | collective-permute-start | bytes 61448 | tf_op jit(solution)/shard_map/ppermute | solution.py:176
  64.6 2.9 %collective-permute-start.13 = (bf16[264,512]{1,0:T(8,128)(2,1)S(1)}, bf16[264,512]{1,0:T(8,128)(2,1)S(1)}, u32[]{:S(2)}, u32[]{:S(2)}) collective-permute-start(bf16[264,512]{1,0:T(8,128)(2,1)S(1)} %get-tuple-element.66), channel_id=1, source_target_pairs={{0,1},{1,0},{2,3},{3,2},{4,5},{5,4},{6,7},{7,6},{8,9},{9,8},{10,11... | collective-permute-start | bytes 811016 | tf_op jit(solution)/shard_map/ppermute | solution.py:171
  64.6 2.8 %collective-permute-start.12 = (bf16[264,512]{1,0:T(8,128)(2,1)S(1)}, bf16[264,512]{1,0:T(8,128)(2,1)S(1)}, u32[]{:S(2)}, u32[]{:S(2)}) collective-permute-start(bf16[264,512]{1,0:T(8,128)(2,1)S(1)} %get-tuple-element.67), channel_id=1, source_target_pairs={{0,1},{1,0},{2,3},{3,2},{4,5},{5,4},{6,7},{7,6},{8,9},{9,8},{10,11... | collective-permute-start | bytes 811016 | tf_op jit(solution)/shard_map/ppermute | solution.py:171
  66.2 4.1 %collective-permute-start.11 = (bf16[528,512]{1,0:T(8,128)(2,1)S(1)}, bf16[528,512]{1,0:T(8,128)(2,1)S(1)}, u32[]{:S(2)}, u32[]{:S(2)}) collective-permute-start(bf16[528,512]{1,0:T(8,128)(2,1)S(1)} %get-tuple-element.47.refs_6_), channel_id=1, source_target_pairs={{0,1},{1,0},{2,3},{3,2},{4,5},{5,4},{6,7},{7,6},{8,9},{9,8},{10,11... | collective-permute-start | bytes 1622024 | tf_op jit(solution)/shard_map/ppermute | solution.py:171
  68.5 8.9 %collective-permute-start.14 = (bf16[272,512]{1,0:T(8,128)(2,1)S(1)}, bf16[272,512]{1,0:T(8,128)(2,1)S(1)}, u32[]{:S(2)}, u32[]{:S(2)}) collective-permute-start(bf16[272,512]{1,0:T(8,128)(2,1)S(1)} %get-tuple-element.52.refs_8_), channel_id=1, source_target_pairs={{0,2},{2,0},{1,3},{3,1},{4,6},{6,4},{5,7},{7,5},{8,10},{10,8},{9,1... | collective-permute-start | bytes 835592 | tf_op jit(solution)/shard_map/ppermute | solution.py:171
  70.2 11.4 %collective-permute-start.19 = (bf16[528,512]{1,0:T(8,128)(2,1)S(1)}, bf16[528,512]{1,0:T(8,128)(2,1)S(1)}, u32[]{:S(2)}, u32[]{:S(2)}) collective-permute-start(bf16[528,512]{1,0:T(8,128)(2,1)S(1)} %get-tuple-element.51.refs_9_), channel_id=1, source_target_pairs={{0,1},{1,0},{2,3},{3,2},{4,5},{5,4},{6,7},{7,6},{8,9},{9,8},{10,11... | collective-permute-start | bytes 1622024 | tf_op jit(solution)/shard_map/ppermute | solution.py:171
  71.8 4.5 %collective-permute-start.15 = (f32[8,64]{1,0:T(8,128)S(1)}, f32[8,64]{1,0:T(8,128)S(1)}, u32[]{:S(2)}, u32[]{:S(2)}) collective-permute-start(f32[8,64]{1,0:T(8,128)S(1)} %get-tuple-element.54.refs_2_), channel_id=1, source_target_pairs={{0,8},{4,12},{8,0},{12,4},{1,9},{5,13},{9,1},{13,5},{2,10},{6,14},... | collective-permute-start | bytes 6152 | tf_op jit(solution)/shard_map/ppermute | solution.py:176
  77.4 22.1 %collective-permute-start.16 = (bf16[272,512]{1,0:T(8,128)(2,1)S(1)}, bf16[272,512]{1,0:T(8,128)(2,1)S(1)}, u32[]{:S(2)}, u32[]{:S(2)}) collective-permute-start(bf16[272,512]{1,0:T(8,128)(2,1)S(1)} %add.34.refs_8_), channel_id=1, source_target_pairs={{0,8},{4,12},{8,0},{12,4},{1,9},{5,13},{9,1},{13,5},{2,10},{6,14},... | collective-permute-start | bytes 835592 | tf_op jit(solution)/shard_map/ppermute | solution.py:176
  80.1 9.2 %collective-permute-start.17 = (bf16[256,512]{1,0:T(8,128)(2,1)S(1)}, bf16[256,512]{1,0:T(8,128)(2,1)S(1)}, u32[]{:S(2)}, u32[]{:S(2)}) collective-permute-start(bf16[256,512]{1,0:T(8,128)(2,1)S(1)} %get-tuple-element.57), channel_id=1, source_target_pairs={{0,2},{2,0},{1,3},{3,1},{4,6},{6,4},{5,7},{7,5},{8,10},{10,8},{9,1... | collective-permute-start | bytes 786440 | tf_op jit(solution)/shard_map/ppermute | solution.py:171
  82.6 18.2 %collective-permute-start.21 = (bf16[264,512]{1,0:T(8,128)(2,1)S(1)}, bf16[264,512]{1,0:T(8,128)(2,1)S(1)}, u32[]{:S(2)}, u32[]{:S(2)}) collective-permute-start(bf16[264,512]{1,0:T(8,128)(2,1)S(1)} %get-tuple-element.62), channel_id=1, source_target_pairs={{0,2},{2,0},{1,3},{3,1},{4,6},{6,4},{5,7},{7,5},{8,10},{10,8},{9,1... | collective-permute-start | bytes 811016 | tf_op jit(solution)/shard_map/ppermute | solution.py:171
  83.2 17.6 %collective-permute-start.20 = (bf16[264,512]{1,0:T(8,128)(2,1)S(1)}, bf16[264,512]{1,0:T(8,128)(2,1)S(1)}, u32[]{:S(2)}, u32[]{:S(2)}) collective-permute-start(bf16[264,512]{1,0:T(8,128)(2,1)S(1)} %get-tuple-element.61.refs_9_), channel_id=1, source_target_pairs={{0,2},{2,0},{1,3},{3,1},{4,6},{6,4},{5,7},{7,5},{8,10},{10,8},{9,1... | collective-permute-start | bytes 811016 | tf_op jit(solution)/shard_map/ppermute | solution.py:171
  89.4 14.3 %collective-permute-start.22 = (bf16[256,512]{1,0:T(8,128)(2,1)S(1)}, bf16[256,512]{1,0:T(8,128)(2,1)S(1)}, u32[]{:S(2)}, u32[]{:S(2)}) collective-permute-start(bf16[256,512]{1,0:T(8,128)(2,1)S(1)} %add.35.refs_6_.refs_4_), channel_id=1, source_target_pairs={{0,8},{4,12},{8,0},{12,4},{1,9},{5,13},{9,1},{13,5},{2,10},{6,14},... | collective-permute-start | bytes 786440 | tf_op jit(solution)/shard_map/ppermute | solution.py:176
  90.8 8.8 %collective-permute-start.18 = (bf16[528,512]{1,0:T(8,128)(2,1)S(1)}, bf16[528,512]{1,0:T(8,128)(2,1)S(1)}, u32[]{:S(2)}, u32[]{:S(2)}) collective-permute-start(bf16[528,512]{1,0:T(8,128)(2,1)S(1)} %get-tuple-element.59), channel_id=1, source_target_pairs={{0,1},{1,0},{2,3},{3,2},{4,5},{5,4},{6,7},{7,6},{8,9},{9,8},{10,11... | collective-permute-start | bytes 1622024 | tf_op jit(solution)/shard_map/ppermute | solution.py:171

commit v5 on v4

--- a/solution.py
+++ b/solution.py
@@ -162,6 +162,8 @@
 FLOOR = -1e29
 MEGA = 2**20
 PAD = 16
+BLOCK = 128
+SETS = (0, 8, 12)
 HBM = pl.BlockSpec(memory_space=pl.ANY)
 VMEM = pl.BlockSpec(memory_space=pltpu.VMEM)
 SMEM = pl.BlockSpec(memory_space=pltpu.SMEM)
@@ -257,31 +259,31 @@
     return [(lo, min(256, lanes - lo)) for lo in range(0, lanes, 256)]
 
 
-def score_kernel(bias_ref, x_ref, *refs, chunk, sets, at):
+def score_kernel(bias_ref, x_ref, *refs, chunk, first, sets, at):
     c_refs, refs = refs[: 2 * len(sets)], refs[2 * len(sets) :]
     before_refs, refs = refs[: len(at) - 1], refs[len(at) - 1 :]
     em_refs, (stats_ref, dots_ref) = refs[: len(sets)], refs[len(sets) :]
     for ref, (row, lane) in zip(before_refs, at[1:]):
         stats_ref[row : row + ref.shape[0], lane : lane + ref.shape[1]] = ref[...]
-    count = bias_ref.shape[1] // 2
-    rows = dots_ref.shape[1] // count
     turn = 0
     for lo, size in tiles(x_ref.shape[0]):
         for i, s in enumerate(sets):
             c_ref, csq_ref = c_refs[2 * i : 2 * i + 2]
+            count, base = c_ref.shape[0] // BLOCK, SETS[s]
             part = slice(lo, lo + size)
             buf = dots_ref.at[turn % 2]
             turn += 1
-            buf[:, 0:size] = lax.dot_general(
+            buf[0 : c_ref.shape[0], 0:size] = lax.dot_general(
                 c_ref[...], x_ref[part, :], (((1,), (1,)), ((), ())), preferred_element_type=jnp.float32
             )
 
             def logits(g):
-                block = pl.ds(g * rows, rows)
+                block = pl.ds(g * BLOCK, BLOCK)
                 less = jnp.concatenate([csq_ref[block, :]] * (size // 128), axis=1)
-                return (buf[block, 0:size] - less).reshape(rows // 8, 8, size)
-
-            bias = [bias_ref[chunk, s * count + g : s * count + g + 1, part] for g in range(count)]
+                return (buf[block, 0:size] - less).reshape(BLOCK // 8, 8, size)
+
+            of_chunk = slice(first + lo, first + lo + size)
+            bias = [bias_ref[chunk, base + g : base + g + 1, of_chunk] for g in range(count)]
             best = jnp.full((8, size), FLOOR, jnp.float32)
             for g in range(count):
                 best = jnp.maximum(best, jnp.max(logits(g), axis=0) + bias[g])
@@ -289,25 +291,25 @@
             total = jnp.zeros((8, size), jnp.float32)
             for g in range(count):
                 expo = jnp.exp(logits(g) + (bias[g] - top)[None])
-                em_refs[i][pl.ds(g * rows, rows), part] = expo.reshape(rows, size).astype(jnp.bfloat16)
+                em_refs[i][pl.ds(g * BLOCK, BLOCK), part] = expo.reshape(BLOCK, size).astype(jnp.bfloat16)
                 total = total + jnp.sum(expo, axis=0)
             row, lane = at[0][0] + 2 * i, at[0][1] + lo
             stats_ref[row : row + 1, lane : lane + size] = top
             stats_ref[row + 1 : row + 2, lane : lane + size] = jnp.sum(total, axis=0, keepdims=True)
 
 
-def score(bias, chunk, x, sets, before=()):
-    cols = next(iter(sets.values()))[0].shape[0]
+def score(bias, chunk, x, sets, before=(), first=0):
+    cols = [c.shape[0] for c, square in sets.values()]
     count = len(sets)
-    at = [(4 * chunk, 0) if before else (0, 0)] + [(row, lane) for part, row, lane in before]
-    stats = shape((8, bias.shape[2]) if before else (2 * count, x.shape[0]))
+    at = [(8 * chunk, first) if before else (0, 0)] + [(row, lane) for part, row, lane in before]
+    stats = shape((16, bias.shape[2]) if before else (2 * count, x.shape[0]))
     return call(
-        lambda *refs: score_kernel(*refs, chunk=chunk, sets=list(sets), at=at),
+        lambda *refs: score_kernel(*refs, chunk=chunk, first=first, sets=list(sets), at=at),
         "scores",
         [VMEM] * (2 + 2 * count + len(before)),
         [bias, x, *[part for c in sets.values() for part in c], *[part[0] for part in before]],
-        [shape((cols, x.shape[0]), jnp.bfloat16)] * count + [stats],
-        [pltpu.VMEM((2, cols, 256), jnp.float32)],
+        [shape((size, x.shape[0]), jnp.bfloat16) for size in cols] + [stats],
+        [pltpu.VMEM((2, max(cols), 256), jnp.float32)],
     )
 
 
@@ -322,18 +324,14 @@
 
 
 def chunk_parts(mine, peer, chunk):
-    other = 1 - chunk
-    return [
-        mine[4 * chunk : 4 * chunk + 2],
-        mine[4 * chunk + 2 : 4 * chunk + 4],
-        peer[4 * other : 4 * other + 2],
-        peer[4 * other + 2 : 4 * other + 4],
-    ]
+    rows = [8 * chunk + 2 * s for s in range(len(SETS))]
+    other = [8 * (1 - chunk) + 2 * s for s in range(len(SETS))]
+    return [mine[row : row + 2] for row in rows] + [peer[row : row + 2] for row in other]
 
 
 def half_rows(mine, count, which=0):
     if which:
-        return pl.ds(0 if mine else count, count)
+        return pl.ds(0, count)
     rep = lax.axis_index("rep")
     return pl.ds(pl.multiple_of((rep if mine else 1 - rep) * count, count), count)
 
@@ -362,7 +360,7 @@
 
 def far_kernel(*refs, which, mine):
     stats_ref, peer_ref = refs[0:2]
-    em_refs, x_refs, (far_ref, mass_ref) = refs[2:4], refs[4:6], refs[6:]
+    em_refs, x_refs, (far_ref, mass_ref) = refs[2:5], refs[5:8], refs[8:]
     count, width = far_ref.shape[0] - PAD, far_ref.shape[1]
     total, masses = weighted(
         stats_ref, peer_ref, em_refs, x_refs, half_rows(mine, count, which), slice(width, 2 * width), which, True
@@ -375,8 +373,8 @@
 
 def near_kernel(*refs, which, mine, final, outs, swaps):
     stats_ref, peer_ref = refs[0:2]
-    em_refs, x_refs, (mass_ref, *came_refs) = refs[2:4], refs[4:6], refs[6 : 7 + swaps]
-    refs = refs[7 + swaps :]
+    em_refs, x_refs, (mass_ref, *came_refs) = refs[2:5], refs[5:8], refs[8 : 9 + swaps]
+    refs = refs[9 + swaps :]
     out_refs = refs[final : final + outs]
     count, width = sum(ref.shape[0] for ref in came_refs) - PAD, came_refs[0].shape[1]
     if final:
@@ -402,11 +400,12 @@
 
 
 def far_sums(stats, peer, em, xs, which, mine, needs=()):
-    count, width = em[0].shape[0] // 2, xs[0].shape[1] // 2
+    width = xs[0].shape[1] // 2
+    count = em[0].shape[0] if which else em[0].shape[0] // 2
     return call(
         lambda *refs: far_kernel(*refs, which=which, mine=mine),
         "far",
-        [VMEM] * 6,
+        [VMEM] * 8,
         [stats, peer, *em, *xs],
         [shape((count + PAD, width), jnp.bfloat16), shape((PAD, width))],
         needs=needs,
@@ -414,13 +413,14 @@
 
 
 def near_sums(stats, peer, em, xs, which, mine, mass, came, dtype, parts=(), previous=None, needs=()):
-    count, width = em[0].shape[0] // 2, xs[0].shape[1] // 2
+    width = xs[0].shape[1] // 2
+    count = em[0].shape[0] if which else em[0].shape[0] // 2
     final = previous is not None
     sizes = list(parts) + [count + PAD - sum(parts)]
     return call(
         lambda *refs: near_kernel(*refs, which=which, mine=mine, final=final, outs=len(sizes), swaps=len(came)),
         "near",
-        [VMEM] * (7 + len(came)) + [HBM] * final,
+        [VMEM] * (9 + len(came)) + [HBM] * final,
         [stats, peer, *em, *xs, mass, *came] + [previous] * final,
         [shape((size, width), dtype) for size in sizes],
         [pltpu.VMEM((count, width), jnp.float32), pltpu.SemaphoreType.DMA] * final,
@@ -428,36 +428,55 @@
     )
 
 
-def add_kernel(a_ref, b_ref, out_ref):
-    out_ref[...] = (a_ref[...] + b_ref[...].astype(jnp.float32)).astype(out_ref.dtype)
+def add_kernel(a_ref, b_ref, *refs):
+    out_ref = refs[-1]
+    total = a_ref[...] + b_ref[...].astype(jnp.float32)
+    out_ref[...] = total.astype(out_ref.dtype)
+    if len(refs) == 2:
+        count, width = out_ref.shape
+        rest = jnp.concatenate([refs[0][k : k + 1, :] for k in range(4)], axis=1)
+        rest = jnp.concatenate([rest, jnp.zeros((1, width - rest.shape[1]), jnp.float32)], axis=1)
+        rows = [total[count - PAD : count - PAD + 8]]
+        for k in range(3):
+            rows.append(rest.astype(jnp.bfloat16).astype(jnp.float32))
+            rest = rest - rows[-1]
+        rows.append(jnp.zeros((5, width), jnp.float32))
+        out_ref[count - PAD :, :] = jnp.concatenate(rows).astype(out_ref.dtype)
 
 
 def early_kernel(came_ref, out_ref):
     out_ref[...] = came_ref[...].astype(out_ref.dtype)
 
 
-def final_kernel(early_ref, sums_ref, *refs, parts):
-    rep_refs, back_refs, out_ref = refs[:parts], refs[parts:-1], refs[-1]
+def final_kernel(energy_ref, masks_ref, sums_ref, *refs, parts):
+    rep_refs, back_refs, (out_ref, placed_ref) = refs[:parts], refs[parts:-2], refs[-2:]
     count, width = out_ref.shape
-    first = early_ref.shape[0]
+    bal, span = placed_ref.shape
     rep = jnp.concatenate([ref[...] for ref in rep_refs]).astype(jnp.float32)
-    back = jnp.concatenate([ref[...] for ref in back_refs]).astype(jnp.float32)
-    later = sums_ref[first:, :] + rep[first:] + back
-    mass = jnp.broadcast_to(later[count - first : count - first + 1], (128, count)).T
-    mass = jnp.concatenate([mass] * (width // 128), axis=1)
-    out_ref[0:first, :] = (sums_ref[0:first, :] + early_ref[...] + rep[0:first]) / mass[0:first]
-    out_ref[first:, :] = later[: count - first] / mass[first:]
-
-
-def energy_kernel(stats_ref, peer_ref, x0_ref, x1_ref, out_ref, last_ref, *, tau, span, handed):
+    back = jnp.concatenate([ref[...].astype(jnp.float32) for ref in back_refs])
+    total = sums_ref[...] + rep + back
+    mass = jnp.broadcast_to(total[count : count + 1], (128, count)).T
+    out_ref[...] = total[:count] / jnp.concatenate([mass] * (width // 128), axis=1)
+    came = back[count + 8 : count + 9] + back[count + 9 : count + 10] + back[count + 10 : count + 11]
+    placed = energy_ref[...]
+    placed = jnp.where(masks_ref[0:bal, :] > 0, came[:, span : 2 * span], placed)
+    placed_ref[...] = jnp.where(masks_ref[bal:, :] > 0, came[:, 2 * span : 3 * span], placed)
+
+
+def energy_kernel(stats_ref, peer_ref, x0_ref, *refs, tau, span, handed):
+    x1_refs, (out_ref, last_ref) = refs[:-2], refs[-2:]
     last_ref[...] = jnp.zeros_like(last_ref)
-    for chunk, x_ref in enumerate((x0_ref, x1_ref)):
-        lanes, depth = x_ref.shape
-        square = jnp.zeros((lanes, 128), jnp.float32)
-        for lane in range(0, depth, 128):
-            part = x_ref[:, lane : lane + 128].astype(jnp.float32)
-            square = square + part * part
-        square = jnp.sum(jnp.broadcast_to(jnp.sum(square, axis=1, keepdims=True), (lanes, 128)).T[0:1], axis=0, keepdims=True)
+    for chunk, x_refs in enumerate(((x0_ref,), x1_refs)):
+        squares = []
+        for x_ref in x_refs:
+            square = jnp.zeros((x_ref.shape[0], 128), jnp.float32)
+            for lane in range(0, x_ref.shape[1], 128):
+                part = x_ref[:, lane : lane + 128].astype(jnp.float32)
+                square = square + part * part
+            square = jnp.sum(square, axis=1, keepdims=True)
+            squares.append(jnp.broadcast_to(square, (x_ref.shape[0], 128)).T[0:1])
+        square = jnp.concatenate(squares, axis=1)
+        lanes = square.shape[1]
         top, denom = combine(chunk_parts(stats_ref[...], peer_ref[...], chunk))
         energy = -tau * (top - square / tau + jnp.log(denom)) / D
         entries = lanes // span
@@ -470,21 +489,31 @@
                 last_ref[row : row + 1, :] = part
 
 
-def place_kernel(facts_ref, energy_ref, last_ref, came_ref, out_ref, *, bal):
+def place_kernel(facts_ref, energy_ref, last_ref, out_ref, masks_ref):
+    out_ref[...] = jnp.zeros_like(out_ref)
+    masks_ref[...] = jnp.zeros_like(masks_ref)
+    bal = out_ref.shape[0]
     me = lax.axis_index("wide")
-    out_ref[...] = jnp.zeros_like(out_ref)
-
-    def put(target, row):
+
+    def put(ref, first, row, entry, energy):
+        target = facts_ref[row, 0, entry]
+
         @pl.when((target >= 0) & (target // bal == me))
         def _():
-            out_ref[pl.ds(target % bal, 1), :] = row
+            ref[pl.ds(first + target % bal, 1), :] = energy
 
     for e in range(bal):
-        put(facts_ref[0, 0, e], energy_ref[e : e + 1, :])
-    odd = me % 2 == 1
-    one = jnp.where(odd, last_ref[2:3, :], came_ref[2:3, :])
-    put(facts_ref[jnp.where(odd, 1, 3), 0, bal], one)
-    put(facts_ref[2, 0, bal + 1], came_ref[1:2, :])
+        put(out_ref, 0, 0, e, energy_ref[e : e + 1, :])
+    ones = jnp.ones((1, out_ref.shape[1]), jnp.float32)
+    put(masks_ref, 0, 2, bal + 1, ones)
+
+    @pl.when(me % 2 == 1)
+    def _():
+        put(out_ref, 0, 1, bal, last_ref[2:3, :])
+
+    @pl.when(me % 2 == 0)
+    def _():
+        put(masks_ref, bal, 3, bal, ones)
 
 
 def grid_plan(samples, centroids, move_target, fetch_ids, cand):
@@ -501,6 +530,7 @@
     handed = slots_in - bal
     span = rows // 2
     lanes = slots_in * span
+    cut = 6 * span
     pair_x, pair_c = 1, 2
 
     table = [move_target.reshape(1, slots_in), fetch_ids.reshape(1, pool), cand.reshape(bal, lists)]
@@ -529,85 +559,91 @@
     took = swapped(give, "sub")
     own = lax.dynamic_slice_in_dim(blocks, sub * span, span, 1).reshape(lanes, width)
     full = jnp.concatenate([own, took], axis=1)
-    x1 = paired(after(full, facts), pair_x)
-
-    set_a = joined([(c0_own, c0_oth)])
-    em_a0, stats_a0 = score(bias, 0, full, {0: set_a})
-    c1_oth = [swapped(part, "sub") for part in (c1_own[0], after(c1_own[1], stats_a0))]
-    set_b = joined(list(zip(c1_own, c1_oth)), [stats_a0])
-    em_b0, stats_b0 = score(bias, 0, full, {1: set_b})
-    before = [(stats_a0, 0, 0), (stats_b0, 2, 0)]
-    em_a1, em_b1, stats = score(bias, 1, x1, {0: set_a, 1: set_b}, before)
-    em = ((em_a0, em_a1), (em_b0, em_b1))
+    x1 = [paired(after(part, facts), pair_x) for part in (full[:cut], full[cut:])]
+
+    set_0 = joined([(c0_own, c0_oth)])
+    set_1 = joined([(c1_own[0], swapped(c1_own[0], "sub"))])
+    *em_0, stats_0 = score(bias, 0, full, {0: set_0, 1: set_1})
+    *em_1, stats_1 = score(bias, 1, x1[0], {0: set_0, 1: set_1})
+    later = lax.optimization_barrier((c1_own[1], stats_0, stats_1))[0]
+    later = jnp.split(later, 2)
+    set_2 = joined([(part, swapped(part, "sub")) for part in later])
+    em_02, stats_02 = score(bias, 0, full, {2: set_2})
+    em_12, stats_12 = score(bias, 1, x1[0], {2: set_2})
+    before = [(stats_0, 0, 0), (stats_02, 4, 0), (stats_1, 8, 0), (stats_12, 12, 0)]
+    *em_2, stats = score(bias, 1, x1[1], {0: set_0, 1: set_1, 2: set_2}, before, cut)
+    em = list(zip((*em_0, em_02), (*em_1, em_12), em_2))
     peer = paired(stats, pair_x)
 
-    xs = (full, x1)
+    xs = (full, *x1)
     half = jnp.bfloat16
-    first, equal = (272,), (264,)
-
-    far_a, mass_a = far_sums(stats, peer, em[1], xs, 1, False)
+    first, equal = (192,176), (264,)
+
+    far_a, mass_a = far_sums(stats, peer, em[2], xs, 2, False)
     far_b, mass_b = far_sums(stats, peer, em[1], xs, 1, True, [far_a])
-    far_c, mass_c = far_sums(stats, peer, em[0], xs, 0, False, [far_b])
     near_a = [swapped(part, "sub") for part in jnp.split(far_a, 2)]
-    near_b, near_c = [[swapped(far, "sub")] for far in (far_b, far_c)]
     sent_a = near_sums(
-        stats, peer, em[1], xs, 1, False, mass_a, near_a, half, first, needs=[far_c]
-    )
+        stats, peer, em[2], xs, 2, False, mass_a, near_a, half, first, needs=[far_b]
+    )
+    far_c, mass_c = far_sums(stats, peer, em[0], xs, 0, False, sent_a[:1])
+    near_c = [swapped(part, "sub") for part in jnp.split(far_c, 4)]
+    near_b = [swapped(after(far_b, sent_a[0]), "sub")]
     part_b = near_sums(
         stats, peer, em[1], xs, 1, True, mass_b, near_b, jnp.float32, first, needs=sent_a[:1]
     )
     energy, last = call(
         lambda *refs: energy_kernel(*refs, tau=tau, span=span, handed=handed),
         "energy",
-        [VMEM] * 4,
+        [VMEM] * 5,
         [stats, peer, *xs],
         [shape((slots_in, span)), shape((8, span))],
         needs=part_b[:1],
     )
-    came_last = paired(last, 2)
-
-    def returned(part, came, needs):
+
+    def returned(part, came, needs, energies=()):
+        args = [part, came, *energies]
         back = call(
-            add_kernel, "add", [VMEM] * 2, [part, came], [shape(part.shape, half)], needs=needs
+            add_kernel, "add", [VMEM] * len(args), args, [shape(part.shape, half)], needs=needs
         )[0]
         return back, paired(back, pair_c)
 
-    back, came_back_0 = returned(part_b[0], swapped(sent_a[0], "rep"), [came_last])
-    came = swapped(after(sent_a[1], back), "rep")
-    sent_c = near_sums(
-        stats, peer, em[0], xs, 0, False, mass_c, near_c, half, equal, needs=[back]
-    )
-    came_c = [swapped(part, "rep") for part in sent_c]
-    back, came_back_1 = returned(part_b[1], came, [])
-    came_back = [came_back_0, came_back_1]
-    far_d, mass_d = far_sums(stats, peer, em[0], xs, 0, True, [back])
+    came_back, backs = [], []
+    for i, part in enumerate(part_b):
+        sent = after(sent_a[i], backs[-1]) if i >= 1 else sent_a[i]
+        energies = [last] if i == len(first) else []
+        back, came = returned(part, swapped(sent, "rep"), backs[-1:], energies)
+        backs.append(back)
+        came_back.append(came)
+        if i == 1:
+            sent_c = near_sums(
+                stats, peer, em[0], xs, 0, False, mass_c, near_c, half, equal, needs=[back]
+            )
+            came_c = [swapped(part, "rep") for part in sent_c]
+    far_d, mass_d = far_sums(stats, peer, em[0], xs, 0, True, backs[-1:])
     near_d = [swapped(far_d, "sub")]
     (part_d,) = near_sums(
         stats, peer, em[0], xs, 0, True, mass_d, near_d, jnp.float32, (), centroids, sent_c[:1]
     )
-    early = call(
-        early_kernel,
-        "early",
-        [VMEM],
-        [came_back[0]],
-        [shape((first[0], width))],
-        flops=2 * 10**10,
-    )[0]
-    energy = call(
-        lambda *refs: place_kernel(*refs, bal=bal),
+    early = []
+    for came in came_back[:-1]:
+        early += call(
+            early_kernel, "early", [VMEM], [came], [shape(came.shape)], needs=early[-1:], flops=2 * 10**10
+        )
+    placed = call(
+        place_kernel,
         "place",
-        [SMEM] + [VMEM] * 3,
-        [facts, energy, last, came_last],
-        [shape((bal, span))],
-        needs=[back],
-    )[0]
-    fresh = call(
+        [SMEM] + [VMEM] * 2,
+        [facts, energy, last],
+        [shape((bal, span)), shape((2 * bal, span))],
+        needs=backs[-1:],
+    )
+    fresh, energy = call(
         lambda *refs: final_kernel(*refs, parts=len(came_c)),
         "final",
-        [VMEM] * (2 + len(came_c) + len(came_back[1:])),
-        [early, part_d, *came_c, *came_back[1:]],
-        [shape((share, width))],
-    )[0]
+        [VMEM] * (4 + len(came_c) + len(early)),
+        [*placed, part_d, *came_c, *early, came_back[-1]],
+        [shape((share, width)), shape((bal, span))],
+    )
     return (fresh, energy.reshape(1, 1, bal, span))
 
 

time: 105 us -> 102 us (0.971)
  waiting for transfers between devices: 51.1 us -> 42.8 us
  starting transfers between devices: 22.8 us -> 25.9 us
  other arithmetic: 2.34 us -> 4.54 us
    ppermute x9 -> x10, waiting for transfers between devices: 38.2 us -> 28.8 us  [paired(): return lax.ppermute(value, 'wide', [(w, w ^ flip) for w in range(count)])]
    ppermute x14 -> x19, starting transfers between devices: 8.55 us -> 11 us  [swapped(): return lax.ppermute(value, axis, [(0, 1), (1, 0)])]
    concatenate x1 -> x3, other arithmetic: 1.23 us -> 3.28 us  [grid_plan(): full = jnp.concatenate([own, took], axis=1)]
    ppermute x14 -> x19, waiting for transfers between devices: 12.9 us -> 14 us  [swapped(): return lax.ppermute(value, axis, [(0, 1), (1, 0)])]
    ppermute x9 -> x10, starting transfers between devices: 14.3 us -> 15 us  [paired(): return lax.ppermute(value, 'wide', [(w, w ^ flip) for w in range(count)])]
    pallas_call x20 -> x25, Pallas kernels: 25.1 us -> 25.1 us  [call(): pl.pallas_call(run, in_specs=in_specs + [HBM] * len(needs), out_specs=[VM...]
  transfers between devices with their start and end apart: 23 -> 29, of which waited for: 11 -> 13; matrix products, arithmetic and copies ran while one was open for 4% -> 6% of each run, Pallas kernels for 17% -> 20%
where the time goes in v5:
time: 102 us
  waiting for transfers between devices  42.8 us (42%)
  starting transfers between devices  25.9 us (25%)
  Pallas kernels  25.1 us (25%)
  other arithmetic  4.54 us (4%)
  local copies, waits for them, and re-layouts  2.61 us (3%)
    ppermute x10, waiting for transfers between devices, paired(): return lax.ppermute(value, 'wide', [(w, w ^ flip) for w in range(count)])  28.8 us
    pallas_call x25, Pallas kernels, call(): pl.pallas_call(run, in_specs=in_specs + [HBM] * len(needs), out_specs=[VM...  25.1 us
    ppermute x10, starting transfers between devices, paired(): return lax.ppermute(value, 'wide', [(w, w ^ flip) for w in range(count)])  15 us
    ppermute x19, waiting for transfers between devices, swapped(): return lax.ppermute(value, axis, [(0, 1), (1, 0)])  14 us
    ppermute x19, starting transfers between devices, swapped(): return lax.ppermute(value, axis, [(0, 1), (1, 0)])  11 us
    concatenate x3, other arithmetic, grid_plan(): full = jnp.concatenate([own, took], axis=1)  3.28 us
    dynamic_slice x1, local copies, waits for them, and re-layouts, grid_plan(): lax.dynamic_slice_in_dim(blocks, (1 - sub) * span, span, 1)  2.46 us
  transfers between devices with their start and end apart: 29, of which 13 were waited for; matrix products, arithmetic and copies ran while one was open for 6% of the time, Pallas kernels for 20%

profile of v5, /device:TPU:0, one launch (start us, length us, event | category | flops | bytes accessed | tf_op | source)
XLA Modules:
  0.0 101.9 jit_solution(4674311559031310547)
XLA Ops:
  0.6 0.9 fusion.2
  1.5 4.1 %collective-permute-start.1 = (s32[10,24]{1,0:T(8,128)S(1)}, s32[10,24]{1,0:T(8,128)S(1)}, u32[]{:S(2)}, u32[]{:S(2)}) collective-permute-start(s32[10,24]{1,0:T(8,128)S(1)} %get-tuple-element.111), channel_id=1, source_target_pairs={{0,8},{4,12},{8,0},{12,4},{1,9},{5,13},{9,1},{13,5},{2,10},{6,14},... | collective-permute-start | bytes 2888 | tf_op jit(solution)/shard_map/ppermute | solution.py:178
  5.6 1.6 %collective-permute-start = (s32[10,24]{1,0:T(8,128)S(1)}, s32[10,24]{1,0:T(8,128)S(1)}, u32[]{:S(2)}, u32[]{:S(2)}) collective-permute-start(s32[10,24]{1,0:T(8,128)S(1)} %get-tuple-element.111), channel_id=1, source_target_pairs={{0,4},{4,0},{8,12},{12,8},{1,5},{5,1},{9,13},{13,9},{2,6},{6,2},{1... | collective-permute-start | bytes 2888 | tf_op jit(solution)/shard_map/ppermute | solution.py:178
  7.2 2.5 %constant_dynamic-slice_fusion = (bf16[1,1,10,64,512]{4,3,2,1,0:T(8,128)(2,1)}, bf16[1,1,10,64,512]{4,3,2,1,0:T(8,128)(2,1)}) fusion(bf16[1,1,10,128,512]{4,3,2,1,0:T(8,128)(2,1)} %param.5, s32[]{:T(128)S(6)} %select_n.10, s32[]{:T(128)S(6)} %select_n.9), kind=kLoop, calls=%fused_computation.12 | loop fusion | bytes 2621448 | tf_op jit(solution)/shard_map/dynamic_slice | solution.py:558
  9.6 0.3 multiply_convert_fusion.refs_0_
  9.9 0.6 collective-permute-start.5
  10.5 0.1 multiply_convert_fusion.1
  10.6 2.0 %collective-permute-done.2 = s32[10,24]{1,0:T(8,128)S(1)} collective-permute-done((s32[10,24]{1,0:T(8,128)S(1)}, s32[10,24]{1,0:T(8,128)S(1)}, u32[]{:S(2)}, u32[]{:S(2)}) %collective-permute-start.2) | collective-permute-done | bytes 992 | tf_op jit(solution)/shard_map/ppermute | solution.py:178
  12.7 1.1 %fusion = bf16[384,1024]{1,0:T(8,128)(2,1)S(1)} fusion(bf16[640,512]{1,0:T(8,128)(2,1)S(1)} %bitcast.11, bf16[640,512]{1,0:T(8,128)(2,1)} %collective-permute-done.3), kind=kLoop, calls=%fused_computation.7 | loop fusion | flops 1572864 | bytes 2097152 | tf_op jit(solution)/shard_map/concatenate | solution.py:561
  13.7 2.5 %collective-permute-start.9 = (bf16[384,1024]{1,0:T(8,128)(2,1)S(1)}, bf16[384,1024]{1,0:T(8,128)(2,1)S(1)}, u32[]{:S(2)}, u32[]{:S(2)}) collective-permute-start(bf16[384,1024]{1,0:T(8,128)(2,1)S(1)} %fusion), channel_id=1, source_target_pairs={{0,4},{4,0},{8,12},{12,8},{1,5},{5,1},{9,13},{13,9},{2,6},{6,2},{1... | collective-permute-start | bytes 2359304 | tf_op jit(solution)/shard_map/ppermute | solution.py:178
  16.3 20.6 %collective-permute-done.6.refs_0_ = bf16[512,512]{1,0:T(8,128)(2,1)S(1)} collective-permute-done((bf16[512,512]{1,0:T(8,128)(2,1)S(1)}, bf16[512,512]{1,0:T(8,128)(2,1)S(1)}, u32[]{:S(2)}, u32[]{:S(2)}) %collective-permute-start.6) | collective-permute-done | bytes 524320 | tf_op jit(solution)/shard_map/ppermute | solution.py:178
  36.9 1.7 %collective-permute-start.8 = (bf16[512,512]{1,0:T(8,128)(2,1)S(1)}, bf16[512,512]{1,0:T(8,128)(2,1)S(1)}, u32[]{:S(2)}, u32[]{:S(2)}) collective-permute-start(bf16[512,512]{1,0:T(8,128)(2,1)S(1)} %collective-permute-done.6.refs_0_), channel_id=1, source_target_pairs={{0,2},{2,0},{1,3},{3,1},{4,6},{6,4},{5,7},{7,5},{8,10},{10,8},{9,1... | collective-permute-start | bytes 1572872 | tf_op jit(solution)/shard_map/ppermute | solution.py:173
  38.6 1.6 %bias.1.refs_0_ = f32[2,16,640]{2,1,0:T(8,128)S(1)} custom-call(s32[4,10,24]{2,1,0:T(8,128)S(1)} %pad_add_fusion.refs_0_), custom_call_target="tpu_custom_call" | custom-call | flops 1 | bytes 1 | tf_op jit(solution)/shard_map/bias/pallas_call | solution.py:195
  40.2 1.0 fusion.1
  41.2 0.1 collective-permute-start.4
  41.3 1.2 %pad_maximum_fusion.refs_1_.refs_5_.refs_2_ = bf16[640,1024]{1,0:T(8,128)(2,1)S(1)} fusion(bf16[640,512]{1,0:T(8,128)(2,1)} %collective-permute-done.3, bf16[640,512]{1,0:T(8,128)(2,1)S(1)} %bitcast.13), kind=kLoop, calls=%fused_computation.3 | loop fusion | flops 2621440 | bytes 2621440 | tf_op jit(solution)/shard_map/concatenate | solution.py:561
  42.5 1.7 %join.3 = (bf16[1024,1024]{1,0:T(8,128)(2,1)S(1)}, f32[1024,128]{1,0:T(8,128)S(1)}) custom-call(bf16[1024,512]{1,0:T(8,128)(2,1)S(1)} %multiply_convert_fusion.refs_0_, bf16[1024,512]{1,0:T(8,128)(2,1)} %collective-permute-done.5.refs_1_), custom_call_target="tpu_custom_call" | custom-call | flops 1 | bytes 1 | tf_op jit(solution)/shard_map/join/pallas_call | solution.py:195
  44.3 0.3 join.4
  44.6 3.5 %scores.5 = (bf16[1024,640]{1,0:T(8,128)(2,1)S(1)}, bf16[512,640]{1,0:T(8,128)(2,1)S(1)}, f32[4,640]{1,0:T(4,128)S(1)}) custom-call(f32[2,16,640]{2,1,0:T(8,128)S(1)} %bias.1.refs_0_, bf16[640,1024]{1,0:T(8,128)(2,1)S(1)} %pad_maximum_fusion.refs_1_.refs_5_.refs_2_, bf16[1024,1024]{1,0:T(8,128)(2,1)S(1)} %get-tuple-element.52.refs_2_, ...), custom_call_target="tpu_custom_call" | custom-call | flops 1 | bytes 1 | tf_op jit(solution)/shard_map/scores/pallas_call | solution.py:195
  48.0 2.3 %scores.6 = (bf16[1024,384]{1,0:T(8,128)(2,1)S(1)}, bf16[512,384]{1,0:T(8,128)(2,1)S(1)}, f32[4,384]{1,0:T(4,128)S(1)}) custom-call(f32[2,16,640]{2,1,0:T(8,128)S(1)} %bias.1.refs_0_, bf16[384,1024]{1,0:T(8,128)(2,1)S(1)} %collective-permute-done.9.refs_1_.refs_6_.refs_3_, bf16[1024,1024]{1,0:T(8,128)(2,1)S(1)} %get-tuple-element.52.refs_2_, ...), custom_call_target="tpu_custom_call" | custom-call | flops 1 | bytes 1 | tf_op jit(solution)/shard_map/scores/pallas_call | solution.py:195
  50.4 0.8 collective-permute-done.8
  51.3 0.1 collective-permute-start.11
  51.3 0.5 collective-permute-start.10
  51.8 1.0 %collective-permute-done.11.refs_3_ = bf16[256,512]{1,0:T(8,128)(2,1)S(1)} collective-permute-done((bf16[256,512]{1,0:T(8,128)(2,1)S(1)}, bf16[256,512]{1,0:T(8,128)(2,1)S(1)}, u32[]{:S(2)}, u32[]{:S(2)}) %collective-permute-start.11) | collective-permute-done | bytes 262176 | tf_op jit(solution)/shard_map/ppermute | solution.py:173
  52.9 0.4 collective-permute-done.10.refs_1_
  53.2 0.3 join.5
  53.5 1.3 %scores.7 = (bf16[512,640]{1,0:T(8,128)(2,1)S(1)}, f32[2,640]{1,0:T(2,128)S(1)}) custom-call(f32[2,16,640]{2,1,0:T(8,128)S(1)} %bias.1.refs_0_, bf16[640,1024]{1,0:T(8,128)(2,1)S(1)} %pad_maximum_fusion.refs_1_.refs_5_.refs_2_, bf16[512,1024]{1,0:T(8,128)(2,1)S(1)} %get-tuple-element.61.refs_2_.refs_6_, f32[512,128]{1,0:T(8,128)S(1)} %get-tuple-element.62.refs_3_.refs_7_), custom_call_target="tpu_custom_call" | custom-call | flops 1 | bytes 1 | tf_op jit(solution)/shard_map/scores/pallas_call | solution.py:195
  54.8 0.9 scores.8
  55.7 1.7 %scores.9 = (bf16[1024,256]{1,0:T(8,128)(2,1)S(1)}, bf16[512,256]{1,0:T(8,128)(2,1)S(1)}, bf16[512,256]{1,0:T(8,128)(2,1)S(1)}, f32[16,640]{1,0:T(8,128)S(1)}) custom-call(f32[2,16,640]{2,1,0:T(8,128)S(1)} %bias.1.refs_0_, bf16[256,1024]{1,0:T(8,128)(2,1)S(1)} %collective-permute-done.4.refs_1_.refs_7_.refs_4_, ...), custom_call_target="tpu_custom_call" | custom-call | flops 1 | bytes 1 | tf_op jit(solution)/shard_map/scores/pallas_call | solution.py:195
  57.4 1.3 %collective-permute-start.12 = (f32[16,640]{1,0:T(8,128)S(1)}, f32[16,640]{1,0:T(8,128)S(1)}, u32[]{:S(2)}, u32[]{:S(2)}) collective-permute-start(f32[16,640]{1,0:T(8,128)S(1)} %get-tuple-element.65.refs_0_), channel_id=1, source_target_pairs={{0,4},{4,0},{8,12},{12,8},{1,5},{5,1},{9,13},{13,9},{2,6},{6,2},{1... | collective-permute-start | bytes 122888 | tf_op jit(solution)/shard_map/ppermute | solution.py:178
  58.7 2.8 %collective-permute-done.12.refs_1_ = f32[16,640]{1,0:T(8,128)S(1)} collective-permute-done((f32[16,640]{1,0:T(8,128)S(1)}, f32[16,640]{1,0:T(8,128)S(1)}, u32[]{:S(2)}, u32[]{:S(2)}) %collective-permute-start.12) | collective-permute-done | bytes 40992 | tf_op jit(solution)/shard_map/ppermute | solution.py:178
  61.5 1.0 %far.4 = (bf16[528,512]{1,0:T(8,128)(2,1)S(1)}, f32[16,512]{1,0:T(8,128)S(1)}) custom-call(f32[16,640]{1,0:T(8,128)S(1)} %get-tuple-element.65.refs_0_, f32[16,640]{1,0:T(8,128)S(1)} %collective-permute-done.12.refs_1_, bf16[512,640]{1,0:T(8,128)(2,1)S(1)} %get-tuple-element.69.refs_2_, bf16[512,384]{1,0:T(8,128)(2,1)S(1)} %get-tuple-element.70.refs_3_, ...), custom_call_target="tpu_custom_call" | custom-call | flops 1 | bytes 1 | tf_op jit(solution)/shard_map/far/pallas_call | solution.py:195
  62.5 0.3 collective-permute-start.14
  62.8 0.5 collective-permute-start.13
  63.3 1.0 far.5
  64.3 0.4 collective-permute-done.13.refs_9_
  64.7 1.0 near.4
  65.7 0.2 collective-permute-start.15
  65.9 1.7 %collective-permute-start.16 = (bf16[192,512]{1,0:T(8,128)(2,1)S(1)}, bf16[192,512]{1,0:T(8,128)(2,1)S(1)}, u32[]{:S(2)}, u32[]{:S(2)}) collective-permute-start(bf16[192,512]{1,0:T(8,128)(2,1)S(1)} %get-tuple-element.76.refs_10_.refs_8_), channel_id=1, source_target_pairs={{0,2},{2,0},{1,3},{3,1},{4,6},{6,4},{5,7},{7,5},{8,10},{10,8},{9,1... | collective-permute-start | bytes 589832 | tf_op jit(solution)/shard_map/ppermute | solution.py:173
  67.6 1.0 far.7
  68.7 1.0 near.5
  69.7 3.4 %collective-permute-done.16.refs_1_ = bf16[192,512]{1,0:T(8,128)(2,1)S(1)} collective-permute-done((bf16[192,512]{1,0:T(8,128)(2,1)S(1)}, bf16[192,512]{1,0:T(8,128)(2,1)S(1)}, u32[]{:S(2)}, u32[]{:S(2)}) %collective-permute-start.16) | collective-permute-done | bytes 196640 | tf_op jit(solution)/shard_map/ppermute | solution.py:173
  73.2 2.4 %collective-permute-start.26 = (bf16[192,512]{1,0:T(8,128)(2,1)S(1)}, bf16[192,512]{1,0:T(8,128)(2,1)S(1)}, u32[]{:S(2)}, u32[]{:S(2)}) collective-permute-start(bf16[192,512]{1,0:T(8,128)(2,1)S(1)} %add.35.refs_2_), channel_id=1, source_target_pairs={{0,8},{4,12},{8,0},{12,4},{1,9},{5,13},{9,1},{13,5},{2,10},{6,14},... | collective-permute-start | bytes 589832 | tf_op jit(solution)/shard_map/ppermute | solution.py:178
  75.5 1.0 %collective-permute-start.17 = (bf16[176,512]{1,0:T(8,128)(2,1)S(1)}, bf16[176,512]{1,0:T(8,128)(2,1)S(1)}, u32[]{:S(2)}, u32[]{:S(2)}) collective-permute-start(bf16[176,512]{1,0:T(8,128)(2,1)S(1)} %get-tuple-element.85), channel_id=1, source_target_pairs={{0,2},{2,0},{1,3},{3,1},{4,6},{6,4},{5,7},{7,5},{8,10},{10,8},{9,1... | collective-permute-start | bytes 540680 | tf_op jit(solution)/shard_map/ppermute | solution.py:173
  76.7 0.5 collective-permute-start.22
  77.2 0.1 collective-permute-start.21
  77.3 4.0 %collective-permute-done.17.refs_1_ = bf16[176,512]{1,0:T(8,128)(2,1)S(1)} collective-permute-done((bf16[176,512]{1,0:T(8,128)(2,1)S(1)}, bf16[176,512]{1,0:T(8,128)(2,1)S(1)}, u32[]{:S(2)}, u32[]{:S(2)}) %collective-permute-start.17) | collective-permute-done | bytes 180256 | tf_op jit(solution)/shard_map/ppermute | solution.py:173
  81.3 0.5 energy.1
  81.9 0.7 collective-permute-start.27
  82.5 1.7 %collective-permute-start.18 = (bf16[160,512]{1,0:T(8,128)(2,1)S(1)}, bf16[160,512]{1,0:T(8,128)(2,1)S(1)}, u32[]{:S(2)}, u32[]{:S(2)}) collective-permute-start(bf16[160,512]{1,0:T(8,128)(2,1)S(1)} %get-tuple-element.86), channel_id=1, source_target_pairs={{0,2},{2,0},{1,3},{3,1},{4,6},{6,4},{5,7},{7,5},{8,10},{10,8},{9,1... | collective-permute-start | bytes 491528 | tf_op jit(solution)/shard_map/ppermute | solution.py:173
  84.2 1.0 near.6
  85.3 0.4 collective-permute-start.25
  85.7 1.7 %collective-permute-start.24 = (bf16[264,512]{1,0:T(8,128)(2,1)S(1)}, bf16[264,512]{1,0:T(8,128)(2,1)S(1)}, u32[]{:S(2)}, u32[]{:S(2)}) collective-permute-start(bf16[264,512]{1,0:T(8,128)(2,1)S(1)} %get-tuple-element.96.refs_11_), channel_id=1, source_target_pairs={{0,2},{2,0},{1,3},{3,1},{4,6},{6,4},{5,7},{7,5},{8,10},{10,8},{9,1... | collective-permute-start | bytes 811016 | tf_op jit(solution)/shard_map/ppermute | solution.py:173
  87.4 2.2 %collective-permute-done.18.refs_1_ = bf16[160,512]{1,0:T(8,128)(2,1)S(1)} collective-permute-done((bf16[160,512]{1,0:T(8,128)(2,1)S(1)}, bf16[160,512]{1,0:T(8,128)(2,1)S(1)}, u32[]{:S(2)}, u32[]{:S(2)}) %collective-permute-start.18) | collective-permute-done | bytes 163872 | tf_op jit(solution)/shard_map/ppermute | solution.py:173
  89.6 0.1 add.37.refs_3_.refs_8_
  89.7 2.4 %collective-permute-start.28 = (bf16[160,512]{1,0:T(8,128)(2,1)S(1)}, bf16[160,512]{1,0:T(8,128)(2,1)S(1)}, u32[]{:S(2)}, u32[]{:S(2)}) collective-permute-start(bf16[160,512]{1,0:T(8,128)(2,1)S(1)} %add.37.refs_3_.refs_8_), channel_id=1, source_target_pairs={{0,8},{4,12},{8,0},{12,4},{1,9},{5,13},{9,1},{13,5},{2,10},{6,14},... | collective-permute-start | bytes 491528 | tf_op jit(solution)/shard_map/ppermute | solution.py:178
  92.0 1.2 %place.1 = (f32[8,64]{1,0:T(8,128)S(1)}, f32[16,64]{1,0:T(8,128)S(1)}) custom-call(s32[4,10,24]{2,1,0:T(8,128)S(1)} %pad_add_fusion.refs_0_, f32[10,64]{1,0:T(8,128)S(1)} %get-tuple-element.79.refs_1_, f32[8,64]{1,0:T(8,128)S(1)} %get-tuple-element.80.refs_2_, bf16[160,512]{1,0:T(8,128)(2,1)S(1)} %add.37.refs_3_.refs_8_), custom_call_target="tpu_custom_call" | custom-call | flops 1 | bytes 1 | tf_op jit(solution)/shard_map/place/pallas_call | solution.py:195
  93.3 1.0 %far.6 = (bf16[528,512]{1,0:T(8,128)(2,1)S(1)}, f32[16,512]{1,0:T(8,128)S(1)}) custom-call(f32[16,640]{1,0:T(8,128)S(1)} %get-tuple-element.65.refs_0_, f32[16,640]{1,0:T(8,128)S(1)} %collective-permute-done.12.refs_1_, bf16[1024,640]{1,0:T(8,128)(2,1)S(1)} %get-tuple-element.89.refs_2_, bf16[1024,384]{1,0:T(8,128)(2,1)S(1)} %get-tuple-element.90.refs_3_, ...), custom_call_target="tpu_custom_call" | custom-call | flops 1 | bytes 1 | tf_op jit(solution)/shard_map/far/pallas_call | solution.py:195
  94.3 0.1 collective-permute-start.19
  94.4 3.2 %collective-permute-done.27.refs_0_ = bf16[176,512]{1,0:T(8,128)(2,1)S(1)} collective-permute-done((bf16[176,512]{1,0:T(8,128)(2,1)S(1)}, bf16[176,512]{1,0:T(8,128)(2,1)S(1)}, u32[]{:S(2)}, u32[]{:S(2)}) %collective-permute-start.27) | collective-permute-done | bytes 180256 | tf_op jit(solution)/shard_map/ppermute | solution.py:178
  97.6 1.2 %near.7.refs_2_ = f32[528,512]{1,0:T(8,128)S(1)} custom-call(f32[16,640]{1,0:T(8,128)S(1)} %get-tuple-element.65.refs_0_, f32[16,640]{1,0:T(8,128)S(1)} %collective-permute-done.12.refs_1_, bf16[1024,640]{1,0:T(8,128)(2,1)S(1)} %get-tuple-element.89.refs_2_, bf16[1024,384]{1,0:T(8,128)(2,1)S(1)} %get-tuple-element.90.refs_3_, ...), custom_call_target="tpu_custom_call" | custom-call | flops 1 | bytes 1 | tf_op jit(solution)/shard_map/near/pallas_call | solution.py:195
  98.8 1.7 %collective-permute-done.24.refs_3_ = bf16[264,512]{1,0:T(8,128)(2,1)S(1)} collective-permute-done((bf16[264,512]{1,0:T(8,128)(2,1)S(1)}, bf16[264,512]{1,0:T(8,128)(2,1)S(1)}, u32[]{:S(2)}, u32[]{:S(2)}) %collective-permute-start.24) | collective-permute-done | bytes 270368 | tf_op jit(solution)/shard_map/ppermute | solution.py:173
  100.5 0.2 collective-permute-done.28.refs_7_
  100.7 1.2 %final.1 = (f32[512,512]{1,0:T(8,128)}, f32[8,64]{1,0:T(8,128)}) custom-call(f32[8,64]{1,0:T(8,128)S(1)} %get-tuple-element.87.refs_0_, f32[16,64]{1,0:T(8,128)S(1)} %get-tuple-element.88.refs_1_, f32[528,512]{1,0:T(8,128)S(1)} %near.7.refs_2_, bf16[264,512]{1,0:T(8,128)(2,1)S(1)} %collective-permute-done.24.refs_3_, ...), custom_call_target="tpu_custom_call" | custom-call | flops 1 | bytes 1 | tf_op jit(solution)/shard_map/final/pallas_call | solution.py:195
  (34 shorter events, 0.5 us)
Async XLA Ops:
  0.6 9.0 %copy-start = (f32[1024,512]{1,0:T(8,128)S(1)}, f32[1024,512]{1,0:T(8,128)}, u32[]{:S(2)}) copy-start(f32[1024,512]{1,0:T(8,128)} %refs_10_.1) | copy-start | bytes 6291460
  1.5 9.1 %collective-permute-start.1 = (s32[10,24]{1,0:T(8,128)S(1)}, s32[10,24]{1,0:T(8,128)S(1)}, u32[]{:S(2)}, u32[]{:S(2)}) collective-permute-start(s32[10,24]{1,0:T(8,128)S(1)} %get-tuple-element.111), channel_id=1, source_target_pairs={{0,8},{4,12},{8,0},{12,4},{1,9},{5,13},{9,1},{13,5},{2,10},{6,14},... | collective-permute-start | bytes 2888 | tf_op jit(solution)/shard_map/ppermute | solution.py:178
  5.6 5.0 %collective-permute-start = (s32[10,24]{1,0:T(8,128)S(1)}, s32[10,24]{1,0:T(8,128)S(1)}, u32[]{:S(2)}, u32[]{:S(2)}) collective-permute-start(s32[10,24]{1,0:T(8,128)S(1)} %get-tuple-element.111), channel_id=1, source_target_pairs={{0,4},{4,0},{8,12},{12,8},{1,5},{5,1},{9,13},{13,9},{2,6},{6,2},{1... | collective-permute-start | bytes 2888 | tf_op jit(solution)/shard_map/ppermute | solution.py:178
  7.2 5.4 %collective-permute-start.2 = (s32[10,24]{1,0:T(8,128)S(1)}, s32[10,24]{1,0:T(8,128)S(1)}, u32[]{:S(2)}, u32[]{:S(2)}) collective-permute-start(s32[10,24]{1,0:T(8,128)S(1)} %get-tuple-element.111), channel_id=1, source_target_pairs={{0,12},{4,8},{8,4},{12,0},{1,13},{5,9},{9,5},{13,1},{2,14},{6,10},... | collective-permute-start | bytes 2888 | tf_op jit(solution)/shard_map/ppermute | solution.py:178
  9.6 3.0 %collective-permute-start.3 = (bf16[640,512]{1,0:T(8,128)(2,1)}, bf16[640,512]{1,0:T(8,128)(2,1)}, u32[]{:S(2)}, u32[]{:S(2)}) collective-permute-start(bf16[640,512]{1,0:T(8,128)(2,1)} %bitcast.8), channel_id=1, source_target_pairs={{0,1},{1,0},{2,3},{3,2},{4,5},{5,4},{6,7},{7,6},{8,9},{9,8},{10,11... | collective-permute-start | bytes 1966088 | tf_op jit(solution)/shard_map/ppermute | solution.py:173
  9.9 32.6 %collective-permute-start.5 = (bf16[1024,512]{1,0:T(8,128)(2,1)S(1)}, bf16[1024,512]{1,0:T(8,128)(2,1)}, u32[]{:S(2)}, u32[]{:S(2)}) collective-permute-start(bf16[1024,512]{1,0:T(8,128)(2,1)S(1)} %multiply_convert_fusion.refs_0_), channel_id=1, source_target_pairs={{0,1},{1,0},{2,3},{3,2},{4,5},{5,4},{6,7},{7,6},{8,9},{9,8},{10,11... | collective-permute-start | bytes 3145736 | tf_op jit(solution)/shard_map/ppermute | solution.py:173
  10.5 2.2 %copy-start.1 = (bf16[1,1,10,64,512]{4,3,2,1,0:T(8,128)(2,1)S(1)}, bf16[1,1,10,64,512]{4,3,2,1,0:T(8,128)(2,1)}, u32[]{:S(2)}) copy-start(bf16[1,1,10,64,512]{4,3,2,1,0:T(8,128)(2,1)} %get-tuple-element.101) | copy-start | bytes 1966084
  12.6 24.2 %collective-permute-start.6 = (bf16[512,512]{1,0:T(8,128)(2,1)S(1)}, bf16[512,512]{1,0:T(8,128)(2,1)S(1)}, u32[]{:S(2)}, u32[]{:S(2)}) collective-permute-start(bf16[512,512]{1,0:T(8,128)(2,1)S(1)} %multiply_convert_fusion.1), channel_id=1, source_target_pairs={{0,8},{4,12},{8,0},{12,4},{1,9},{5,13},{9,1},{13,5},{2,10},{6,14},... | collective-permute-start | bytes 1572872 | tf_op jit(solution)/shard_map/ppermute | solution.py:178
  13.7 34.3 %collective-permute-start.9 = (bf16[384,1024]{1,0:T(8,128)(2,1)S(1)}, bf16[384,1024]{1,0:T(8,128)(2,1)S(1)}, u32[]{:S(2)}, u32[]{:S(2)}) collective-permute-start(bf16[384,1024]{1,0:T(8,128)(2,1)S(1)} %fusion), channel_id=1, source_target_pairs={{0,4},{4,0},{8,12},{12,8},{1,5},{5,1},{9,13},{13,9},{2,6},{6,2},{1... | collective-permute-start | bytes 2359304 | tf_op jit(solution)/shard_map/ppermute | solution.py:178
  36.9 7.4 %collective-permute-start.7 = (bf16[512,512]{1,0:T(8,128)(2,1)S(1)}, bf16[512,512]{1,0:T(8,128)(2,1)S(1)}, u32[]{:S(2)}, u32[]{:S(2)}) collective-permute-start(bf16[512,512]{1,0:T(8,128)(2,1)S(1)} %collective-permute-done.6.refs_0_), channel_id=1, source_target_pairs={{0,1},{1,0},{2,3},{3,2},{4,5},{5,4},{6,7},{7,6},{8,9},{9,8},{10,11... | collective-permute-start | bytes 1572872 | tf_op jit(solution)/shard_map/ppermute | solution.py:173
  36.9 14.3 %collective-permute-start.8 = (bf16[512,512]{1,0:T(8,128)(2,1)S(1)}, bf16[512,512]{1,0:T(8,128)(2,1)S(1)}, u32[]{:S(2)}, u32[]{:S(2)}) collective-permute-start(bf16[512,512]{1,0:T(8,128)(2,1)S(1)} %collective-permute-done.6.refs_0_), channel_id=1, source_target_pairs={{0,2},{2,0},{1,3},{3,1},{4,6},{6,4},{5,7},{7,5},{8,10},{10,8},{9,1... | collective-permute-start | bytes 1572872 | tf_op jit(solution)/shard_map/ppermute | solution.py:173
  41.2 14.5 %collective-permute-start.4 = (bf16[256,1024]{1,0:T(8,128)(2,1)S(1)}, bf16[256,1024]{1,0:T(8,128)(2,1)S(1)}, u32[]{:S(2)}, u32[]{:S(2)}) collective-permute-start(bf16[256,1024]{1,0:T(8,128)(2,1)S(1)} %fusion.1), channel_id=1, source_target_pairs={{0,4},{4,0},{8,12},{12,8},{1,5},{5,1},{9,13},{13,9},{2,6},{6,2},{1... | collective-permute-start | bytes 1572872 | tf_op jit(solution)/shard_map/ppermute | solution.py:178
  51.3 1.6 %collective-permute-start.11 = (bf16[256,512]{1,0:T(8,128)(2,1)S(1)}, bf16[256,512]{1,0:T(8,128)(2,1)S(1)}, u32[]{:S(2)}, u32[]{:S(2)}) collective-permute-start(bf16[256,512]{1,0:T(8,128)(2,1)S(1)} %get-tuple-element.108.refs_2_), channel_id=1, source_target_pairs={{0,1},{1,0},{2,3},{3,2},{4,5},{5,4},{6,7},{7,6},{8,9},{9,8},{10,11... | collective-permute-start | bytes 786440 | tf_op jit(solution)/shard_map/ppermute | solution.py:173
  51.3 1.9 %collective-permute-start.10 = (bf16[256,512]{1,0:T(8,128)(2,1)S(1)}, bf16[256,512]{1,0:T(8,128)(2,1)S(1)}, u32[]{:S(2)}, u32[]{:S(2)}) collective-permute-start(bf16[256,512]{1,0:T(8,128)(2,1)S(1)} %get-tuple-element.109.refs_0_), channel_id=1, source_target_pairs={{0,1},{1,0},{2,3},{3,2},{4,5},{5,4},{6,7},{7,6},{8,9},{9,8},{10,11... | collective-permute-start | bytes 786440 | tf_op jit(solution)/shard_map/ppermute | solution.py:173
  57.4 4.1 %collective-permute-start.12 = (f32[16,640]{1,0:T(8,128)S(1)}, f32[16,640]{1,0:T(8,128)S(1)}, u32[]{:S(2)}, u32[]{:S(2)}) collective-permute-start(f32[16,640]{1,0:T(8,128)S(1)} %get-tuple-element.65.refs_0_), channel_id=1, source_target_pairs={{0,4},{4,0},{8,12},{12,8},{1,5},{5,1},{9,13},{13,9},{2,6},{6,2},{1... | collective-permute-start | bytes 122888 | tf_op jit(solution)/shard_map/ppermute | solution.py:178
  62.5 1.8 %collective-permute-start.14 = (bf16[264,512]{1,0:T(8,128)(2,1)S(1)}, bf16[264,512]{1,0:T(8,128)(2,1)S(1)}, u32[]{:S(2)}, u32[]{:S(2)}) collective-permute-start(bf16[264,512]{1,0:T(8,128)(2,1)S(1)} %get-tuple-element.106), channel_id=1, source_target_pairs={{0,1},{1,0},{2,3},{3,2},{4,5},{5,4},{6,7},{7,6},{8,9},{9,8},{10,11... | collective-permute-start | bytes 811016 | tf_op jit(solution)/shard_map/ppermute | solution.py:173
  62.8 1.9 %collective-permute-start.13 = (bf16[264,512]{1,0:T(8,128)(2,1)S(1)}, bf16[264,512]{1,0:T(8,128)(2,1)S(1)}, u32[]{:S(2)}, u32[]{:S(2)}) collective-permute-start(bf16[264,512]{1,0:T(8,128)(2,1)S(1)} %get-tuple-element.107), channel_id=1, source_target_pairs={{0,1},{1,0},{2,3},{3,2},{4,5},{5,4},{6,7},{7,6},{8,9},{9,8},{10,11... | collective-permute-start | bytes 811016 | tf_op jit(solution)/shard_map/ppermute | solution.py:173
  65.7 2.9 %collective-permute-start.15 = (bf16[528,512]{1,0:T(8,128)(2,1)S(1)}, bf16[528,512]{1,0:T(8,128)(2,1)S(1)}, u32[]{:S(2)}, u32[]{:S(2)}) collective-permute-start(bf16[528,512]{1,0:T(8,128)(2,1)S(1)} %get-tuple-element.77.refs_11_), channel_id=1, source_target_pairs={{0,1},{1,0},{2,3},{3,2},{4,5},{5,4},{6,7},{7,6},{8,9},{9,8},{10,11... | collective-permute-start | bytes 1622024 | tf_op jit(solution)/shard_map/ppermute | solution.py:173
  65.9 7.2 %collective-permute-start.16 = (bf16[192,512]{1,0:T(8,128)(2,1)S(1)}, bf16[192,512]{1,0:T(8,128)(2,1)S(1)}, u32[]{:S(2)}, u32[]{:S(2)}) collective-permute-start(bf16[192,512]{1,0:T(8,128)(2,1)S(1)} %get-tuple-element.76.refs_10_.refs_8_), channel_id=1, source_target_pairs={{0,2},{2,0},{1,3},{3,1},{4,6},{6,4},{5,7},{7,5},{8,10},{10,8},{9,1... | collective-permute-start | bytes 589832 | tf_op jit(solution)/shard_map/ppermute | solution.py:173
  73.2 14.2 %collective-permute-start.26 = (bf16[192,512]{1,0:T(8,128)(2,1)S(1)}, bf16[192,512]{1,0:T(8,128)(2,1)S(1)}, u32[]{:S(2)}, u32[]{:S(2)}) collective-permute-start(bf16[192,512]{1,0:T(8,128)(2,1)S(1)} %add.35.refs_2_), channel_id=1, source_target_pairs={{0,8},{4,12},{8,0},{12,4},{1,9},{5,13},{9,1},{13,5},{2,10},{6,14},... | collective-permute-start | bytes 589832 | tf_op jit(solution)/shard_map/ppermute | solution.py:178
  75.5 5.7 %collective-permute-start.17 = (bf16[176,512]{1,0:T(8,128)(2,1)S(1)}, bf16[176,512]{1,0:T(8,128)(2,1)S(1)}, u32[]{:S(2)}, u32[]{:S(2)}) collective-permute-start(bf16[176,512]{1,0:T(8,128)(2,1)S(1)} %get-tuple-element.85), channel_id=1, source_target_pairs={{0,2},{2,0},{1,3},{3,1},{4,6},{6,4},{5,7},{7,5},{8,10},{10,8},{9,1... | collective-permute-start | bytes 540680 | tf_op jit(solution)/shard_map/ppermute | solution.py:173
  76.7 5.2 %collective-permute-start.23 = (bf16[132,512]{1,0:T(8,128)(2,1)S(1)}, bf16[132,512]{1,0:T(8,128)(2,1)S(1)}, u32[]{:S(2)}, u32[]{:S(2)}) collective-permute-start(bf16[132,512]{1,0:T(8,128)(2,1)S(1)} %get-tuple-element.102), channel_id=1, source_target_pairs={{0,1},{1,0},{2,3},{3,2},{4,5},{5,4},{6,7},{7,6},{8,9},{9,8},{10,11... | collective-permute-start | bytes 405512 | tf_op jit(solution)/shard_map/ppermute | solution.py:173
  76.7 5.8 %collective-permute-start.22 = (bf16[132,512]{1,0:T(8,128)(2,1)S(1)}, bf16[132,512]{1,0:T(8,128)(2,1)S(1)}, u32[]{:S(2)}, u32[]{:S(2)}) collective-permute-start(bf16[132,512]{1,0:T(8,128)(2,1)S(1)} %get-tuple-element.103), channel_id=1, source_target_pairs={{0,1},{1,0},{2,3},{3,2},{4,5},{5,4},{6,7},{7,6},{8,9},{9,8},{10,11... | collective-permute-start | bytes 405512 | tf_op jit(solution)/shard_map/ppermute | solution.py:173
  77.2 7.0 %collective-permute-start.21 = (bf16[132,512]{1,0:T(8,128)(2,1)S(1)}, bf16[132,512]{1,0:T(8,128)(2,1)S(1)}, u32[]{:S(2)}, u32[]{:S(2)}) collective-permute-start(bf16[132,512]{1,0:T(8,128)(2,1)S(1)} %get-tuple-element.104), channel_id=1, source_target_pairs={{0,1},{1,0},{2,3},{3,2},{4,5},{5,4},{6,7},{7,6},{8,9},{9,8},{10,11... | collective-permute-start | bytes 405512 | tf_op jit(solution)/shard_map/ppermute | solution.py:173
  81.3 3.0 %collective-permute-start.20 = (bf16[132,512]{1,0:T(8,128)(2,1)S(1)}, bf16[132,512]{1,0:T(8,128)(2,1)S(1)}, u32[]{:S(2)}, u32[]{:S(2)}) collective-permute-start(bf16[132,512]{1,0:T(8,128)(2,1)S(1)} %get-tuple-element.105), channel_id=1, source_target_pairs={{0,1},{1,0},{2,3},{3,2},{4,5},{5,4},{6,7},{7,6},{8,9},{9,8},{10,11... | collective-permute-start | bytes 405512 | tf_op jit(solution)/shard_map/ppermute | solution.py:173
  81.9 15.7 %collective-permute-start.27 = (bf16[176,512]{1,0:T(8,128)(2,1)S(1)}, bf16[176,512]{1,0:T(8,128)(2,1)S(1)}, u32[]{:S(2)}, u32[]{:S(2)}) collective-permute-start(bf16[176,512]{1,0:T(8,128)(2,1)S(1)} %add.36.refs_3_.refs_13_), channel_id=1, source_target_pairs={{0,8},{4,12},{8,0},{12,4},{1,9},{5,13},{9,1},{13,5},{2,10},{6,14},... | collective-permute-start | bytes 540680 | tf_op jit(solution)/shard_map/ppermute | solution.py:178
  82.5 7.0 %collective-permute-start.18 = (bf16[160,512]{1,0:T(8,128)(2,1)S(1)}, bf16[160,512]{1,0:T(8,128)(2,1)S(1)}, u32[]{:S(2)}, u32[]{:S(2)}) collective-permute-start(bf16[160,512]{1,0:T(8,128)(2,1)S(1)} %get-tuple-element.86), channel_id=1, source_target_pairs={{0,2},{2,0},{1,3},{3,1},{4,6},{6,4},{5,7},{7,5},{8,10},{10,8},{9,1... | collective-permute-start | bytes 491528 | tf_op jit(solution)/shard_map/ppermute | solution.py:173
  85.3 13.5 %collective-permute-start.25 = (bf16[264,512]{1,0:T(8,128)(2,1)S(1)}, bf16[264,512]{1,0:T(8,128)(2,1)S(1)}, u32[]{:S(2)}, u32[]{:S(2)}) collective-permute-start(bf16[264,512]{1,0:T(8,128)(2,1)S(1)} %get-tuple-element.97), channel_id=1, source_target_pairs={{0,2},{2,0},{1,3},{3,1},{4,6},{6,4},{5,7},{7,5},{8,10},{10,8},{9,1... | collective-permute-start | bytes 811016 | tf_op jit(solution)/shard_map/ppermute | solution.py:173
  85.7 14.8 %collective-permute-start.24 = (bf16[264,512]{1,0:T(8,128)(2,1)S(1)}, bf16[264,512]{1,0:T(8,128)(2,1)S(1)}, u32[]{:S(2)}, u32[]{:S(2)}) collective-permute-start(bf16[264,512]{1,0:T(8,128)(2,1)S(1)} %get-tuple-element.96.refs_11_), channel_id=1, source_target_pairs={{0,2},{2,0},{1,3},{3,1},{4,6},{6,4},{5,7},{7,5},{8,10},{10,8},{9,1... | collective-permute-start | bytes 811016 | tf_op jit(solution)/shard_map/ppermute | solution.py:173
  89.7 11.0 %collective-permute-start.28 = (bf16[160,512]{1,0:T(8,128)(2,1)S(1)}, bf16[160,512]{1,0:T(8,128)(2,1)S(1)}, u32[]{:S(2)}, u32[]{:S(2)}) collective-permute-start(bf16[160,512]{1,0:T(8,128)(2,1)S(1)} %add.37.refs_3_.refs_8_), channel_id=1, source_target_pairs={{0,8},{4,12},{8,0},{12,4},{1,9},{5,13},{9,1},{13,5},{2,10},{6,14},... | collective-permute-start | bytes 491528 | tf_op jit(solution)/shard_map/ppermute | solution.py:178
  94.3 3.3 %collective-permute-start.19 = (bf16[528,512]{1,0:T(8,128)(2,1)S(1)}, bf16[528,512]{1,0:T(8,128)(2,1)S(1)}, u32[]{:S(2)}, u32[]{:S(2)}) collective-permute-start(bf16[528,512]{1,0:T(8,128)(2,1)S(1)} %get-tuple-element.93), channel_id=1, source_target_pairs={{0,1},{1,0},{2,3},{3,2},{4,5},{5,4},{6,7},{7,6},{8,9},{9,8},{10,11... | collective-permute-start | bytes 1622024 | tf_op jit(solution)/shard_map/ppermute | solution.py:173

commit v6 on v5

--- a/solution.py
+++ b/solution.py
@@ -577,7 +577,7 @@
 
     xs = (full, *x1)
     half = jnp.bfloat16
-    first, equal = (192,176), (264,)
+    first, equal = (144,192), (264,)
 
     far_a, mass_a = far_sums(stats, peer, em[2], xs, 2, False)
     far_b, mass_b = far_sums(stats, peer, em[1], xs, 1, True, [far_a])
@@ -609,7 +609,7 @@
 
     came_back, backs = [], []
     for i, part in enumerate(part_b):
-        sent = after(sent_a[i], backs[-1]) if i >= 1 else sent_a[i]
+        sent = after(sent_a[i], backs[-1]) if i >= 2 else sent_a[i]
         energies = [last] if i == len(first) else []
         back, came = returned(part, swapped(sent, "rep"), backs[-1:], energies)
         backs.append(back)

time: 102 us -> 99.9 us (0.979)
  starting transfers between devices: 25.9 us -> 24.4 us
    ppermute x19, waiting for transfers between devices: 14 us -> 5.96 us  [swapped(): return lax.ppermute(value, axis, [(0, 1), (1, 0)])]
    ppermute x10, waiting for transfers between devices: 28.8 us -> 36.1 us  [paired(): return lax.ppermute(value, 'wide', [(w, w ^ flip) for w in range(count)])]
    ppermute x19, starting transfers between devices: 11 us -> 9.62 us  [swapped(): return lax.ppermute(value, axis, [(0, 1), (1, 0)])]
where the time goes in v6:
time: 99.9 us; the launch traced here: 99.6 us
  waiting for transfers between devices  42 us (42%)
  Pallas kernels  25 us (25%)
  starting transfers between devices  24.4 us (24%)
  other arithmetic  4.54 us (5%)
  local copies, waits for them, and re-layouts  2.61 us (3%)
    ppermute x10, waiting for transfers between devices, paired(): return lax.ppermute(value, 'wide', [(w, w ^ flip) for w in range(count)])  36.1 us
    pallas_call x25, Pallas kernels, call(): pl.pallas_call(run, in_specs=in_specs + [HBM] * len(needs), out_specs=[VM...  25 us
    ppermute x10, starting transfers between devices, paired(): return lax.ppermute(value, 'wide', [(w, w ^ flip) for w in range(count)])  14.8 us
    ppermute x19, starting transfers between devices, swapped(): return lax.ppermute(value, axis, [(0, 1), (1, 0)])  9.62 us
    ppermute x19, waiting for transfers between devices, swapped(): return lax.ppermute(value, axis, [(0, 1), (1, 0)])  5.96 us
    concatenate x3, other arithmetic, grid_plan(): full = jnp.concatenate([own, took], axis=1)  3.28 us
    dynamic_slice x1, local copies, waits for them, and re-layouts, grid_plan(): lax.dynamic_slice_in_dim(blocks, (1 - sub) * span, span, 1)  2.46 us
  transfers between devices with their start and end apart: 29, of which 13 were waited for; matrix products, arithmetic and copies ran while one was open for 6% of the time, Pallas kernels for 20%

profile of v6, /device:TPU:0, one launch (start us, length us, event | category | flops | bytes accessed | tf_op | source)
XLA Modules:
  0.0 99.6 jit_solution(11297691829633921456)
XLA Ops:
  0.6 0.9 fusion.2
  1.5 4.1 %collective-permute-start.1 = (s32[10,24]{1,0:T(8,128)S(1)}, s32[10,24]{1,0:T(8,128)S(1)}, u32[]{:S(2)}, u32[]{:S(2)}) collective-permute-start(s32[10,24]{1,0:T(8,128)S(1)} %get-tuple-element.109), channel_id=1, source_target_pairs={{0,8},{4,12},{8,0},{12,4},{1,9},{5,13},{9,1},{13,5},{2,10},{6,14},... | collective-permute-start | bytes 2888 | tf_op jit(solution)/shard_map/ppermute | solution.py:178
  5.6 1.6 %collective-permute-start = (s32[10,24]{1,0:T(8,128)S(1)}, s32[10,24]{1,0:T(8,128)S(1)}, u32[]{:S(2)}, u32[]{:S(2)}) collective-permute-start(s32[10,24]{1,0:T(8,128)S(1)} %get-tuple-element.109), channel_id=1, source_target_pairs={{0,4},{4,0},{8,12},{12,8},{1,5},{5,1},{9,13},{13,9},{2,6},{6,2},{1... | collective-permute-start | bytes 2888 | tf_op jit(solution)/shard_map/ppermute | solution.py:178
  7.2 2.5 %constant_dynamic-slice_fusion = (bf16[1,1,10,64,512]{4,3,2,1,0:T(8,128)(2,1)}, bf16[1,1,10,64,512]{4,3,2,1,0:T(8,128)(2,1)}) fusion(bf16[1,1,10,128,512]{4,3,2,1,0:T(8,128)(2,1)} %param.5, s32[]{:T(128)S(6)} %select_n.10, s32[]{:T(128)S(6)} %select_n.9), kind=kLoop, calls=%fused_computation.12 | loop fusion | bytes 2621448 | tf_op jit(solution)/shard_map/dynamic_slice | solution.py:558
  9.6 0.3 multiply_convert_fusion.refs_0_
  9.9 0.6 collective-permute-start.5
  10.5 0.1 multiply_convert_fusion.1
  10.6 2.0 %collective-permute-done.2 = s32[10,24]{1,0:T(8,128)S(1)} collective-permute-done((s32[10,24]{1,0:T(8,128)S(1)}, s32[10,24]{1,0:T(8,128)S(1)}, u32[]{:S(2)}, u32[]{:S(2)}) %collective-permute-start.2) | collective-permute-done | bytes 992 | tf_op jit(solution)/shard_map/ppermute | solution.py:178
  12.7 1.1 %fusion = bf16[384,1024]{1,0:T(8,128)(2,1)S(1)} fusion(bf16[640,512]{1,0:T(8,128)(2,1)S(1)} %bitcast.11, bf16[640,512]{1,0:T(8,128)(2,1)} %collective-permute-done.3), kind=kLoop, calls=%fused_computation.7 | loop fusion | flops 1572864 | bytes 2097152 | tf_op jit(solution)/shard_map/concatenate | solution.py:561
  13.7 2.5 %collective-permute-start.9 = (bf16[384,1024]{1,0:T(8,128)(2,1)S(1)}, bf16[384,1024]{1,0:T(8,128)(2,1)S(1)}, u32[]{:S(2)}, u32[]{:S(2)}) collective-permute-start(bf16[384,1024]{1,0:T(8,128)(2,1)S(1)} %fusion), channel_id=1, source_target_pairs={{0,4},{4,0},{8,12},{12,8},{1,5},{5,1},{9,13},{13,9},{2,6},{6,2},{1... | collective-permute-start | bytes 2359304 | tf_op jit(solution)/shard_map/ppermute | solution.py:178
  16.3 20.6 %collective-permute-done.6.refs_0_ = bf16[512,512]{1,0:T(8,128)(2,1)S(1)} collective-permute-done((bf16[512,512]{1,0:T(8,128)(2,1)S(1)}, bf16[512,512]{1,0:T(8,128)(2,1)S(1)}, u32[]{:S(2)}, u32[]{:S(2)}) %collective-permute-start.6) | collective-permute-done | bytes 524320 | tf_op jit(solution)/shard_map/ppermute | solution.py:178
  36.9 1.7 %collective-permute-start.8 = (bf16[512,512]{1,0:T(8,128)(2,1)S(1)}, bf16[512,512]{1,0:T(8,128)(2,1)S(1)}, u32[]{:S(2)}, u32[]{:S(2)}) collective-permute-start(bf16[512,512]{1,0:T(8,128)(2,1)S(1)} %collective-permute-done.6.refs_0_), channel_id=1, source_target_pairs={{0,2},{2,0},{1,3},{3,1},{4,6},{6,4},{5,7},{7,5},{8,10},{10,8},{9,1... | collective-permute-start | bytes 1572872 | tf_op jit(solution)/shard_map/ppermute | solution.py:173
  38.6 1.6 %bias.1.refs_0_ = f32[2,16,640]{2,1,0:T(8,128)S(1)} custom-call(s32[4,10,24]{2,1,0:T(8,128)S(1)} %pad_add_fusion.refs_0_), custom_call_target="tpu_custom_call" | custom-call | flops 1 | bytes 1 | tf_op jit(solution)/shard_map/bias/pallas_call | solution.py:195
  40.2 1.0 %fusion.1 = bf16[256,1024]{1,0:T(8,128)(2,1)S(1)} fusion(bf16[640,512]{1,0:T(8,128)(2,1)S(1)} %bitcast.12, bf16[640,512]{1,0:T(8,128)(2,1)} %collective-permute-done.3), kind=kLoop, calls=%fused_computation.8 | loop fusion | flops 1048576 | bytes 1835008 | tf_op jit(solution)/shard_map/concatenate | solution.py:561
  41.2 0.1 collective-permute-start.4
  41.3 1.2 %pad_maximum_fusion.refs_1_.refs_5_.refs_2_ = bf16[640,1024]{1,0:T(8,128)(2,1)S(1)} fusion(bf16[640,512]{1,0:T(8,128)(2,1)} %collective-permute-done.3, bf16[640,512]{1,0:T(8,128)(2,1)S(1)} %bitcast.13), kind=kLoop, calls=%fused_computation.3 | loop fusion | flops 2621440 | bytes 2621440 | tf_op jit(solution)/shard_map/concatenate | solution.py:561
  42.5 1.7 %join.3 = (bf16[1024,1024]{1,0:T(8,128)(2,1)S(1)}, f32[1024,128]{1,0:T(8,128)S(1)}) custom-call(bf16[1024,512]{1,0:T(8,128)(2,1)S(1)} %multiply_convert_fusion.refs_0_, bf16[1024,512]{1,0:T(8,128)(2,1)} %collective-permute-done.5.refs_1_), custom_call_target="tpu_custom_call" | custom-call | flops 1 | bytes 1 | tf_op jit(solution)/shard_map/join/pallas_call | solution.py:195
  44.3 0.3 join.4
  44.6 3.5 %scores.5 = (bf16[1024,640]{1,0:T(8,128)(2,1)S(1)}, bf16[512,640]{1,0:T(8,128)(2,1)S(1)}, f32[4,640]{1,0:T(4,128)S(1)}) custom-call(f32[2,16,640]{2,1,0:T(8,128)S(1)} %bias.1.refs_0_, bf16[640,1024]{1,0:T(8,128)(2,1)S(1)} %pad_maximum_fusion.refs_1_.refs_5_.refs_2_, bf16[1024,1024]{1,0:T(8,128)(2,1)S(1)} %get-tuple-element.51.refs_2_, ...), custom_call_target="tpu_custom_call" | custom-call | flops 1 | bytes 1 | tf_op jit(solution)/shard_map/scores/pallas_call | solution.py:195
  48.1 2.3 %scores.6 = (bf16[1024,384]{1,0:T(8,128)(2,1)S(1)}, bf16[512,384]{1,0:T(8,128)(2,1)S(1)}, f32[4,384]{1,0:T(4,128)S(1)}) custom-call(f32[2,16,640]{2,1,0:T(8,128)S(1)} %bias.1.refs_0_, bf16[384,1024]{1,0:T(8,128)(2,1)S(1)} %collective-permute-done.9.refs_1_.refs_6_.refs_3_, bf16[1024,1024]{1,0:T(8,128)(2,1)S(1)} %get-tuple-element.51.refs_2_, ...), custom_call_target="tpu_custom_call" | custom-call | flops 1 | bytes 1 | tf_op jit(solution)/shard_map/scores/pallas_call | solution.py:195
  50.4 0.8 collective-permute-done.8
  51.3 0.1 collective-permute-start.11
  51.3 0.5 collective-permute-start.10
  51.8 1.0 %collective-permute-done.11.refs_3_ = bf16[256,512]{1,0:T(8,128)(2,1)S(1)} collective-permute-done((bf16[256,512]{1,0:T(8,128)(2,1)S(1)}, bf16[256,512]{1,0:T(8,128)(2,1)S(1)}, u32[]{:S(2)}, u32[]{:S(2)}) %collective-permute-start.11) | collective-permute-done | bytes 262176 | tf_op jit(solution)/shard_map/ppermute | solution.py:173
  52.9 0.4 collective-permute-done.10.refs_1_
  53.2 0.3 join.5
  53.5 1.3 %scores.7 = (bf16[512,640]{1,0:T(8,128)(2,1)S(1)}, f32[2,640]{1,0:T(2,128)S(1)}) custom-call(f32[2,16,640]{2,1,0:T(8,128)S(1)} %bias.1.refs_0_, bf16[640,1024]{1,0:T(8,128)(2,1)S(1)} %pad_maximum_fusion.refs_1_.refs_5_.refs_2_, bf16[512,1024]{1,0:T(8,128)(2,1)S(1)} %get-tuple-element.60.refs_2_.refs_6_, f32[512,128]{1,0:T(8,128)S(1)} %get-tuple-element.61.refs_3_.refs_7_), custom_call_target="tpu_custom_call" | custom-call | flops 1 | bytes 1 | tf_op jit(solution)/shard_map/scores/pallas_call | solution.py:195
  54.8 0.9 scores.8
  55.7 1.7 %scores.9 = (bf16[1024,256]{1,0:T(8,128)(2,1)S(1)}, bf16[512,256]{1,0:T(8,128)(2,1)S(1)}, bf16[512,256]{1,0:T(8,128)(2,1)S(1)}, f32[16,640]{1,0:T(8,128)S(1)}) custom-call(f32[2,16,640]{2,1,0:T(8,128)S(1)} %bias.1.refs_0_, bf16[256,1024]{1,0:T(8,128)(2,1)S(1)} %collective-permute-done.4.refs_1_.refs_7_.refs_4_, ...), custom_call_target="tpu_custom_call" | custom-call | flops 1 | bytes 1 | tf_op jit(solution)/shard_map/scores/pallas_call | solution.py:195
  57.4 1.3 %collective-permute-start.12 = (f32[16,640]{1,0:T(8,128)S(1)}, f32[16,640]{1,0:T(8,128)S(1)}, u32[]{:S(2)}, u32[]{:S(2)}) collective-permute-start(f32[16,640]{1,0:T(8,128)S(1)} %get-tuple-element.64.refs_0_), channel_id=1, source_target_pairs={{0,4},{4,0},{8,12},{12,8},{1,5},{5,1},{9,13},{13,9},{2,6},{6,2},{1... | collective-permute-start | bytes 122888 | tf_op jit(solution)/shard_map/ppermute | solution.py:178
  58.7 2.8 %collective-permute-done.12.refs_1_ = f32[16,640]{1,0:T(8,128)S(1)} collective-permute-done((f32[16,640]{1,0:T(8,128)S(1)}, f32[16,640]{1,0:T(8,128)S(1)}, u32[]{:S(2)}, u32[]{:S(2)}) %collective-permute-start.12) | collective-permute-done | bytes 40992 | tf_op jit(solution)/shard_map/ppermute | solution.py:178
  61.5 1.0 %far.4 = (bf16[528,512]{1,0:T(8,128)(2,1)S(1)}, f32[16,512]{1,0:T(8,128)S(1)}) custom-call(f32[16,640]{1,0:T(8,128)S(1)} %get-tuple-element.64.refs_0_, f32[16,640]{1,0:T(8,128)S(1)} %collective-permute-done.12.refs_1_, bf16[512,640]{1,0:T(8,128)(2,1)S(1)} %get-tuple-element.68.refs_2_, bf16[512,384]{1,0:T(8,128)(2,1)S(1)} %get-tuple-element.69.refs_3_, ...), custom_call_target="tpu_custom_call" | custom-call | flops 1 | bytes 1 | tf_op jit(solution)/shard_map/far/pallas_call | solution.py:195
  62.5 0.3 collective-permute-start.14
  62.8 0.5 collective-permute-start.13
  63.3 1.0 %far.5 = (bf16[528,512]{1,0:T(8,128)(2,1)S(1)}, f32[16,512]{1,0:T(8,128)S(1)}) custom-call(f32[16,640]{1,0:T(8,128)S(1)} %get-tuple-element.64.refs_0_, f32[16,640]{1,0:T(8,128)S(1)} %collective-permute-done.12.refs_1_, bf16[512,640]{1,0:T(8,128)(2,1)S(1)} %get-tuple-element.65.refs_2_, bf16[512,384]{1,0:T(8,128)(2,1)S(1)} %get-tuple-element.66.refs_3_, ...), custom_call_target="tpu_custom_call" | custom-call | flops 1 | bytes 1 | tf_op jit(solution)/shard_map/far/pallas_call | solution.py:195
  64.3 0.4 collective-permute-done.13.refs_9_
  64.7 1.0 %near.4 = (bf16[144,512]{1,0:T(8,128)(2,1)S(1)}, bf16[192,512]{1,0:T(8,128)(2,1)S(1)}, bf16[192,512]{1,0:T(8,128)(2,1)S(1)}) custom-call(f32[16,640]{1,0:T(8,128)S(1)} %get-tuple-element.64.refs_0_, f32[16,640]{1,0:T(8,128)S(1)} %collective-permute-done.12.refs_1_, bf16[512,640]{1,0:T(8,128)(2,1)S(1)} %get-tuple-element.68.refs_2_, ...), custom_call_target="tpu_custom_call" | custom-call | flops 1 | bytes 1 | tf_op jit(solution)/shard_map/near/pallas_call | solution.py:195
  65.7 0.2 collective-permute-start.15
  65.9 1.7 %collective-permute-start.17 = (bf16[144,512]{1,0:T(8,128)(2,1)S(1)}, bf16[144,512]{1,0:T(8,128)(2,1)S(1)}, u32[]{:S(2)}, u32[]{:S(2)}) collective-permute-start(bf16[144,512]{1,0:T(8,128)(2,1)S(1)} %get-tuple-element.75.refs_10_.refs_8_), channel_id=1, source_target_pairs={{0,2},{2,0},{1,3},{3,1},{4,6},{6,4},{5,7},{7,5},{8,10},{10,8},{9,1... | collective-permute-start | bytes 442376 | tf_op jit(solution)/shard_map/ppermute | solution.py:173
  67.6 0.4 collective-permute-start.16
  68.0 1.0 %far.7 = (bf16[528,512]{1,0:T(8,128)(2,1)S(1)}, f32[16,512]{1,0:T(8,128)S(1)}) custom-call(f32[16,640]{1,0:T(8,128)S(1)} %get-tuple-element.64.refs_0_, f32[16,640]{1,0:T(8,128)S(1)} %collective-permute-done.12.refs_1_, bf16[1024,640]{1,0:T(8,128)(2,1)S(1)} %get-tuple-element.87.refs_2_, bf16[1024,384]{1,0:T(8,128)(2,1)S(1)} %get-tuple-element.88.refs_3_, ...), custom_call_target="tpu_custom_call" | custom-call | flops 1 | bytes 1 | tf_op jit(solution)/shard_map/far/pallas_call | solution.py:195
  69.0 1.0 %near.5 = (f32[144,512]{1,0:T(8,128)S(1)}, f32[192,512]{1,0:T(8,128)S(1)}, f32[192,512]{1,0:T(8,128)S(1)}) custom-call(f32[16,640]{1,0:T(8,128)S(1)} %get-tuple-element.64.refs_0_, f32[16,640]{1,0:T(8,128)S(1)} %collective-permute-done.12.refs_1_, bf16[512,640]{1,0:T(8,128)(2,1)S(1)} %get-tuple-element.65.refs_2_, ...), custom_call_target="tpu_custom_call" | custom-call | flops 1 | bytes 1 | tf_op jit(solution)/shard_map/near/pallas_call | solution.py:195
  70.0 2.6 %collective-permute-done.17.refs_1_ = bf16[144,512]{1,0:T(8,128)(2,1)S(1)} collective-permute-done((bf16[144,512]{1,0:T(8,128)(2,1)S(1)}, bf16[144,512]{1,0:T(8,128)(2,1)S(1)}, u32[]{:S(2)}, u32[]{:S(2)}) %collective-permute-start.17) | collective-permute-done | bytes 147488 | tf_op jit(solution)/shard_map/ppermute | solution.py:173
  72.7 2.4 %collective-permute-start.26 = (bf16[144,512]{1,0:T(8,128)(2,1)S(1)}, bf16[144,512]{1,0:T(8,128)(2,1)S(1)}, u32[]{:S(2)}, u32[]{:S(2)}) collective-permute-start(bf16[144,512]{1,0:T(8,128)(2,1)S(1)} %add.35.refs_2_), channel_id=1, source_target_pairs={{0,8},{4,12},{8,0},{12,4},{1,9},{5,13},{9,1},{13,5},{2,10},{6,14},... | collective-permute-start | bytes 442376 | tf_op jit(solution)/shard_map/ppermute | solution.py:178
  75.2 0.5 collective-permute-start.22
  75.7 0.1 collective-permute-start.21
  75.8 0.5 collective-permute-done.16.refs_1_
  76.3 0.2 collective-permute-done.23.refs_12_
  76.6 2.2 %collective-permute-start.27 = (bf16[192,512]{1,0:T(8,128)(2,1)S(1)}, bf16[192,512]{1,0:T(8,128)(2,1)S(1)}, u32[]{:S(2)}, u32[]{:S(2)}) collective-permute-start(bf16[192,512]{1,0:T(8,128)(2,1)S(1)} %add.36.refs_3_.refs_13_), channel_id=1, source_target_pairs={{0,8},{4,12},{8,0},{12,4},{1,9},{5,13},{9,1},{13,5},{2,10},{6,14},... | collective-permute-start | bytes 589832 | tf_op jit(solution)/shard_map/ppermute | solution.py:178
  78.7 1.0 %collective-permute-start.18 = (bf16[192,512]{1,0:T(8,128)(2,1)S(1)}, bf16[192,512]{1,0:T(8,128)(2,1)S(1)}, u32[]{:S(2)}, u32[]{:S(2)}) collective-permute-start(bf16[192,512]{1,0:T(8,128)(2,1)S(1)} %get-tuple-element.84), channel_id=1, source_target_pairs={{0,2},{2,0},{1,3},{3,1},{4,6},{6,4},{5,7},{7,5},{8,10},{10,8},{9,1... | collective-permute-start | bytes 589832 | tf_op jit(solution)/shard_map/ppermute | solution.py:173
  79.8 1.0 near.6
  80.8 1.1 %collective-permute-start.25 = (bf16[264,512]{1,0:T(8,128)(2,1)S(1)}, bf16[264,512]{1,0:T(8,128)(2,1)S(1)}, u32[]{:S(2)}, u32[]{:S(2)}) collective-permute-start(bf16[264,512]{1,0:T(8,128)(2,1)S(1)} %get-tuple-element.95), channel_id=1, source_target_pairs={{0,2},{2,0},{1,3},{3,1},{4,6},{6,4},{5,7},{7,5},{8,10},{10,8},{9,1... | collective-permute-start | bytes 811016 | tf_op jit(solution)/shard_map/ppermute | solution.py:173
  81.8 1.0 %collective-permute-start.24 = (bf16[264,512]{1,0:T(8,128)(2,1)S(1)}, bf16[264,512]{1,0:T(8,128)(2,1)S(1)}, u32[]{:S(2)}, u32[]{:S(2)}) collective-permute-start(bf16[264,512]{1,0:T(8,128)(2,1)S(1)} %get-tuple-element.94.refs_11_), channel_id=1, source_target_pairs={{0,2},{2,0},{1,3},{3,1},{4,6},{6,4},{5,7},{7,5},{8,10},{10,8},{9,1... | collective-permute-start | bytes 811016 | tf_op jit(solution)/shard_map/ppermute | solution.py:173
  82.8 0.5 energy.1
  83.3 3.2 %collective-permute-done.26.refs_0_ = bf16[144,512]{1,0:T(8,128)(2,1)S(1)} collective-permute-done((bf16[144,512]{1,0:T(8,128)(2,1)S(1)}, bf16[144,512]{1,0:T(8,128)(2,1)S(1)}, u32[]{:S(2)}, u32[]{:S(2)}) %collective-permute-start.26) | collective-permute-done | bytes 147488 | tf_op jit(solution)/shard_map/ppermute | solution.py:178
  86.6 0.1 add.37.refs_3_.refs_8_
  86.7 0.7 collective-permute-start.28
  87.4 1.0 %far.6 = (bf16[528,512]{1,0:T(8,128)(2,1)S(1)}, f32[16,512]{1,0:T(8,128)S(1)}) custom-call(f32[16,640]{1,0:T(8,128)S(1)} %get-tuple-element.64.refs_0_, f32[16,640]{1,0:T(8,128)S(1)} %collective-permute-done.12.refs_1_, bf16[1024,640]{1,0:T(8,128)(2,1)S(1)} %get-tuple-element.87.refs_2_, bf16[1024,384]{1,0:T(8,128)(2,1)S(1)} %get-tuple-element.88.refs_3_, ...), custom_call_target="tpu_custom_call" | custom-call | flops 1 | bytes 1 | tf_op jit(solution)/shard_map/far/pallas_call | solution.py:195
  88.4 0.1 collective-permute-start.19
  88.5 6.5 %collective-permute-done.27.refs_0_ = bf16[192,512]{1,0:T(8,128)(2,1)S(1)} collective-permute-done((bf16[192,512]{1,0:T(8,128)(2,1)S(1)}, bf16[192,512]{1,0:T(8,128)(2,1)S(1)}, u32[]{:S(2)}, u32[]{:S(2)}) %collective-permute-start.27) | collective-permute-done | bytes 196640 | tf_op jit(solution)/shard_map/ppermute | solution.py:178
  95.0 1.2 %place.1 = (f32[8,64]{1,0:T(8,128)S(1)}, f32[16,64]{1,0:T(8,128)S(1)}) custom-call(s32[4,10,24]{2,1,0:T(8,128)S(1)} %pad_add_fusion.refs_0_, f32[10,64]{1,0:T(8,128)S(1)} %get-tuple-element.78.refs_1_, f32[8,64]{1,0:T(8,128)S(1)} %get-tuple-element.79.refs_2_, bf16[192,512]{1,0:T(8,128)(2,1)S(1)} %add.37.refs_3_.refs_8_), custom_call_target="tpu_custom_call" | custom-call | flops 1 | bytes 1 | tf_op jit(solution)/shard_map/place/pallas_call | solution.py:195
  96.3 1.2 %near.7.refs_2_ = f32[528,512]{1,0:T(8,128)S(1)} custom-call(f32[16,640]{1,0:T(8,128)S(1)} %get-tuple-element.64.refs_0_, f32[16,640]{1,0:T(8,128)S(1)} %collective-permute-done.12.refs_1_, bf16[1024,640]{1,0:T(8,128)(2,1)S(1)} %get-tuple-element.87.refs_2_, bf16[1024,384]{1,0:T(8,128)(2,1)S(1)} %get-tuple-element.88.refs_3_, ...), custom_call_target="tpu_custom_call" | custom-call | flops 1 | bytes 1 | tf_op jit(solution)/shard_map/near/pallas_call | solution.py:195
  97.5 0.9 collective-permute-done.28.refs_7_
  98.4 1.2 %final.1 = (f32[512,512]{1,0:T(8,128)}, f32[8,64]{1,0:T(8,128)}) custom-call(f32[8,64]{1,0:T(8,128)S(1)} %get-tuple-element.85.refs_0_, f32[16,64]{1,0:T(8,128)S(1)} %get-tuple-element.86.refs_1_, f32[528,512]{1,0:T(8,128)S(1)} %near.7.refs_2_, bf16[264,512]{1,0:T(8,128)(2,1)S(1)} %collective-permute-done.24.refs_3_, ...), custom_call_target="tpu_custom_call" | custom-call | flops 1 | bytes 1 | tf_op jit(solution)/shard_map/final/pallas_call | solution.py:195
  (34 shorter events, 0.4 us)
Async XLA Ops:
  0.6 9.0 %copy-start = (f32[1024,512]{1,0:T(8,128)S(1)}, f32[1024,512]{1,0:T(8,128)}, u32[]{:S(2)}) copy-start(f32[1024,512]{1,0:T(8,128)} %refs_10_.1) | copy-start | bytes 6291460
  1.5 9.1 %collective-permute-start.1 = (s32[10,24]{1,0:T(8,128)S(1)}, s32[10,24]{1,0:T(8,128)S(1)}, u32[]{:S(2)}, u32[]{:S(2)}) collective-permute-start(s32[10,24]{1,0:T(8,128)S(1)} %get-tuple-element.109), channel_id=1, source_target_pairs={{0,8},{4,12},{8,0},{12,4},{1,9},{5,13},{9,1},{13,5},{2,10},{6,14},... | collective-permute-start | bytes 2888 | tf_op jit(solution)/shard_map/ppermute | solution.py:178
  5.6 5.0 %collective-permute-start = (s32[10,24]{1,0:T(8,128)S(1)}, s32[10,24]{1,0:T(8,128)S(1)}, u32[]{:S(2)}, u32[]{:S(2)}) collective-permute-start(s32[10,24]{1,0:T(8,128)S(1)} %get-tuple-element.109), channel_id=1, source_target_pairs={{0,4},{4,0},{8,12},{12,8},{1,5},{5,1},{9,13},{13,9},{2,6},{6,2},{1... | collective-permute-start | bytes 2888 | tf_op jit(solution)/shard_map/ppermute | solution.py:178
  7.2 5.4 %collective-permute-start.2 = (s32[10,24]{1,0:T(8,128)S(1)}, s32[10,24]{1,0:T(8,128)S(1)}, u32[]{:S(2)}, u32[]{:S(2)}) collective-permute-start(s32[10,24]{1,0:T(8,128)S(1)} %get-tuple-element.109), channel_id=1, source_target_pairs={{0,12},{4,8},{8,4},{12,0},{1,13},{5,9},{9,5},{13,1},{2,14},{6,10},... | collective-permute-start | bytes 2888 | tf_op jit(solution)/shard_map/ppermute | solution.py:178
  9.6 3.0 %collective-permute-start.3 = (bf16[640,512]{1,0:T(8,128)(2,1)}, bf16[640,512]{1,0:T(8,128)(2,1)}, u32[]{:S(2)}, u32[]{:S(2)}) collective-permute-start(bf16[640,512]{1,0:T(8,128)(2,1)} %bitcast.8), channel_id=1, source_target_pairs={{0,1},{1,0},{2,3},{3,2},{4,5},{5,4},{6,7},{7,6},{8,9},{9,8},{10,11... | collective-permute-start | bytes 1966088 | tf_op jit(solution)/shard_map/ppermute | solution.py:173
  9.9 32.6 %collective-permute-start.5 = (bf16[1024,512]{1,0:T(8,128)(2,1)S(1)}, bf16[1024,512]{1,0:T(8,128)(2,1)}, u32[]{:S(2)}, u32[]{:S(2)}) collective-permute-start(bf16[1024,512]{1,0:T(8,128)(2,1)S(1)} %multiply_convert_fusion.refs_0_), channel_id=1, source_target_pairs={{0,1},{1,0},{2,3},{3,2},{4,5},{5,4},{6,7},{7,6},{8,9},{9,8},{10,11... | collective-permute-start | bytes 3145736 | tf_op jit(solution)/shard_map/ppermute | solution.py:173
  10.5 2.2 %copy-start.1 = (bf16[1,1,10,64,512]{4,3,2,1,0:T(8,128)(2,1)S(1)}, bf16[1,1,10,64,512]{4,3,2,1,0:T(8,128)(2,1)}, u32[]{:S(2)}) copy-start(bf16[1,1,10,64,512]{4,3,2,1,0:T(8,128)(2,1)} %get-tuple-element.99) | copy-start | bytes 1966084
  12.6 24.2 %collective-permute-start.6 = (bf16[512,512]{1,0:T(8,128)(2,1)S(1)}, bf16[512,512]{1,0:T(8,128)(2,1)S(1)}, u32[]{:S(2)}, u32[]{:S(2)}) collective-permute-start(bf16[512,512]{1,0:T(8,128)(2,1)S(1)} %multiply_convert_fusion.1), channel_id=1, source_target_pairs={{0,8},{4,12},{8,0},{12,4},{1,9},{5,13},{9,1},{13,5},{2,10},{6,14},... | collective-permute-start | bytes 1572872 | tf_op jit(solution)/shard_map/ppermute | solution.py:178
  13.7 34.3 %collective-permute-start.9 = (bf16[384,1024]{1,0:T(8,128)(2,1)S(1)}, bf16[384,1024]{1,0:T(8,128)(2,1)S(1)}, u32[]{:S(2)}, u32[]{:S(2)}) collective-permute-start(bf16[384,1024]{1,0:T(8,128)(2,1)S(1)} %fusion), channel_id=1, source_target_pairs={{0,4},{4,0},{8,12},{12,8},{1,5},{5,1},{9,13},{13,9},{2,6},{6,2},{1... | collective-permute-start | bytes 2359304 | tf_op jit(solution)/shard_map/ppermute | solution.py:178
  36.9 7.4 %collective-permute-start.7 = (bf16[512,512]{1,0:T(8,128)(2,1)S(1)}, bf16[512,512]{1,0:T(8,128)(2,1)S(1)}, u32[]{:S(2)}, u32[]{:S(2)}) collective-permute-start(bf16[512,512]{1,0:T(8,128)(2,1)S(1)} %collective-permute-done.6.refs_0_), channel_id=1, source_target_pairs={{0,1},{1,0},{2,3},{3,2},{4,5},{5,4},{6,7},{7,6},{8,9},{9,8},{10,11... | collective-permute-start | bytes 1572872 | tf_op jit(solution)/shard_map/ppermute | solution.py:173
  36.9 14.3 %collective-permute-start.8 = (bf16[512,512]{1,0:T(8,128)(2,1)S(1)}, bf16[512,512]{1,0:T(8,128)(2,1)S(1)}, u32[]{:S(2)}, u32[]{:S(2)}) collective-permute-start(bf16[512,512]{1,0:T(8,128)(2,1)S(1)} %collective-permute-done.6.refs_0_), channel_id=1, source_target_pairs={{0,2},{2,0},{1,3},{3,1},{4,6},{6,4},{5,7},{7,5},{8,10},{10,8},{9,1... | collective-permute-start | bytes 1572872 | tf_op jit(solution)/shard_map/ppermute | solution.py:173
  41.2 14.5 %collective-permute-start.4 = (bf16[256,1024]{1,0:T(8,128)(2,1)S(1)}, bf16[256,1024]{1,0:T(8,128)(2,1)S(1)}, u32[]{:S(2)}, u32[]{:S(2)}) collective-permute-start(bf16[256,1024]{1,0:T(8,128)(2,1)S(1)} %fusion.1), channel_id=1, source_target_pairs={{0,4},{4,0},{8,12},{12,8},{1,5},{5,1},{9,13},{13,9},{2,6},{6,2},{1... | collective-permute-start | bytes 1572872 | tf_op jit(solution)/shard_map/ppermute | solution.py:178
  51.3 1.6 %collective-permute-start.11 = (bf16[256,512]{1,0:T(8,128)(2,1)S(1)}, bf16[256,512]{1,0:T(8,128)(2,1)S(1)}, u32[]{:S(2)}, u32[]{:S(2)}) collective-permute-start(bf16[256,512]{1,0:T(8,128)(2,1)S(1)} %get-tuple-element.106.refs_2_), channel_id=1, source_target_pairs={{0,1},{1,0},{2,3},{3,2},{4,5},{5,4},{6,7},{7,6},{8,9},{9,8},{10,11... | collective-permute-start | bytes 786440 | tf_op jit(solution)/shard_map/ppermute | solution.py:173
  51.3 1.9 %collective-permute-start.10 = (bf16[256,512]{1,0:T(8,128)(2,1)S(1)}, bf16[256,512]{1,0:T(8,128)(2,1)S(1)}, u32[]{:S(2)}, u32[]{:S(2)}) collective-permute-start(bf16[256,512]{1,0:T(8,128)(2,1)S(1)} %get-tuple-element.107.refs_0_), channel_id=1, source_target_pairs={{0,1},{1,0},{2,3},{3,2},{4,5},{5,4},{6,7},{7,6},{8,9},{9,8},{10,11... | collective-permute-start | bytes 786440 | tf_op jit(solution)/shard_map/ppermute | solution.py:173
  57.4 4.1 %collective-permute-start.12 = (f32[16,640]{1,0:T(8,128)S(1)}, f32[16,640]{1,0:T(8,128)S(1)}, u32[]{:S(2)}, u32[]{:S(2)}) collective-permute-start(f32[16,640]{1,0:T(8,128)S(1)} %get-tuple-element.64.refs_0_), channel_id=1, source_target_pairs={{0,4},{4,0},{8,12},{12,8},{1,5},{5,1},{9,13},{13,9},{2,6},{6,2},{1... | collective-permute-start | bytes 122888 | tf_op jit(solution)/shard_map/ppermute | solution.py:178
  62.5 1.8 %collective-permute-start.14 = (bf16[264,512]{1,0:T(8,128)(2,1)S(1)}, bf16[264,512]{1,0:T(8,128)(2,1)S(1)}, u32[]{:S(2)}, u32[]{:S(2)}) collective-permute-start(bf16[264,512]{1,0:T(8,128)(2,1)S(1)} %get-tuple-element.104), channel_id=1, source_target_pairs={{0,1},{1,0},{2,3},{3,2},{4,5},{5,4},{6,7},{7,6},{8,9},{9,8},{10,11... | collective-permute-start | bytes 811016 | tf_op jit(solution)/shard_map/ppermute | solution.py:173
  62.8 1.9 %collective-permute-start.13 = (bf16[264,512]{1,0:T(8,128)(2,1)S(1)}, bf16[264,512]{1,0:T(8,128)(2,1)S(1)}, u32[]{:S(2)}, u32[]{:S(2)}) collective-permute-start(bf16[264,512]{1,0:T(8,128)(2,1)S(1)} %get-tuple-element.105), channel_id=1, source_target_pairs={{0,1},{1,0},{2,3},{3,2},{4,5},{5,4},{6,7},{7,6},{8,9},{9,8},{10,11... | collective-permute-start | bytes 811016 | tf_op jit(solution)/shard_map/ppermute | solution.py:173
  65.7 3.3 %collective-permute-start.15 = (bf16[528,512]{1,0:T(8,128)(2,1)S(1)}, bf16[528,512]{1,0:T(8,128)(2,1)S(1)}, u32[]{:S(2)}, u32[]{:S(2)}) collective-permute-start(bf16[528,512]{1,0:T(8,128)(2,1)S(1)} %get-tuple-element.76.refs_11_), channel_id=1, source_target_pairs={{0,1},{1,0},{2,3},{3,2},{4,5},{5,4},{6,7},{7,6},{8,9},{9,8},{10,11... | collective-permute-start | bytes 1622024 | tf_op jit(solution)/shard_map/ppermute | solution.py:173
  65.9 6.7 %collective-permute-start.17 = (bf16[144,512]{1,0:T(8,128)(2,1)S(1)}, bf16[144,512]{1,0:T(8,128)(2,1)S(1)}, u32[]{:S(2)}, u32[]{:S(2)}) collective-permute-start(bf16[144,512]{1,0:T(8,128)(2,1)S(1)} %get-tuple-element.75.refs_10_.refs_8_), channel_id=1, source_target_pairs={{0,2},{2,0},{1,3},{3,1},{4,6},{6,4},{5,7},{7,5},{8,10},{10,8},{9,1... | collective-permute-start | bytes 442376 | tf_op jit(solution)/shard_map/ppermute | solution.py:173
  67.6 8.7 %collective-permute-start.16 = (bf16[192,512]{1,0:T(8,128)(2,1)S(1)}, bf16[192,512]{1,0:T(8,128)(2,1)S(1)}, u32[]{:S(2)}, u32[]{:S(2)}) collective-permute-start(bf16[192,512]{1,0:T(8,128)(2,1)S(1)} %get-tuple-element.83), channel_id=1, source_target_pairs={{0,2},{2,0},{1,3},{3,1},{4,6},{6,4},{5,7},{7,5},{8,10},{10,8},{9,1... | collective-permute-start | bytes 589832 | tf_op jit(solution)/shard_map/ppermute | solution.py:173
  72.7 13.9 %collective-permute-start.26 = (bf16[144,512]{1,0:T(8,128)(2,1)S(1)}, bf16[144,512]{1,0:T(8,128)(2,1)S(1)}, u32[]{:S(2)}, u32[]{:S(2)}) collective-permute-start(bf16[144,512]{1,0:T(8,128)(2,1)S(1)} %add.35.refs_2_), channel_id=1, source_target_pairs={{0,8},{4,12},{8,0},{12,4},{1,9},{5,13},{9,1},{13,5},{2,10},{6,14},... | collective-permute-start | bytes 442376 | tf_op jit(solution)/shard_map/ppermute | solution.py:178
  75.1 1.4 %collective-permute-start.23 = (bf16[132,512]{1,0:T(8,128)(2,1)S(1)}, bf16[132,512]{1,0:T(8,128)(2,1)S(1)}, u32[]{:S(2)}, u32[]{:S(2)}) collective-permute-start(bf16[132,512]{1,0:T(8,128)(2,1)S(1)} %get-tuple-element.100), channel_id=1, source_target_pairs={{0,1},{1,0},{2,3},{3,2},{4,5},{5,4},{6,7},{7,6},{8,9},{9,8},{10,11... | collective-permute-start | bytes 405512 | tf_op jit(solution)/shard_map/ppermute | solution.py:173
  75.2 3.5 %collective-permute-start.22 = (bf16[132,512]{1,0:T(8,128)(2,1)S(1)}, bf16[132,512]{1,0:T(8,128)(2,1)S(1)}, u32[]{:S(2)}, u32[]{:S(2)}) collective-permute-start(bf16[132,512]{1,0:T(8,128)(2,1)S(1)} %get-tuple-element.101), channel_id=1, source_target_pairs={{0,1},{1,0},{2,3},{3,2},{4,5},{5,4},{6,7},{7,6},{8,9},{9,8},{10,11... | collective-permute-start | bytes 405512 | tf_op jit(solution)/shard_map/ppermute | solution.py:173
  75.7 4.0 %collective-permute-start.21 = (bf16[132,512]{1,0:T(8,128)(2,1)S(1)}, bf16[132,512]{1,0:T(8,128)(2,1)S(1)}, u32[]{:S(2)}, u32[]{:S(2)}) collective-permute-start(bf16[132,512]{1,0:T(8,128)(2,1)S(1)} %get-tuple-element.102), channel_id=1, source_target_pairs={{0,1},{1,0},{2,3},{3,2},{4,5},{5,4},{6,7},{7,6},{8,9},{9,8},{10,11... | collective-permute-start | bytes 405512 | tf_op jit(solution)/shard_map/ppermute | solution.py:173
  76.3 3.5 %collective-permute-start.20 = (bf16[132,512]{1,0:T(8,128)(2,1)S(1)}, bf16[132,512]{1,0:T(8,128)(2,1)S(1)}, u32[]{:S(2)}, u32[]{:S(2)}) collective-permute-start(bf16[132,512]{1,0:T(8,128)(2,1)S(1)} %get-tuple-element.103), channel_id=1, source_target_pairs={{0,1},{1,0},{2,3},{3,2},{4,5},{5,4},{6,7},{7,6},{8,9},{9,8},{10,11... | collective-permute-start | bytes 405512 | tf_op jit(solution)/shard_map/ppermute | solution.py:173
  76.6 18.4 %collective-permute-start.27 = (bf16[192,512]{1,0:T(8,128)(2,1)S(1)}, bf16[192,512]{1,0:T(8,128)(2,1)S(1)}, u32[]{:S(2)}, u32[]{:S(2)}) collective-permute-start(bf16[192,512]{1,0:T(8,128)(2,1)S(1)} %add.36.refs_3_.refs_13_), channel_id=1, source_target_pairs={{0,8},{4,12},{8,0},{12,4},{1,9},{5,13},{9,1},{13,5},{2,10},{6,14},... | collective-permute-start | bytes 589832 | tf_op jit(solution)/shard_map/ppermute | solution.py:178
  78.7 7.9 %collective-permute-start.18 = (bf16[192,512]{1,0:T(8,128)(2,1)S(1)}, bf16[192,512]{1,0:T(8,128)(2,1)S(1)}, u32[]{:S(2)}, u32[]{:S(2)}) collective-permute-start(bf16[192,512]{1,0:T(8,128)(2,1)S(1)} %get-tuple-element.84), channel_id=1, source_target_pairs={{0,2},{2,0},{1,3},{3,1},{4,6},{6,4},{5,7},{7,5},{8,10},{10,8},{9,1... | collective-permute-start | bytes 589832 | tf_op jit(solution)/shard_map/ppermute | solution.py:173
  80.8 16.7 %collective-permute-start.25 = (bf16[264,512]{1,0:T(8,128)(2,1)S(1)}, bf16[264,512]{1,0:T(8,128)(2,1)S(1)}, u32[]{:S(2)}, u32[]{:S(2)}) collective-permute-start(bf16[264,512]{1,0:T(8,128)(2,1)S(1)} %get-tuple-element.95), channel_id=1, source_target_pairs={{0,2},{2,0},{1,3},{3,1},{4,6},{6,4},{5,7},{7,5},{8,10},{10,8},{9,1... | collective-permute-start | bytes 811016 | tf_op jit(solution)/shard_map/ppermute | solution.py:173
  81.8 15.6 %collective-permute-start.24 = (bf16[264,512]{1,0:T(8,128)(2,1)S(1)}, bf16[264,512]{1,0:T(8,128)(2,1)S(1)}, u32[]{:S(2)}, u32[]{:S(2)}) collective-permute-start(bf16[264,512]{1,0:T(8,128)(2,1)S(1)} %get-tuple-element.94.refs_11_), channel_id=1, source_target_pairs={{0,2},{2,0},{1,3},{3,1},{4,6},{6,4},{5,7},{7,5},{8,10},{10,8},{9,1... | collective-permute-start | bytes 811016 | tf_op jit(solution)/shard_map/ppermute | solution.py:173
  86.7 11.7 %collective-permute-start.28 = (bf16[192,512]{1,0:T(8,128)(2,1)S(1)}, bf16[192,512]{1,0:T(8,128)(2,1)S(1)}, u32[]{:S(2)}, u32[]{:S(2)}) collective-permute-start(bf16[192,512]{1,0:T(8,128)(2,1)S(1)} %add.37.refs_3_.refs_8_), channel_id=1, source_target_pairs={{0,8},{4,12},{8,0},{12,4},{1,9},{5,13},{9,1},{13,5},{2,10},{6,14},... | collective-permute-start | bytes 589832 | tf_op jit(solution)/shard_map/ppermute | solution.py:178
  88.4 7.9 %collective-permute-start.19 = (bf16[528,512]{1,0:T(8,128)(2,1)S(1)}, bf16[528,512]{1,0:T(8,128)(2,1)S(1)}, u32[]{:S(2)}, u32[]{:S(2)}) collective-permute-start(bf16[528,512]{1,0:T(8,128)(2,1)S(1)} %get-tuple-element.91), channel_id=1, source_target_pairs={{0,1},{1,0},{2,3},{3,2},{4,5},{5,4},{6,7},{7,6},{8,9},{9,8},{10,11... | collective-permute-start | bytes 1622024 | tf_op jit(solution)/shard_map/ppermute | solution.py:173

commit v7 on v6

--- a/solution.py
+++ b/solution.py
@@ -336,10 +336,10 @@
     return pl.ds(pl.multiple_of((rep if mine else 1 - rep) * count, count), count)
 
 
-def weighted(mine_ref, peer_ref, em_refs, x_refs, rows, cols, which, mass):
+def weighted(mine_ref, peer_ref, em_refs, x_refs, rows, cols, which, mass, skip=0):
     stats, peer = mine_ref[...], peer_ref[...]
     count = rows.size
-    total = jnp.zeros((count, cols.stop - cols.start), jnp.float32)
+    total = jnp.zeros((count - skip, cols.stop - cols.start), jnp.float32)
     masses = jnp.zeros((count, 128), jnp.float32)
     lo = 0
     for em_ref, x_ref in zip(em_refs, x_refs):
@@ -353,37 +353,36 @@
             wide = weights.astype(jnp.float32)
             for lane in range(0, size, 128):
                 masses = masses + wide[:, lane : lane + 128]
-        total = total + jnp.dot(weights, x_ref[:, cols], preferred_element_type=jnp.float32)
+        total = total + jnp.dot(weights[skip:], x_ref[:, cols], preferred_element_type=jnp.float32)
         lo += size
     return total, masses
 
 
-def far_kernel(*refs, which, mine):
+def far_kernel(*refs, which, mine, skip):
     stats_ref, peer_ref = refs[0:2]
     em_refs, x_refs, (far_ref, mass_ref) = refs[2:5], refs[5:8], refs[8:]
-    count, width = far_ref.shape[0] - PAD, far_ref.shape[1]
-    total, masses = weighted(
-        stats_ref, peer_ref, em_refs, x_refs, half_rows(mine, count, which), slice(width, 2 * width), which, True
-    )
+    count, width = far_ref.shape[0] - PAD + skip, far_ref.shape[1]
+    rows, cols = half_rows(mine, count, which), slice(width, 2 * width)
+    total, masses = weighted(stats_ref, peer_ref, em_refs, x_refs, rows, cols, which, True, skip)
     masses = jnp.broadcast_to(jnp.sum(masses, axis=1, keepdims=True), (count, 128)).T[0:PAD]
-    far_ref[0:count, :] = total.astype(jnp.bfloat16)
-    far_ref[count:, :] = masses.astype(jnp.bfloat16)
+    far_ref[0 : count - skip, :] = total.astype(jnp.bfloat16)
+    far_ref[count - skip :, :] = masses.astype(jnp.bfloat16)
     mass_ref[...] = masses
 
 
-def near_kernel(*refs, which, mine, final, outs, swaps):
+def near_kernel(*refs, which, mine, final, outs, swaps, skip):
     stats_ref, peer_ref = refs[0:2]
     em_refs, x_refs, (mass_ref, *came_refs) = refs[2:5], refs[5:8], refs[8 : 9 + swaps]
     refs = refs[9 + swaps :]
     out_refs = refs[final : final + outs]
-    count, width = sum(ref.shape[0] for ref in came_refs) - PAD, came_refs[0].shape[1]
+    count, width = sum(ref.shape[0] for ref in came_refs) - PAD + skip, came_refs[0].shape[1]
     if final:
         previous_ref, sem = refs[1 + outs :]
         copy = pltpu.make_async_copy(refs[0].at[half_rows(mine, count), :], previous_ref, sem)
         copy.start()
-    total, unused = weighted(
-        stats_ref, peer_ref, em_refs, x_refs, half_rows(mine, count, which), slice(0, width), which, False
-    )
+    rows = pl.ds(skip, count - skip) if skip else half_rows(mine, count, which)
+    total, unused = weighted(stats_ref, peer_ref, em_refs, x_refs, rows, slice(0, width), which, False)
+    count = count - skip
     came = jnp.concatenate([ref[...] for ref in came_refs]).astype(jnp.float32)
     total = total + came[0:count]
     masses = mass_ref[...] + came[count:]
@@ -399,26 +398,48 @@
     out_refs[-1][size:, :] = masses.astype(out_refs[-1].dtype)
 
 
-def far_sums(stats, peer, em, xs, which, mine, needs=()):
+def far_sums(stats, peer, em, xs, which, mine, needs=(), skip=0):
     width = xs[0].shape[1] // 2
     count = em[0].shape[0] if which else em[0].shape[0] // 2
     return call(
-        lambda *refs: far_kernel(*refs, which=which, mine=mine),
+        lambda *refs: far_kernel(*refs, which=which, mine=mine, skip=skip),
         "far",
         [VMEM] * 8,
         [stats, peer, *em, *xs],
-        [shape((count + PAD, width), jnp.bfloat16), shape((PAD, width))],
+        [shape((count - skip + PAD, width), jnp.bfloat16), shape((PAD, width))],
         needs=needs,
     )
 
 
-def near_sums(stats, peer, em, xs, which, mine, mass, came, dtype, parts=(), previous=None, needs=()):
+def lead_kernel(*refs, which, far):
+    out_ref = refs[-1]
+    count, width = out_ref.shape
+    cols = slice(width, 2 * width) if far else slice(0, width)
+    total, unused = weighted(refs[0], refs[1], refs[2:5], refs[5:8], pl.ds(0, count), cols, which, False)
+    if not far:
+        total = total + refs[8][...].astype(jnp.float32)
+    out_ref[...] = total.astype(out_ref.dtype)
+
+
+def lead_sums(stats, peer, em, xs, which, count, came=(), needs=()):
+    width = xs[0].shape[1] // 2
+    return call(
+        lambda *refs: lead_kernel(*refs, which=which, far=not came),
+        "lead",
+        [VMEM] * (8 + len(came)),
+        [stats, peer, *em, *xs, *came],
+        [shape((count, width), jnp.bfloat16)],
+        needs=needs,
+    )[0]
+
+
+def near_sums(stats, peer, em, xs, which, mine, mass, came, dtype, parts=(), previous=None, needs=(), skip=0):
     width = xs[0].shape[1] // 2
     count = em[0].shape[0] if which else em[0].shape[0] // 2
     final = previous is not None
-    sizes = list(parts) + [count + PAD - sum(parts)]
+    sizes = list(parts) + [count + PAD - skip - sum(parts)]
     return call(
-        lambda *refs: near_kernel(*refs, which=which, mine=mine, final=final, outs=len(sizes), swaps=len(came)),
+        lambda *refs: near_kernel(*refs, which=which, mine=mine, final=final, outs=len(sizes), swaps=len(came), skip=skip),
         "near",
         [VMEM] * (9 + len(came)) + [HBM] * final,
         [stats, peer, *em, *xs, mass, *came] + [previous] * final,
@@ -579,14 +600,15 @@
     half = jnp.bfloat16
     first, equal = (144,192), (264,)
 
-    far_a, mass_a = far_sums(stats, peer, em[2], xs, 2, False)
+    lead = first[0]
+    lead_far = lead_sums(stats, peer, em[2], xs, 2, lead)
+    far_a, mass_a = far_sums(stats, peer, em[2], xs, 2, False, [lead_far], lead)
     far_b, mass_b = far_sums(stats, peer, em[1], xs, 1, True, [far_a])
-    near_a = [swapped(part, "sub") for part in jnp.split(far_a, 2)]
-    sent_a = near_sums(
-        stats, peer, em[2], xs, 2, False, mass_a, near_a, half, first, needs=[far_b]
-    )
-    far_c, mass_c = far_sums(stats, peer, em[0], xs, 0, False, sent_a[:1])
-    near_c = [swapped(part, "sub") for part in jnp.split(far_c, 4)]
+    sent_a = [lead_sums(stats, peer, em[2], xs, 2, lead, [swapped(lead_far, "sub")], [far_b])]
+    near_a = [swapped(after(far_a, sent_a[0]), "sub")]
+    sent_a += near_sums(
+        stats, peer, em[2], xs, 2, False, mass_a, near_a, half, first[1:], needs=[far_b], skip=lead
+    )
     near_b = [swapped(after(far_b, sent_a[0]), "sub")]
     part_b = near_sums(
         stats, peer, em[1], xs, 1, True, mass_b, near_b, jnp.float32, first, needs=sent_a[:1]
@@ -614,6 +636,9 @@
         back, came = returned(part, swapped(sent, "rep"), backs[-1:], energies)
         backs.append(back)
         came_back.append(came)
+        if i == 0:
+            far_c, mass_c = far_sums(stats, peer, em[0], xs, 0, False, backs[:1])
+            near_c = [swapped(part, "sub") for part in jnp.split(far_c, 4)]
         if i == 1:
             sent_c = near_sums(
                 stats, peer, em[0], xs, 0, False, mass_c, near_c, half, equal, needs=[back]

time: 99.9 us -> 99.3 us (level)
  waiting for transfers between devices: 42 us -> 39 us
  starting transfers between devices: 24.4 us -> 26.2 us
    ppermute x10, waiting for transfers between devices: 36.1 us -> 31.1 us  [paired(): return lax.ppermute(value, 'wide', [(w, w ^ flip) for w in range(count)])]
    ppermute x19, waiting for transfers between devices: 5.96 us -> 7.83 us  [swapped(): return lax.ppermute(value, axis, [(0, 1), (1, 0)])]
    ppermute x19, starting transfers between devices: 9.62 us -> 11.2 us  [swapped(): return lax.ppermute(value, axis, [(0, 1), (1, 0)])]
    pallas_call x25 -> x27, Pallas kernels: 25 us -> 25.7 us  [call(): pl.pallas_call(run, in_specs=in_specs + [HBM] * len(needs), out_specs=[VM...]
  transfers between devices with their start and end apart: 29 -> 29, of which waited for: 13 -> 12; matrix products, arithmetic and copies ran while one was open for 6% -> 6% of each run, Pallas kernels for 20% -> 22%
where the time goes in v7:
time: 99.3 us; the launch traced here: 99 us
  waiting for transfers between devices  39 us (39%)
  starting transfers between devices  26.2 us (26%)
  Pallas kernels  25.7 us (26%)
  other arithmetic  4.54 us (5%)
  local copies, waits for them, and re-layouts  2.56 us (3%)
    ppermute x10, waiting for transfers between devices, paired(): return lax.ppermute(value, 'wide', [(w, w ^ flip) for w in range(count)])  31.1 us
    pallas_call x27, Pallas kernels, call(): pl.pallas_call(run, in_specs=in_specs + [HBM] * len(needs), out_specs=[VM...  25.7 us
    ppermute x10, starting transfers between devices, paired(): return lax.ppermute(value, 'wide', [(w, w ^ flip) for w in range(count)])  15 us
    ppermute x19, starting transfers between devices, swapped(): return lax.ppermute(value, axis, [(0, 1), (1, 0)])  11.2 us
    ppermute x19, waiting for transfers between devices, swapped(): return lax.ppermute(value, axis, [(0, 1), (1, 0)])  7.83 us
    concatenate x3, other arithmetic, grid_plan(): full = jnp.concatenate([own, took], axis=1)  3.28 us
    dynamic_slice x1, local copies, waits for them, and re-layouts, grid_plan(): lax.dynamic_slice_in_dim(blocks, (1 - sub) * span, span, 1)  2.44 us
  transfers between devices with their start and end apart: 29, of which 12 were waited for; matrix products, arithmetic and copies ran while one was open for 6% of the time, Pallas kernels for 22%

profile of v7, /device:TPU:0, one launch (start us, length us, event | category | flops | bytes accessed | tf_op | source)
XLA Modules:
  0.0 99.0 jit_solution(3246012269737574053)
XLA Ops:
  0.6 0.9 fusion.2
  1.5 4.1 %collective-permute-start.1 = (s32[10,24]{1,0:T(8,128)S(1)}, s32[10,24]{1,0:T(8,128)S(1)}, u32[]{:S(2)}, u32[]{:S(2)}) collective-permute-start(s32[10,24]{1,0:T(8,128)S(1)} %get-tuple-element.107), channel_id=1, source_target_pairs={{0,8},{4,12},{8,0},{12,4},{1,9},{5,13},{9,1},{13,5},{2,10},{6,14},... | collective-permute-start | bytes 2888 | tf_op jit(solution)/shard_map/ppermute | solution.py:178
  5.6 1.6 %collective-permute-start = (s32[10,24]{1,0:T(8,128)S(1)}, s32[10,24]{1,0:T(8,128)S(1)}, u32[]{:S(2)}, u32[]{:S(2)}) collective-permute-start(s32[10,24]{1,0:T(8,128)S(1)} %get-tuple-element.107), channel_id=1, source_target_pairs={{0,4},{4,0},{8,12},{12,8},{1,5},{5,1},{9,13},{13,9},{2,6},{6,2},{1... | collective-permute-start | bytes 2888 | tf_op jit(solution)/shard_map/ppermute | solution.py:178
  7.2 2.4 %constant_dynamic-slice_fusion = (bf16[1,1,10,64,512]{4,3,2,1,0:T(8,128)(2,1)}, bf16[1,1,10,64,512]{4,3,2,1,0:T(8,128)(2,1)}) fusion(bf16[1,1,10,128,512]{4,3,2,1,0:T(8,128)(2,1)} %param.5, s32[]{:T(128)S(6)} %select_n.10, s32[]{:T(128)S(6)} %select_n.9), kind=kLoop, calls=%fused_computation.12 | loop fusion | bytes 2621448 | tf_op jit(solution)/shard_map/dynamic_slice | solution.py:579
  9.6 0.3 multiply_convert_fusion.refs_0_
  9.9 0.6 collective-permute-start.5
  10.5 0.1 multiply_convert_fusion.1
  10.6 2.0 %collective-permute-done.2 = s32[10,24]{1,0:T(8,128)S(1)} collective-permute-done((s32[10,24]{1,0:T(8,128)S(1)}, s32[10,24]{1,0:T(8,128)S(1)}, u32[]{:S(2)}, u32[]{:S(2)}) %collective-permute-start.2) | collective-permute-done | bytes 992 | tf_op jit(solution)/shard_map/ppermute | solution.py:178
  12.7 1.1 %fusion = bf16[384,1024]{1,0:T(8,128)(2,1)S(1)} fusion(bf16[640,512]{1,0:T(8,128)(2,1)S(1)} %bitcast.11, bf16[640,512]{1,0:T(8,128)(2,1)} %collective-permute-done.3), kind=kLoop, calls=%fused_computation.7 | loop fusion | flops 1572864 | bytes 2097152 | tf_op jit(solution)/shard_map/concatenate | solution.py:582
  13.7 2.5 %collective-permute-start.9 = (bf16[384,1024]{1,0:T(8,128)(2,1)S(1)}, bf16[384,1024]{1,0:T(8,128)(2,1)S(1)}, u32[]{:S(2)}, u32[]{:S(2)}) collective-permute-start(bf16[384,1024]{1,0:T(8,128)(2,1)S(1)} %fusion), channel_id=1, source_target_pairs={{0,4},{4,0},{8,12},{12,8},{1,5},{5,1},{9,13},{13,9},{2,6},{6,2},{1... | collective-permute-start | bytes 2359304 | tf_op jit(solution)/shard_map/ppermute | solution.py:178
  16.2 20.6 %collective-permute-done.6.refs_0_ = bf16[512,512]{1,0:T(8,128)(2,1)S(1)} collective-permute-done((bf16[512,512]{1,0:T(8,128)(2,1)S(1)}, bf16[512,512]{1,0:T(8,128)(2,1)S(1)}, u32[]{:S(2)}, u32[]{:S(2)}) %collective-permute-start.6) | collective-permute-done | bytes 524320 | tf_op jit(solution)/shard_map/ppermute | solution.py:178
  36.9 1.7 %collective-permute-start.8 = (bf16[512,512]{1,0:T(8,128)(2,1)S(1)}, bf16[512,512]{1,0:T(8,128)(2,1)S(1)}, u32[]{:S(2)}, u32[]{:S(2)}) collective-permute-start(bf16[512,512]{1,0:T(8,128)(2,1)S(1)} %collective-permute-done.6.refs_0_), channel_id=1, source_target_pairs={{0,2},{2,0},{1,3},{3,1},{4,6},{6,4},{5,7},{7,5},{8,10},{10,8},{9,1... | collective-permute-start | bytes 1572872 | tf_op jit(solution)/shard_map/ppermute | solution.py:173
  38.5 1.6 %bias.1.refs_0_ = f32[2,16,640]{2,1,0:T(8,128)S(1)} custom-call(s32[4,10,24]{2,1,0:T(8,128)S(1)} %pad_add_fusion.refs_0_), custom_call_target="tpu_custom_call" | custom-call | flops 1 | bytes 1 | tf_op jit(solution)/shard_map/bias/pallas_call | solution.py:195
  40.2 1.0 %fusion.1 = bf16[256,1024]{1,0:T(8,128)(2,1)S(1)} fusion(bf16[640,512]{1,0:T(8,128)(2,1)S(1)} %bitcast.12, bf16[640,512]{1,0:T(8,128)(2,1)} %collective-permute-done.3), kind=kLoop, calls=%fused_computation.8 | loop fusion | flops 1048576 | bytes 1835008 | tf_op jit(solution)/shard_map/concatenate | solution.py:582
  41.2 0.1 collective-permute-start.4
  41.3 1.2 %pad_maximum_fusion.refs_1_.refs_5_.refs_2_ = bf16[640,1024]{1,0:T(8,128)(2,1)S(1)} fusion(bf16[640,512]{1,0:T(8,128)(2,1)} %collective-permute-done.3, bf16[640,512]{1,0:T(8,128)(2,1)S(1)} %bitcast.13), kind=kLoop, calls=%fused_computation.3 | loop fusion | flops 2621440 | bytes 2621440 | tf_op jit(solution)/shard_map/concatenate | solution.py:582
  42.5 1.7 %join.3 = (bf16[1024,1024]{1,0:T(8,128)(2,1)S(1)}, f32[1024,128]{1,0:T(8,128)S(1)}) custom-call(bf16[1024,512]{1,0:T(8,128)(2,1)S(1)} %multiply_convert_fusion.refs_0_, bf16[1024,512]{1,0:T(8,128)(2,1)} %collective-permute-done.5.refs_1_), custom_call_target="tpu_custom_call" | custom-call | flops 1 | bytes 1 | tf_op jit(solution)/shard_map/join/pallas_call | solution.py:195
  44.2 0.3 join.4
  44.5 3.5 %scores.5 = (bf16[1024,640]{1,0:T(8,128)(2,1)S(1)}, bf16[512,640]{1,0:T(8,128)(2,1)S(1)}, f32[4,640]{1,0:T(4,128)S(1)}) custom-call(f32[2,16,640]{2,1,0:T(8,128)S(1)} %bias.1.refs_0_, bf16[640,1024]{1,0:T(8,128)(2,1)S(1)} %pad_maximum_fusion.refs_1_.refs_5_.refs_2_, bf16[1024,1024]{1,0:T(8,128)(2,1)S(1)} %get-tuple-element.51.refs_2_, ...), custom_call_target="tpu_custom_call" | custom-call | flops 1 | bytes 1 | tf_op jit(solution)/shard_map/scores/pallas_call | solution.py:195
  48.0 2.3 %scores.6 = (bf16[1024,384]{1,0:T(8,128)(2,1)S(1)}, bf16[512,384]{1,0:T(8,128)(2,1)S(1)}, f32[4,384]{1,0:T(4,128)S(1)}) custom-call(f32[2,16,640]{2,1,0:T(8,128)S(1)} %bias.1.refs_0_, bf16[384,1024]{1,0:T(8,128)(2,1)S(1)} %collective-permute-done.9.refs_1_.refs_6_.refs_3_, bf16[1024,1024]{1,0:T(8,128)(2,1)S(1)} %get-tuple-element.51.refs_2_, ...), custom_call_target="tpu_custom_call" | custom-call | flops 1 | bytes 1 | tf_op jit(solution)/shard_map/scores/pallas_call | solution.py:195
  50.4 0.8 collective-permute-done.8
  51.2 0.1 collective-permute-start.11
  51.3 0.5 collective-permute-start.10
  51.8 1.0 %collective-permute-done.11.refs_3_ = bf16[256,512]{1,0:T(8,128)(2,1)S(1)} collective-permute-done((bf16[256,512]{1,0:T(8,128)(2,1)S(1)}, bf16[256,512]{1,0:T(8,128)(2,1)S(1)}, u32[]{:S(2)}, u32[]{:S(2)}) %collective-permute-start.11) | collective-permute-done | bytes 262176 | tf_op jit(solution)/shard_map/ppermute | solution.py:173
  52.8 0.4 collective-permute-done.10.refs_1_
  53.2 0.3 join.5
  53.5 1.3 %scores.7 = (bf16[512,640]{1,0:T(8,128)(2,1)S(1)}, f32[2,640]{1,0:T(2,128)S(1)}) custom-call(f32[2,16,640]{2,1,0:T(8,128)S(1)} %bias.1.refs_0_, bf16[640,1024]{1,0:T(8,128)(2,1)S(1)} %pad_maximum_fusion.refs_1_.refs_5_.refs_2_, bf16[512,1024]{1,0:T(8,128)(2,1)S(1)} %get-tuple-element.60.refs_2_.refs_6_, f32[512,128]{1,0:T(8,128)S(1)} %get-tuple-element.61.refs_3_.refs_7_), custom_call_target="tpu_custom_call" | custom-call | flops 1 | bytes 1 | tf_op jit(solution)/shard_map/scores/pallas_call | solution.py:195
  54.8 0.9 scores.8
  55.7 1.7 %scores.9 = (bf16[1024,256]{1,0:T(8,128)(2,1)S(1)}, bf16[512,256]{1,0:T(8,128)(2,1)S(1)}, bf16[512,256]{1,0:T(8,128)(2,1)S(1)}, f32[16,640]{1,0:T(8,128)S(1)}) custom-call(f32[2,16,640]{2,1,0:T(8,128)S(1)} %bias.1.refs_0_, bf16[256,1024]{1,0:T(8,128)(2,1)S(1)} %collective-permute-done.4.refs_1_.refs_7_.refs_4_, ...), custom_call_target="tpu_custom_call" | custom-call | flops 1 | bytes 1 | tf_op jit(solution)/shard_map/scores/pallas_call | solution.py:195
  57.4 1.3 %collective-permute-start.12 = (f32[16,640]{1,0:T(8,128)S(1)}, f32[16,640]{1,0:T(8,128)S(1)}, u32[]{:S(2)}, u32[]{:S(2)}) collective-permute-start(f32[16,640]{1,0:T(8,128)S(1)} %get-tuple-element.64.refs_0_), channel_id=1, source_target_pairs={{0,4},{4,0},{8,12},{12,8},{1,5},{5,1},{9,13},{13,9},{2,6},{6,2},{1... | collective-permute-start | bytes 122888 | tf_op jit(solution)/shard_map/ppermute | solution.py:178
  58.7 2.8 %collective-permute-done.12.refs_1_ = f32[16,640]{1,0:T(8,128)S(1)} collective-permute-done((f32[16,640]{1,0:T(8,128)S(1)}, f32[16,640]{1,0:T(8,128)S(1)}, u32[]{:S(2)}, u32[]{:S(2)}) %collective-permute-start.12) | collective-permute-done | bytes 40992 | tf_op jit(solution)/shard_map/ppermute | solution.py:178
  61.5 0.4 lead.2.refs_8_
  62.0 1.1 %far.4 = (bf16[384,512]{1,0:T(8,128)(2,1)S(1)}, f32[16,512]{1,0:T(8,128)S(1)}) custom-call(f32[16,640]{1,0:T(8,128)S(1)} %get-tuple-element.64.refs_0_, f32[16,640]{1,0:T(8,128)S(1)} %collective-permute-done.12.refs_1_, bf16[512,640]{1,0:T(8,128)(2,1)S(1)} %get-tuple-element.68.refs_2_, bf16[512,384]{1,0:T(8,128)(2,1)S(1)} %get-tuple-element.69.refs_3_, ...), custom_call_target="tpu_custom_call" | custom-call | flops 1 | bytes 1 | tf_op jit(solution)/shard_map/far/pallas_call | solution.py:195
  63.0 1.0 %far.5 = (bf16[528,512]{1,0:T(8,128)(2,1)S(1)}, f32[16,512]{1,0:T(8,128)S(1)}) custom-call(f32[16,640]{1,0:T(8,128)S(1)} %get-tuple-element.64.refs_0_, f32[16,640]{1,0:T(8,128)S(1)} %collective-permute-done.12.refs_1_, bf16[512,640]{1,0:T(8,128)(2,1)S(1)} %get-tuple-element.65.refs_2_, bf16[512,384]{1,0:T(8,128)(2,1)S(1)} %get-tuple-element.66.refs_3_, ...), custom_call_target="tpu_custom_call" | custom-call | flops 1 | bytes 1 | tf_op jit(solution)/shard_map/far/pallas_call | solution.py:195
  64.1 0.4 lead.3.refs_10_
  64.5 0.6 collective-permute-start.14
  65.1 0.1 collective-permute-start.15
  65.1 1.7 %collective-permute-start.17 = (bf16[144,512]{1,0:T(8,128)(2,1)S(1)}, bf16[144,512]{1,0:T(8,128)(2,1)S(1)}, u32[]{:S(2)}, u32[]{:S(2)}) collective-permute-start(bf16[144,512]{1,0:T(8,128)(2,1)S(1)} %lead.3.refs_10_), channel_id=1, source_target_pairs={{0,2},{2,0},{1,3},{3,1},{4,6},{6,4},{5,7},{7,5},{8,10},{10,8},{9,1... | collective-permute-start | bytes 442376 | tf_op jit(solution)/shard_map/ppermute | solution.py:173
  66.8 0.4 collective-permute-done.15.refs_9_
  67.2 0.8 near.5
  68.0 1.7 %collective-permute-start.16 = (bf16[192,512]{1,0:T(8,128)(2,1)S(1)}, bf16[192,512]{1,0:T(8,128)(2,1)S(1)}, u32[]{:S(2)}, u32[]{:S(2)}) collective-permute-start(bf16[192,512]{1,0:T(8,128)(2,1)S(1)} %get-tuple-element.83), channel_id=1, source_target_pairs={{0,2},{2,0},{1,3},{3,1},{4,6},{6,4},{5,7},{7,5},{8,10},{10,8},{9,1... | collective-permute-start | bytes 589832 | tf_op jit(solution)/shard_map/ppermute | solution.py:173
  69.7 1.0 %near.4 = (f32[144,512]{1,0:T(8,128)S(1)}, f32[192,512]{1,0:T(8,128)S(1)}, f32[192,512]{1,0:T(8,128)S(1)}) custom-call(f32[16,640]{1,0:T(8,128)S(1)} %get-tuple-element.64.refs_0_, f32[16,640]{1,0:T(8,128)S(1)} %collective-permute-done.12.refs_1_, bf16[512,640]{1,0:T(8,128)(2,1)S(1)} %get-tuple-element.65.refs_2_, ...), custom_call_target="tpu_custom_call" | custom-call | flops 1 | bytes 1 | tf_op jit(solution)/shard_map/near/pallas_call | solution.py:195
  70.7 0.9 collective-permute-done.17.refs_1_
  71.7 2.4 %collective-permute-start.26 = (bf16[144,512]{1,0:T(8,128)(2,1)S(1)}, bf16[144,512]{1,0:T(8,128)(2,1)S(1)}, u32[]{:S(2)}, u32[]{:S(2)}) collective-permute-start(bf16[144,512]{1,0:T(8,128)(2,1)S(1)} %add.35.refs_2_.refs_8_), channel_id=1, source_target_pairs={{0,8},{4,12},{8,0},{12,4},{1,9},{5,13},{9,1},{13,5},{2,10},{6,14},... | collective-permute-start | bytes 442376 | tf_op jit(solution)/shard_map/ppermute | solution.py:178
  74.1 1.0 %far.7 = (bf16[528,512]{1,0:T(8,128)(2,1)S(1)}, f32[16,512]{1,0:T(8,128)S(1)}) custom-call(f32[16,640]{1,0:T(8,128)S(1)} %get-tuple-element.64.refs_0_, f32[16,640]{1,0:T(8,128)S(1)} %collective-permute-done.12.refs_1_, bf16[1024,640]{1,0:T(8,128)(2,1)S(1)} %get-tuple-element.87.refs_2_, bf16[1024,384]{1,0:T(8,128)(2,1)S(1)} %get-tuple-element.88.refs_3_, ...), custom_call_target="tpu_custom_call" | custom-call | flops 1 | bytes 1 | tf_op jit(solution)/shard_map/far/pallas_call | solution.py:195
  75.2 0.5 collective-permute-start.22
  75.7 0.1 collective-permute-start.21
  75.8 0.4 collective-permute-start.20
  76.2 0.5 energy.1
  76.8 1.7 %collective-permute-start.27 = (bf16[192,512]{1,0:T(8,128)(2,1)S(1)}, bf16[192,512]{1,0:T(8,128)(2,1)S(1)}, u32[]{:S(2)}, u32[]{:S(2)}) collective-permute-start(bf16[192,512]{1,0:T(8,128)(2,1)S(1)} %add.36.refs_3_.refs_13_), channel_id=1, source_target_pairs={{0,8},{4,12},{8,0},{12,4},{1,9},{5,13},{9,1},{13,5},{2,10},{6,14},... | collective-permute-start | bytes 589832 | tf_op jit(solution)/shard_map/ppermute | solution.py:178
  78.6 1.0 %collective-permute-start.18 = (bf16[192,512]{1,0:T(8,128)(2,1)S(1)}, bf16[192,512]{1,0:T(8,128)(2,1)S(1)}, u32[]{:S(2)}, u32[]{:S(2)}) collective-permute-start(bf16[192,512]{1,0:T(8,128)(2,1)S(1)} %get-tuple-element.84), channel_id=1, source_target_pairs={{0,2},{2,0},{1,3},{3,1},{4,6},{6,4},{5,7},{7,5},{8,10},{10,8},{9,1... | collective-permute-start | bytes 589832 | tf_op jit(solution)/shard_map/ppermute | solution.py:173
  79.6 1.0 %near.6 = (bf16[264,512]{1,0:T(8,128)(2,1)S(1)}, bf16[264,512]{1,0:T(8,128)(2,1)S(1)}) custom-call(f32[16,640]{1,0:T(8,128)S(1)} %get-tuple-element.64.refs_0_, f32[16,640]{1,0:T(8,128)S(1)} %collective-permute-done.12.refs_1_, bf16[1024,640]{1,0:T(8,128)(2,1)S(1)} %get-tuple-element.87.refs_2_, bf16[1024,384]{1,0:T(8,128)(2,1)S(1)} %get-tuple-element.88.refs_3_, ...), custom_call_target="tpu_custom_call" | custom-call | flops 1 | bytes 1 | tf_op jit(solution)/shard_map/near/pallas_call | solution.py:195
  80.6 1.1 %collective-permute-start.25 = (bf16[264,512]{1,0:T(8,128)(2,1)S(1)}, bf16[264,512]{1,0:T(8,128)(2,1)S(1)}, u32[]{:S(2)}, u32[]{:S(2)}) collective-permute-start(bf16[264,512]{1,0:T(8,128)(2,1)S(1)} %get-tuple-element.95), channel_id=1, source_target_pairs={{0,2},{2,0},{1,3},{3,1},{4,6},{6,4},{5,7},{7,5},{8,10},{10,8},{9,1... | collective-permute-start | bytes 811016 | tf_op jit(solution)/shard_map/ppermute | solution.py:173
  81.7 1.0 %collective-permute-start.24 = (bf16[264,512]{1,0:T(8,128)(2,1)S(1)}, bf16[264,512]{1,0:T(8,128)(2,1)S(1)}, u32[]{:S(2)}, u32[]{:S(2)}) collective-permute-start(bf16[264,512]{1,0:T(8,128)(2,1)S(1)} %get-tuple-element.94.refs_11_), channel_id=1, source_target_pairs={{0,2},{2,0},{1,3},{3,1},{4,6},{6,4},{5,7},{7,5},{8,10},{10,8},{9,1... | collective-permute-start | bytes 811016 | tf_op jit(solution)/shard_map/ppermute | solution.py:173
  82.7 3.6 %collective-permute-done.18.refs_1_ = bf16[192,512]{1,0:T(8,128)(2,1)S(1)} collective-permute-done((bf16[192,512]{1,0:T(8,128)(2,1)S(1)}, bf16[192,512]{1,0:T(8,128)(2,1)S(1)}, u32[]{:S(2)}, u32[]{:S(2)}) %collective-permute-start.18) | collective-permute-done | bytes 196640 | tf_op jit(solution)/shard_map/ppermute | solution.py:173
  86.3 0.1 add.37.refs_3_.refs_8_
  86.4 1.4 %collective-permute-start.28 = (bf16[192,512]{1,0:T(8,128)(2,1)S(1)}, bf16[192,512]{1,0:T(8,128)(2,1)S(1)}, u32[]{:S(2)}, u32[]{:S(2)}) collective-permute-start(bf16[192,512]{1,0:T(8,128)(2,1)S(1)} %add.37.refs_3_.refs_8_), channel_id=1, source_target_pairs={{0,8},{4,12},{8,0},{12,4},{1,9},{5,13},{9,1},{13,5},{2,10},{6,14},... | collective-permute-start | bytes 589832 | tf_op jit(solution)/shard_map/ppermute | solution.py:178
  87.8 1.0 %far.6 = (bf16[528,512]{1,0:T(8,128)(2,1)S(1)}, f32[16,512]{1,0:T(8,128)S(1)}) custom-call(f32[16,640]{1,0:T(8,128)S(1)} %get-tuple-element.64.refs_0_, f32[16,640]{1,0:T(8,128)S(1)} %collective-permute-done.12.refs_1_, bf16[1024,640]{1,0:T(8,128)(2,1)S(1)} %get-tuple-element.87.refs_2_, bf16[1024,384]{1,0:T(8,128)(2,1)S(1)} %get-tuple-element.88.refs_3_, ...), custom_call_target="tpu_custom_call" | custom-call | flops 1 | bytes 1 | tf_op jit(solution)/shard_map/far/pallas_call | solution.py:195
  88.9 5.1 %collective-permute-done.27.refs_0_ = bf16[192,512]{1,0:T(8,128)(2,1)S(1)} collective-permute-done((bf16[192,512]{1,0:T(8,128)(2,1)S(1)}, bf16[192,512]{1,0:T(8,128)(2,1)S(1)}, u32[]{:S(2)}, u32[]{:S(2)}) %collective-permute-start.27) | collective-permute-done | bytes 196640 | tf_op jit(solution)/shard_map/ppermute | solution.py:178
  94.0 1.2 %place.1 = (f32[8,64]{1,0:T(8,128)S(1)}, f32[16,64]{1,0:T(8,128)S(1)}) custom-call(s32[4,10,24]{2,1,0:T(8,128)S(1)} %pad_add_fusion.refs_0_, f32[10,64]{1,0:T(8,128)S(1)} %get-tuple-element.76.refs_1_, f32[8,64]{1,0:T(8,128)S(1)} %get-tuple-element.77.refs_2_, bf16[192,512]{1,0:T(8,128)(2,1)S(1)} %add.37.refs_3_.refs_8_), custom_call_target="tpu_custom_call" | custom-call | flops 1 | bytes 1 | tf_op jit(solution)/shard_map/place/pallas_call | solution.py:195
  95.3 1.2 %near.7.refs_2_ = f32[528,512]{1,0:T(8,128)S(1)} custom-call(f32[16,640]{1,0:T(8,128)S(1)} %get-tuple-element.64.refs_0_, f32[16,640]{1,0:T(8,128)S(1)} %collective-permute-done.12.refs_1_, bf16[1024,640]{1,0:T(8,128)(2,1)S(1)} %get-tuple-element.87.refs_2_, bf16[1024,384]{1,0:T(8,128)(2,1)S(1)} %get-tuple-element.88.refs_3_, ...), custom_call_target="tpu_custom_call" | custom-call | flops 1 | bytes 1 | tf_op jit(solution)/shard_map/near/pallas_call | solution.py:195
  96.5 0.7 collective-permute-done.24.refs_3_
  97.2 0.6 collective-permute-done.28.refs_7_
  97.8 1.2 %final.1 = (f32[512,512]{1,0:T(8,128)}, f32[8,64]{1,0:T(8,128)}) custom-call(f32[8,64]{1,0:T(8,128)S(1)} %get-tuple-element.85.refs_0_, f32[16,64]{1,0:T(8,128)S(1)} %get-tuple-element.86.refs_1_, f32[528,512]{1,0:T(8,128)S(1)} %near.7.refs_2_, bf16[264,512]{1,0:T(8,128)(2,1)S(1)} %collective-permute-done.24.refs_3_, ...), custom_call_target="tpu_custom_call" | custom-call | flops 1 | bytes 1 | tf_op jit(solution)/shard_map/final/pallas_call | solution.py:195
  (35 shorter events, 0.5 us)
Async XLA Ops:
  0.6 9.0 %copy-start = (f32[1024,512]{1,0:T(8,128)S(1)}, f32[1024,512]{1,0:T(8,128)}, u32[]{:S(2)}) copy-start(f32[1024,512]{1,0:T(8,128)} %refs_10_.1) | copy-start | bytes 6291460
  1.5 9.1 %collective-permute-start.1 = (s32[10,24]{1,0:T(8,128)S(1)}, s32[10,24]{1,0:T(8,128)S(1)}, u32[]{:S(2)}, u32[]{:S(2)}) collective-permute-start(s32[10,24]{1,0:T(8,128)S(1)} %get-tuple-element.107), channel_id=1, source_target_pairs={{0,8},{4,12},{8,0},{12,4},{1,9},{5,13},{9,1},{13,5},{2,10},{6,14},... | collective-permute-start | bytes 2888 | tf_op jit(solution)/shard_map/ppermute | solution.py:178
  5.6 5.0 %collective-permute-start = (s32[10,24]{1,0:T(8,128)S(1)}, s32[10,24]{1,0:T(8,128)S(1)}, u32[]{:S(2)}, u32[]{:S(2)}) collective-permute-start(s32[10,24]{1,0:T(8,128)S(1)} %get-tuple-element.107), channel_id=1, source_target_pairs={{0,4},{4,0},{8,12},{12,8},{1,5},{5,1},{9,13},{13,9},{2,6},{6,2},{1... | collective-permute-start | bytes 2888 | tf_op jit(solution)/shard_map/ppermute | solution.py:178
  7.2 5.4 %collective-permute-start.2 = (s32[10,24]{1,0:T(8,128)S(1)}, s32[10,24]{1,0:T(8,128)S(1)}, u32[]{:S(2)}, u32[]{:S(2)}) collective-permute-start(s32[10,24]{1,0:T(8,128)S(1)} %get-tuple-element.107), channel_id=1, source_target_pairs={{0,12},{4,8},{8,4},{12,0},{1,13},{5,9},{9,5},{13,1},{2,14},{6,10},... | collective-permute-start | bytes 2888 | tf_op jit(solution)/shard_map/ppermute | solution.py:178
  9.6 3.0 %collective-permute-start.3 = (bf16[640,512]{1,0:T(8,128)(2,1)}, bf16[640,512]{1,0:T(8,128)(2,1)}, u32[]{:S(2)}, u32[]{:S(2)}) collective-permute-start(bf16[640,512]{1,0:T(8,128)(2,1)} %bitcast.8), channel_id=1, source_target_pairs={{0,1},{1,0},{2,3},{3,2},{4,5},{5,4},{6,7},{7,6},{8,9},{9,8},{10,11... | collective-permute-start | bytes 1966088 | tf_op jit(solution)/shard_map/ppermute | solution.py:173
  9.9 32.6 %collective-permute-start.5 = (bf16[1024,512]{1,0:T(8,128)(2,1)S(1)}, bf16[1024,512]{1,0:T(8,128)(2,1)}, u32[]{:S(2)}, u32[]{:S(2)}) collective-permute-start(bf16[1024,512]{1,0:T(8,128)(2,1)S(1)} %multiply_convert_fusion.refs_0_), channel_id=1, source_target_pairs={{0,1},{1,0},{2,3},{3,2},{4,5},{5,4},{6,7},{7,6},{8,9},{9,8},{10,11... | collective-permute-start | bytes 3145736 | tf_op jit(solution)/shard_map/ppermute | solution.py:173
  10.5 2.2 %copy-start.1 = (bf16[1,1,10,64,512]{4,3,2,1,0:T(8,128)(2,1)S(1)}, bf16[1,1,10,64,512]{4,3,2,1,0:T(8,128)(2,1)}, u32[]{:S(2)}) copy-start(bf16[1,1,10,64,512]{4,3,2,1,0:T(8,128)(2,1)} %get-tuple-element.99) | copy-start | bytes 1966084
  12.6 24.2 %collective-permute-start.6 = (bf16[512,512]{1,0:T(8,128)(2,1)S(1)}, bf16[512,512]{1,0:T(8,128)(2,1)S(1)}, u32[]{:S(2)}, u32[]{:S(2)}) collective-permute-start(bf16[512,512]{1,0:T(8,128)(2,1)S(1)} %multiply_convert_fusion.1), channel_id=1, source_target_pairs={{0,8},{4,12},{8,0},{12,4},{1,9},{5,13},{9,1},{13,5},{2,10},{6,14},... | collective-permute-start | bytes 1572872 | tf_op jit(solution)/shard_map/ppermute | solution.py:178
  13.7 34.3 %collective-permute-start.9 = (bf16[384,1024]{1,0:T(8,128)(2,1)S(1)}, bf16[384,1024]{1,0:T(8,128)(2,1)S(1)}, u32[]{:S(2)}, u32[]{:S(2)}) collective-permute-start(bf16[384,1024]{1,0:T(8,128)(2,1)S(1)} %fusion), channel_id=1, source_target_pairs={{0,4},{4,0},{8,12},{12,8},{1,5},{5,1},{9,13},{13,9},{2,6},{6,2},{1... | collective-permute-start | bytes 2359304 | tf_op jit(solution)/shard_map/ppermute | solution.py:178
  36.9 7.4 %collective-permute-start.7 = (bf16[512,512]{1,0:T(8,128)(2,1)S(1)}, bf16[512,512]{1,0:T(8,128)(2,1)S(1)}, u32[]{:S(2)}, u32[]{:S(2)}) collective-permute-start(bf16[512,512]{1,0:T(8,128)(2,1)S(1)} %collective-permute-done.6.refs_0_), channel_id=1, source_target_pairs={{0,1},{1,0},{2,3},{3,2},{4,5},{5,4},{6,7},{7,6},{8,9},{9,8},{10,11... | collective-permute-start | bytes 1572872 | tf_op jit(solution)/shard_map/ppermute | solution.py:173
  36.9 14.3 %collective-permute-start.8 = (bf16[512,512]{1,0:T(8,128)(2,1)S(1)}, bf16[512,512]{1,0:T(8,128)(2,1)S(1)}, u32[]{:S(2)}, u32[]{:S(2)}) collective-permute-start(bf16[512,512]{1,0:T(8,128)(2,1)S(1)} %collective-permute-done.6.refs_0_), channel_id=1, source_target_pairs={{0,2},{2,0},{1,3},{3,1},{4,6},{6,4},{5,7},{7,5},{8,10},{10,8},{9,1... | collective-permute-start | bytes 1572872 | tf_op jit(solution)/shard_map/ppermute | solution.py:173
  41.2 14.5 %collective-permute-start.4 = (bf16[256,1024]{1,0:T(8,128)(2,1)S(1)}, bf16[256,1024]{1,0:T(8,128)(2,1)S(1)}, u32[]{:S(2)}, u32[]{:S(2)}) collective-permute-start(bf16[256,1024]{1,0:T(8,128)(2,1)S(1)} %fusion.1), channel_id=1, source_target_pairs={{0,4},{4,0},{8,12},{12,8},{1,5},{5,1},{9,13},{13,9},{2,6},{6,2},{1... | collective-permute-start | bytes 1572872 | tf_op jit(solution)/shard_map/ppermute | solution.py:178
  51.2 1.6 %collective-permute-start.11 = (bf16[256,512]{1,0:T(8,128)(2,1)S(1)}, bf16[256,512]{1,0:T(8,128)(2,1)S(1)}, u32[]{:S(2)}, u32[]{:S(2)}) collective-permute-start(bf16[256,512]{1,0:T(8,128)(2,1)S(1)} %get-tuple-element.104.refs_2_), channel_id=1, source_target_pairs={{0,1},{1,0},{2,3},{3,2},{4,5},{5,4},{6,7},{7,6},{8,9},{9,8},{10,11... | collective-permute-start | bytes 786440 | tf_op jit(solution)/shard_map/ppermute | solution.py:173
  51.3 1.9 %collective-permute-start.10 = (bf16[256,512]{1,0:T(8,128)(2,1)S(1)}, bf16[256,512]{1,0:T(8,128)(2,1)S(1)}, u32[]{:S(2)}, u32[]{:S(2)}) collective-permute-start(bf16[256,512]{1,0:T(8,128)(2,1)S(1)} %get-tuple-element.105.refs_0_), channel_id=1, source_target_pairs={{0,1},{1,0},{2,3},{3,2},{4,5},{5,4},{6,7},{7,6},{8,9},{9,8},{10,11... | collective-permute-start | bytes 786440 | tf_op jit(solution)/shard_map/ppermute | solution.py:173
  57.4 4.1 %collective-permute-start.12 = (f32[16,640]{1,0:T(8,128)S(1)}, f32[16,640]{1,0:T(8,128)S(1)}, u32[]{:S(2)}, u32[]{:S(2)}) collective-permute-start(f32[16,640]{1,0:T(8,128)S(1)} %get-tuple-element.64.refs_0_), channel_id=1, source_target_pairs={{0,4},{4,0},{8,12},{12,8},{1,5},{5,1},{9,13},{13,9},{2,6},{6,2},{1... | collective-permute-start | bytes 122888 | tf_op jit(solution)/shard_map/ppermute | solution.py:178
  61.9 2.2 %collective-permute-start.13 = (bf16[144,512]{1,0:T(8,128)(2,1)S(1)}, bf16[144,512]{1,0:T(8,128)(2,1)S(1)}, u32[]{:S(2)}, u32[]{:S(2)}) collective-permute-start(bf16[144,512]{1,0:T(8,128)(2,1)S(1)} %lead.2.refs_8_), channel_id=1, source_target_pairs={{0,1},{1,0},{2,3},{3,2},{4,5},{5,4},{6,7},{7,6},{8,9},{9,8},{10,11... | collective-permute-start | bytes 442376 | tf_op jit(solution)/shard_map/ppermute | solution.py:173
  64.5 5.2 %collective-permute-start.14 = (bf16[528,512]{1,0:T(8,128)(2,1)S(1)}, bf16[528,512]{1,0:T(8,128)(2,1)S(1)}, u32[]{:S(2)}, u32[]{:S(2)}) collective-permute-start(bf16[528,512]{1,0:T(8,128)(2,1)S(1)} %get-tuple-element.74.refs_9_.refs_10_), channel_id=1, source_target_pairs={{0,1},{1,0},{2,3},{3,2},{4,5},{5,4},{6,7},{7,6},{8,9},{9,8},{10,11... | collective-permute-start | bytes 1622024 | tf_op jit(solution)/shard_map/ppermute | solution.py:173
  65.1 2.1 %collective-permute-start.15 = (bf16[384,512]{1,0:T(8,128)(2,1)S(1)}, bf16[384,512]{1,0:T(8,128)(2,1)S(1)}, u32[]{:S(2)}, u32[]{:S(2)}) collective-permute-start(bf16[384,512]{1,0:T(8,128)(2,1)S(1)} %get-tuple-element.80.refs_8_), channel_id=1, source_target_pairs={{0,1},{1,0},{2,3},{3,2},{4,5},{5,4},{6,7},{7,6},{8,9},{9,8},{10,11... | collective-permute-start | bytes 1179656 | tf_op jit(solution)/shard_map/ppermute | solution.py:173
  65.1 6.5 %collective-permute-start.17 = (bf16[144,512]{1,0:T(8,128)(2,1)S(1)}, bf16[144,512]{1,0:T(8,128)(2,1)S(1)}, u32[]{:S(2)}, u32[]{:S(2)}) collective-permute-start(bf16[144,512]{1,0:T(8,128)(2,1)S(1)} %lead.3.refs_10_), channel_id=1, source_target_pairs={{0,2},{2,0},{1,3},{3,1},{4,6},{6,4},{5,7},{7,5},{8,10},{10,8},{9,1... | collective-permute-start | bytes 442376 | tf_op jit(solution)/shard_map/ppermute | solution.py:173
  68.0 7.8 %collective-permute-start.16 = (bf16[192,512]{1,0:T(8,128)(2,1)S(1)}, bf16[192,512]{1,0:T(8,128)(2,1)S(1)}, u32[]{:S(2)}, u32[]{:S(2)}) collective-permute-start(bf16[192,512]{1,0:T(8,128)(2,1)S(1)} %get-tuple-element.83), channel_id=1, source_target_pairs={{0,2},{2,0},{1,3},{3,1},{4,6},{6,4},{5,7},{7,5},{8,10},{10,8},{9,1... | collective-permute-start | bytes 589832 | tf_op jit(solution)/shard_map/ppermute | solution.py:173
  71.7 11.0 %collective-permute-start.26 = (bf16[144,512]{1,0:T(8,128)(2,1)S(1)}, bf16[144,512]{1,0:T(8,128)(2,1)S(1)}, u32[]{:S(2)}, u32[]{:S(2)}) collective-permute-start(bf16[144,512]{1,0:T(8,128)(2,1)S(1)} %add.35.refs_2_.refs_8_), channel_id=1, source_target_pairs={{0,8},{4,12},{8,0},{12,4},{1,9},{5,13},{9,1},{13,5},{2,10},{6,14},... | collective-permute-start | bytes 442376 | tf_op jit(solution)/shard_map/ppermute | solution.py:178
  75.2 1.7 %collective-permute-start.23 = (bf16[132,512]{1,0:T(8,128)(2,1)S(1)}, bf16[132,512]{1,0:T(8,128)(2,1)S(1)}, u32[]{:S(2)}, u32[]{:S(2)}) collective-permute-start(bf16[132,512]{1,0:T(8,128)(2,1)S(1)} %get-tuple-element.100), channel_id=1, source_target_pairs={{0,1},{1,0},{2,3},{3,2},{4,5},{5,4},{6,7},{7,6},{8,9},{9,8},{10,11... | collective-permute-start | bytes 405512 | tf_op jit(solution)/shard_map/ppermute | solution.py:173
  75.2 3.3 %collective-permute-start.22 = (bf16[132,512]{1,0:T(8,128)(2,1)S(1)}, bf16[132,512]{1,0:T(8,128)(2,1)S(1)}, u32[]{:S(2)}, u32[]{:S(2)}) collective-permute-start(bf16[132,512]{1,0:T(8,128)(2,1)S(1)} %get-tuple-element.101), channel_id=1, source_target_pairs={{0,1},{1,0},{2,3},{3,2},{4,5},{5,4},{6,7},{7,6},{8,9},{9,8},{10,11... | collective-permute-start | bytes 405512 | tf_op jit(solution)/shard_map/ppermute | solution.py:173
  75.7 3.8 %collective-permute-start.21 = (bf16[132,512]{1,0:T(8,128)(2,1)S(1)}, bf16[132,512]{1,0:T(8,128)(2,1)S(1)}, u32[]{:S(2)}, u32[]{:S(2)}) collective-permute-start(bf16[132,512]{1,0:T(8,128)(2,1)S(1)} %get-tuple-element.102), channel_id=1, source_target_pairs={{0,1},{1,0},{2,3},{3,2},{4,5},{5,4},{6,7},{7,6},{8,9},{9,8},{10,11... | collective-permute-start | bytes 405512 | tf_op jit(solution)/shard_map/ppermute | solution.py:173
  75.8 3.7 %collective-permute-start.20 = (bf16[132,512]{1,0:T(8,128)(2,1)S(1)}, bf16[132,512]{1,0:T(8,128)(2,1)S(1)}, u32[]{:S(2)}, u32[]{:S(2)}) collective-permute-start(bf16[132,512]{1,0:T(8,128)(2,1)S(1)} %get-tuple-element.103), channel_id=1, source_target_pairs={{0,1},{1,0},{2,3},{3,2},{4,5},{5,4},{6,7},{7,6},{8,9},{9,8},{10,11... | collective-permute-start | bytes 405512 | tf_op jit(solution)/shard_map/ppermute | solution.py:173
  76.8 17.1 %collective-permute-start.27 = (bf16[192,512]{1,0:T(8,128)(2,1)S(1)}, bf16[192,512]{1,0:T(8,128)(2,1)S(1)}, u32[]{:S(2)}, u32[]{:S(2)}) collective-permute-start(bf16[192,512]{1,0:T(8,128)(2,1)S(1)} %add.36.refs_3_.refs_13_), channel_id=1, source_target_pairs={{0,8},{4,12},{8,0},{12,4},{1,9},{5,13},{9,1},{13,5},{2,10},{6,14},... | collective-permute-start | bytes 589832 | tf_op jit(solution)/shard_map/ppermute | solution.py:178
  78.6 7.7 %collective-permute-start.18 = (bf16[192,512]{1,0:T(8,128)(2,1)S(1)}, bf16[192,512]{1,0:T(8,128)(2,1)S(1)}, u32[]{:S(2)}, u32[]{:S(2)}) collective-permute-start(bf16[192,512]{1,0:T(8,128)(2,1)S(1)} %get-tuple-element.84), channel_id=1, source_target_pairs={{0,2},{2,0},{1,3},{3,1},{4,6},{6,4},{5,7},{7,5},{8,10},{10,8},{9,1... | collective-permute-start | bytes 589832 | tf_op jit(solution)/shard_map/ppermute | solution.py:173
  80.6 15.9 %collective-permute-start.25 = (bf16[264,512]{1,0:T(8,128)(2,1)S(1)}, bf16[264,512]{1,0:T(8,128)(2,1)S(1)}, u32[]{:S(2)}, u32[]{:S(2)}) collective-permute-start(bf16[264,512]{1,0:T(8,128)(2,1)S(1)} %get-tuple-element.95), channel_id=1, source_target_pairs={{0,2},{2,0},{1,3},{3,1},{4,6},{6,4},{5,7},{7,5},{8,10},{10,8},{9,1... | collective-permute-start | bytes 811016 | tf_op jit(solution)/shard_map/ppermute | solution.py:173
  81.7 15.5 %collective-permute-start.24 = (bf16[264,512]{1,0:T(8,128)(2,1)S(1)}, bf16[264,512]{1,0:T(8,128)(2,1)S(1)}, u32[]{:S(2)}, u32[]{:S(2)}) collective-permute-start(bf16[264,512]{1,0:T(8,128)(2,1)S(1)} %get-tuple-element.94.refs_11_), channel_id=1, source_target_pairs={{0,2},{2,0},{1,3},{3,1},{4,6},{6,4},{5,7},{7,5},{8,10},{10,8},{9,1... | collective-permute-start | bytes 811016 | tf_op jit(solution)/shard_map/ppermute | solution.py:173
  86.4 11.4 %collective-permute-start.28 = (bf16[192,512]{1,0:T(8,128)(2,1)S(1)}, bf16[192,512]{1,0:T(8,128)(2,1)S(1)}, u32[]{:S(2)}, u32[]{:S(2)}) collective-permute-start(bf16[192,512]{1,0:T(8,128)(2,1)S(1)} %add.37.refs_3_.refs_8_), channel_id=1, source_target_pairs={{0,8},{4,12},{8,0},{12,4},{1,9},{5,13},{9,1},{13,5},{2,10},{6,14},... | collective-permute-start | bytes 589832 | tf_op jit(solution)/shard_map/ppermute | solution.py:178
  88.8 6.5 %collective-permute-start.19 = (bf16[528,512]{1,0:T(8,128)(2,1)S(1)}, bf16[528,512]{1,0:T(8,128)(2,1)S(1)}, u32[]{:S(2)}, u32[]{:S(2)}) collective-permute-start(bf16[528,512]{1,0:T(8,128)(2,1)S(1)} %get-tuple-element.91), channel_id=1, source_target_pairs={{0,1},{1,0},{2,3},{3,2},{4,5},{5,4},{6,7},{7,6},{8,9},{9,8},{10,11... | collective-permute-start | bytes 1622024 | tf_op jit(solution)/shard_map/ppermute | solution.py:173

commit v8 on v7

--- a/solution.py
+++ b/solution.py
@@ -469,16 +469,27 @@
     out_ref[...] = came_ref[...].astype(out_ref.dtype)
 
 
-def final_kernel(energy_ref, masks_ref, sums_ref, *refs, parts):
-    rep_refs, back_refs, (out_ref, placed_ref) = refs[:parts], refs[parts:-2], refs[-2:]
+def middle_kernel(sums_ref, *refs, parts):
+    rep_refs, back_refs, out_ref = refs[:parts], refs[parts:-1], refs[-1]
+    rep = jnp.concatenate([ref[...] for ref in rep_refs]).astype(jnp.float32)
+    total = sums_ref[...] + rep
+    back = jnp.concatenate([ref[...] for ref in back_refs])
+    out_ref[0 : back.shape[0], :] = total[0 : back.shape[0]] + back
+    out_ref[back.shape[0] :, :] = total[back.shape[0] :]
+
+
+def final_kernel(energy_ref, masks_ref, sums_ref, last_ref, out_ref, placed_ref):
     count, width = out_ref.shape
     bal, span = placed_ref.shape
-    rep = jnp.concatenate([ref[...] for ref in rep_refs]).astype(jnp.float32)
-    back = jnp.concatenate([ref[...].astype(jnp.float32) for ref in back_refs])
-    total = sums_ref[...] + rep + back
-    mass = jnp.broadcast_to(total[count : count + 1], (128, count)).T
-    out_ref[...] = total[:count] / jnp.concatenate([mass] * (width // 128), axis=1)
-    came = back[count + 8 : count + 9] + back[count + 9 : count + 10] + back[count + 10 : count + 11]
+    first = sums_ref.shape[0] - last_ref.shape[0]
+    last = last_ref[...].astype(jnp.float32)
+    later = sums_ref[first:, :] + last
+    mass = jnp.broadcast_to(later[count - first : count - first + 1], (128, count)).T
+    mass = jnp.concatenate([mass] * (width // 128), axis=1)
+    out_ref[0:first, :] = sums_ref[0:first, :] / mass[0:first]
+    out_ref[first:, :] = later[: count - first] / mass[first:]
+    row = count - first + 8
+    came = last[row : row + 1] + last[row + 1 : row + 2] + last[row + 2 : row + 3]
     placed = energy_ref[...]
     placed = jnp.where(masks_ref[0:bal, :] > 0, came[:, span : 2 * span], placed)
     placed_ref[...] = jnp.where(masks_ref[bal:, :] > 0, came[:, 2 * span : 3 * span], placed)
@@ -662,11 +673,18 @@
         [shape((bal, span)), shape((2 * bal, span))],
         needs=backs[-1:],
     )
+    middle = call(
+        lambda *refs: middle_kernel(*refs, parts=len(came_c)),
+        "middle",
+        [VMEM] * (1 + len(came_c) + len(early)),
+        [part_d, *came_c, *early],
+        [shape(part_d.shape)],
+    )[0]
     fresh, energy = call(
-        lambda *refs: final_kernel(*refs, parts=len(came_c)),
+        final_kernel,
         "final",
-        [VMEM] * (4 + len(came_c) + len(early)),
-        [*placed, part_d, *came_c, *early, came_back[-1]],
+        [VMEM] * 4,
+        [*placed, middle, came_back[-1]],
         [shape((share, width)), shape((bal, span))],
     )
     return (fresh, energy.reshape(1, 1, bal, span))

time: 99.3 us -> 99.2 us (level)
    ppermute x10, waiting for transfers between devices: 31.1 us -> 28.6 us  [paired(): return lax.ppermute(value, 'wide', [(w, w ^ flip) for w in range(count)])]
    ppermute x19, waiting for transfers between devices: 7.83 us -> 9.77 us  [swapped(): return lax.ppermute(value, axis, [(0, 1), (1, 0)])]
    pallas_call x27 -> x28, Pallas kernels: 25.7 us -> 25.8 us  [call(): pl.pallas_call(run, in_specs=in_specs + [HBM] * len(needs), out_specs=[VM...]
where the time goes in v8:
time: 99.2 us; the launch traced here: 98.9 us
  waiting for transfers between devices  38.4 us (39%)
  starting transfers between devices  26.6 us (27%)
  Pallas kernels  25.8 us (26%)
  other arithmetic  4.39 us (4%)
  local copies, waits for them, and re-layouts  2.71 us (3%)
    ppermute x10, waiting for transfers between devices, paired(): return lax.ppermute(value, 'wide', [(w, w ^ flip) for w in range(count)])  28.6 us
    pallas_call x28, Pallas kernels, call(): pl.pallas_call(run, in_specs=in_specs + [HBM] * len(needs), out_specs=[VM...  25.8 us
    ppermute x10, starting transfers between devices, paired(): return lax.ppermute(value, 'wide', [(w, w ^ flip) for w in range(count)])  15.3 us
    ppermute x19, starting transfers between devices, swapped(): return lax.ppermute(value, axis, [(0, 1), (1, 0)])  11.3 us
    ppermute x19, waiting for transfers between devices, swapped(): return lax.ppermute(value, axis, [(0, 1), (1, 0)])  9.77 us
    concatenate x3, other arithmetic, grid_plan(): full = jnp.concatenate([own, took], axis=1)  3.28 us
    dynamic_slice x1, local copies, waits for them, and re-layouts, grid_plan(): lax.dynamic_slice_in_dim(blocks, (1 - sub) * span, span, 1)  2.59 us
  transfers between devices with their start and end apart: 29, of which 12 were waited for; matrix products, arithmetic and copies ran while one was open for 6% of the time, Pallas kernels for 22%

profile of v8, /device:TPU:0, one launch (start us, length us, event | category | flops | bytes accessed | tf_op | source)
XLA Modules:
  0.0 98.9 jit_solution(5766628703025182089)
XLA Ops:
  0.6 0.7 fusion.2
  1.3 4.1 %collective-permute-start.1 = (s32[10,24]{1,0:T(8,128)S(1)}, s32[10,24]{1,0:T(8,128)S(1)}, u32[]{:S(2)}, u32[]{:S(2)}) collective-permute-start(s32[10,24]{1,0:T(8,128)S(1)} %get-tuple-element.107), channel_id=1, source_target_pairs={{0,8},{4,12},{8,0},{12,4},{1,9},{5,13},{9,1},{13,5},{2,10},{6,14},... | collective-permute-start | bytes 2888 | tf_op jit(solution)/shard_map/ppermute | solution.py:178
  5.4 1.6 %collective-permute-start = (s32[10,24]{1,0:T(8,128)S(1)}, s32[10,24]{1,0:T(8,128)S(1)}, u32[]{:S(2)}, u32[]{:S(2)}) collective-permute-start(s32[10,24]{1,0:T(8,128)S(1)} %get-tuple-element.107), channel_id=1, source_target_pairs={{0,4},{4,0},{8,12},{12,8},{1,5},{5,1},{9,13},{13,9},{2,6},{6,2},{1... | collective-permute-start | bytes 2888 | tf_op jit(solution)/shard_map/ppermute | solution.py:178
  7.0 2.6 %constant_dynamic-slice_fusion = (bf16[1,1,10,64,512]{4,3,2,1,0:T(8,128)(2,1)}, bf16[1,1,10,64,512]{4,3,2,1,0:T(8,128)(2,1)}) fusion(bf16[1,1,10,128,512]{4,3,2,1,0:T(8,128)(2,1)} %param.5, s32[]{:T(128)S(6)} %select_n.10, s32[]{:T(128)S(6)} %select_n.9), kind=kLoop, calls=%fused_computation.12 | loop fusion | bytes 2621448 | tf_op jit(solution)/shard_map/dynamic_slice | solution.py:590
  9.6 0.3 multiply_convert_fusion.refs_0_
  9.9 0.6 collective-permute-start.5
  10.5 0.1 multiply_convert_fusion.1
  10.6 1.9 %collective-permute-done.2 = s32[10,24]{1,0:T(8,128)S(1)} collective-permute-done((s32[10,24]{1,0:T(8,128)S(1)}, s32[10,24]{1,0:T(8,128)S(1)}, u32[]{:S(2)}, u32[]{:S(2)}) %collective-permute-start.2) | collective-permute-done | bytes 992 | tf_op jit(solution)/shard_map/ppermute | solution.py:178
  12.5 0.1 collective-permute-start.6
  12.6 1.1 %fusion = bf16[384,1024]{1,0:T(8,128)(2,1)S(1)} fusion(bf16[640,512]{1,0:T(8,128)(2,1)S(1)} %bitcast.11, bf16[640,512]{1,0:T(8,128)(2,1)} %collective-permute-done.3), kind=kLoop, calls=%fused_computation.7 | loop fusion | flops 1572864 | bytes 2097152 | tf_op jit(solution)/shard_map/concatenate | solution.py:593
  13.7 2.5 %collective-permute-start.9 = (bf16[384,1024]{1,0:T(8,128)(2,1)S(1)}, bf16[384,1024]{1,0:T(8,128)(2,1)S(1)}, u32[]{:S(2)}, u32[]{:S(2)}) collective-permute-start(bf16[384,1024]{1,0:T(8,128)(2,1)S(1)} %fusion), channel_id=1, source_target_pairs={{0,4},{4,0},{8,12},{12,8},{1,5},{5,1},{9,13},{13,9},{2,6},{6,2},{1... | collective-permute-start | bytes 2359304 | tf_op jit(solution)/shard_map/ppermute | solution.py:178
  16.2 20.6 %collective-permute-done.6.refs_0_ = bf16[512,512]{1,0:T(8,128)(2,1)S(1)} collective-permute-done((bf16[512,512]{1,0:T(8,128)(2,1)S(1)}, bf16[512,512]{1,0:T(8,128)(2,1)S(1)}, u32[]{:S(2)}, u32[]{:S(2)}) %collective-permute-start.6) | collective-permute-done | bytes 524320 | tf_op jit(solution)/shard_map/ppermute | solution.py:178
  36.8 1.7 %collective-permute-start.8 = (bf16[512,512]{1,0:T(8,128)(2,1)S(1)}, bf16[512,512]{1,0:T(8,128)(2,1)S(1)}, u32[]{:S(2)}, u32[]{:S(2)}) collective-permute-start(bf16[512,512]{1,0:T(8,128)(2,1)S(1)} %collective-permute-done.6.refs_0_), channel_id=1, source_target_pairs={{0,2},{2,0},{1,3},{3,1},{4,6},{6,4},{5,7},{7,5},{8,10},{10,8},{9,1... | collective-permute-start | bytes 1572872 | tf_op jit(solution)/shard_map/ppermute | solution.py:173
  38.5 1.6 %bias.1.refs_0_ = f32[2,16,640]{2,1,0:T(8,128)S(1)} custom-call(s32[4,10,24]{2,1,0:T(8,128)S(1)} %pad_add_fusion.refs_0_), custom_call_target="tpu_custom_call" | custom-call | flops 1 | bytes 1 | tf_op jit(solution)/shard_map/bias/pallas_call | solution.py:195
  40.2 1.0 %fusion.1 = bf16[256,1024]{1,0:T(8,128)(2,1)S(1)} fusion(bf16[640,512]{1,0:T(8,128)(2,1)S(1)} %bitcast.12, bf16[640,512]{1,0:T(8,128)(2,1)} %collective-permute-done.3), kind=kLoop, calls=%fused_computation.8 | loop fusion | flops 1048576 | bytes 1835008 | tf_op jit(solution)/shard_map/concatenate | solution.py:593
  41.3 1.2 %pad_maximum_fusion.refs_1_.refs_5_.refs_2_ = bf16[640,1024]{1,0:T(8,128)(2,1)S(1)} fusion(bf16[640,512]{1,0:T(8,128)(2,1)} %collective-permute-done.3, bf16[640,512]{1,0:T(8,128)(2,1)S(1)} %bitcast.13), kind=kLoop, calls=%fused_computation.3 | loop fusion | flops 2621440 | bytes 2621440 | tf_op jit(solution)/shard_map/concatenate | solution.py:593
  42.5 1.7 %join.3 = (bf16[1024,1024]{1,0:T(8,128)(2,1)S(1)}, f32[1024,128]{1,0:T(8,128)S(1)}) custom-call(bf16[1024,512]{1,0:T(8,128)(2,1)S(1)} %multiply_convert_fusion.refs_0_, bf16[1024,512]{1,0:T(8,128)(2,1)} %collective-permute-done.5.refs_1_), custom_call_target="tpu_custom_call" | custom-call | flops 1 | bytes 1 | tf_op jit(solution)/shard_map/join/pallas_call | solution.py:195
  44.2 0.3 join.4
  44.5 3.5 %scores.5 = (bf16[1024,640]{1,0:T(8,128)(2,1)S(1)}, bf16[512,640]{1,0:T(8,128)(2,1)S(1)}, f32[4,640]{1,0:T(4,128)S(1)}) custom-call(f32[2,16,640]{2,1,0:T(8,128)S(1)} %bias.1.refs_0_, bf16[640,1024]{1,0:T(8,128)(2,1)S(1)} %pad_maximum_fusion.refs_1_.refs_5_.refs_2_, bf16[1024,1024]{1,0:T(8,128)(2,1)S(1)} %get-tuple-element.51.refs_2_, ...), custom_call_target="tpu_custom_call" | custom-call | flops 1 | bytes 1 | tf_op jit(solution)/shard_map/scores/pallas_call | solution.py:195
  48.0 2.3 %scores.6 = (bf16[1024,384]{1,0:T(8,128)(2,1)S(1)}, bf16[512,384]{1,0:T(8,128)(2,1)S(1)}, f32[4,384]{1,0:T(4,128)S(1)}) custom-call(f32[2,16,640]{2,1,0:T(8,128)S(1)} %bias.1.refs_0_, bf16[384,1024]{1,0:T(8,128)(2,1)S(1)} %collective-permute-done.9.refs_1_.refs_6_.refs_3_, bf16[1024,1024]{1,0:T(8,128)(2,1)S(1)} %get-tuple-element.51.refs_2_, ...), custom_call_target="tpu_custom_call" | custom-call | flops 1 | bytes 1 | tf_op jit(solution)/shard_map/scores/pallas_call | solution.py:195
  50.4 0.8 collective-permute-done.8
  51.3 0.5 collective-permute-start.10
  51.8 1.0 %collective-permute-done.11.refs_3_ = bf16[256,512]{1,0:T(8,128)(2,1)S(1)} collective-permute-done((bf16[256,512]{1,0:T(8,128)(2,1)S(1)}, bf16[256,512]{1,0:T(8,128)(2,1)S(1)}, u32[]{:S(2)}, u32[]{:S(2)}) %collective-permute-start.11) | collective-permute-done | bytes 262176 | tf_op jit(solution)/shard_map/ppermute | solution.py:173
  52.8 0.4 collective-permute-done.10.refs_1_
  53.2 0.3 join.5
  53.5 1.3 %scores.7 = (bf16[512,640]{1,0:T(8,128)(2,1)S(1)}, f32[2,640]{1,0:T(2,128)S(1)}) custom-call(f32[2,16,640]{2,1,0:T(8,128)S(1)} %bias.1.refs_0_, bf16[640,1024]{1,0:T(8,128)(2,1)S(1)} %pad_maximum_fusion.refs_1_.refs_5_.refs_2_, bf16[512,1024]{1,0:T(8,128)(2,1)S(1)} %get-tuple-element.60.refs_2_.refs_6_, f32[512,128]{1,0:T(8,128)S(1)} %get-tuple-element.61.refs_3_.refs_7_), custom_call_target="tpu_custom_call" | custom-call | flops 1 | bytes 1 | tf_op jit(solution)/shard_map/scores/pallas_call | solution.py:195
  54.7 0.9 scores.8
  55.6 1.7 %scores.9 = (bf16[1024,256]{1,0:T(8,128)(2,1)S(1)}, bf16[512,256]{1,0:T(8,128)(2,1)S(1)}, bf16[512,256]{1,0:T(8,128)(2,1)S(1)}, f32[16,640]{1,0:T(8,128)S(1)}) custom-call(f32[2,16,640]{2,1,0:T(8,128)S(1)} %bias.1.refs_0_, bf16[256,1024]{1,0:T(8,128)(2,1)S(1)} %collective-permute-done.4.refs_1_.refs_7_.refs_4_, ...), custom_call_target="tpu_custom_call" | custom-call | flops 1 | bytes 1 | tf_op jit(solution)/shard_map/scores/pallas_call | solution.py:195
  57.3 1.3 %collective-permute-start.12 = (f32[16,640]{1,0:T(8,128)S(1)}, f32[16,640]{1,0:T(8,128)S(1)}, u32[]{:S(2)}, u32[]{:S(2)}) collective-permute-start(f32[16,640]{1,0:T(8,128)S(1)} %get-tuple-element.64.refs_0_), channel_id=1, source_target_pairs={{0,4},{4,0},{8,12},{12,8},{1,5},{5,1},{9,13},{13,9},{2,6},{6,2},{1... | collective-permute-start | bytes 122888 | tf_op jit(solution)/shard_map/ppermute | solution.py:178
  58.7 2.7 %collective-permute-done.12.refs_1_ = f32[16,640]{1,0:T(8,128)S(1)} collective-permute-done((f32[16,640]{1,0:T(8,128)S(1)}, f32[16,640]{1,0:T(8,128)S(1)}, u32[]{:S(2)}, u32[]{:S(2)}) %collective-permute-start.12) | collective-permute-done | bytes 40992 | tf_op jit(solution)/shard_map/ppermute | solution.py:178
  61.4 0.4 lead.2.refs_8_
  61.9 1.1 %far.4 = (bf16[384,512]{1,0:T(8,128)(2,1)S(1)}, f32[16,512]{1,0:T(8,128)S(1)}) custom-call(f32[16,640]{1,0:T(8,128)S(1)} %get-tuple-element.64.refs_0_, f32[16,640]{1,0:T(8,128)S(1)} %collective-permute-done.12.refs_1_, bf16[512,640]{1,0:T(8,128)(2,1)S(1)} %get-tuple-element.68.refs_2_, bf16[512,384]{1,0:T(8,128)(2,1)S(1)} %get-tuple-element.69.refs_3_, ...), custom_call_target="tpu_custom_call" | custom-call | flops 1 | bytes 1 | tf_op jit(solution)/shard_map/far/pallas_call | solution.py:195
  63.0 1.0 %far.5 = (bf16[528,512]{1,0:T(8,128)(2,1)S(1)}, f32[16,512]{1,0:T(8,128)S(1)}) custom-call(f32[16,640]{1,0:T(8,128)S(1)} %get-tuple-element.64.refs_0_, f32[16,640]{1,0:T(8,128)S(1)} %collective-permute-done.12.refs_1_, bf16[512,640]{1,0:T(8,128)(2,1)S(1)} %get-tuple-element.65.refs_2_, bf16[512,384]{1,0:T(8,128)(2,1)S(1)} %get-tuple-element.66.refs_3_, ...), custom_call_target="tpu_custom_call" | custom-call | flops 1 | bytes 1 | tf_op jit(solution)/shard_map/far/pallas_call | solution.py:195
  64.0 0.4 lead.3.refs_10_
  64.5 0.6 collective-permute-start.14
  65.0 0.1 collective-permute-start.15
  65.1 1.7 %collective-permute-start.17 = (bf16[144,512]{1,0:T(8,128)(2,1)S(1)}, bf16[144,512]{1,0:T(8,128)(2,1)S(1)}, u32[]{:S(2)}, u32[]{:S(2)}) collective-permute-start(bf16[144,512]{1,0:T(8,128)(2,1)S(1)} %lead.3.refs_10_), channel_id=1, source_target_pairs={{0,2},{2,0},{1,3},{3,1},{4,6},{6,4},{5,7},{7,5},{8,10},{10,8},{9,1... | collective-permute-start | bytes 442376 | tf_op jit(solution)/shard_map/ppermute | solution.py:173
  66.8 0.3 collective-permute-done.15.refs_9_
  67.1 0.8 near.5
  67.9 1.8 %collective-permute-start.16 = (bf16[192,512]{1,0:T(8,128)(2,1)S(1)}, bf16[192,512]{1,0:T(8,128)(2,1)S(1)}, u32[]{:S(2)}, u32[]{:S(2)}) collective-permute-start(bf16[192,512]{1,0:T(8,128)(2,1)S(1)} %get-tuple-element.83), channel_id=1, source_target_pairs={{0,2},{2,0},{1,3},{3,1},{4,6},{6,4},{5,7},{7,5},{8,10},{10,8},{9,1... | collective-permute-start | bytes 589832 | tf_op jit(solution)/shard_map/ppermute | solution.py:173
  69.7 1.0 %near.4 = (f32[144,512]{1,0:T(8,128)S(1)}, f32[192,512]{1,0:T(8,128)S(1)}, f32[192,512]{1,0:T(8,128)S(1)}) custom-call(f32[16,640]{1,0:T(8,128)S(1)} %get-tuple-element.64.refs_0_, f32[16,640]{1,0:T(8,128)S(1)} %collective-permute-done.12.refs_1_, bf16[512,640]{1,0:T(8,128)(2,1)S(1)} %get-tuple-element.65.refs_2_, ...), custom_call_target="tpu_custom_call" | custom-call | flops 1 | bytes 1 | tf_op jit(solution)/shard_map/near/pallas_call | solution.py:195
  70.7 0.8 collective-permute-done.17.refs_1_
  71.6 2.4 %collective-permute-start.26 = (bf16[144,512]{1,0:T(8,128)(2,1)S(1)}, bf16[144,512]{1,0:T(8,128)(2,1)S(1)}, u32[]{:S(2)}, u32[]{:S(2)}) collective-permute-start(bf16[144,512]{1,0:T(8,128)(2,1)S(1)} %add.35.refs_2_.refs_8_), channel_id=1, source_target_pairs={{0,8},{4,12},{8,0},{12,4},{1,9},{5,13},{9,1},{13,5},{2,10},{6,14},... | collective-permute-start | bytes 442376 | tf_op jit(solution)/shard_map/ppermute | solution.py:178
  74.0 1.0 %far.7 = (bf16[528,512]{1,0:T(8,128)(2,1)S(1)}, f32[16,512]{1,0:T(8,128)S(1)}) custom-call(f32[16,640]{1,0:T(8,128)S(1)} %get-tuple-element.64.refs_0_, f32[16,640]{1,0:T(8,128)S(1)} %collective-permute-done.12.refs_1_, bf16[1024,640]{1,0:T(8,128)(2,1)S(1)} %get-tuple-element.87.refs_2_, bf16[1024,384]{1,0:T(8,128)(2,1)S(1)} %get-tuple-element.88.refs_3_, ...), custom_call_target="tpu_custom_call" | custom-call | flops 1 | bytes 1 | tf_op jit(solution)/shard_map/far/pallas_call | solution.py:195
  75.2 0.5 collective-permute-start.22
  75.7 0.1 collective-permute-start.21
  75.8 0.4 collective-permute-start.20
  76.2 0.5 energy.1
  76.8 1.7 %collective-permute-start.27 = (bf16[192,512]{1,0:T(8,128)(2,1)S(1)}, bf16[192,512]{1,0:T(8,128)(2,1)S(1)}, u32[]{:S(2)}, u32[]{:S(2)}) collective-permute-start(bf16[192,512]{1,0:T(8,128)(2,1)S(1)} %add.36.refs_3_.refs_13_), channel_id=1, source_target_pairs={{0,8},{4,12},{8,0},{12,4},{1,9},{5,13},{9,1},{13,5},{2,10},{6,14},... | collective-permute-start | bytes 589832 | tf_op jit(solution)/shard_map/ppermute | solution.py:178
  78.5 1.0 %collective-permute-start.18 = (bf16[192,512]{1,0:T(8,128)(2,1)S(1)}, bf16[192,512]{1,0:T(8,128)(2,1)S(1)}, u32[]{:S(2)}, u32[]{:S(2)}) collective-permute-start(bf16[192,512]{1,0:T(8,128)(2,1)S(1)} %get-tuple-element.84), channel_id=1, source_target_pairs={{0,2},{2,0},{1,3},{3,1},{4,6},{6,4},{5,7},{7,5},{8,10},{10,8},{9,1... | collective-permute-start | bytes 589832 | tf_op jit(solution)/shard_map/ppermute | solution.py:173
  79.6 1.0 %near.6 = (bf16[264,512]{1,0:T(8,128)(2,1)S(1)}, bf16[264,512]{1,0:T(8,128)(2,1)S(1)}) custom-call(f32[16,640]{1,0:T(8,128)S(1)} %get-tuple-element.64.refs_0_, f32[16,640]{1,0:T(8,128)S(1)} %collective-permute-done.12.refs_1_, bf16[1024,640]{1,0:T(8,128)(2,1)S(1)} %get-tuple-element.87.refs_2_, bf16[1024,384]{1,0:T(8,128)(2,1)S(1)} %get-tuple-element.88.refs_3_, ...), custom_call_target="tpu_custom_call" | custom-call | flops 1 | bytes 1 | tf_op jit(solution)/shard_map/near/pallas_call | solution.py:195
  80.6 1.1 %collective-permute-start.25 = (bf16[264,512]{1,0:T(8,128)(2,1)S(1)}, bf16[264,512]{1,0:T(8,128)(2,1)S(1)}, u32[]{:S(2)}, u32[]{:S(2)}) collective-permute-start(bf16[264,512]{1,0:T(8,128)(2,1)S(1)} %get-tuple-element.95), channel_id=1, source_target_pairs={{0,2},{2,0},{1,3},{3,1},{4,6},{6,4},{5,7},{7,5},{8,10},{10,8},{9,1... | collective-permute-start | bytes 811016 | tf_op jit(solution)/shard_map/ppermute | solution.py:173
  81.7 1.0 %collective-permute-start.24 = (bf16[264,512]{1,0:T(8,128)(2,1)S(1)}, bf16[264,512]{1,0:T(8,128)(2,1)S(1)}, u32[]{:S(2)}, u32[]{:S(2)}) collective-permute-start(bf16[264,512]{1,0:T(8,128)(2,1)S(1)} %get-tuple-element.94.refs_11_), channel_id=1, source_target_pairs={{0,2},{2,0},{1,3},{3,1},{4,6},{6,4},{5,7},{7,5},{8,10},{10,8},{9,1... | collective-permute-start | bytes 811016 | tf_op jit(solution)/shard_map/ppermute | solution.py:173
  82.7 3.6 %collective-permute-done.18.refs_1_ = bf16[192,512]{1,0:T(8,128)(2,1)S(1)} collective-permute-done((bf16[192,512]{1,0:T(8,128)(2,1)S(1)}, bf16[192,512]{1,0:T(8,128)(2,1)S(1)}, u32[]{:S(2)}, u32[]{:S(2)}) %collective-permute-start.18) | collective-permute-done | bytes 196640 | tf_op jit(solution)/shard_map/ppermute | solution.py:173
  86.3 0.1 add.37.refs_3_.refs_8_
  86.4 1.4 %collective-permute-start.28 = (bf16[192,512]{1,0:T(8,128)(2,1)S(1)}, bf16[192,512]{1,0:T(8,128)(2,1)S(1)}, u32[]{:S(2)}, u32[]{:S(2)}) collective-permute-start(bf16[192,512]{1,0:T(8,128)(2,1)S(1)} %add.37.refs_3_.refs_8_), channel_id=1, source_target_pairs={{0,8},{4,12},{8,0},{12,4},{1,9},{5,13},{9,1},{13,5},{2,10},{6,14},... | collective-permute-start | bytes 589832 | tf_op jit(solution)/shard_map/ppermute | solution.py:178
  87.7 1.0 %far.6 = (bf16[528,512]{1,0:T(8,128)(2,1)S(1)}, f32[16,512]{1,0:T(8,128)S(1)}) custom-call(f32[16,640]{1,0:T(8,128)S(1)} %get-tuple-element.64.refs_0_, f32[16,640]{1,0:T(8,128)S(1)} %collective-permute-done.12.refs_1_, bf16[1024,640]{1,0:T(8,128)(2,1)S(1)} %get-tuple-element.87.refs_2_, bf16[1024,384]{1,0:T(8,128)(2,1)S(1)} %get-tuple-element.88.refs_3_, ...), custom_call_target="tpu_custom_call" | custom-call | flops 1 | bytes 1 | tf_op jit(solution)/shard_map/far/pallas_call | solution.py:195
  88.8 3.0 %collective-permute-done.27.refs_0_ = bf16[192,512]{1,0:T(8,128)(2,1)S(1)} collective-permute-done((bf16[192,512]{1,0:T(8,128)(2,1)S(1)}, bf16[192,512]{1,0:T(8,128)(2,1)S(1)}, u32[]{:S(2)}, u32[]{:S(2)}) %collective-permute-start.27) | collective-permute-done | bytes 196640 | tf_op jit(solution)/shard_map/ppermute | solution.py:178
  91.9 1.2 %place.1 = (f32[8,64]{1,0:T(8,128)S(1)}, f32[16,64]{1,0:T(8,128)S(1)}) custom-call(s32[4,10,24]{2,1,0:T(8,128)S(1)} %pad_add_fusion.refs_0_, f32[10,64]{1,0:T(8,128)S(1)} %get-tuple-element.76.refs_1_, f32[8,64]{1,0:T(8,128)S(1)} %get-tuple-element.77.refs_2_, bf16[192,512]{1,0:T(8,128)(2,1)S(1)} %add.37.refs_3_.refs_8_), custom_call_target="tpu_custom_call" | custom-call | flops 1 | bytes 1 | tf_op jit(solution)/shard_map/place/pallas_call | solution.py:195
  93.1 1.2 %near.7.refs_0_ = f32[528,512]{1,0:T(8,128)S(1)} custom-call(f32[16,640]{1,0:T(8,128)S(1)} %get-tuple-element.64.refs_0_, f32[16,640]{1,0:T(8,128)S(1)} %collective-permute-done.12.refs_1_, bf16[1024,640]{1,0:T(8,128)(2,1)S(1)} %get-tuple-element.87.refs_2_, bf16[1024,384]{1,0:T(8,128)(2,1)S(1)} %get-tuple-element.88.refs_3_, ...), custom_call_target="tpu_custom_call" | custom-call | flops 1 | bytes 1 | tf_op jit(solution)/shard_map/near/pallas_call | solution.py:195
  94.3 2.8 %collective-permute-done.24.refs_1_ = bf16[264,512]{1,0:T(8,128)(2,1)S(1)} collective-permute-done((bf16[264,512]{1,0:T(8,128)(2,1)S(1)}, bf16[264,512]{1,0:T(8,128)(2,1)S(1)}, u32[]{:S(2)}, u32[]{:S(2)}) %collective-permute-start.24) | collective-permute-done | bytes 270368 | tf_op jit(solution)/shard_map/ppermute | solution.py:173
  97.2 0.1 middle.1.refs_2_
  97.3 0.4 collective-permute-done.28.refs_3_
  97.7 1.1 %final.1 = (f32[512,512]{1,0:T(8,128)}, f32[8,64]{1,0:T(8,128)}) custom-call(f32[8,64]{1,0:T(8,128)S(1)} %get-tuple-element.85.refs_0_, f32[16,64]{1,0:T(8,128)S(1)} %get-tuple-element.86.refs_1_, f32[528,512]{1,0:T(8,128)S(1)} %middle.1.refs_2_, bf16[192,512]{1,0:T(8,128)(2,1)S(1)} %collective-permute-done.28.refs_3_), custom_call_target="tpu_custom_call" | custom-call | flops 1 | bytes 1 | tf_op jit(solution)/shard_map/final/pallas_call | solution.py:195
  (36 shorter events, 0.7 us)
Async XLA Ops:
  1.3 9.3 %collective-permute-start.1 = (s32[10,24]{1,0:T(8,128)S(1)}, s32[10,24]{1,0:T(8,128)S(1)}, u32[]{:S(2)}, u32[]{:S(2)}) collective-permute-start(s32[10,24]{1,0:T(8,128)S(1)} %get-tuple-element.107), channel_id=1, source_target_pairs={{0,8},{4,12},{8,0},{12,4},{1,9},{5,13},{9,1},{13,5},{2,10},{6,14},... | collective-permute-start | bytes 2888 | tf_op jit(solution)/shard_map/ppermute | solution.py:178
  5.4 5.2 %collective-permute-start = (s32[10,24]{1,0:T(8,128)S(1)}, s32[10,24]{1,0:T(8,128)S(1)}, u32[]{:S(2)}, u32[]{:S(2)}) collective-permute-start(s32[10,24]{1,0:T(8,128)S(1)} %get-tuple-element.107), channel_id=1, source_target_pairs={{0,4},{4,0},{8,12},{12,8},{1,5},{5,1},{9,13},{13,9},{2,6},{6,2},{1... | collective-permute-start | bytes 2888 | tf_op jit(solution)/shard_map/ppermute | solution.py:178
  7.0 5.4 %collective-permute-start.2 = (s32[10,24]{1,0:T(8,128)S(1)}, s32[10,24]{1,0:T(8,128)S(1)}, u32[]{:S(2)}, u32[]{:S(2)}) collective-permute-start(s32[10,24]{1,0:T(8,128)S(1)} %get-tuple-element.107), channel_id=1, source_target_pairs={{0,12},{4,8},{8,4},{12,0},{1,13},{5,9},{9,5},{13,1},{2,14},{6,10},... | collective-permute-start | bytes 2888 | tf_op jit(solution)/shard_map/ppermute | solution.py:178
  7.0 2.6 %copy-start = (f32[1024,512]{1,0:T(8,128)S(1)}, f32[1024,512]{1,0:T(8,128)}, u32[]{:S(2)}) copy-start(f32[1024,512]{1,0:T(8,128)} %refs_10_.1) | copy-start | bytes 6291460
  9.6 3.0 %collective-permute-start.3 = (bf16[640,512]{1,0:T(8,128)(2,1)}, bf16[640,512]{1,0:T(8,128)(2,1)}, u32[]{:S(2)}, u32[]{:S(2)}) collective-permute-start(bf16[640,512]{1,0:T(8,128)(2,1)} %bitcast.8), channel_id=1, source_target_pairs={{0,1},{1,0},{2,3},{3,2},{4,5},{5,4},{6,7},{7,6},{8,9},{9,8},{10,11... | collective-permute-start | bytes 1966088 | tf_op jit(solution)/shard_map/ppermute | solution.py:173
  9.9 32.6 %collective-permute-start.5 = (bf16[1024,512]{1,0:T(8,128)(2,1)S(1)}, bf16[1024,512]{1,0:T(8,128)(2,1)}, u32[]{:S(2)}, u32[]{:S(2)}) collective-permute-start(bf16[1024,512]{1,0:T(8,128)(2,1)S(1)} %multiply_convert_fusion.refs_0_), channel_id=1, source_target_pairs={{0,1},{1,0},{2,3},{3,2},{4,5},{5,4},{6,7},{7,6},{8,9},{9,8},{10,11... | collective-permute-start | bytes 3145736 | tf_op jit(solution)/shard_map/ppermute | solution.py:173
  10.5 2.2 %copy-start.1 = (bf16[1,1,10,64,512]{4,3,2,1,0:T(8,128)(2,1)S(1)}, bf16[1,1,10,64,512]{4,3,2,1,0:T(8,128)(2,1)}, u32[]{:S(2)}) copy-start(bf16[1,1,10,64,512]{4,3,2,1,0:T(8,128)(2,1)} %get-tuple-element.99) | copy-start | bytes 1966084
  12.5 24.3 %collective-permute-start.6 = (bf16[512,512]{1,0:T(8,128)(2,1)S(1)}, bf16[512,512]{1,0:T(8,128)(2,1)S(1)}, u32[]{:S(2)}, u32[]{:S(2)}) collective-permute-start(bf16[512,512]{1,0:T(8,128)(2,1)S(1)} %multiply_convert_fusion.1), channel_id=1, source_target_pairs={{0,8},{4,12},{8,0},{12,4},{1,9},{5,13},{9,1},{13,5},{2,10},{6,14},... | collective-permute-start | bytes 1572872 | tf_op jit(solution)/shard_map/ppermute | solution.py:178
  13.7 34.3 %collective-permute-start.9 = (bf16[384,1024]{1,0:T(8,128)(2,1)S(1)}, bf16[384,1024]{1,0:T(8,128)(2,1)S(1)}, u32[]{:S(2)}, u32[]{:S(2)}) collective-permute-start(bf16[384,1024]{1,0:T(8,128)(2,1)S(1)} %fusion), channel_id=1, source_target_pairs={{0,4},{4,0},{8,12},{12,8},{1,5},{5,1},{9,13},{13,9},{2,6},{6,2},{1... | collective-permute-start | bytes 2359304 | tf_op jit(solution)/shard_map/ppermute | solution.py:178
  36.8 7.4 %collective-permute-start.7 = (bf16[512,512]{1,0:T(8,128)(2,1)S(1)}, bf16[512,512]{1,0:T(8,128)(2,1)S(1)}, u32[]{:S(2)}, u32[]{:S(2)}) collective-permute-start(bf16[512,512]{1,0:T(8,128)(2,1)S(1)} %collective-permute-done.6.refs_0_), channel_id=1, source_target_pairs={{0,1},{1,0},{2,3},{3,2},{4,5},{5,4},{6,7},{7,6},{8,9},{9,8},{10,11... | collective-permute-start | bytes 1572872 | tf_op jit(solution)/shard_map/ppermute | solution.py:173
  36.8 14.3 %collective-permute-start.8 = (bf16[512,512]{1,0:T(8,128)(2,1)S(1)}, bf16[512,512]{1,0:T(8,128)(2,1)S(1)}, u32[]{:S(2)}, u32[]{:S(2)}) collective-permute-start(bf16[512,512]{1,0:T(8,128)(2,1)S(1)} %collective-permute-done.6.refs_0_), channel_id=1, source_target_pairs={{0,2},{2,0},{1,3},{3,1},{4,6},{6,4},{5,7},{7,5},{8,10},{10,8},{9,1... | collective-permute-start | bytes 1572872 | tf_op jit(solution)/shard_map/ppermute | solution.py:173
  41.2 14.4 %collective-permute-start.4 = (bf16[256,1024]{1,0:T(8,128)(2,1)S(1)}, bf16[256,1024]{1,0:T(8,128)(2,1)S(1)}, u32[]{:S(2)}, u32[]{:S(2)}) collective-permute-start(bf16[256,1024]{1,0:T(8,128)(2,1)S(1)} %fusion.1), channel_id=1, source_target_pairs={{0,4},{4,0},{8,12},{12,8},{1,5},{5,1},{9,13},{13,9},{2,6},{6,2},{1... | collective-permute-start | bytes 1572872 | tf_op jit(solution)/shard_map/ppermute | solution.py:178
  51.2 1.6 %collective-permute-start.11 = (bf16[256,512]{1,0:T(8,128)(2,1)S(1)}, bf16[256,512]{1,0:T(8,128)(2,1)S(1)}, u32[]{:S(2)}, u32[]{:S(2)}) collective-permute-start(bf16[256,512]{1,0:T(8,128)(2,1)S(1)} %get-tuple-element.104.refs_2_), channel_id=1, source_target_pairs={{0,1},{1,0},{2,3},{3,2},{4,5},{5,4},{6,7},{7,6},{8,9},{9,8},{10,11... | collective-permute-start | bytes 786440 | tf_op jit(solution)/shard_map/ppermute | solution.py:173
  51.3 1.9 %collective-permute-start.10 = (bf16[256,512]{1,0:T(8,128)(2,1)S(1)}, bf16[256,512]{1,0:T(8,128)(2,1)S(1)}, u32[]{:S(2)}, u32[]{:S(2)}) collective-permute-start(bf16[256,512]{1,0:T(8,128)(2,1)S(1)} %get-tuple-element.105.refs_0_), channel_id=1, source_target_pairs={{0,1},{1,0},{2,3},{3,2},{4,5},{5,4},{6,7},{7,6},{8,9},{9,8},{10,11... | collective-permute-start | bytes 786440 | tf_op jit(solution)/shard_map/ppermute | solution.py:173
  57.3 4.1 %collective-permute-start.12 = (f32[16,640]{1,0:T(8,128)S(1)}, f32[16,640]{1,0:T(8,128)S(1)}, u32[]{:S(2)}, u32[]{:S(2)}) collective-permute-start(f32[16,640]{1,0:T(8,128)S(1)} %get-tuple-element.64.refs_0_), channel_id=1, source_target_pairs={{0,4},{4,0},{8,12},{12,8},{1,5},{5,1},{9,13},{13,9},{2,6},{6,2},{1... | collective-permute-start | bytes 122888 | tf_op jit(solution)/shard_map/ppermute | solution.py:178
  61.8 2.2 %collective-permute-start.13 = (bf16[144,512]{1,0:T(8,128)(2,1)S(1)}, bf16[144,512]{1,0:T(8,128)(2,1)S(1)}, u32[]{:S(2)}, u32[]{:S(2)}) collective-permute-start(bf16[144,512]{1,0:T(8,128)(2,1)S(1)} %lead.2.refs_8_), channel_id=1, source_target_pairs={{0,1},{1,0},{2,3},{3,2},{4,5},{5,4},{6,7},{7,6},{8,9},{9,8},{10,11... | collective-permute-start | bytes 442376 | tf_op jit(solution)/shard_map/ppermute | solution.py:173
  64.5 5.3 %collective-permute-start.14 = (bf16[528,512]{1,0:T(8,128)(2,1)S(1)}, bf16[528,512]{1,0:T(8,128)(2,1)S(1)}, u32[]{:S(2)}, u32[]{:S(2)}) collective-permute-start(bf16[528,512]{1,0:T(8,128)(2,1)S(1)} %get-tuple-element.74.refs_9_.refs_10_), channel_id=1, source_target_pairs={{0,1},{1,0},{2,3},{3,2},{4,5},{5,4},{6,7},{7,6},{8,9},{9,8},{10,11... | collective-permute-start | bytes 1622024 | tf_op jit(solution)/shard_map/ppermute | solution.py:173
  65.0 2.1 %collective-permute-start.15 = (bf16[384,512]{1,0:T(8,128)(2,1)S(1)}, bf16[384,512]{1,0:T(8,128)(2,1)S(1)}, u32[]{:S(2)}, u32[]{:S(2)}) collective-permute-start(bf16[384,512]{1,0:T(8,128)(2,1)S(1)} %get-tuple-element.80.refs_8_), channel_id=1, source_target_pairs={{0,1},{1,0},{2,3},{3,2},{4,5},{5,4},{6,7},{7,6},{8,9},{9,8},{10,11... | collective-permute-start | bytes 1179656 | tf_op jit(solution)/shard_map/ppermute | solution.py:173
  65.1 6.5 %collective-permute-start.17 = (bf16[144,512]{1,0:T(8,128)(2,1)S(1)}, bf16[144,512]{1,0:T(8,128)(2,1)S(1)}, u32[]{:S(2)}, u32[]{:S(2)}) collective-permute-start(bf16[144,512]{1,0:T(8,128)(2,1)S(1)} %lead.3.refs_10_), channel_id=1, source_target_pairs={{0,2},{2,0},{1,3},{3,1},{4,6},{6,4},{5,7},{7,5},{8,10},{10,8},{9,1... | collective-permute-start | bytes 442376 | tf_op jit(solution)/shard_map/ppermute | solution.py:173
  67.9 7.9 %collective-permute-start.16 = (bf16[192,512]{1,0:T(8,128)(2,1)S(1)}, bf16[192,512]{1,0:T(8,128)(2,1)S(1)}, u32[]{:S(2)}, u32[]{:S(2)}) collective-permute-start(bf16[192,512]{1,0:T(8,128)(2,1)S(1)} %get-tuple-element.83), channel_id=1, source_target_pairs={{0,2},{2,0},{1,3},{3,1},{4,6},{6,4},{5,7},{7,5},{8,10},{10,8},{9,1... | collective-permute-start | bytes 589832 | tf_op jit(solution)/shard_map/ppermute | solution.py:173
  71.6 11.1 %collective-permute-start.26 = (bf16[144,512]{1,0:T(8,128)(2,1)S(1)}, bf16[144,512]{1,0:T(8,128)(2,1)S(1)}, u32[]{:S(2)}, u32[]{:S(2)}) collective-permute-start(bf16[144,512]{1,0:T(8,128)(2,1)S(1)} %add.35.refs_2_.refs_8_), channel_id=1, source_target_pairs={{0,8},{4,12},{8,0},{12,4},{1,9},{5,13},{9,1},{13,5},{2,10},{6,14},... | collective-permute-start | bytes 442376 | tf_op jit(solution)/shard_map/ppermute | solution.py:178
  75.1 1.7 %collective-permute-start.23 = (bf16[132,512]{1,0:T(8,128)(2,1)S(1)}, bf16[132,512]{1,0:T(8,128)(2,1)S(1)}, u32[]{:S(2)}, u32[]{:S(2)}) collective-permute-start(bf16[132,512]{1,0:T(8,128)(2,1)S(1)} %get-tuple-element.100), channel_id=1, source_target_pairs={{0,1},{1,0},{2,3},{3,2},{4,5},{5,4},{6,7},{7,6},{8,9},{9,8},{10,11... | collective-permute-start | bytes 405512 | tf_op jit(solution)/shard_map/ppermute | solution.py:173
  75.2 3.3 %collective-permute-start.22 = (bf16[132,512]{1,0:T(8,128)(2,1)S(1)}, bf16[132,512]{1,0:T(8,128)(2,1)S(1)}, u32[]{:S(2)}, u32[]{:S(2)}) collective-permute-start(bf16[132,512]{1,0:T(8,128)(2,1)S(1)} %get-tuple-element.101), channel_id=1, source_target_pairs={{0,1},{1,0},{2,3},{3,2},{4,5},{5,4},{6,7},{7,6},{8,9},{9,8},{10,11... | collective-permute-start | bytes 405512 | tf_op jit(solution)/shard_map/ppermute | solution.py:173
  75.7 3.8 %collective-permute-start.21 = (bf16[132,512]{1,0:T(8,128)(2,1)S(1)}, bf16[132,512]{1,0:T(8,128)(2,1)S(1)}, u32[]{:S(2)}, u32[]{:S(2)}) collective-permute-start(bf16[132,512]{1,0:T(8,128)(2,1)S(1)} %get-tuple-element.102), channel_id=1, source_target_pairs={{0,1},{1,0},{2,3},{3,2},{4,5},{5,4},{6,7},{7,6},{8,9},{9,8},{10,11... | collective-permute-start | bytes 405512 | tf_op jit(solution)/shard_map/ppermute | solution.py:173
  75.8 3.8 %collective-permute-start.20 = (bf16[132,512]{1,0:T(8,128)(2,1)S(1)}, bf16[132,512]{1,0:T(8,128)(2,1)S(1)}, u32[]{:S(2)}, u32[]{:S(2)}) collective-permute-start(bf16[132,512]{1,0:T(8,128)(2,1)S(1)} %get-tuple-element.103), channel_id=1, source_target_pairs={{0,1},{1,0},{2,3},{3,2},{4,5},{5,4},{6,7},{7,6},{8,9},{9,8},{10,11... | collective-permute-start | bytes 405512 | tf_op jit(solution)/shard_map/ppermute | solution.py:173
  76.8 15.0 %collective-permute-start.27 = (bf16[192,512]{1,0:T(8,128)(2,1)S(1)}, bf16[192,512]{1,0:T(8,128)(2,1)S(1)}, u32[]{:S(2)}, u32[]{:S(2)}) collective-permute-start(bf16[192,512]{1,0:T(8,128)(2,1)S(1)} %add.36.refs_3_.refs_13_), channel_id=1, source_target_pairs={{0,8},{4,12},{8,0},{12,4},{1,9},{5,13},{9,1},{13,5},{2,10},{6,14},... | collective-permute-start | bytes 589832 | tf_op jit(solution)/shard_map/ppermute | solution.py:178
  78.5 7.7 %collective-permute-start.18 = (bf16[192,512]{1,0:T(8,128)(2,1)S(1)}, bf16[192,512]{1,0:T(8,128)(2,1)S(1)}, u32[]{:S(2)}, u32[]{:S(2)}) collective-permute-start(bf16[192,512]{1,0:T(8,128)(2,1)S(1)} %get-tuple-element.84), channel_id=1, source_target_pairs={{0,2},{2,0},{1,3},{3,1},{4,6},{6,4},{5,7},{7,5},{8,10},{10,8},{9,1... | collective-permute-start | bytes 589832 | tf_op jit(solution)/shard_map/ppermute | solution.py:173
  80.6 13.8 %collective-permute-start.25 = (bf16[264,512]{1,0:T(8,128)(2,1)S(1)}, bf16[264,512]{1,0:T(8,128)(2,1)S(1)}, u32[]{:S(2)}, u32[]{:S(2)}) collective-permute-start(bf16[264,512]{1,0:T(8,128)(2,1)S(1)} %get-tuple-element.95), channel_id=1, source_target_pairs={{0,2},{2,0},{1,3},{3,1},{4,6},{6,4},{5,7},{7,5},{8,10},{10,8},{9,1... | collective-permute-start | bytes 811016 | tf_op jit(solution)/shard_map/ppermute | solution.py:173
  81.7 15.5 %collective-permute-start.24 = (bf16[264,512]{1,0:T(8,128)(2,1)S(1)}, bf16[264,512]{1,0:T(8,128)(2,1)S(1)}, u32[]{:S(2)}, u32[]{:S(2)}) collective-permute-start(bf16[264,512]{1,0:T(8,128)(2,1)S(1)} %get-tuple-element.94.refs_11_), channel_id=1, source_target_pairs={{0,2},{2,0},{1,3},{3,1},{4,6},{6,4},{5,7},{7,5},{8,10},{10,8},{9,1... | collective-permute-start | bytes 811016 | tf_op jit(solution)/shard_map/ppermute | solution.py:173
  86.4 11.4 %collective-permute-start.28 = (bf16[192,512]{1,0:T(8,128)(2,1)S(1)}, bf16[192,512]{1,0:T(8,128)(2,1)S(1)}, u32[]{:S(2)}, u32[]{:S(2)}) collective-permute-start(bf16[192,512]{1,0:T(8,128)(2,1)S(1)} %add.37.refs_3_.refs_8_), channel_id=1, source_target_pairs={{0,8},{4,12},{8,0},{12,4},{1,9},{5,13},{9,1},{13,5},{2,10},{6,14},... | collective-permute-start | bytes 589832 | tf_op jit(solution)/shard_map/ppermute | solution.py:178
  88.8 4.4 %collective-permute-start.19 = (bf16[528,512]{1,0:T(8,128)(2,1)S(1)}, bf16[528,512]{1,0:T(8,128)(2,1)S(1)}, u32[]{:S(2)}, u32[]{:S(2)}) collective-permute-start(bf16[528,512]{1,0:T(8,128)(2,1)S(1)} %get-tuple-element.91), channel_id=1, source_target_pairs={{0,1},{1,0},{2,3},{3,2},{4,5},{5,4},{6,7},{7,6},{8,9},{9,8},{10,11... | collective-permute-start | bytes 1622024 | tf_op jit(solution)/shard_map/ppermute | solution.py:173
